TPU v7x, 32 devices: a whole 2x2x4 slice. The times are simulated.
32 devices in a mesh: groups: 2 (over x), pts: 4 (over y, core), feat: 4 (over z).
Axes of the slice: x: 2, y: 2, z: 4, core: 2. Of those that a mesh axis runs over, the one named last changes fastest.
Arguments:
- points: bfloat16 [16384, 256], P(('groups', 'pts')), parts along dimension 0, may hold values from -6 to 6
- picks: int32 [2, 4096], P(None, ('groups', 'pts')), parts along dimension 1, may hold values from 0 to 2047, as said below
- omega: bfloat16 [256, 32768], P(None, 'feat'), may hold values from -1 to 1
- phase: float32 [32768], P('feat'), may hold values from -3.140625 to 3.140625
- weights: bfloat16 [65536, 256], P(('groups', 'feat')), parts along dimension 0, may hold values from -3 to 3
- counts: int32 [2, 4096, 256], P(None, ('groups', 'pts')), parts along dimension 1, may hold values from 0 to 2
- master: float32 [8, 8192, 256], P(('groups', 'feat'), 'pts'), parts along dimension 0, may hold values from -0.06 to 0.06
- moment_one: float32 [8, 8192, 256], P(('groups', 'feat'), 'pts'), parts along dimension 0, may hold values from -1.8 to 1.8
- moment_two: float32 [8, 8192, 256], P(('groups', 'feat'), 'pts'), parts along dimension 0, may hold values from 1 to 20
- task_cov: bfloat16 [256, 256], replicated, may hold values from -1 to 3, as said below
Outputs:
- log_rates: float32 [2, 4096, 256], P(None, ('groups', 'pts')), parts along dimension 1
- new_master: float32 [8, 8192, 256], P(('groups', 'feat'), 'pts'), parts along dimension 0
- new_first: float32 [8, 8192, 256], P(('groups', 'feat'), 'pts'), parts along dimension 0
- new_second: float32 [8, 8192, 256], P(('groups', 'feat'), 'pts'), parts along dimension 0
- new_working: bfloat16 [65536, 256], P(('groups', 'feat')), parts along dimension 0
There are 2 independent parts, one for each index of `groups`. A program takes and returns all parts, laid end to end along the dimension named above; an argument that names none is the same for every part. Nothing has to cross between parts.
Inputs may be any that keep to these rules, and one draw needn't show every extreme that they name: picks[m, i] names a point among the 2048 points of the same pts index as point i. `task_cov`: symmetric, diagonal entries between 1 and 3, entries off the diagonal at most 1 in magnitude.
All inputs are finite; a program needn't handle non-finite values.
Results may differ from a plain program's by a relative error of at most 0.0055.
Values may be sent and summed in bfloat16 or wider, within the bound.
No kernel may reach another device: no remote copies, remote signals or barrier semaphores. Data moves between devices by JAX's collectives and lax.ppermute only.
A program may use at most 128 MiB of HBM per device.

v0:
```python
import math

import jax
import jax.numpy as jnp
from jax import lax
from jax.sharding import PartitionSpec as P

F = 32768
STEP = 20


beta_one = 0.9
beta_two = 0.999
learn_rate = 0.2


def features_for(points, chosen_index, omega, phase):
    chosen = jnp.take(points, chosen_index, axis=0)
    angle = jnp.dot(chosen, omega, preferred_element_type=jnp.float32) + phase
    return (math.sqrt(2.0 / F) * jnp.cos(angle)).astype(jnp.bfloat16)


def rates_for(feature_rows, weights, observed):
    partial_value = jnp.dot(feature_rows, weights, preferred_element_type=jnp.float32)
    log_rate = lax.psum(partial_value, "feat")
    residual = (jnp.exp(log_rate) - observed.astype(jnp.float32)).astype(jnp.bfloat16)
    return (log_rate, residual)


def row_term(feature_rows, residual):
    return lax.dot_general(
        feature_rows, residual, (((0,), (0,)), ((), ())), preferred_element_type=jnp.float32
    )


def share_for(feature_rows, residual):
    return lax.psum_scatter(
        row_term(feature_rows, residual).astype(jnp.bfloat16),
        "pts",
        scatter_dimension=0,
        tiled=True,
    ).astype(jnp.float32)


def body(points, picks, omega, phase, weights, counts, master, moment_one, moment_two, task_cov):
    features_zero = features_for(points, picks[0], omega, phase)
    rate_zero, residual_zero = rates_for(features_zero, weights, counts[0])
    share_zero = share_for(features_zero, residual_zero)
    features_one = features_for(points, picks[1], omega, phase)
    rate_one, residual_one = rates_for(features_one, weights, counts[1])
    share_one = share_for(features_one, residual_one)
    gradient = share_zero + share_one + master[0]
    conditioned = jnp.dot(
        gradient.astype(jnp.bfloat16), task_cov, preferred_element_type=jnp.float32
    )
    correction_one = 1.0 - beta_one**STEP
    correction_two = 1.0 - beta_two**STEP
    new_first = beta_one * moment_one[0] + (1.0 - beta_one) * conditioned
    new_second = beta_two * moment_two[0] + (1.0 - beta_two) * conditioned * conditioned
    new_master = master[0] - learn_rate * (new_first / correction_one) / (
        jnp.sqrt(new_second / correction_two) + 1e-08
    )
    new_working = lax.all_gather(new_master.astype(jnp.bfloat16), "pts", axis=0, tiled=True)
    log_rates = jnp.stack([rate_zero, rate_one])
    return (log_rates, new_master[None], new_first[None], new_second[None], new_working)


def solution(mesh):
    placed = (
        P(("groups", "pts"), None),
        P(None, ("groups", "pts")),
        P(None, "feat"),
        P("feat"),
        P(("groups", "feat"), None),
        P(None, ("groups", "pts"), None),
        P(("groups", "feat"), "pts", None),
        P(("groups", "feat"), "pts", None),
        P(("groups", "feat"), "pts", None),
        P(),
    )
    return jax.shard_map(
        body,
        mesh=mesh,
        in_specs=placed,
        out_specs=(
            P(None, ("groups", "pts"), None),
            P(("groups", "feat"), "pts", None),
            P(("groups", "feat"), "pts", None),
            P(("groups", "feat"), "pts", None),
            P(("groups", "feat"), None),
        ),
        check_vma=False,
    )
```

profile of v0, /device:TPU:0, one launch (start us, length us, event | category | flops | bytes accessed | tf_op | source)
XLA Modules:
  0.0 348.0 jit_solution(10739109388799823845)
XLA Ops:
  7.2 0.0 copy-start
  7.2 0.0 copy-start.7
  7.2 0.0 all-reduce.3.cloned.1.call-start
  7.2 0.8 fusion.19
  8.1 0.3 copy-done
  8.4 1.9 gather_fusion.1
  10.4 2.0 gather_fusion
  12.3 0.0 copy-done.7
  12.4 0.0 copy-start.4
  12.4 57.6 %multiply_convert_fusion.1 = bf16[512,8192]{1,0:T(8,128)(2,1)S(1)} fusion(bf16[256,8192]{1,0:T(8,128)(2,1)} %param.14, f32[8192]{0:T(1024)S(1)} %copy-done.7, bf16[512,256]{1,0:T(8,128)(2,1)S(1)} %gather_fusion, pred[512]{0:T(512)(128)(4,1)S(1)} %compare_and_fusion.1), kind=kOutput, calls=%fused_computation.3 | convolution fusion | flops 2160197632 | bytes 12878336 | tf_op jit(solution)/shard_map/dot_general | solution.py:19
  70.0 0.0 copy-done.4
  70.0 0.0 copy-start.8
  70.0 0.0 copy-start.3
  70.0 3.1 fusion.22
  73.1 1.3 copy-done.8
  74.5 0.9 copy-done.3
  75.3 57.7 %multiply_convert_fusion = bf16[512,8192]{1,0:T(8,128)(2,1)S(1)} fusion(bf16[256,8192]{1,0:T(8,128)(2,1)S(1)} %copy-done.3, f32[8192]{0:T(1024)S(1)} %copy-done.7, bf16[512,256]{1,0:T(8,128)(2,1)S(1)} %gather_fusion.1, pred[512]{0:T(512)(128)(4,1)S(1)} %compare_and_fusion), kind=kOutput, calls=%fused_computation.2 | convolution fusion | flops 2160197632 | bytes 12878336 | tf_op jit(solution)/shard_map/dot_general | solution.py:19
  133.1 0.0 copy-start.9
  133.1 3.2 copy-done.9
  136.3 0.0 copy-start.5
  136.3 3.1 fusion.23
  139.4 0.0 all-reduce.3.cloned.1.call-update
  139.4 0.3 reduce-scatter.5.cloned.1.call-start
  139.7 54.8 %all-reduce.3.cloned.1.call-done = (f32[512,256]{1,0:T(8,128)}, f32[512,256]{1,0:T(8,128)}) async-done(((f32[512,256]{1,0:T(8,128)}, f32[512,256]{1,0:T(8,128)}), (f32[512,256]{1,0:T(8,128)}, f32[512,256]{1,0:T(8,128)})) %all-reduce.3.cloned.1.call-update) | async-done | bytes 1048592 | tf_op jit(solution)/shard_map/psum | solution.py:25
  194.5 0.0 copy-done.5
  194.5 7.9 %convolution_convert_fusion = bf16[8192,256]{1,0:T(8,128)(2,1)} fusion(bf16[512,8192]{1,0:T(8,128)(2,1)} %copy-done.9, s32[2,512,256]{2,1,0:T(8,128)S(1)} %copy-done.5, f32[512,256]{1,0:T(8,128)} %get-tuple-element.6), kind=kOutput, calls=%fused_computation.4 | convolution fusion | flops 2149974016 | bytes 13631488 | tf_op jit(solution)/shard_map/dot_general | solution.py:31
  202.4 0.0 copy-start.2
  202.4 0.0 reduce-scatter.5.cloned.1.call-update
  202.4 0.0 reduce-scatter.3.cloned.1.call-start
  202.5 1.0 copy-done.2
  203.4 8.1 %convolution_convert_fusion.1 = bf16[8192,256]{1,0:T(8,128)(2,1)} fusion(bf16[512,8192]{1,0:T(8,128)(2,1)} %copy-done.8, s32[2,512,256]{2,1,0:T(8,128)S(1)} %copy-done.5, f32[512,256]{1,0:T(8,128)S(1)} %copy-done.2), kind=kOutput, calls=%fused_computation.5 | convolution fusion | flops 2149974016 | bytes 13631488 | tf_op jit(solution)/shard_map/dot_general | solution.py:31
  211.5 0.0 copy-start.6
  211.5 0.0 reduce-scatter.3.cloned.1.call-update
  211.6 0.0 copy-start.1
  211.6 0.0 all-gather.2.cloned.1.call-start
  211.6 34.8 %reduce-scatter.5.cloned.1.call-done = bf16[2048,256]{1,0:T(8,128)(2,1)} async-done(((bf16[8192,256]{1,0:T(8,128)(2,1)}), bf16[2048,256]{1,0:T(8,128)(2,1)}) %reduce-scatter.5.cloned.1.call-update) | async-done | bytes 1048592 | tf_op jit(solution)/shard_map/reduce_scatter | solution.py:37
  246.4 47.0 %reduce-scatter.3.cloned.1.call-done = bf16[2048,256]{1,0:T(8,128)(2,1)} async-done(((bf16[8192,256]{1,0:T(8,128)(2,1)}), bf16[2048,256]{1,0:T(8,128)(2,1)}) %reduce-scatter.3.cloned.1.call-update) | async-done | bytes 1048592 | tf_op jit(solution)/shard_map/reduce_scatter | solution.py:37
  293.5 0.0 copy-done.6
  293.5 8.9 %fusion.18 = (bf16[2048,256]{1,0:T(8,128)(2,1)}, f32[2048,256]{1,0:T(8,128)}, f32[1,2048,256]{2,1,0:T(8,128)}, f32[1,2048,256]{2,1,0:T(8,128)}) fusion(f32[1,2048,256]{2,1,0:T(8,128)} %param.20, f32[1,2048,256]{2,1,0:T(8,128)} %param.19, f32[1,2048,256]{2,1,0:T(8,128)} %param.18, bf16[256,256]{1,0:T(8,128)(2,1)S(1)} %copy-done.6, ...), kind=kOutput, calls=%fused_computation.34 | convolution fusion | flops 277872640 | bytes 15859712 | tf_op jit(solution)/shard_map/dot_general | solution.py:53
  302.4 0.0 all-gather.2.cloned.1.call-update
  302.4 0.0 copy-done.1
  302.4 1.0 pad_maximum_fusion
  303.4 33.6 %all-gather.2.cloned.1.call-done = bf16[8192,256]{1,0:T(8,128)(2,1)} async-done(((bf16[2048,256]{1,0:T(8,128)(2,1)}), bf16[8192,256]{1,0:T(8,128)(2,1)}) %all-gather.2.cloned.1.call-update) | async-done | bytes 4194320 | tf_op jit(solution)/shard_map/all_gather | solution.py:63
  337.0 4.5 %copy.18 = bf16[8192,256]{1,0:T(8,128)(2,1)} copy(bf16[8192,256]{1,0:T(8,128)(2,1)} %all-gather.2.cloned.1.call-done) | data formatting | bytes 8388608
  (6 shorter events, 0.0 us)
Async XLA Ops:
  7.2 1.3 copy-start
  7.2 5.2 %copy-start.7 = (f32[8192]{0:T(1024)S(1)}, f32[8192]{0:T(1024)}, u32[]{:S(2)}) copy-start(f32[8192]{0:T(1024)} %param.15) | copy-start | bytes 98308
  7.2 187.3 %all-reduce.3.cloned.1.call-start = ((), (), s32[]{:S(2)}) async-start(), calls=%async_computation.5 | async-start | bytes 2097152 | tf_op jit(solution)/shard_map/psum | solution.py:25
  12.4 57.6 %copy-start.4 = (bf16[8192,256]{1,0:T(8,128)(2,1)S(1)}, bf16[8192,256]{1,0:T(8,128)(2,1)}, u32[]{:S(2)}) copy-start(bf16[8192,256]{1,0:T(8,128)(2,1)} %param.16) | copy-start | bytes 12582916
  70.0 4.5 %copy-start.8 = (bf16[512,8192]{1,0:T(8,128)(2,1)}, bf16[512,8192]{1,0:T(8,128)(2,1)S(1)}, u32[]{:S(2)}) copy-start(bf16[512,8192]{1,0:T(8,128)(2,1)S(1)} %multiply_convert_fusion.1) | copy-start | bytes 25165828
  70.0 5.3 %copy-start.3 = (bf16[256,8192]{1,0:T(8,128)(2,1)S(1)}, bf16[256,8192]{1,0:T(8,128)(2,1)}, u32[]{:S(2)}) copy-start(bf16[256,8192]{1,0:T(8,128)(2,1)} %param.14) | copy-start | bytes 12582916
  133.1 3.2 copy-start.9
  136.3 58.2 %copy-start.5 = (s32[2,512,256]{2,1,0:T(8,128)S(1)}, s32[2,512,256]{2,1,0:T(8,128)}, u32[]{:S(2)}) copy-start(s32[2,512,256]{2,1,0:T(8,128)} %param.17) | copy-start | bytes 3145732
  139.4 107.0 %reduce-scatter.5.cloned.1.call-start = ((), (), s32[]{:S(2)}) async-start(), calls=%async_computation.3 | async-start | bytes 5242880 | tf_op jit(solution)/shard_map/reduce_scatter | solution.py:37
  202.4 1.0 copy-start.2
  202.4 91.1 %reduce-scatter.3.cloned.1.call-start = ((), (), s32[]{:S(2)}) async-start(), calls=%async_computation.2 | async-start | bytes 5242880 | tf_op jit(solution)/shard_map/reduce_scatter | solution.py:37
  211.5 81.9 %copy-start.6 = (bf16[256,256]{1,0:T(8,128)(2,1)S(1)}, bf16[256,256]{1,0:T(8,128)(2,1)}, u32[]{:S(2)}) copy-start(bf16[256,256]{1,0:T(8,128)(2,1)} %param.21) | copy-start | bytes 393220
  211.6 90.8 %copy-start.1 = (f32[512,256]{1,0:T(8,128)S(1)}, f32[512,256]{1,0:T(8,128)}, u32[]{:S(2)}) copy-start(f32[512,256]{1,0:T(8,128)} %get-tuple-element.6) | copy-start | bytes 1572868
  211.6 125.5 %all-gather.2.cloned.1.call-start = ((), (), s32[]{:S(2)}) async-start(), calls=%async_computation.4 | async-start | bytes 5242880 | tf_op jit(solution)/shard_map/all_gather | solution.py:63
Sparse Core Ops, SparseCore 0:
  139.6 54.8 all-reduce.2
  202.5 43.8 reduce-scatter.4
  249.0 44.4 reduce-scatter.2
  302.5 34.4 all-gather.1
where the time goes:
time: 348 us
  waiting for transfers between devices  170 us (49%)
  matrix products  146 us (42%)
  local copies, waits for them, and re-layouts  15.9 us (5%)
  between operations  13.9 us (4%)
    dot_general x2, matrix products, features_for(): angle = jnp.dot(chosen, omega, preferred_element_type=jnp.float32) + phase  115 us
    reduce_scatter x2, waiting for transfers between devices, share_for(): lax.psum_scatter(row_term(feature_rows, residual).astype(jnp.bfloat16), '...  81.9 us
    psum x1, waiting for transfers between devices, rates_for(): log_rate = lax.psum(partial_value, 'feat')  54.8 us
    all_gather x1, waiting for transfers between devices, body(): lax.all_gather(new_master.astype(jnp.bfloat16), 'pts', axis=0, tiled=True)  33.6 us
    dot_general x2, matrix products, row_term(): lax.dot_general(feature_rows, residual, (((0,), (0,)), ((), ())), preferr...  16 us
    unnamed x21, local copies, waits for them, and re-layouts  11.2 us
    dot_general x1, matrix products, body(): jnp.dot(gradient.astype(jnp.bfloat16), task_cov, preferred_element_type=j...  8.88 us
  transfers between devices with their start and end apart: 4, of which 4 were waited for; matrix products, arithmetic and copies ran while one was open for 3% of the time, Pallas kernels for 0%

commit v1 on v0

v1 whole, which is shorter than its diff:
```python
import functools
import math

import jax
import jax.numpy as jnp
from jax import lax
from jax.experimental import pallas as pl
from jax.experimental.pallas import tpu as pltpu
from jax.sharding import PartitionSpec as P

F = 32768
STEP = 20
CORES = 2

beta_one = 0.9
beta_two = 0.999
learn_rate = 0.2

SINE = tuple(
    c / 8.0
    for c in (3.141582022078924, -5.167142793540227, 2.541899000696469, -0.5546361258792201)
)
ROUNDER = 12582912.0
TURN = 1.0 / (2.0 * math.pi)
VMEM = 56 * 1024 * 1024

f32 = jnp.float32
bf16 = jnp.bfloat16


def scaled_cos(product, phase_turns):
    turns = product * TURN + phase_turns
    r = turns - ((turns + ROUNDER) - ROUNDER)
    s = r * r
    w = ((SINE[3] * s + SINE[2]) * s + SINE[1]) * s + SINE[0]
    w = w * r
    return (math.sqrt(2.0 / F) - w * w).astype(bf16)


def cost(seconds, moved):
    return pl.CostEstimate(flops=int(seconds * 1.0e15), bytes_accessed=int(moved), transcendentals=0)


def params(*semantics):
    return pltpu.CompilerParams(vmem_limit_bytes=VMEM, dimension_semantics=semantics or None)


def rates_kernel(n, tile, place, chosen, omega, phase, weights, own, *rest):
    others, feats, total = rest[: n - 1], rest[n - 1], rest[n]
    step = pl.program_id(0)
    width = omega.shape[1]
    for c in range(width // tile):
        cols = slice(c * tile, (c + 1) * tile)
        product = jnp.dot(chosen[...], omega[:, cols], preferred_element_type=f32)
        feats[:, cols] = scaled_cos(product, phase[:, cols])
    part = jnp.dot(feats[...], weights[...], preferred_element_type=f32)

    @pl.when(step == 0)
    def _():
        total[...] = part

    @pl.when(step > 0)
    def _():
        total[...] += part

    @pl.when(step == pl.num_programs(0) - 1)
    def _():
        rows = own.shape[0]
        me = place[0]
        own[...] = total[pl.ds(pl.multiple_of(me * rows, rows), rows), :]
        for d in range(1, n):
            c = lax.rem(me + d, n)
            others[d - 1][...] = total[pl.ds(pl.multiple_of(c * rows, rows), rows), :].astype(bf16)


def rates(place, chosen, m, omega, phase, weights, n):
    ins, feat_dev = omega.shape
    k = weights.shape[1]
    batch = chosen.shape[0] // 2
    width = min(1024, feat_dev)
    rows = batch // n
    grid = feat_dev // width
    return pl.pallas_call(
        functools.partial(rates_kernel, n, min(256, width)),
        grid_spec=pltpu.PrefetchScalarGridSpec(
            num_scalar_prefetch=1,
            grid=(grid,),
            in_specs=[
                pl.BlockSpec((batch, ins), lambda i, _: (m, 0)),
                pl.BlockSpec((ins, width), lambda i, _: (0, i)),
                pl.BlockSpec((1, width), lambda i, _: (0, i)),
                pl.BlockSpec((width, k), lambda i, _: (i, 0)),
            ],
            out_specs=[pl.BlockSpec((rows, k), lambda i, _: (0, 0))] * n,
            scratch_shapes=[pltpu.VMEM((batch, width), bf16), pltpu.VMEM((batch, k), f32)],
        ),
        out_shape=[jax.ShapeDtypeStruct((rows, k), f32)]
        + [jax.ShapeDtypeStruct((rows, k), bf16)] * (n - 1),
        compiler_params=params("arbitrary"),
        cost_estimate=cost(9e-6, 8 << 20),
        name="partial_log_rates",
    )(place, chosen, omega, phase, weights)


def features_kernel(tile, omega_rows, phase, chosen, out):
    for c in range(chosen.shape[0] // tile):
        cols = slice(c * tile, (c + 1) * tile)
        product = lax.dot_general(
            omega_rows[...], chosen[cols, :], (((1,), (1,)), ((), ())), preferred_element_type=f32
        )
        out[:, cols] = scaled_cos(product, phase[...])


def owned_features(omega_rows, phase, chosen):
    owned, ins = omega_rows.shape
    points = chosen.shape[0]
    rows = min(256, owned)
    return pl.pallas_call(
        functools.partial(features_kernel, min(256, points)),
        grid=(owned // rows,),
        in_specs=[
            pl.BlockSpec((rows, ins), lambda i: (i, 0)),
            pl.BlockSpec((rows, 1), lambda i: (i, 0)),
            pl.BlockSpec((points, ins), lambda i: (0, 0)),
        ],
        out_specs=pl.BlockSpec((rows, points), lambda i: (i, 0)),
        out_shape=jax.ShapeDtypeStruct((owned, points), bf16),
        compiler_params=params("arbitrary"),
        cost_estimate=cost(4.5e-6, 8 << 20),
        name="owned_features",
    )(omega_rows, phase, chosen)


def residual_kernel(n, has_out, place, *refs):
    chunks, observed = refs[:n], refs[n]
    rate_out, residual_out = refs[-2], refs[-1]
    rows = chunks[0].shape[0]
    me = place[0]
    for d in range(n):
        c = lax.rem(me + n - d, n)
        at = pl.ds(pl.multiple_of(c * rows, rows), rows)
        rate = chunks[d][...].astype(f32)
        rate_out[0, at, :] = rate
        residual_out[at, :] = (jnp.exp(rate) - observed[0, at, :].astype(f32)).astype(bf16)


def residuals(place, chunks, counts, m, before):
    n = len(chunks)
    rows, k = chunks[0].shape
    batch = counts.shape[1]
    args = [place, *chunks, counts]
    specs = [pl.BlockSpec((rows, k), lambda i, _: (0, 0))] * n + [
        pl.BlockSpec((1, batch, k), lambda i, _: (m, 0, 0))
    ]
    aliases = {}
    if before is not None:
        aliases = {len(args): 0}
        args.append(before)
        specs.append(pl.BlockSpec(memory_space=pl.ANY))
    return pl.pallas_call(
        functools.partial(residual_kernel, n, before is not None),
        grid_spec=pltpu.PrefetchScalarGridSpec(
            num_scalar_prefetch=1,
            grid=(1,),
            in_specs=specs,
            out_specs=[
                pl.BlockSpec((1, batch, k), lambda i, _: (m, 0, 0)),
                pl.BlockSpec((batch, k), lambda i, _: (0, 0)),
            ],
        ),
        out_shape=[
            jax.ShapeDtypeStruct(counts.shape, f32),
            jax.ShapeDtypeStruct((batch, k), bf16),
        ],
        input_output_aliases=aliases,
        compiler_params=params("arbitrary"),
        cost_estimate=cost(1e-6, 2 << 20),
        name="residuals",
    )(*args)


def update_kernel(n, features, residual, cov, master, first, second, *refs):
    new_master, new_first, new_second, sent, working = refs[-5:]
    batch = residual[0][0].shape[0]
    gradient = master[0]
    for s in range(n):
        for m in range(2):
            gradient += jnp.dot(
                features[s][:, m * batch : (m + 1) * batch],
                residual[s][m][...],
                preferred_element_type=f32,
            )
    conditioned = jnp.dot(gradient.astype(bf16), cov[...], preferred_element_type=f32)
    moved_first = beta_one * first[0] + (1.0 - beta_one) * conditioned
    moved_second = beta_two * second[0] + (1.0 - beta_two) * conditioned * conditioned
    correction_one = 1.0 - beta_one**STEP
    correction_two = 1.0 - beta_two**STEP
    moved = master[0] - learn_rate * (moved_first / correction_one) / (
        jnp.sqrt(moved_second / correction_two) + 1e-08
    )
    new_first[0] = moved_first
    new_second[0] = moved_second
    new_master[0] = moved
    rounded = moved.astype(bf16)
    sent[...] = rounded
    working[...] = rounded


def update(place, features, residual, cov, master, first, second, chunk, chunks, n_pts, before):
    n = len(features)
    owned, k = master.shape[1:]
    rows = min(256, owned // chunks)
    steps = owned // chunks // rows
    at = chunk * steps
    points = features[0].shape[1]
    batch = points // 2
    flat = [r for pair in residual for r in pair]
    state = pl.BlockSpec((1, rows, k), lambda i, _: (0, at + i, 0))
    args = [place, *features, *flat, cov, master, first, second]
    specs = (
        [pl.BlockSpec((rows, points), lambda i, _: (at + i, 0))] * n
        + [pl.BlockSpec((batch, k), lambda i, _: (0, 0))] * (2 * n)
        + [pl.BlockSpec(cov.shape, lambda i, _: (0, 0)), state, state, state]
    )
    aliases = {}
    if before is not None:
        aliases = {len(args) + j: o for j, o in enumerate((0, 1, 2, 4))}
        args += list(before)
        specs += [pl.BlockSpec(memory_space=pl.ANY)] * 4
    blocks = owned // rows

    def kernel(place, *refs):
        fs = refs[:n]
        rs = [refs[n + 2 * s : n + 2 * s + 2] for s in range(n)]
        update_kernel(n, fs, rs, *refs[3 * n :])

    return pl.pallas_call(
        kernel,
        grid_spec=pltpu.PrefetchScalarGridSpec(
            num_scalar_prefetch=1,
            grid=(steps,),
            in_specs=specs,
            out_specs=[
                state,
                state,
                state,
                pl.BlockSpec((rows, k), lambda i, _: (i, 0)),
                pl.BlockSpec((rows, k), lambda i, pt: (pt[1] * blocks + at + i, 0)),
            ],
        ),
        out_shape=[jax.ShapeDtypeStruct(master.shape, f32)] * 3
        + [
            jax.ShapeDtypeStruct((owned // chunks, k), bf16),
            jax.ShapeDtypeStruct((owned * n_pts, k), bf16),
        ],
        input_output_aliases=aliases,
        compiler_params=params("arbitrary"),
        cost_estimate=cost(4e-6, 8 << 20),
        name="update",
    )(*args)


def put_kernel(n, place, *refs):
    pieces, out, sems = refs[:n], refs[n + 1], refs[n + 2]
    copies = []
    for j in range(n):
        rows = pieces[j].shape[0]
        at = pl.ds(pl.multiple_of(place[j] * rows, rows), rows)
        copies.append(pltpu.make_async_copy(pieces[j], out.at[at, :], sems.at[j]))
    for copy in copies:
        copy.start()
    for copy in copies:
        copy.wait()


def put(working, pieces, blocks):
    n = len(pieces)
    any_spec = pl.BlockSpec(memory_space=pl.ANY)
    return pl.pallas_call(
        functools.partial(put_kernel, n),
        grid_spec=pltpu.PrefetchScalarGridSpec(
            num_scalar_prefetch=1,
            grid=(1,),
            in_specs=[any_spec] * (n + 1),
            out_specs=any_spec,
            scratch_shapes=[pltpu.SemaphoreType.DMA((n,))],
        ),
        out_shape=jax.ShapeDtypeStruct(working.shape, working.dtype),
        input_output_aliases={n + 1: 0},
        compiler_params=params("arbitrary"),
        cost_estimate=cost(1e-6, 1 << 20),
        name="put_rows",
    )(jnp.stack(blocks).astype(jnp.int32), *pieces, working)


def ring(x, axis, n, distance):
    return lax.ppermute(x, axis, [(i, (i + distance) % n) for i in range(n)])


def mate(x, n):
    return lax.ppermute(x, "pts", [(i, i ^ 1) for i in range(n)])


def across(x, n, distance):
    return ring(x, "pts", n, distance * CORES)


def spread(x, n):
    chips = n // CORES
    got = [x if d == 0 else across(x, n, d) for d in range(chips)]
    return [y for g in got for y in (g, mate(g, n))]


def body(n_feat, n_pts, points, picks, omega, phase, weights, counts, master, first, second, cov):
    f, p = lax.axis_index("feat"), lax.axis_index("pts")
    place = jnp.stack([f, p]).astype(jnp.int32)
    owned, k = master.shape[1:]
    chosen = points.at[picks.reshape(-1)].get(mode="promise_in_bounds")
    everyone = spread(chosen, n_pts)
    turns = phase * TURN
    omega_rows = lax.dynamic_slice_in_dim(omega, p * owned, owned, 1).T
    own_turns = lax.dynamic_slice_in_dim(turns, p * owned, owned, 0)[:, None]
    turns = turns[None, :]

    out_rates = None
    residual = []
    partial = [rates(place, chosen, m, omega, turns, weights, n_feat) for m in range(2)]
    omega_rows, own_turns, _ = lax.optimization_barrier((omega_rows, own_turns, partial[1][0]))
    for m in range(2):
        own, others = partial[m][0], partial[m][1:]
        total = own
        for d in range(1, n_feat):
            total = total + ring(others[d - 1], "feat", n_feat, d).astype(f32)
        chunk = total.astype(bf16)
        chunks = [chunk] + [ring(chunk, "feat", n_feat, d) for d in range(1, n_feat)]
        out_rates, res = residuals(place, chunks, counts, m, out_rates)
        residual.append(spread(res, n_pts))
    features = [owned_features(omega_rows, own_turns, e) for e in everyone]

    pairs = [(residual[0][s], residual[1][s]) for s in range(n_pts)]
    chunks = 4
    state = None
    sent = []
    for c in range(chunks):
        done = update(
            place, features, pairs, cov, master, first, second, c, chunks, n_pts, state
        )
        state = (done[0], done[1], done[2], done[4])
        sent.append(done[3])
    working = state[3]
    for c in range(chunks):
        pieces = spread(sent[c], n_pts)[1:]
        blocks = []
        for j in range(1, n_pts):
            d, other = j // CORES, j % CORES
            home = lax.rem(p + n_pts - d * CORES, n_pts)
            home = home + other * (1 - 2 * lax.rem(home, 2))
            blocks.append(home * chunks + c)
        working = put(working, pieces, blocks)
    return out_rates, state[0], state[1], state[2], working


def solution(mesh):
    placed = (
        P(("groups", "pts"), None),
        P(None, ("groups", "pts")),
        P(None, "feat"),
        P("feat"),
        P(("groups", "feat"), None),
        P(None, ("groups", "pts"), None),
        P(("groups", "feat"), "pts", None),
        P(("groups", "feat"), "pts", None),
        P(("groups", "feat"), "pts", None),
        P(),
    )
    return jax.shard_map(
        functools.partial(body, mesh.shape["feat"], mesh.shape["pts"]),
        mesh=mesh,
        in_specs=placed,
        out_specs=(
            P(None, ("groups", "pts"), None),
            P(("groups", "feat"), "pts", None),
            P(("groups", "feat"), "pts", None),
            P(("groups", "feat"), "pts", None),
            P(("groups", "feat"), None),
        ),
        check_vma=False,
    )
```

time: 348 us -> 279 us (0.80)
  Pallas kernels: 0 us -> 200 us
  matrix products: 146 us -> 0 us
  waiting for transfers between devices: 170 us -> 28.3 us
  starting transfers between devices: 0.38 us -> 27.9 us
  between operations: 13.9 us -> 1.22 us
    pallas_call x0 -> x16, Pallas kernels: none -> 200 us  [the longest x4 102 us: put(): pl.pallas_call(functools.partial(put_kernel, n), grid_spec=pltpu.Prefetch...]
    dot_general x7 -> x0, matrix products: 146 us -> none  [the longest x2 115 us: features_for(): angle = jnp.dot(chosen, omega, preferred_element_type=jnp.float32) + phase]
    reduce_scatter x2 -> x0, waiting for transfers between devices: 81.9 us -> none  [share_for(): lax.psum_scatter(row_term(feature_rows, residual).astype(jnp.bfloat16), '...]
    psum x1 -> x0, waiting for transfers between devices: 54.8 us -> none  [rates_for(): log_rate = lax.psum(partial_value, 'feat')]
    all_gather x1 -> x0, waiting for transfers between devices: 33.6 us -> none  [body(): lax.all_gather(new_master.astype(jnp.bfloat16), 'pts', axis=0, tiled=True)]
    ppermute x0 -> x33, waiting for transfers between devices: none -> 28.3 us  [the longest x19 28.3 us: ring(): return lax.ppermute(x, axis, [(i, (i + distance) % n) for i in range(n)])]
    ppermute x0 -> x33, starting transfers between devices: none -> 27.9 us  [the longest x19 25.3 us: ring(): return lax.ppermute(x, axis, [(i, (i + distance) % n) for i in range(n)])]
    unnamed x21 -> x78, local copies, waits for them, and re-layouts: 11.2 us -> 9.39 us
  transfers between devices with their start and end apart: 4 -> 33, of which waited for: 4 -> 8; matrix products, arithmetic and copies ran while one was open for 3% -> 3% of each run, Pallas kernels for 0% -> 53%
where the time goes in v1:
time: 279 us; the launch traced here: 278 us
  Pallas kernels  200 us (72%)
  waiting for transfers between devices  28.3 us (10%)
  starting transfers between devices  27.9 us (10%)
  local copies, waits for them, and re-layouts  16.7 us (6%)
  other arithmetic  3.79 us (1%)
    pallas_call x4, Pallas kernels, put(): pl.pallas_call(functools.partial(put_kernel, n), grid_spec=pltpu.Prefetch...  102 us
    pallas_call x4, Pallas kernels, owned_features(): pl.pallas_call(functools.partial(features_kernel, min(256, points)), grid...  37.4 us
    pallas_call x2, Pallas kernels, rates(): pl.pallas_call(functools.partial(rates_kernel, n, min(256, width)), grid_...  28.4 us
    ppermute x19, waiting for transfers between devices, ring(): return lax.ppermute(x, axis, [(i, (i + distance) % n) for i in range(n)])  28.3 us
    pallas_call x4, Pallas kernels, update(): pl.pallas_call(kernel, grid_spec=pltpu.PrefetchScalarGridSpec(num_scalar_...  26.3 us
    ppermute x19, starting transfers between devices, ring(): return lax.ppermute(x, axis, [(i, (i + distance) % n) for i in range(n)])  25.3 us
    unnamed x78, local copies, waits for them, and re-layouts  9.39 us
    pallas_call x2, Pallas kernels, residuals(): pl.pallas_call(functools.partial(residual_kernel, n, before is not None),...  5.63 us
  transfers between devices with their start and end apart: 33, of which 8 were waited for; matrix products, arithmetic and copies ran while one was open for 3% of the time, Pallas kernels for 53%

profile of v1, /device:TPU:0, one launch (start us, length us, event | category | flops | bytes accessed | tf_op | source)
XLA Modules:
  0.0 278.2 jit_solution(13378699767776253362)
XLA Ops:
  0.7 0.8 copy.39
  1.5 0.4 copy-done
  1.9 3.9 %gather_fusion = bf16[1024,256]{1,0:T(8,128)(2,1)S(1)} fusion(bf16[2048,256]{1,0:T(8,128)(2,1)S(1)} %copy-done, s32[1024]{0:T(1024)S(1)} %broadcast_clamp_fusion), kind=kCustom, calls=%fused_computation | custom fusion | bytes 1052672 | tf_op jit(solution)/shard_map/gather | solution.py:318
  5.8 0.5 collective-permute-start.12
  6.4 2.6 collective-permute-start.13
  8.9 0.6 broadcast_multiply_fusion
  9.6 0.7 pad_add_fusion.place
  10.2 14.2 %partial_log_rates.3 = (f32[128,256]{1,0:T(8,128)}, bf16[128,256]{1,0:T(8,128)(2,1)}, bf16[128,256]{1,0:T(8,128)(2,1)}, bf16[128,256]{1,0:T(8,128)(2,1)}) custom-call(s32[2]{0:T(128)} %pad_add_fusion.place, bf16[1024,256]{1,0:T(8,128)(2,1)} %copy-done.8, bf16[256,8192]{1,0:T(8,128)(2,1)} %omega.3, f32[1,8192]{1,0:T(1,128)} %bitcast.26, bf16[8192,256]{1,0:T(8,128)(2,1)} %weights.3), custom_call_target="tpu_custom_call" | custom-call | flops 8999999488 | bytes 8388608 | tf_op jit(solution)/shard_map/partial_log_rates/pallas_call | solution.py:83
  24.4 3.6 %collective-permute-start.8 = (bf16[128,256]{1,0:T(8,128)(2,1)}, bf16[128,256]{1,0:T(8,128)(2,1)S(1)}, u32[]{:S(2)}, u32[]{:S(2)}) collective-permute-start(bf16[128,256]{1,0:T(8,128)(2,1)} %get-tuple-element.46), channel_id=1, source_target_pairs={{0,3},{1,0},{2,1},{3,2},{4,7},{5,4},{6,5},{7,6},{8,11},{9,8},{10,9... | collective-permute-start | bytes 196616 | tf_op jit(solution)/shard_map/ppermute | solution.py:297
  28.0 1.0 collective-permute-start.6
  29.0 14.2 %partial_log_rates.2 = (f32[128,256]{1,0:T(8,128)}, bf16[128,256]{1,0:T(8,128)(2,1)}, bf16[128,256]{1,0:T(8,128)(2,1)}, bf16[128,256]{1,0:T(8,128)(2,1)}) custom-call(s32[2]{0:T(128)} %pad_add_fusion.place, bf16[1024,256]{1,0:T(8,128)(2,1)} %copy-done.8, bf16[256,8192]{1,0:T(8,128)(2,1)} %omega.3, f32[1,8192]{1,0:T(1,128)} %bitcast.27, bf16[8192,256]{1,0:T(8,128)(2,1)} %weights.3), custom_call_target="tpu_custom_call" | custom-call | flops 8999999488 | bytes 8388608 | tf_op jit(solution)/shard_map/partial_log_rates/pallas_call | solution.py:83
  43.2 1.3 constant_dynamic-slice_fusion
  44.5 0.7 dynamic_slice.7
  45.2 1.3 copy.38
  46.5 1.3 copy.34.phase
  47.9 9.4 %owned_features.4.refs_0_ = bf16[2048,1024]{1,0:T(8,128)(2,1)} custom-call(bf16[2048,256]{1,0:T(8,128)(2,1)} %bitcast.22, f32[2048,1]{1,0:T(8,128)} %copy.34.phase, bf16[1024,256]{1,0:T(8,128)(2,1)} %copy-done.8), custom_call_target="tpu_custom_call" | custom-call | flops 4499999744 | bytes 8388608 | tf_op jit(solution)/shard_map/owned_features/pallas_call | solution.py:118
  57.3 2.9 %collective-permute-start.2 = (bf16[128,256]{1,0:T(8,128)(2,1)S(1)}, bf16[128,256]{1,0:T(8,128)(2,1)S(1)}, u32[]{:S(2)}, u32[]{:S(2)}) collective-permute-start(bf16[128,256]{1,0:T(8,128)(2,1)S(1)} %copy-done.31), channel_id=1, source_target_pairs={{0,3},{1,0},{2,1},{3,2},{4,7},{5,4},{6,5},{7,6},{8,11},{9,8},{10,9... | collective-permute-start | bytes 196616 | tf_op jit(solution)/shard_map/ppermute | solution.py:297
  60.2 1.1 collective-permute-start.1
  61.4 1.3 collective-permute-done.2
  62.7 4.5 %collective-permute-start.9 = (bf16[128,256]{1,0:T(8,128)(2,1)S(1)}, bf16[128,256]{1,0:T(8,128)(2,1)S(1)}, u32[]{:S(2)}, u32[]{:S(2)}) collective-permute-start(bf16[128,256]{1,0:T(8,128)(2,1)S(1)} %add_convert_fusion.refs_0_), channel_id=1, source_target_pairs={{0,1},{1,2},{2,3},{3,0},{4,5},{5,6},{6,7},{7,4},{8,9},{9,10},{10,1... | collective-permute-start | bytes 196616 | tf_op jit(solution)/shard_map/ppermute | solution.py:297
  67.1 2.3 collective-permute-done.1
  69.6 2.2 collective-permute-start.3
  71.7 4.1 %collective-permute-done.10.refs_2_ = bf16[128,256]{1,0:T(8,128)(2,1)S(1)} collective-permute-done((bf16[128,256]{1,0:T(8,128)(2,1)S(1)}, bf16[128,256]{1,0:T(8,128)(2,1)S(1)}, u32[]{:S(2)}, u32[]{:S(2)}) %collective-permute-start.10) | collective-permute-done | bytes 65568 | tf_op jit(solution)/shard_map/ppermute | solution.py:297
  75.8 1.3 collective-permute-start.5
  77.1 2.8 %residuals.2 = (f32[2,512,256]{2,1,0:T(8,128)}, bf16[512,256]{1,0:T(8,128)(2,1)}) custom-call(s32[2]{0:T(128)} %pad_add_fusion.place, bf16[128,256]{1,0:T(8,128)(2,1)} %copy-done.23, bf16[128,256]{1,0:T(8,128)(2,1)} %copy-done.32, bf16[128,256]{1,0:T(8,128)(2,1)} %copy-done.34, bf16[128,256]{1,0:T(8,128)(2,1)} %copy-done.36, s32[2,512,256]{2,1,0:T(8,128)} %refs_4_.3), custom_call_target="tpu_custom_call" | custom-call | flops 1000000000 | bytes 2097152 | tf_op jit(solution)/shard_map/residuals/pallas_call | solution.py:160
  80.0 1.1 collective-permute-done.4.refs_2_
  81.1 0.5 collective-permute-start.17
  81.7 0.5 copy-done.37
  82.2 2.8 %residuals.3 = (f32[2,512,256]{2,1,0:T(8,128)}, bf16[512,256]{1,0:T(8,128)(2,1)}) custom-call(s32[2]{0:T(128)} %pad_add_fusion.place, bf16[128,256]{1,0:T(8,128)(2,1)} %copy-done.24, bf16[128,256]{1,0:T(8,128)(2,1)} %copy-done.33, bf16[128,256]{1,0:T(8,128)(2,1)} %copy-done.35, bf16[128,256]{1,0:T(8,128)(2,1)} %copy-done.37, ...), custom_call_target="tpu_custom_call", output_to_operand_aliasing={{0}: (6, {})} | custom-call | flops 1000000000 | bytes 2097152 | tf_op jit(solution)/shard_map/residuals/pallas_call | solution.py:160
  85.0 1.5 collective-permute-start.18
  86.6 9.4 %owned_features.6.refs_2_ = bf16[2048,1024]{1,0:T(8,128)(2,1)} custom-call(bf16[2048,256]{1,0:T(8,128)(2,1)} %bitcast.23, f32[2048,1]{1,0:T(8,128)} %copy.34.phase, bf16[1024,256]{1,0:T(8,128)(2,1)} %collective-permute-done.13.chosen), custom_call_target="tpu_custom_call" | custom-call | flops 4499999744 | bytes 8388608 | tf_op jit(solution)/shard_map/owned_features/pallas_call | solution.py:118
  95.9 0.5 collective-permute-start.16
  97.0 9.4 %owned_features.5.refs_1_ = bf16[2048,1024]{1,0:T(8,128)(2,1)} custom-call(bf16[2048,256]{1,0:T(8,128)(2,1)} %bitcast.24, f32[2048,1]{1,0:T(8,128)} %copy.34.phase, bf16[1024,256]{1,0:T(8,128)(2,1)} %collective-permute-done.12.chosen), custom_call_target="tpu_custom_call" | custom-call | flops 4499999744 | bytes 8388608 | tf_op jit(solution)/shard_map/owned_features/pallas_call | solution.py:118
  106.4 0.8 copy-done.26
  107.2 9.3 %owned_features.7.refs_3_ = bf16[2048,1024]{1,0:T(8,128)(2,1)} custom-call(bf16[2048,256]{1,0:T(8,128)(2,1)} %bitcast.25, f32[2048,1]{1,0:T(8,128)} %copy.34.phase, bf16[1024,256]{1,0:T(8,128)(2,1)} %copy-done.26), custom_call_target="tpu_custom_call" | custom-call | flops 4499999744 | bytes 8388608 | tf_op jit(solution)/shard_map/owned_features/pallas_call | solution.py:118
  116.6 0.7 copy-done.1
  117.4 0.7 copy-done.7
  118.1 6.5 %update.4 = (f32[1,2048,256]{2,1,0:T(8,128)}, f32[1,2048,256]{2,1,0:T(8,128)}, f32[1,2048,256]{2,1,0:T(8,128)}, bf16[512,256]{1,0:T(8,128)(2,1)}, bf16[8192,256]{1,0:T(8,128)(2,1)}) custom-call(s32[2]{0:T(128)} %pad_add_fusion.place, bf16[2048,1024]{1,0:T(8,128)(2,1)} %owned_features.4.refs_0_, bf16[2048,1024]{1,0:T(8,128)(2,1)} %owned_features.5.refs_1_, ...), custom_call_target="tpu_custom_call" | custom-call | flops 4000000000 | bytes 8388608 | tf_op jit(solution)/shard_map/update/pallas_call | solution.py:237
  124.7 6.6 %update.5 = (f32[1,2048,256]{2,1,0:T(8,128)}, f32[1,2048,256]{2,1,0:T(8,128)}, f32[1,2048,256]{2,1,0:T(8,128)}, bf16[512,256]{1,0:T(8,128)(2,1)}, bf16[8192,256]{1,0:T(8,128)(2,1)}) custom-call(s32[2]{0:T(128)} %pad_add_fusion.place, ...), custom_call_target="tpu_custom_call", output_to_operand_aliasing={{0}: (17, {}), {1}: (18, {}), {2}: (19, {}), {4}: (20, {})} | custom-call | flops 4000000000 | bytes 8388608 | tf_op jit(solution)/shard_map/update/pallas_call | solution.py:237
  131.2 6.6 %update.6 = (f32[1,2048,256]{2,1,0:T(8,128)}, f32[1,2048,256]{2,1,0:T(8,128)}, f32[1,2048,256]{2,1,0:T(8,128)}, bf16[512,256]{1,0:T(8,128)(2,1)}, bf16[8192,256]{1,0:T(8,128)(2,1)}) custom-call(s32[2]{0:T(128)} %pad_add_fusion.place, ...), custom_call_target="tpu_custom_call", output_to_operand_aliasing={{0}: (17, {}), {1}: (18, {}), {2}: (19, {}), {4}: (20, {})} | custom-call | flops 4000000000 | bytes 8388608 | tf_op jit(solution)/shard_map/update/pallas_call | solution.py:237
  137.8 6.7 %update.7 = (f32[1,2048,256]{2,1,0:T(8,128)}, f32[1,2048,256]{2,1,0:T(8,128)}, f32[1,2048,256]{2,1,0:T(8,128)}, bf16[512,256]{1,0:T(8,128)(2,1)}, bf16[8192,256]{1,0:T(8,128)(2,1)}) custom-call(s32[2]{0:T(128)} %pad_add_fusion.place, ...), custom_call_target="tpu_custom_call", output_to_operand_aliasing={{0}: (17, {}), {1}: (18, {}), {2}: (19, {}), {4}: (20, {})} | custom-call | flops 4000000000 | bytes 8388608 | tf_op jit(solution)/shard_map/update/pallas_call | solution.py:237
  144.5 0.6 collective-permute-start.22
  145.1 1.5 collective-permute-start.31
  146.6 0.5 collective-permute-start.28
  147.1 1.5 collective-permute-start.25
  148.6 0.7 pad_add_fusion.1.place
  149.3 4.6 %collective-permute-done.22.refs_1_ = bf16[512,256]{1,0:T(8,128)(2,1)S(1)} collective-permute-done((bf16[512,256]{1,0:T(8,128)(2,1)}, bf16[512,256]{1,0:T(8,128)(2,1)S(1)}, u32[]{:S(2)}, u32[]{:S(2)}) %collective-permute-start.22) | collective-permute-done | bytes 262176 | tf_op jit(solution)/shard_map/ppermute | solution.py:297
  153.9 5.6 %collective-permute-done.31.refs_1_ = bf16[512,256]{1,0:T(8,128)(2,1)S(1)} collective-permute-done((bf16[512,256]{1,0:T(8,128)(2,1)S(1)}, bf16[512,256]{1,0:T(8,128)(2,1)S(1)}, u32[]{:S(2)}, u32[]{:S(2)}) %collective-permute-start.31) | collective-permute-done | bytes 262176 | tf_op jit(solution)/shard_map/ppermute | solution.py:297
  159.6 0.6 pad_add_fusion.2.place
  160.1 5.0 %collective-permute-done.28.refs_1_ = bf16[512,256]{1,0:T(8,128)(2,1)S(1)} collective-permute-done((bf16[512,256]{1,0:T(8,128)(2,1)}, bf16[512,256]{1,0:T(8,128)(2,1)S(1)}, u32[]{:S(2)}, u32[]{:S(2)}) %collective-permute-start.28) | collective-permute-done | bytes 262176 | tf_op jit(solution)/shard_map/ppermute | solution.py:297
  165.2 0.6 pad_add_fusion.3.place
  165.8 4.2 %collective-permute-done.25.refs_1_ = bf16[512,256]{1,0:T(8,128)(2,1)S(1)} collective-permute-done((bf16[512,256]{1,0:T(8,128)(2,1)S(1)}, bf16[512,256]{1,0:T(8,128)(2,1)S(1)}, u32[]{:S(2)}, u32[]{:S(2)}) %collective-permute-start.25) | collective-permute-done | bytes 262176 | tf_op jit(solution)/shard_map/ppermute | solution.py:297
  170.0 0.5 collective-permute-start.26
  170.5 0.6 pad_add_fusion.4.place
  171.1 0.4 collective-permute-start.23
  171.9 25.6 %put_rows.4.refs_3_ = bf16[8192,256]{1,0:T(8,128)(2,1)} custom-call(s32[3]{0:T(128)} %pad_add_fusion.4.place, bf16[512,256]{1,0:T(8,128)(2,1)} %copy-done.14, bf16[512,256]{1,0:T(8,128)(2,1)} %copy-done.11, bf16[512,256]{1,0:T(8,128)(2,1)} %copy-done.15, bf16[8192,256]{1,0:T(8,128)(2,1)} %get-tuple-element.72.refs_3_), custom_call_target="tpu_custom_call", output_to_operand_aliasing={{}: (4, {})} | custom-call | flops 1000000000 | bytes 1048576 | tf_op jit(solution)/shard_map/put_rows/pallas_call | solution.py:279
  197.6 0.7 copy-done.17
  198.3 25.6 %put_rows.5.refs_3_ = bf16[8192,256]{1,0:T(8,128)(2,1)} custom-call(s32[3]{0:T(128)} %pad_add_fusion.3.place, bf16[512,256]{1,0:T(8,128)(2,1)} %copy-done.13, bf16[512,256]{1,0:T(8,128)(2,1)} %copy-done.10, bf16[512,256]{1,0:T(8,128)(2,1)} %copy-done.17, bf16[8192,256]{1,0:T(8,128)(2,1)} %put_rows.4.refs_3_), custom_call_target="tpu_custom_call", output_to_operand_aliasing={{}: (4, {})} | custom-call | flops 1000000000 | bytes 1048576 | tf_op jit(solution)/shard_map/put_rows/pallas_call | solution.py:279
  223.9 0.7 copy-done.16
  224.6 0.7 copy-done.18
  225.3 25.6 %put_rows.6.refs_3_ = bf16[8192,256]{1,0:T(8,128)(2,1)} custom-call(s32[3]{0:T(128)} %pad_add_fusion.2.place, bf16[512,256]{1,0:T(8,128)(2,1)} %copy-done.16, bf16[512,256]{1,0:T(8,128)(2,1)} %copy-done.12, bf16[512,256]{1,0:T(8,128)(2,1)} %copy-done.18, bf16[8192,256]{1,0:T(8,128)(2,1)} %put_rows.5.refs_3_), custom_call_target="tpu_custom_call", output_to_operand_aliasing={{}: (4, {})} | custom-call | flops 1000000000 | bytes 1048576 | tf_op jit(solution)/shard_map/put_rows/pallas_call | solution.py:279
  251.0 0.7 copy-done.19
  251.7 0.7 copy-done.20
  252.4 25.6 %put_rows.7 = bf16[8192,256]{1,0:T(8,128)(2,1)} custom-call(s32[3]{0:T(128)} %pad_add_fusion.1.place, bf16[512,256]{1,0:T(8,128)(2,1)} %copy-done.19, bf16[512,256]{1,0:T(8,128)(2,1)} %copy-done.9, bf16[512,256]{1,0:T(8,128)(2,1)} %copy-done.20, bf16[8192,256]{1,0:T(8,128)(2,1)} %put_rows.6.refs_3_), custom_call_target="tpu_custom_call", output_to_operand_aliasing={{}: (4, {})} | custom-call | flops 1000000000 | bytes 1048576 | tf_op jit(solution)/shard_map/put_rows/pallas_call | solution.py:279
  (110 shorter events, 1.5 us)
Async XLA Ops:
  0.6 1.2 copy-start
  0.6 8.3 %copy-start.25 = (f32[8192]{0:T(1024)S(1)}, f32[8192]{0:T(1024)}, u32[]{:S(2)}) copy-start(f32[8192]{0:T(1024)} %param.13) | copy-start | bytes 98308
  5.8 4.4 %copy-start.8 = (bf16[1024,256]{1,0:T(8,128)(2,1)}, bf16[1024,256]{1,0:T(8,128)(2,1)S(1)}, u32[]{:S(2)}) copy-start(bf16[1024,256]{1,0:T(8,128)(2,1)S(1)} %gather_fusion) | copy-start | bytes 1572868
  5.8 90.8 %collective-permute-start.12 = (bf16[1024,256]{1,0:T(8,128)(2,1)S(1)}, bf16[1024,256]{1,0:T(8,128)(2,1)}, u32[]{:S(2)}, u32[]{:S(2)}) collective-permute-start(bf16[1024,256]{1,0:T(8,128)(2,1)S(1)} %gather_fusion), channel_id=1, source_target_pairs={{0,4},{4,0},{8,12},{12,8},{1,5},{5,1},{9,13},{13,9},{2,6},{6,2},{1... | collective-permute-start | bytes 1572872 | tf_op jit(solution)/shard_map/ppermute | solution.py:301
  6.4 80.2 %collective-permute-start.13 = (bf16[1024,256]{1,0:T(8,128)(2,1)S(1)}, bf16[1024,256]{1,0:T(8,128)(2,1)}, u32[]{:S(2)}, u32[]{:S(2)}) collective-permute-start(bf16[1024,256]{1,0:T(8,128)(2,1)S(1)} %gather_fusion), channel_id=1, source_target_pairs={{0,8},{4,12},{8,0},{12,4},{1,9},{5,13},{9,1},{13,5},{2,10},{6,14},... | collective-permute-start | bytes 1572872 | tf_op jit(solution)/shard_map/ppermute | solution.py:297
  24.4 32.9 %collective-permute-start.8 = (bf16[128,256]{1,0:T(8,128)(2,1)}, bf16[128,256]{1,0:T(8,128)(2,1)S(1)}, u32[]{:S(2)}, u32[]{:S(2)}) collective-permute-start(bf16[128,256]{1,0:T(8,128)(2,1)} %get-tuple-element.46), channel_id=1, source_target_pairs={{0,3},{1,0},{2,1},{3,2},{4,7},{5,4},{6,5},{7,6},{8,11},{9,8},{10,9... | collective-permute-start | bytes 196616 | tf_op jit(solution)/shard_map/ppermute | solution.py:297
  28.0 32.1 %collective-permute-start.7 = (bf16[128,256]{1,0:T(8,128)(2,1)}, bf16[128,256]{1,0:T(8,128)(2,1)S(1)}, u32[]{:S(2)}, u32[]{:S(2)}) collective-permute-start(bf16[128,256]{1,0:T(8,128)(2,1)} %get-tuple-element.45), channel_id=1, source_target_pairs={{0,2},{1,3},{2,0},{3,1},{4,6},{5,7},{6,4},{7,5},{8,10},{9,11},{10,... | collective-permute-start | bytes 196616 | tf_op jit(solution)/shard_map/ppermute | solution.py:297
  28.0 33.3 %collective-permute-start.6 = (bf16[128,256]{1,0:T(8,128)(2,1)}, bf16[128,256]{1,0:T(8,128)(2,1)S(1)}, u32[]{:S(2)}, u32[]{:S(2)}) collective-permute-start(bf16[128,256]{1,0:T(8,128)(2,1)} %get-tuple-element.44), channel_id=1, source_target_pairs={{0,1},{1,2},{2,3},{3,0},{4,5},{5,6},{6,7},{7,4},{8,9},{9,10},{10,1... | collective-permute-start | bytes 196616 | tf_op jit(solution)/shard_map/ppermute | solution.py:297
  47.9 9.4 %copy-start.31 = (bf16[128,256]{1,0:T(8,128)(2,1)S(1)}, bf16[128,256]{1,0:T(8,128)(2,1)}, u32[]{:S(2)}) copy-start(bf16[128,256]{1,0:T(8,128)(2,1)} %get-tuple-element.42) | copy-start | bytes 196612
  47.9 12.3 %copy-start.30 = (bf16[128,256]{1,0:T(8,128)(2,1)S(1)}, bf16[128,256]{1,0:T(8,128)(2,1)}, u32[]{:S(2)}) copy-start(bf16[128,256]{1,0:T(8,128)(2,1)} %get-tuple-element.41) | copy-start | bytes 196612
  47.9 13.4 %copy-start.29 = (bf16[128,256]{1,0:T(8,128)(2,1)S(1)}, bf16[128,256]{1,0:T(8,128)(2,1)}, u32[]{:S(2)}) copy-start(bf16[128,256]{1,0:T(8,128)(2,1)} %get-tuple-element.40) | copy-start | bytes 196612
  47.9 13.4 %copy-start.22 = (f32[128,256]{1,0:T(8,128)S(1)}, f32[128,256]{1,0:T(8,128)}, u32[]{:S(2)}) copy-start(f32[128,256]{1,0:T(8,128)} %get-tuple-element.43) | copy-start | bytes 393220
  47.9 21.6 %copy-start.21 = (f32[128,256]{1,0:T(8,128)S(1)}, f32[128,256]{1,0:T(8,128)}, u32[]{:S(2)}) copy-start(f32[128,256]{1,0:T(8,128)} %get-tuple-element.39) | copy-start | bytes 393220
  57.3 5.4 %collective-permute-start.2 = (bf16[128,256]{1,0:T(8,128)(2,1)S(1)}, bf16[128,256]{1,0:T(8,128)(2,1)S(1)}, u32[]{:S(2)}, u32[]{:S(2)}) collective-permute-start(bf16[128,256]{1,0:T(8,128)(2,1)S(1)} %copy-done.31), channel_id=1, source_target_pairs={{0,3},{1,0},{2,1},{3,2},{4,7},{5,4},{6,5},{7,6},{8,11},{9,8},{10,9... | collective-permute-start | bytes 196616 | tf_op jit(solution)/shard_map/ppermute | solution.py:297
  60.2 9.3 %collective-permute-start.1 = (bf16[128,256]{1,0:T(8,128)(2,1)S(1)}, bf16[128,256]{1,0:T(8,128)(2,1)S(1)}, u32[]{:S(2)}, u32[]{:S(2)}) collective-permute-start(bf16[128,256]{1,0:T(8,128)(2,1)S(1)} %copy-done.30), channel_id=1, source_target_pairs={{0,2},{1,3},{2,0},{3,1},{4,6},{5,7},{6,4},{7,5},{8,10},{9,11},{10,... | collective-permute-start | bytes 196616 | tf_op jit(solution)/shard_map/ppermute | solution.py:297
  61.3 8.2 %collective-permute-start = (bf16[128,256]{1,0:T(8,128)(2,1)S(1)}, bf16[128,256]{1,0:T(8,128)(2,1)S(1)}, u32[]{:S(2)}, u32[]{:S(2)}) collective-permute-start(bf16[128,256]{1,0:T(8,128)(2,1)S(1)} %copy-done.29), channel_id=1, source_target_pairs={{0,1},{1,2},{2,3},{3,0},{4,5},{5,6},{6,7},{7,4},{8,9},{9,10},{10,1... | collective-permute-start | bytes 196616 | tf_op jit(solution)/shard_map/ppermute | solution.py:297
  61.3 15.8 %copy-start.23 = (bf16[128,256]{1,0:T(8,128)(2,1)}, bf16[128,256]{1,0:T(8,128)(2,1)S(1)}, u32[]{:S(2)}) copy-start(bf16[128,256]{1,0:T(8,128)(2,1)S(1)} %add_convert_fusion.refs_0_) | copy-start | bytes 196612
  62.7 6.9 %collective-permute-start.9 = (bf16[128,256]{1,0:T(8,128)(2,1)S(1)}, bf16[128,256]{1,0:T(8,128)(2,1)S(1)}, u32[]{:S(2)}, u32[]{:S(2)}) collective-permute-start(bf16[128,256]{1,0:T(8,128)(2,1)S(1)} %add_convert_fusion.refs_0_), channel_id=1, source_target_pairs={{0,1},{1,2},{2,3},{3,0},{4,5},{5,6},{6,7},{7,4},{8,9},{9,10},{10,1... | collective-permute-start | bytes 196616 | tf_op jit(solution)/shard_map/ppermute | solution.py:297
  69.5 6.3 %collective-permute-start.10 = (bf16[128,256]{1,0:T(8,128)(2,1)S(1)}, bf16[128,256]{1,0:T(8,128)(2,1)S(1)}, u32[]{:S(2)}, u32[]{:S(2)}) collective-permute-start(bf16[128,256]{1,0:T(8,128)(2,1)S(1)} %add_convert_fusion.refs_0_), channel_id=1, source_target_pairs={{0,2},{1,3},{2,0},{3,1},{4,6},{5,7},{6,4},{7,5},{8,10},{9,11},{10,... | collective-permute-start | bytes 196616 | tf_op jit(solution)/shard_map/ppermute | solution.py:297
  69.5 6.3 %collective-permute-start.11 = (bf16[128,256]{1,0:T(8,128)(2,1)S(1)}, bf16[128,256]{1,0:T(8,128)(2,1)S(1)}, u32[]{:S(2)}, u32[]{:S(2)}) collective-permute-start(bf16[128,256]{1,0:T(8,128)(2,1)S(1)} %add_convert_fusion.refs_0_), channel_id=1, source_target_pairs={{0,3},{1,0},{2,1},{3,2},{4,7},{5,4},{6,5},{7,6},{8,11},{9,8},{10,9... | collective-permute-start | bytes 196616 | tf_op jit(solution)/shard_map/ppermute | solution.py:297
  69.5 12.0 %copy-start.24 = (bf16[128,256]{1,0:T(8,128)(2,1)}, bf16[128,256]{1,0:T(8,128)(2,1)S(1)}, u32[]{:S(2)}) copy-start(bf16[128,256]{1,0:T(8,128)(2,1)S(1)} %add_convert_fusion.1.refs_0_) | copy-start | bytes 196612
  69.6 7.5 %copy-start.32 = (bf16[128,256]{1,0:T(8,128)(2,1)}, bf16[128,256]{1,0:T(8,128)(2,1)S(1)}, u32[]{:S(2)}) copy-start(bf16[128,256]{1,0:T(8,128)(2,1)S(1)} %collective-permute-done.9.refs_1_) | copy-start | bytes 196612
  69.6 10.3 %collective-permute-start.3 = (bf16[128,256]{1,0:T(8,128)(2,1)S(1)}, bf16[128,256]{1,0:T(8,128)(2,1)S(1)}, u32[]{:S(2)}, u32[]{:S(2)}) collective-permute-start(bf16[128,256]{1,0:T(8,128)(2,1)S(1)} %add_convert_fusion.1.refs_0_), channel_id=1, source_target_pairs={{0,1},{1,2},{2,3},{3,0},{4,5},{5,6},{6,7},{7,4},{8,9},{9,10},{10,1... | collective-permute-start | bytes 196616 | tf_op jit(solution)/shard_map/ppermute | solution.py:297
  75.8 1.3 copy-start.34
  75.8 5.3 %collective-permute-start.4 = (bf16[128,256]{1,0:T(8,128)(2,1)S(1)}, bf16[128,256]{1,0:T(8,128)(2,1)S(1)}, u32[]{:S(2)}, u32[]{:S(2)}) collective-permute-start(bf16[128,256]{1,0:T(8,128)(2,1)S(1)} %add_convert_fusion.1.refs_0_), channel_id=1, source_target_pairs={{0,2},{1,3},{2,0},{3,1},{4,6},{5,7},{6,4},{7,5},{8,10},{9,11},{10,... | collective-permute-start | bytes 196616 | tf_op jit(solution)/shard_map/ppermute | solution.py:297
  75.8 1.3 copy-start.36
  75.8 5.8 %collective-permute-start.5 = (bf16[128,256]{1,0:T(8,128)(2,1)S(1)}, bf16[128,256]{1,0:T(8,128)(2,1)S(1)}, u32[]{:S(2)}, u32[]{:S(2)}) collective-permute-start(bf16[128,256]{1,0:T(8,128)(2,1)S(1)} %add_convert_fusion.1.refs_0_), channel_id=1, source_target_pairs={{0,3},{1,0},{2,1},{3,2},{4,7},{5,4},{6,5},{7,6},{8,11},{9,8},{10,9... | collective-permute-start | bytes 196616 | tf_op jit(solution)/shard_map/ppermute | solution.py:297
  79.9 1.7 copy-start.33
  79.9 36.6 %collective-permute-start.15 = (bf16[512,256]{1,0:T(8,128)(2,1)}, bf16[512,256]{1,0:T(8,128)(2,1)S(1)}, u32[]{:S(2)}, u32[]{:S(2)}) collective-permute-start(bf16[512,256]{1,0:T(8,128)(2,1)} %get-tuple-element.51.refs_4_), channel_id=1, source_target_pairs={{0,4},{4,0},{8,12},{12,8},{1,5},{5,1},{9,13},{13,9},{2,6},{6,2},{1... | collective-permute-start | bytes 786440 | tf_op jit(solution)/shard_map/ppermute | solution.py:301
  81.1 14.8 %collective-permute-start.17 = (bf16[512,256]{1,0:T(8,128)(2,1)}, bf16[512,256]{1,0:T(8,128)(2,1)S(1)}, u32[]{:S(2)}, u32[]{:S(2)}) collective-permute-start(bf16[512,256]{1,0:T(8,128)(2,1)} %get-tuple-element.51.refs_4_), channel_id=1, source_target_pairs={{0,8},{4,12},{8,0},{12,4},{1,9},{5,13},{9,1},{13,5},{2,10},{6,14},... | collective-permute-start | bytes 786440 | tf_op jit(solution)/shard_map/ppermute | solution.py:297
  85.0 10.9 %copy-start.3 = (bf16[512,256]{1,0:T(8,128)(2,1)S(1)}, bf16[512,256]{1,0:T(8,128)(2,1)}, u32[]{:S(2)}) copy-start(bf16[512,256]{1,0:T(8,128)(2,1)} %get-tuple-element.52.refs_5_) | copy-start | bytes 786436
  85.0 11.5 %collective-permute-start.18 = (bf16[512,256]{1,0:T(8,128)(2,1)}, bf16[512,256]{1,0:T(8,128)(2,1)S(1)}, u32[]{:S(2)}, u32[]{:S(2)}) collective-permute-start(bf16[512,256]{1,0:T(8,128)(2,1)} %get-tuple-element.52.refs_5_), channel_id=1, source_target_pairs={{0,8},{4,12},{8,0},{12,4},{1,9},{5,13},{9,1},{13,5},{2,10},{6,14},... | collective-permute-start | bytes 786440 | tf_op jit(solution)/shard_map/ppermute | solution.py:297
  86.6 19.8 %collective-permute-start.14 = (bf16[1024,256]{1,0:T(8,128)(2,1)}, bf16[1024,256]{1,0:T(8,128)(2,1)S(1)}, u32[]{:S(2)}, u32[]{:S(2)}) collective-permute-start(bf16[1024,256]{1,0:T(8,128)(2,1)} %collective-permute-done.13.chosen), channel_id=1, source_target_pairs={{0,4},{4,0},{8,12},{12,8},{1,5},{5,1},{9,13},{13,9},{2,6},{6,2},{1... | collective-permute-start | bytes 1572872 | tf_op jit(solution)/shard_map/ppermute | solution.py:301
  95.9 10.4 %copy-start.2 = (bf16[512,256]{1,0:T(8,128)(2,1)}, bf16[512,256]{1,0:T(8,128)(2,1)S(1)}, u32[]{:S(2)}) copy-start(bf16[512,256]{1,0:T(8,128)(2,1)S(1)} %collective-permute-done.17.refs_8_) | copy-start | bytes 786436
  95.9 20.6 %collective-permute-start.16 = (bf16[512,256]{1,0:T(8,128)(2,1)S(1)}, bf16[512,256]{1,0:T(8,128)(2,1)S(1)}, u32[]{:S(2)}, u32[]{:S(2)}) collective-permute-start(bf16[512,256]{1,0:T(8,128)(2,1)S(1)} %copy-done.3), channel_id=1, source_target_pairs={{0,4},{4,0},{8,12},{12,8},{1,5},{5,1},{9,13},{13,9},{2,6},{6,2},{1... | collective-permute-start | bytes 786440 | tf_op jit(solution)/shard_map/ppermute | solution.py:301
  96.5 9.9 %copy-start.4 = (bf16[512,256]{1,0:T(8,128)(2,1)}, bf16[512,256]{1,0:T(8,128)(2,1)S(1)}, u32[]{:S(2)}) copy-start(bf16[512,256]{1,0:T(8,128)(2,1)S(1)} %collective-permute-done.18.refs_9_) | copy-start | bytes 786436
  96.5 20.1 %collective-permute-start.19 = (bf16[512,256]{1,0:T(8,128)(2,1)S(1)}, bf16[512,256]{1,0:T(8,128)(2,1)S(1)}, u32[]{:S(2)}, u32[]{:S(2)}) collective-permute-start(bf16[512,256]{1,0:T(8,128)(2,1)S(1)} %collective-permute-done.17.refs_8_), channel_id=1, source_target_pairs={{0,4},{4,0},{8,12},{12,8},{1,5},{5,1},{9,13},{13,9},{2,6},{6,2},{1... | collective-permute-start | bytes 786440 | tf_op jit(solution)/shard_map/ppermute | solution.py:301
  96.6 20.0 %collective-permute-start.20 = (bf16[512,256]{1,0:T(8,128)(2,1)S(1)}, bf16[512,256]{1,0:T(8,128)(2,1)S(1)}, u32[]{:S(2)}, u32[]{:S(2)}) collective-permute-start(bf16[512,256]{1,0:T(8,128)(2,1)S(1)} %collective-permute-done.18.refs_9_), channel_id=1, source_target_pairs={{0,4},{4,0},{8,12},{12,8},{1,5},{5,1},{9,13},{13,9},{2,6},{6,2},{1... | collective-permute-start | bytes 786440 | tf_op jit(solution)/shard_map/ppermute | solution.py:301
  106.4 0.8 copy-start.26
  116.5 0.7 copy-start.1
  116.5 0.8 copy-start.5
  116.6 0.8 copy-start.6
  117.4 0.7 copy-start.7
  137.8 7.3 %copy-start.28 = (bf16[512,256]{1,0:T(8,128)(2,1)S(1)}, bf16[512,256]{1,0:T(8,128)(2,1)}, u32[]{:S(2)}) copy-start(bf16[512,256]{1,0:T(8,128)(2,1)} %get-tuple-element.71) | copy-start | bytes 786436
  137.8 9.3 %copy-start.27 = (bf16[512,256]{1,0:T(8,128)(2,1)S(1)}, bf16[512,256]{1,0:T(8,128)(2,1)}, u32[]{:S(2)}) copy-start(bf16[512,256]{1,0:T(8,128)(2,1)} %get-tuple-element.69) | copy-start | bytes 786436
  144.5 9.4 %collective-permute-start.22 = (bf16[512,256]{1,0:T(8,128)(2,1)}, bf16[512,256]{1,0:T(8,128)(2,1)S(1)}, u32[]{:S(2)}, u32[]{:S(2)}) collective-permute-start(bf16[512,256]{1,0:T(8,128)(2,1)} %get-tuple-element.68), channel_id=1, source_target_pairs={{0,8},{4,12},{8,0},{12,4},{1,9},{5,13},{9,1},{13,5},{2,10},{6,14},... | collective-permute-start | bytes 786440 | tf_op jit(solution)/shard_map/ppermute | solution.py:297
  145.1 14.5 %collective-permute-start.31 = (bf16[512,256]{1,0:T(8,128)(2,1)S(1)}, bf16[512,256]{1,0:T(8,128)(2,1)S(1)}, u32[]{:S(2)}, u32[]{:S(2)}) collective-permute-start(bf16[512,256]{1,0:T(8,128)(2,1)S(1)} %copy-done.28), channel_id=1, source_target_pairs={{0,8},{4,12},{8,0},{12,4},{1,9},{5,13},{9,1},{13,5},{2,10},{6,14},... | collective-permute-start | bytes 786440 | tf_op jit(solution)/shard_map/ppermute | solution.py:297
  146.6 18.6 %collective-permute-start.28 = (bf16[512,256]{1,0:T(8,128)(2,1)}, bf16[512,256]{1,0:T(8,128)(2,1)S(1)}, u32[]{:S(2)}, u32[]{:S(2)}) collective-permute-start(bf16[512,256]{1,0:T(8,128)(2,1)} %get-tuple-element.70), channel_id=1, source_target_pairs={{0,8},{4,12},{8,0},{12,4},{1,9},{5,13},{9,1},{13,5},{2,10},{6,14},... | collective-permute-start | bytes 786440 | tf_op jit(solution)/shard_map/ppermute | solution.py:297
  147.1 22.9 %collective-permute-start.27 = (bf16[512,256]{1,0:T(8,128)(2,1)}, bf16[512,256]{1,0:T(8,128)(2,1)S(1)}, u32[]{:S(2)}, u32[]{:S(2)}) collective-permute-start(bf16[512,256]{1,0:T(8,128)(2,1)} %get-tuple-element.70), channel_id=1, source_target_pairs={{0,4},{4,0},{8,12},{12,8},{1,5},{5,1},{9,13},{13,9},{2,6},{6,2},{1... | collective-permute-start | bytes 786440 | tf_op jit(solution)/shard_map/ppermute | solution.py:301
  147.1 22.8 %collective-permute-start.25 = (bf16[512,256]{1,0:T(8,128)(2,1)S(1)}, bf16[512,256]{1,0:T(8,128)(2,1)S(1)}, u32[]{:S(2)}, u32[]{:S(2)}) collective-permute-start(bf16[512,256]{1,0:T(8,128)(2,1)S(1)} %copy-done.27), channel_id=1, source_target_pairs={{0,8},{4,12},{8,0},{12,4},{1,9},{5,13},{9,1},{13,5},{2,10},{6,14},... | collective-permute-start | bytes 786440 | tf_op jit(solution)/shard_map/ppermute | solution.py:297
  153.9 43.6 %copy-start.9 = (bf16[512,256]{1,0:T(8,128)(2,1)}, bf16[512,256]{1,0:T(8,128)(2,1)S(1)}, u32[]{:S(2)}) copy-start(bf16[512,256]{1,0:T(8,128)(2,1)S(1)} %collective-permute-done.22.refs_1_) | copy-start | bytes 786436
  153.9 17.1 %collective-permute-start.30 = (bf16[512,256]{1,0:T(8,128)(2,1)S(1)}, bf16[512,256]{1,0:T(8,128)(2,1)S(1)}, u32[]{:S(2)}, u32[]{:S(2)}) collective-permute-start(bf16[512,256]{1,0:T(8,128)(2,1)S(1)} %copy-done.28), channel_id=1, source_target_pairs={{0,4},{4,0},{8,12},{12,8},{1,5},{5,1},{9,13},{13,9},{2,6},{6,2},{1... | collective-permute-start | bytes 786440 | tf_op jit(solution)/shard_map/ppermute | solution.py:301
  159.6 12.0 %copy-start.11 = (bf16[512,256]{1,0:T(8,128)(2,1)}, bf16[512,256]{1,0:T(8,128)(2,1)S(1)}, u32[]{:S(2)}) copy-start(bf16[512,256]{1,0:T(8,128)(2,1)S(1)} %collective-permute-done.31.refs_1_) | copy-start | bytes 786436
  159.6 11.6 %collective-permute-start.32 = (bf16[512,256]{1,0:T(8,128)(2,1)S(1)}, bf16[512,256]{1,0:T(8,128)(2,1)S(1)}, u32[]{:S(2)}, u32[]{:S(2)}) collective-permute-start(bf16[512,256]{1,0:T(8,128)(2,1)S(1)} %collective-permute-done.31.refs_1_), channel_id=1, source_target_pairs={{0,4},{4,0},{8,12},{12,8},{1,5},{5,1},{9,13},{13,9},{2,6},{6,2},{1... | collective-permute-start | bytes 786440 | tf_op jit(solution)/shard_map/ppermute | solution.py:301
  165.2 32.3 %copy-start.10 = (bf16[512,256]{1,0:T(8,128)(2,1)}, bf16[512,256]{1,0:T(8,128)(2,1)S(1)}, u32[]{:S(2)}) copy-start(bf16[512,256]{1,0:T(8,128)(2,1)S(1)} %collective-permute-done.28.refs_1_) | copy-start | bytes 786436
  165.2 32.4 %collective-permute-start.29 = (bf16[512,256]{1,0:T(8,128)(2,1)S(1)}, bf16[512,256]{1,0:T(8,128)(2,1)S(1)}, u32[]{:S(2)}, u32[]{:S(2)}) collective-permute-start(bf16[512,256]{1,0:T(8,128)(2,1)S(1)} %collective-permute-done.28.refs_1_), channel_id=1, source_target_pairs={{0,4},{4,0},{8,12},{12,8},{1,5},{5,1},{9,13},{13,9},{2,6},{6,2},{1... | collective-permute-start | bytes 786440 | tf_op jit(solution)/shard_map/ppermute | solution.py:301
  169.9 27.6 %copy-start.12 = (bf16[512,256]{1,0:T(8,128)(2,1)}, bf16[512,256]{1,0:T(8,128)(2,1)S(1)}, u32[]{:S(2)}) copy-start(bf16[512,256]{1,0:T(8,128)(2,1)S(1)} %collective-permute-done.25.refs_1_) | copy-start | bytes 786436
  169.9 53.9 %collective-permute-start.24 = (bf16[512,256]{1,0:T(8,128)(2,1)S(1)}, bf16[512,256]{1,0:T(8,128)(2,1)S(1)}, u32[]{:S(2)}, u32[]{:S(2)}) collective-permute-start(bf16[512,256]{1,0:T(8,128)(2,1)S(1)} %copy-done.27), channel_id=1, source_target_pairs={{0,4},{4,0},{8,12},{12,8},{1,5},{5,1},{9,13},{13,9},{2,6},{6,2},{1... | collective-permute-start | bytes 786440 | tf_op jit(solution)/shard_map/ppermute | solution.py:301
  170.0 27.6 %copy-start.13 = (bf16[512,256]{1,0:T(8,128)(2,1)}, bf16[512,256]{1,0:T(8,128)(2,1)S(1)}, u32[]{:S(2)}) copy-start(bf16[512,256]{1,0:T(8,128)(2,1)S(1)} %collective-permute-done.27.refs_0_) | copy-start | bytes 786436
  170.0 53.9 %collective-permute-start.26 = (bf16[512,256]{1,0:T(8,128)(2,1)S(1)}, bf16[512,256]{1,0:T(8,128)(2,1)S(1)}, u32[]{:S(2)}, u32[]{:S(2)}) collective-permute-start(bf16[512,256]{1,0:T(8,128)(2,1)S(1)} %collective-permute-done.25.refs_1_), channel_id=1, source_target_pairs={{0,4},{4,0},{8,12},{12,8},{1,5},{5,1},{9,13},{13,9},{2,6},{6,2},{1... | collective-permute-start | bytes 786440 | tf_op jit(solution)/shard_map/ppermute | solution.py:301
  171.1 79.9 %collective-permute-start.21 = (bf16[512,256]{1,0:T(8,128)(2,1)}, bf16[512,256]{1,0:T(8,128)(2,1)S(1)}, u32[]{:S(2)}, u32[]{:S(2)}) collective-permute-start(bf16[512,256]{1,0:T(8,128)(2,1)} %get-tuple-element.68), channel_id=1, source_target_pairs={{0,4},{4,0},{8,12},{12,8},{1,5},{5,1},{9,13},{13,9},{2,6},{6,2},{1... | collective-permute-start | bytes 786440 | tf_op jit(solution)/shard_map/ppermute | solution.py:301
  171.1 0.7 copy-start.15
  171.1 79.8 %collective-permute-start.23 = (bf16[512,256]{1,0:T(8,128)(2,1)S(1)}, bf16[512,256]{1,0:T(8,128)(2,1)S(1)}, u32[]{:S(2)}, u32[]{:S(2)}) collective-permute-start(bf16[512,256]{1,0:T(8,128)(2,1)S(1)} %collective-permute-done.22.refs_1_), channel_id=1, source_target_pairs={{0,4},{4,0},{8,12},{12,8},{1,5},{5,1},{9,13},{13,9},{2,6},{6,2},{1... | collective-permute-start | bytes 786440 | tf_op jit(solution)/shard_map/ppermute | solution.py:301
  224.6 0.7 copy-start.18
  (7 other events, 4.8 us)

commit v2 on v0

v2 whole, which is shorter than its diff:
```python
import functools
import math

import jax
import jax.numpy as jnp
from jax import lax
from jax.experimental import pallas as pl
from jax.experimental.pallas import tpu as pltpu
from jax.sharding import PartitionSpec as P

F = 32768
STEP = 20
CORES = 2

beta_one = 0.9
beta_two = 0.999
learn_rate = 0.2

SINE = tuple(
    c / 8.0
    for c in (3.141582022078924, -5.167142793540227, 2.541899000696469, -0.5546361258792201)
)
ROUNDER = 12582912.0
TURN = 1.0 / (2.0 * math.pi)
VMEM = 30 * 1024 * 1024

f32 = jnp.float32
bf16 = jnp.bfloat16
IN_VMEM = pl.BlockSpec(memory_space=pltpu.VMEM)
ANYWHERE = pl.BlockSpec(memory_space=pl.ANY)


def scaled_cos(product, phase_turns):
    turns = product * TURN + phase_turns
    r = turns - ((turns + ROUNDER) - ROUNDER)
    s = r * r
    w = ((SINE[3] * s + SINE[2]) * s + SINE[1]) * s + SINE[0]
    w = w * r
    return (math.sqrt(2.0 / F) - w * w).astype(bf16)


TOKEN = jax.ShapeDtypeStruct((8, 128), f32)


def cost(microseconds):
    return pl.CostEstimate(
        flops=int(microseconds * 1.0e9), bytes_accessed=1 << 10, transcendentals=0
    )


def params():
    return pltpu.CompilerParams(vmem_limit_bytes=VMEM)


def rates_kernel(n, m, owned_blocks, f, p, picks, points, omega, phase, weights, *refs):
    chosen, owned, own, *others, token, feats, total = refs[-(n + 5) :]
    token[...] = jnp.zeros_like(token)
    step = pl.program_id(0)
    width = omega.shape[1]
    tile = min(256, width)
    pair = min(512, width)

    @pl.when(step == 0)
    def _():
        batch, pool = chosen.shape[0], points.shape[0]
        wanted = jnp.broadcast_to(picks[m : m + 1, :], (128, batch)).T
        lane = lax.broadcasted_iota(jnp.int32, (batch, 128), 1)
        hot = [
            jnp.where(wanted == lane + 128 * j, 1.0, 0.0).astype(bf16) for j in range(pool // 128)
        ]
        chosen[...] = jnp.dot(
            jnp.concatenate(hot, axis=1), points[...], preferred_element_type=f32
        ).astype(bf16)
        total[...] = jnp.zeros_like(total)

    turns = phase[...] * TURN
    part = None
    for c in range(width // tile):
        cols = slice(c * tile, (c + 1) * tile)
        product = jnp.dot(chosen[...], omega[:, cols], preferred_element_type=f32)
        feats[:, cols] = scaled_cos(product, turns[:, cols])
        if (c + 1) * tile % pair == 0:
            rows = slice((c + 1) * tile - pair, (c + 1) * tile)
            term = jnp.dot(feats[:, rows], weights[rows, :], preferred_element_type=f32)
            part = term if part is None else part + term
    total[...] += part

    @pl.when(step < owned_blocks)
    def _():
        owned[...] = feats[...]

    @pl.when(step == pl.num_programs(0) - 1)
    def _():
        rows = own.shape[0]
        me = f[0]
        own[...] = total[pl.ds(pl.multiple_of(me * rows, rows), rows), :]
        for d in range(1, n):
            c = lax.rem(me + d, n)
            others[d - 1][...] = total[pl.ds(pl.multiple_of(c * rows, rows), rows), :].astype(bf16)


def rates(f, p, picks, points, omega, phase, weights, m, n, owned, deps):
    ins, feat_dev = omega.shape
    k = weights.shape[1]
    batch = picks.shape[1]
    width = min(1024, owned)
    rows = batch // n
    grid = feat_dev // width
    blocks = owned // width

    def turned(i, p):
        return lax.rem(i + p[0] * blocks, grid)

    return pl.pallas_call(
        functools.partial(rates_kernel, n, m, blocks),
        grid_spec=pltpu.PrefetchScalarGridSpec(
            num_scalar_prefetch=2,
            grid=(grid,),
            in_specs=[
                IN_VMEM,
                IN_VMEM,
                pl.BlockSpec((ins, width), lambda i, f, p: (0, turned(i, p))),
                pl.BlockSpec((1, width), lambda i, f, p: (0, turned(i, p))),
                pl.BlockSpec((width, k), lambda i, f, p: (turned(i, p), 0)),
            ]
            + [IN_VMEM] * len(deps),
            out_specs=[
                IN_VMEM,
                pl.BlockSpec((batch, width), lambda i, f, p: (0, jnp.minimum(i, blocks - 1))),
            ]
            + [IN_VMEM] * (n + 1),
            scratch_shapes=[pltpu.VMEM((batch, width), bf16), pltpu.VMEM((batch, k), f32)],
        ),
        out_shape=[
            jax.ShapeDtypeStruct((batch, ins), bf16),
            jax.ShapeDtypeStruct((batch, owned), bf16),
            jax.ShapeDtypeStruct((rows, k), f32),
        ]
        + [jax.ShapeDtypeStruct((rows, k), bf16)] * (n - 1)
        + [TOKEN],
        compiler_params=params(),
        cost_estimate=cost(12),
        name="partial_log_rates",
    )(f, p, picks, points, omega, phase, weights, *deps)


def features_kernel(tile, p, chosen, omega, phase, *refs):
    out, token = refs[-2:]
    token[...] = jnp.zeros_like(token)
    turns = phase[...] * TURN
    for c in range(omega.shape[1] // tile):
        cols = slice(c * tile, (c + 1) * tile)
        product = jnp.dot(chosen[...], omega[:, cols], preferred_element_type=f32)
        out[:, cols] = scaled_cos(product, turns[:, cols])


def owned_features(p, chosen, omega, phase, owned, deps):
    points, ins = chosen.shape
    width = min(512, owned)
    blocks = owned // width
    return pl.pallas_call(
        functools.partial(features_kernel, min(256, width)),
        grid_spec=pltpu.PrefetchScalarGridSpec(
            num_scalar_prefetch=1,
            grid=(blocks,),
            in_specs=[
                IN_VMEM,
                pl.BlockSpec((ins, width), lambda i, p: (0, p[0] * blocks + i)),
                pl.BlockSpec((1, width), lambda i, p: (0, p[0] * blocks + i)),
            ]
            + [IN_VMEM] * len(deps),
            out_specs=[pl.BlockSpec((points, width), lambda i, p: (0, i)), IN_VMEM],
        ),
        out_shape=[jax.ShapeDtypeStruct((points, owned), bf16), TOKEN],
        compiler_params=params(),
        cost_estimate=cost(4),
        name="owned_features",
    )(p, chosen, omega, phase, *deps)


def total_kernel(n, *refs):
    out, token = refs[-2:]
    token[...] = jnp.zeros_like(token)
    value = refs[0][...]
    for r in refs[1:n]:
        value = value + r[...].astype(f32)
    out[...] = value.astype(bf16)


def total(terms, deps):
    return pl.pallas_call(
        functools.partial(total_kernel, len(terms)),
        in_specs=[IN_VMEM] * (len(terms) + len(deps)),
        out_specs=[IN_VMEM] * 2,
        out_shape=[jax.ShapeDtypeStruct(terms[0].shape, bf16), TOKEN],
        compiler_params=params(),
        cost_estimate=cost(0.5),
        name="total_rates",
    )(*terms, *deps)


def residual_kernel(n, m, f, *refs):
    chunks, observed = refs[:n], refs[n]
    rate_out, residual_out, token, held = refs[-4:]
    token[...] = jnp.zeros_like(token)
    rows = chunks[0].shape[0]
    me = f[0]
    for d in range(n):
        c = lax.rem(me + n - d, n)
        at = pl.ds(pl.multiple_of(c * rows, rows), rows)
        rate = chunks[d][...].astype(f32)
        rate_out[0, at, :] = rate
        held[at, :] = jnp.exp(rate) - observed[0, at, :].astype(f32)
    residual_out[...] = held[...].T.astype(bf16)


def residuals(f, chunks, counts, m, before, deps):
    n = len(chunks)
    k = chunks[0].shape[1]
    batch = counts.shape[1]
    args = [f, *chunks, counts, *deps]
    specs = [IN_VMEM] * n + [pl.BlockSpec((1, batch, k), lambda i, _: (m, 0, 0))]
    specs += [IN_VMEM] * len(deps)
    aliases = {}
    if before is not None:
        aliases = {len(args): 0}
        args.append(before)
        specs.append(ANYWHERE)
    return pl.pallas_call(
        functools.partial(residual_kernel, n, m),
        grid_spec=pltpu.PrefetchScalarGridSpec(
            num_scalar_prefetch=1,
            grid=(1,),
            in_specs=specs,
            out_specs=[pl.BlockSpec((1, batch, k), lambda i, _: (m, 0, 0)), IN_VMEM, IN_VMEM],
            scratch_shapes=[pltpu.VMEM((batch, k), f32)],
        ),
        out_shape=[
            jax.ShapeDtypeStruct(counts.shape, f32),
            jax.ShapeDtypeStruct((k, batch), bf16),
            TOKEN,
        ],
        input_output_aliases=aliases,
        compiler_params=params(),
        cost_estimate=cost(1),
        name="residuals",
    )(*args)


def update_kernel(n, *refs):
    features, residual = refs[:n], refs[n : 2 * n]
    cov, master, first, second = refs[2 * n : 2 * n + 4]
    new_master, new_first, new_second, sent = refs[-4:]
    rows = master.shape[1]
    gradient = None
    for j in range(n):
        term = jnp.dot(residual[j][...], features[j][...], preferred_element_type=f32)
        gradient = term if gradient is None else gradient + term
    gradient = gradient.T + master[0]
    conditioned = jnp.dot(gradient.astype(bf16), cov[...], preferred_element_type=f32)
    moved_first = beta_one * first[0] + (1.0 - beta_one) * conditioned
    moved_second = beta_two * second[0] + (1.0 - beta_two) * conditioned * conditioned
    correction_one = 1.0 - beta_one**STEP
    correction_two = 1.0 - beta_two**STEP
    moved = master[0] - learn_rate * (moved_first / correction_one) / (
        jnp.sqrt(moved_second / correction_two) + 1e-08
    )
    new_first[0] = moved_first
    new_second[0] = moved_second
    new_master[0] = moved
    sent[pl.ds(pl.multiple_of(pl.program_id(0) * rows, rows), rows), :] = moved.astype(bf16)


def update(features, residual, cov, master, first, second, chunk, chunks, before, deps):
    n = len(features)
    owned, k = master.shape[1:]
    rows = min(256, owned // chunks)
    steps = owned // chunks // rows
    at = chunk * steps
    batch = features[0].shape[0]
    state = pl.BlockSpec((1, rows, k), lambda i: (0, at + i, 0))
    args = [*features, *residual, cov, master, first, second]
    specs = (
        [pl.BlockSpec((batch, rows), lambda i: (0, at + i))] * n
        + [IN_VMEM] * n
        + [pl.BlockSpec(cov.shape, lambda i: (0, 0)), state, state, state]
    )
    aliases = {}
    if before is not None:
        aliases = {len(args) + j: j for j in range(3)}
        args += list(before)
        specs += [ANYWHERE] * 3
    args += deps
    specs += [IN_VMEM] * len(deps)
    return pl.pallas_call(
        functools.partial(update_kernel, n),
        grid=(steps,),
        in_specs=specs,
        out_specs=[state, state, state, IN_VMEM],
        out_shape=[jax.ShapeDtypeStruct(master.shape, f32)] * 3
        + [jax.ShapeDtypeStruct((owned // chunks, k), bf16)],
        input_output_aliases=aliases,
        compiler_params=params(),
        cost_estimate=cost(4),
        name="update",
    )(*args)


def put_kernel(n, n_pts, chunk, chunks, p, *refs):
    pieces, out, sems = refs[:n], refs[-2], refs[-1]
    me = p[0]
    copies = []
    for j in range(n):
        rows = pieces[j].shape[0]
        distance, other = j // CORES, j % CORES
        home = lax.rem(me + n_pts - distance * CORES, n_pts)
        home = home + other * (1 - 2 * lax.rem(home, 2))
        at = pl.ds(pl.multiple_of((home * chunks + chunk) * rows, rows), rows)
        copies.append(pltpu.make_async_copy(pieces[j], out.at[at, :], sems.at[j]))
    for copy in copies:
        copy.start()
    for copy in copies:
        copy.wait()


def put(p, working, pieces, chunk, chunks, n_pts, shape):
    n = len(pieces)
    args = [p, *pieces]
    specs = [IN_VMEM] * n
    aliases = {}
    if working is not None:
        aliases = {len(args): 0}
        args.append(working)
        specs.append(ANYWHERE)
    return pl.pallas_call(
        functools.partial(put_kernel, n, n_pts, chunk, chunks),
        grid_spec=pltpu.PrefetchScalarGridSpec(
            num_scalar_prefetch=1,
            grid=(1,),
            in_specs=specs,
            out_specs=ANYWHERE,
            scratch_shapes=[pltpu.SemaphoreType.DMA((n,))],
        ),
        out_shape=jax.ShapeDtypeStruct(shape, bf16),
        input_output_aliases=aliases,
        compiler_params=params(),
        cost_estimate=cost(1),
        name="put_rows",
    )(*args)


def ring(x, axis, n, distance):
    return lax.ppermute(x, axis, [(i, (i + distance) % n) for i in range(n)])


def mate(x, n):
    return lax.ppermute(x, "pts", [(i, i ^ 1) for i in range(n)])


def across(x, n, distance):
    return ring(x, "pts", n, distance * CORES)


def spread(x, n):
    chips = n // CORES
    got = [x if d == 0 else across(x, n, d) for d in range(chips)]
    return [y for g in got for y in (g, mate(g, n))]


def body(n_feat, n_pts, points, picks, omega, phase, weights, counts, master, first, second, cov):
    f = lax.axis_index("feat").astype(jnp.int32).reshape(1)
    p = lax.axis_index("pts").astype(jnp.int32).reshape(1)
    owned, k = master.shape[1:]
    phase = phase[None, :]

    terms, chosen, features = [], [], []
    deps = []
    for m in range(2):
        picked, feats, own, *others, token = rates(
            f, p, picks, points, omega, phase, weights, m, n_feat, owned, deps
        )
        deps = [token]
        features.append([feats])
        chosen.append(spread(picked, n_pts)[1:])
        terms.append([own] + [ring(others[d - 1], "feat", n_feat, d) for d in range(1, n_feat)])

    def whole(chunk):
        return [chunk] + [ring(chunk, "feat", n_feat, d) for d in range(1, n_feat)]

    pieces = [(m, j) for m in range(2) for j in range(n_pts - 1)]
    marks = [len(pieces) * i // 6 for i in range(6)]
    residual = []
    for i, (m, j) in enumerate(pieces):
        if i == marks[0]:
            chunk, token = total(terms[0], deps)
            rows_zero = whole(chunk)
            deps = [token]
        if i == marks[2]:
            chunk, first_token = total(terms[1], deps)
            rows_one = whole(chunk)
            out_rates, res, token = residuals(f, rows_zero, counts, 0, None, deps + [first_token])
            residual.append(spread(res, n_pts))
            deps = [token]
        if i == marks[4]:
            out_rates, res, token = residuals(f, rows_one, counts, 1, out_rates, deps)
            residual.append(spread(res, n_pts))
            deps = [token]
        feats, token = owned_features(p, chosen[m][j], omega, phase, owned, deps)
        deps = [token]
        features[m].append(feats)

    flat_features = features[0] + features[1]
    flat_residual = residual[0] + residual[1]
    state = None
    arrived = []
    chunks = max(1, min(4, owned // 256))
    for c in range(chunks):
        deps = [arrived[c - 2][CORES]] if c >= 2 and n_pts > CORES else []
        *state, sent = update(
            flat_features, flat_residual, cov, master, first, second, c, chunks, state, deps
        )
        arrived.append(spread(sent, n_pts))
    working = None
    for c in range(chunks):
        working = put(p, working, arrived[c], c, chunks, n_pts, (owned * n_pts, k))
    return out_rates, *state, working


def solution(mesh):
    placed = (
        P(("groups", "pts"), None),
        P(None, ("groups", "pts")),
        P(None, "feat"),
        P("feat"),
        P(("groups", "feat"), None),
        P(None, ("groups", "pts"), None),
        P(("groups", "feat"), "pts", None),
        P(("groups", "feat"), "pts", None),
        P(("groups", "feat"), "pts", None),
        P(),
    )
    return jax.shard_map(
        functools.partial(body, mesh.shape["feat"], mesh.shape["pts"]),
        mesh=mesh,
        in_specs=placed,
        out_specs=(
            P(None, ("groups", "pts"), None),
            P(("groups", "feat"), "pts", None),
            P(("groups", "feat"), "pts", None),
            P(("groups", "feat"), "pts", None),
            P(("groups", "feat"), None),
        ),
        check_vma=False,
    )
```

time: 348 us -> 126 us (0.36)
  waiting for transfers between devices: 170 us -> 14.3 us
  matrix products: 146 us -> 0 us
  Pallas kernels: 0 us -> 72.8 us
  starting transfers between devices: 0.38 us -> 30.1 us
  between operations: 13.9 us -> 1.11 us
  local copies, waits for them, and re-layouts: 15.9 us -> 7.07 us
    dot_general x7 -> x0, matrix products: 146 us -> none  [the longest x2 115 us: features_for(): angle = jnp.dot(chosen, omega, preferred_element_type=jnp.float32) + phase]
    reduce_scatter x2 -> x0, waiting for transfers between devices: 81.9 us -> none  [share_for(): lax.psum_scatter(row_term(feature_rows, residual).astype(jnp.bfloat16), '...]
    pallas_call x0 -> x20, Pallas kernels: none -> 72.8 us  [the longest x2 30.4 us: rates(): pl.pallas_call(functools.partial(rates_kernel, n, m, blocks), grid_spec=p...]
    psum x1 -> x0, waiting for transfers between devices: 54.8 us -> none  [rates_for(): log_rate = lax.psum(partial_value, 'feat')]
    all_gather x1 -> x0, waiting for transfers between devices: 33.6 us -> none  [body(): lax.all_gather(new_master.astype(jnp.bfloat16), 'pts', axis=0, tiled=True)]
    ppermute x0 -> x36, starting transfers between devices: none -> 30.1 us  [the longest x20 27.3 us: ring(): return lax.ppermute(x, axis, [(i, (i + distance) % n) for i in range(n)])]
    ppermute x0 -> x36, waiting for transfers between devices: none -> 14.3 us  [the longest x20 14.3 us: ring(): return lax.ppermute(x, axis, [(i, (i + distance) % n) for i in range(n)])]
    unnamed x21 -> x22, local copies, waits for them, and re-layouts: 11.2 us -> 7.07 us
  transfers between devices with their start and end apart: 4 -> 36, of which waited for: 4 -> 6; matrix products, arithmetic and copies ran while one was open for 3% -> 0% of each run, Pallas kernels for 0% -> 42%
where the time goes in v2:
time: 126 us; the launch traced here: 125 us
  Pallas kernels  72.8 us (58%)
  starting transfers between devices  30.1 us (24%)
  waiting for transfers between devices  14.3 us (11%)
  local copies, waits for them, and re-layouts  7.07 us (6%)
    pallas_call x2, Pallas kernels, rates(): pl.pallas_call(functools.partial(rates_kernel, n, m, blocks), grid_spec=p...  30.4 us
    ppermute x20, starting transfers between devices, ring(): return lax.ppermute(x, axis, [(i, (i + distance) % n) for i in range(n)])  27.3 us
    pallas_call x6, Pallas kernels, owned_features(): pl.pallas_call(functools.partial(features_kernel, min(256, width)), grid_...  19 us
    pallas_call x4, Pallas kernels, update(): pl.pallas_call(functools.partial(update_kernel, n), grid=(steps,), in_spe...  17.4 us
    ppermute x20, waiting for transfers between devices, ring(): return lax.ppermute(x, axis, [(i, (i + distance) % n) for i in range(n)])  14.3 us
    unnamed x22, local copies, waits for them, and re-layouts  7.07 us
    pallas_call x4, Pallas kernels, put(): pl.pallas_call(functools.partial(put_kernel, n, n_pts, chunk, chunks), gr...  4.01 us
    ppermute x16, starting transfers between devices, mate(): return lax.ppermute(x, 'pts', [(i, i ^ 1) for i in range(n)])  2.8 us
  transfers between devices with their start and end apart: 36, of which 6 were waited for; matrix products, arithmetic and copies ran while one was open for 0% of the time, Pallas kernels for 42%

profile of v2, /device:TPU:0, one launch (start us, length us, event | category | flops | bytes accessed | tf_op | source)
XLA Modules:
  0.0 125.4 jit_solution(6947789505659493452)
XLA Ops:
  0.6 2.2 %copy-done.3 = bf16[8192,256]{1,0:T(8,128)(2,1)S(1)} copy-done((bf16[8192,256]{1,0:T(8,128)(2,1)S(1)}, bf16[8192,256]{1,0:T(8,128)(2,1)}, u32[]{:S(2)}) %copy-start.3) | copy-done | bytes 4194328
  2.8 2.2 %copy-done.4 = bf16[256,8192]{1,0:T(8,128)(2,1)S(1)} copy-done((bf16[256,8192]{1,0:T(8,128)(2,1)S(1)}, bf16[256,8192]{1,0:T(8,128)(2,1)}, u32[]{:S(2)}) %copy-start.4) | copy-done | bytes 4194328
  5.0 1.2 copy-done.6
  6.2 0.8 copy-done.8
  7.0 0.7 copy-done.10
  7.7 15.2 %partial_log_rates.2 = (bf16[512,256]{1,0:T(8,128)(2,1)S(1)}, bf16[512,2048]{1,0:T(8,128)(2,1)S(1)}, f32[128,256]{1,0:T(8,128)S(1)}, bf16[128,256]{1,0:T(8,128)(...) custom-call(s32[1]{0:T(128)} %bitcast.f, s32[1]{0:T(128)} %bitcast.1.p, ...), custom_call_target="tpu_custom_call" | custom-call | flops 12000000000 | bytes 1024 | tf_op jit(solution)/shard_map/partial_log_rates/pallas_call | solution.py:114
  22.9 3.0 %collective-permute-start.3 = (bf16[512,256]{1,0:T(8,128)(2,1)S(1)}, bf16[512,256]{1,0:T(8,128)(2,1)S(1)}, u32[]{:S(2)}, u32[]{:S(2)}) collective-permute-start(bf16[512,256]{1,0:T(8,128)(2,1)S(1)} %get-tuple-element.61), channel_id=1, source_target_pairs={{0,8},{4,12},{8,0},{12,4},{1,9},{5,13},{9,1},{13,5},{2,10},{6,14},... | collective-permute-start | bytes 786440 | tf_op jit(solution)/shard_map/ppermute | solution.py:353
  25.9 0.0 collective-permute-start.4
  25.9 1.6 %collective-permute-start.5 = (bf16[128,256]{1,0:T(8,128)(2,1)S(1)}, bf16[128,256]{1,0:T(8,128)(2,1)S(1)}, u32[]{:S(2)}, u32[]{:S(2)}) collective-permute-start(bf16[128,256]{1,0:T(8,128)(2,1)S(1)} %get-tuple-element.63), channel_id=1, source_target_pairs={{0,1},{1,2},{2,3},{3,0},{4,5},{5,6},{6,7},{7,4},{8,9},{9,10},{10,1... | collective-permute-start | bytes 196616 | tf_op jit(solution)/shard_map/ppermute | solution.py:353
  27.5 2.6 %collective-permute-start.6 = (bf16[128,256]{1,0:T(8,128)(2,1)S(1)}, bf16[128,256]{1,0:T(8,128)(2,1)S(1)}, u32[]{:S(2)}, u32[]{:S(2)}) collective-permute-start(bf16[128,256]{1,0:T(8,128)(2,1)S(1)} %get-tuple-element.64), channel_id=1, source_target_pairs={{0,2},{1,3},{2,0},{3,1},{4,6},{5,7},{6,4},{7,5},{8,10},{9,11},{10,... | collective-permute-start | bytes 196616 | tf_op jit(solution)/shard_map/ppermute | solution.py:353
  30.1 1.3 %collective-permute-start.7 = (bf16[128,256]{1,0:T(8,128)(2,1)S(1)}, bf16[128,256]{1,0:T(8,128)(2,1)S(1)}, u32[]{:S(2)}, u32[]{:S(2)}) collective-permute-start(bf16[128,256]{1,0:T(8,128)(2,1)S(1)} %get-tuple-element.65), channel_id=1, source_target_pairs={{0,3},{1,0},{2,1},{3,2},{4,7},{5,4},{6,5},{7,6},{8,11},{9,8},{10,9... | collective-permute-start | bytes 196616 | tf_op jit(solution)/shard_map/ppermute | solution.py:353
  31.4 15.2 %partial_log_rates.3 = (bf16[512,256]{1,0:T(8,128)(2,1)S(1)}, bf16[512,2048]{1,0:T(8,128)(2,1)S(1)}, f32[128,256]{1,0:T(8,128)S(1)}, bf16[128,256]{1,0:T(8,128)(...) custom-call(s32[1]{0:T(128)} %bitcast.f, s32[1]{0:T(128)} %bitcast.1.p, ...), custom_call_target="tpu_custom_call" | custom-call | flops 12000000000 | bytes 1024 | tf_op jit(solution)/shard_map/partial_log_rates/pallas_call | solution.py:114
  46.7 0.0 collective-permute-done.5.refs_1_
  46.7 0.7 collective-permute-start
  47.4 0.0 collective-permute-done.6.refs_2_
  47.4 0.3 collective-permute-start.1
  47.8 2.9 %collective-permute-start.2 = (bf16[128,256]{1,0:T(8,128)(2,1)S(1)}, bf16[128,256]{1,0:T(8,128)(2,1)S(1)}, u32[]{:S(2)}, u32[]{:S(2)}) collective-permute-start(bf16[128,256]{1,0:T(8,128)(2,1)S(1)} %get-tuple-element.60), channel_id=1, source_target_pairs={{0,3},{1,0},{2,1},{3,2},{4,7},{5,4},{6,5},{7,6},{8,11},{9,8},{10,9... | collective-permute-start | bytes 196616 | tf_op jit(solution)/shard_map/ppermute | solution.py:353
  50.7 0.0 collective-permute-done.4.chosen
  50.7 0.6 collective-permute-start.13
  51.2 3.1 %owned_features.6 = (bf16[512,2048]{1,0:T(8,128)(2,1)S(1)}, f32[8,128]{1,0:T(8,128)S(1)}) custom-call(s32[1]{0:T(128)} %bitcast.1.p, bf16[512,256]{1,0:T(8,128)(2,1)S(1)} %collective-permute-done.4.chosen, bf16[256,8192]{1,0:T(8,128)(2,1)S(1)} %copy-done.5, f32[1,8192]{1,0:T(1,128)S(1)} %bitcast.5, f32[8,128]{1,0:T(8,128)S(1)} %get-tuple-element.67.refs_0_), custom_call_target="tpu_custom_call" | custom-call | flops 4000000000 | bytes 1024 | tf_op jit(solution)/shard_map/owned_features/pallas_call | solution.py:161
  54.3 0.0 collective-permute-done.refs_1_
  54.3 1.6 %collective-permute-start.14 = (bf16[128,256]{1,0:T(8,128)(2,1)S(1)}, bf16[128,256]{1,0:T(8,128)(2,1)S(1)}, u32[]{:S(2)}, u32[]{:S(2)}) collective-permute-start(bf16[128,256]{1,0:T(8,128)(2,1)S(1)} %get-tuple-element.72.refs_0_), channel_id=1, source_target_pairs={{0,2},{1,3},{2,0},{3,1},{4,6},{5,7},{6,4},{7,5},{8,10},{9,11},{10,... | collective-permute-start | bytes 196616 | tf_op jit(solution)/shard_map/ppermute | solution.py:353
  55.9 2.9 %collective-permute-start.15 = (bf16[128,256]{1,0:T(8,128)(2,1)S(1)}, bf16[128,256]{1,0:T(8,128)(2,1)S(1)}, u32[]{:S(2)}, u32[]{:S(2)}) collective-permute-start(bf16[128,256]{1,0:T(8,128)(2,1)S(1)} %get-tuple-element.72.refs_0_), channel_id=1, source_target_pairs={{0,3},{1,0},{2,1},{3,2},{4,7},{5,4},{6,5},{7,6},{8,11},{9,8},{10,9... | collective-permute-start | bytes 196616 | tf_op jit(solution)/shard_map/ppermute | solution.py:353
  58.8 3.1 %owned_features.7 = (bf16[512,2048]{1,0:T(8,128)(2,1)S(1)}, f32[8,128]{1,0:T(8,128)S(1)}) custom-call(s32[1]{0:T(128)} %bitcast.1.p, bf16[512,256]{1,0:T(8,128)(2,1)S(1)} %collective-permute-done.3.chosen, bf16[256,8192]{1,0:T(8,128)(2,1)S(1)} %copy-done.5, f32[1,8192]{1,0:T(1,128)S(1)} %bitcast.6, f32[8,128]{1,0:T(8,128)S(1)} %get-tuple-element.68.refs_0_), custom_call_target="tpu_custom_call" | custom-call | flops 4000000000 | bytes 1024 | tf_op jit(solution)/shard_map/owned_features/pallas_call | solution.py:161
  61.9 0.5 collective-permute-start.11
  62.5 0.6 collective-permute-start.16
  63.1 1.0 collective-permute-start.9
  64.1 1.0 residuals.2
  65.0 2.9 %collective-permute-start.10 = (bf16[128,256]{1,0:T(8,128)(2,1)S(1)}, bf16[128,256]{1,0:T(8,128)(2,1)S(1)}, u32[]{:S(2)}, u32[]{:S(2)}) collective-permute-start(bf16[128,256]{1,0:T(8,128)(2,1)S(1)} %get-tuple-element.70.refs_0_), channel_id=1, source_target_pairs={{0,3},{1,0},{2,1},{3,2},{4,7},{5,4},{6,5},{7,6},{8,11},{9,8},{10,9... | collective-permute-start | bytes 196616 | tf_op jit(solution)/shard_map/ppermute | solution.py:353
  67.9 3.1 %owned_features.8 = (bf16[512,2048]{1,0:T(8,128)(2,1)S(1)}, f32[8,128]{1,0:T(8,128)S(1)}) custom-call(s32[1]{0:T(128)} %bitcast.1.p, bf16[512,256]{1,0:T(8,128)(2,1)S(1)} %collective-permute-done.12.chosen, bf16[256,8192]{1,0:T(8,128)(2,1)S(1)} %copy-done.5, f32[1,8192]{1,0:T(1,128)S(1)} %bitcast.7, f32[8,128]{1,0:T(8,128)S(1)} %get-tuple-element.74.refs_0_), custom_call_target="tpu_custom_call" | custom-call | flops 4000000000 | bytes 1024 | tf_op jit(solution)/shard_map/owned_features/pallas_call | solution.py:161
  71.0 1.6 %collective-permute-start.19 = (bf16[256,512]{1,0:T(8,128)(2,1)S(1)}, bf16[256,512]{1,0:T(8,128)(2,1)S(1)}, u32[]{:S(2)}, u32[]{:S(2)}) collective-permute-start(bf16[256,512]{1,0:T(8,128)(2,1)S(1)} %get-tuple-element.89.refs_8_), channel_id=1, source_target_pairs={{0,8},{4,12},{8,0},{12,4},{1,9},{5,13},{9,1},{13,5},{2,10},{6,14},... | collective-permute-start | bytes 786440 | tf_op jit(solution)/shard_map/ppermute | solution.py:353
  72.6 3.1 %owned_features.9 = (bf16[512,2048]{1,0:T(8,128)(2,1)S(1)}, f32[8,128]{1,0:T(8,128)S(1)}) custom-call(s32[1]{0:T(128)} %bitcast.1.p, bf16[512,256]{1,0:T(8,128)(2,1)S(1)} %collective-permute-done.11.chosen, bf16[256,8192]{1,0:T(8,128)(2,1)S(1)} %copy-done.5, f32[1,8192]{1,0:T(1,128)S(1)} %bitcast.8, f32[8,128]{1,0:T(8,128)S(1)} %get-tuple-element.75.refs_0_), custom_call_target="tpu_custom_call" | custom-call | flops 4000000000 | bytes 1024 | tf_op jit(solution)/shard_map/owned_features/pallas_call | solution.py:161
  75.7 0.1 collective-permute-start.18
  75.8 0.5 collective-permute-start.17
  76.3 1.0 residuals.3
  77.2 0.1 collective-permute-start.21
  77.3 0.5 collective-permute-start.22
  77.8 0.6 collective-permute-done.19.refs_10_
  78.4 3.1 %owned_features.10 = (bf16[512,2048]{1,0:T(8,128)(2,1)S(1)}, f32[8,128]{1,0:T(8,128)S(1)}) custom-call(s32[1]{0:T(128)} %bitcast.1.p, bf16[512,256]{1,0:T(8,128)(2,1)S(1)} %collective-permute-done.16.chosen, bf16[256,8192]{1,0:T(8,128)(2,1)S(1)} %copy-done.5, f32[1,8192]{1,0:T(1,128)S(1)} %bitcast.9, f32[8,128]{1,0:T(8,128)S(1)} %get-tuple-element.85.refs_0_), custom_call_target="tpu_custom_call" | custom-call | flops 4000000000 | bytes 1024 | tf_op jit(solution)/shard_map/owned_features/pallas_call | solution.py:161
  81.5 4.5 %collective-permute-done.22.refs_14_ = bf16[256,512]{1,0:T(8,128)(2,1)S(1)} collective-permute-done((bf16[256,512]{1,0:T(8,128)(2,1)S(1)}, bf16[256,512]{1,0:T(8,128)(2,1)S(1)}, u32[]{:S(2)}, u32[]{:S(2)}) %collective-permute-start.22) | collective-permute-done | bytes 262176 | tf_op jit(solution)/shard_map/ppermute | solution.py:353
  86.0 0.0 copy-start
  86.0 0.0 copy-start.1
  86.0 0.0 copy-start.2
  86.0 3.7 %owned_features.11 = (bf16[512,2048]{1,0:T(8,128)(2,1)S(1)}, f32[8,128]{1,0:T(8,128)}) custom-call(s32[1]{0:T(128)} %bitcast.1.p, bf16[512,256]{1,0:T(8,128)(2,1)S(1)} %collective-permute-done.17.chosen, bf16[256,8192]{1,0:T(8,128)(2,1)S(1)} %copy-done.5, f32[1,8192]{1,0:T(1,128)S(1)} %bitcast.10, f32[8,128]{1,0:T(8,128)S(1)} %get-tuple-element.87.refs_0_), custom_call_target="tpu_custom_call" | custom-call | flops 4000000000 | bytes 1024 | tf_op jit(solution)/shard_map/owned_features/pallas_call | solution.py:161
  89.7 4.4 %update.4 = (f32[1,2048,256]{2,1,0:T(8,128)}, f32[1,2048,256]{2,1,0:T(8,128)}, f32[1,2048,256]{2,1,0:T(8,128)}, bf16[512,256]{1,0:T(8,128)(2,1)S(1)}) custom-call(bf16[512,2048]{1,0:T(8,128)(2,1)S(1)} %get-tuple-element.79.refs_0_, bf16[512,2048]{1,0:T(8,128)(2,1)S(1)} %get-tuple-element.80.refs_1_, bf16[512,2048]{1,0:T(8,128)(2,1)S(1)} %get-tuple-element.81.refs_2_, ...), custom_call_target="tpu_custom_call" | custom-call | flops 4000000000 | bytes 1024 | tf_op jit(solution)/shard_map/update/pallas_call | solution.py:295
  94.1 0.5 collective-permute-start.24
  94.6 4.3 %update.5 = (f32[1,2048,256]{2,1,0:T(8,128)}, f32[1,2048,256]{2,1,0:T(8,128)}, f32[1,2048,256]{2,1,0:T(8,128)}, bf16[512,256]{1,0:T(8,128)(2,1)S(1)}) custom-call(bf16[512,2048]{1,0:T(8,128)(2,1)S(1)} %get-tuple-element.79.refs_0_, bf16[512,2048]{1,0:T(8,128)(2,1)S(1)} %get-tuple-element.80.refs_1_, ...), custom_call_target="tpu_custom_call", output_to_operand_aliasing={{0}: (20, {}), {1}: (21, {}), {2}: (22, {})} | custom-call | flops 4000000000 | bytes 1024 | tf_op jit(solution)/shard_map/update/pallas_call | solution.py:295
  98.9 1.6 %collective-permute-start.25 = (bf16[512,256]{1,0:T(8,128)(2,1)S(1)}, bf16[512,256]{1,0:T(8,128)(2,1)S(1)}, u32[]{:S(2)}, u32[]{:S(2)}) collective-permute-start(bf16[512,256]{1,0:T(8,128)(2,1)S(1)} %get-tuple-element.101.refs_0_), channel_id=1, source_target_pairs={{0,8},{4,12},{8,0},{12,4},{1,9},{5,13},{9,1},{13,5},{2,10},{6,14},... | collective-permute-start | bytes 786440 | tf_op jit(solution)/shard_map/ppermute | solution.py:353
  100.5 0.5 collective-permute-start.34
  101.0 2.2 %collective-permute-done.24.refs_23_.refs_2_ = bf16[512,256]{1,0:T(8,128)(2,1)S(1)} collective-permute-done((bf16[512,256]{1,0:T(8,128)(2,1)S(1)}, bf16[512,256]{1,0:T(8,128)(2,1)S(1)}, u32[]{:S(2)}, u32[]{:S(2)}) %collective-permute-start.24) | collective-permute-done | bytes 262176 | tf_op jit(solution)/shard_map/ppermute | solution.py:353
  103.2 4.3 %update.6 = (f32[1,2048,256]{2,1,0:T(8,128)}, f32[1,2048,256]{2,1,0:T(8,128)}, f32[1,2048,256]{2,1,0:T(8,128)}, bf16[512,256]{1,0:T(8,128)(2,1)S(1)}) custom-call(bf16[512,2048]{1,0:T(8,128)(2,1)S(1)} %get-tuple-element.79.refs_0_, bf16[512,2048]{1,0:T(8,128)(2,1)S(1)} %get-tuple-element.80.refs_1_, ...), custom_call_target="tpu_custom_call", output_to_operand_aliasing={{0}: (20, {}), {1}: (21, {}), {2}: (22, {})} | custom-call | flops 4000000000 | bytes 1024 | tf_op jit(solution)/shard_map/update/pallas_call | solution.py:295
  107.6 0.0 collective-permute-start.30
  107.6 0.8 collective-permute-done.25.refs_23_.refs_2_
  108.4 4.3 %update.7 = (f32[1,2048,256]{2,1,0:T(8,128)}, f32[1,2048,256]{2,1,0:T(8,128)}, f32[1,2048,256]{2,1,0:T(8,128)}, bf16[512,256]{1,0:T(8,128)(2,1)S(1)}) custom-call(bf16[512,2048]{1,0:T(8,128)(2,1)S(1)} %get-tuple-element.79.refs_0_, bf16[512,2048]{1,0:T(8,128)(2,1)S(1)} %get-tuple-element.80.refs_1_, ...), custom_call_target="tpu_custom_call", output_to_operand_aliasing={{0}: (20, {}), {1}: (21, {}), {2}: (22, {})} | custom-call | flops 4000000000 | bytes 1024 | tf_op jit(solution)/shard_map/update/pallas_call | solution.py:295
  112.7 1.2 collective-permute-start.27
  113.9 0.5 collective-permute-start.33
  114.5 0.1 collective-permute-start.29
  114.5 0.5 collective-permute-done.30.refs_2_
  115.0 5.6 %collective-permute-done.27.refs_2_ = bf16[512,256]{1,0:T(8,128)(2,1)S(1)} collective-permute-done((bf16[512,256]{1,0:T(8,128)(2,1)S(1)}, bf16[512,256]{1,0:T(8,128)(2,1)S(1)}, u32[]{:S(2)}, u32[]{:S(2)}) %collective-permute-start.27) | collective-permute-done | bytes 262176 | tf_op jit(solution)/shard_map/ppermute | solution.py:353
  120.7 0.5 collective-permute-start.28
  121.2 1.0 put_rows.4.refs_4_
  122.2 1.0 put_rows.5.refs_4_
  123.2 1.0 put_rows.6.refs_4_
  124.2 1.0 put_rows.7
  (50 shorter events, 0.2 us)
Async XLA Ops:
  0.6 2.2 %copy-start.3 = (bf16[8192,256]{1,0:T(8,128)(2,1)S(1)}, bf16[8192,256]{1,0:T(8,128)(2,1)}, u32[]{:S(2)}) copy-start(bf16[8192,256]{1,0:T(8,128)(2,1)} %weights.3) | copy-start | bytes 12582916
  2.8 2.2 %copy-start.4 = (bf16[256,8192]{1,0:T(8,128)(2,1)S(1)}, bf16[256,8192]{1,0:T(8,128)(2,1)}, u32[]{:S(2)}) copy-start(bf16[256,8192]{1,0:T(8,128)(2,1)} %omega.15) | copy-start | bytes 12582916
  5.0 1.2 copy-start.6
  6.2 0.8 copy-start.8
  7.0 0.7 copy-start.10
  22.9 35.9 %collective-permute-start.3 = (bf16[512,256]{1,0:T(8,128)(2,1)S(1)}, bf16[512,256]{1,0:T(8,128)(2,1)S(1)}, u32[]{:S(2)}, u32[]{:S(2)}) collective-permute-start(bf16[512,256]{1,0:T(8,128)(2,1)S(1)} %get-tuple-element.61), channel_id=1, source_target_pairs={{0,8},{4,12},{8,0},{12,4},{1,9},{5,13},{9,1},{13,5},{2,10},{6,14},... | collective-permute-start | bytes 786440 | tf_op jit(solution)/shard_map/ppermute | solution.py:353
  25.9 24.8 %collective-permute-start.4 = (bf16[512,256]{1,0:T(8,128)(2,1)S(1)}, bf16[512,256]{1,0:T(8,128)(2,1)S(1)}, u32[]{:S(2)}, u32[]{:S(2)}) collective-permute-start(bf16[512,256]{1,0:T(8,128)(2,1)S(1)} %get-tuple-element.61), channel_id=1, source_target_pairs={{0,4},{4,0},{8,12},{12,8},{1,5},{5,1},{9,13},{13,9},{2,6},{6,2},{1... | collective-permute-start | bytes 786440 | tf_op jit(solution)/shard_map/ppermute | solution.py:357
  25.9 20.8 %collective-permute-start.5 = (bf16[128,256]{1,0:T(8,128)(2,1)S(1)}, bf16[128,256]{1,0:T(8,128)(2,1)S(1)}, u32[]{:S(2)}, u32[]{:S(2)}) collective-permute-start(bf16[128,256]{1,0:T(8,128)(2,1)S(1)} %get-tuple-element.63), channel_id=1, source_target_pairs={{0,1},{1,2},{2,3},{3,0},{4,5},{5,6},{6,7},{7,4},{8,9},{9,10},{10,1... | collective-permute-start | bytes 196616 | tf_op jit(solution)/shard_map/ppermute | solution.py:353
  27.5 19.9 %collective-permute-start.6 = (bf16[128,256]{1,0:T(8,128)(2,1)S(1)}, bf16[128,256]{1,0:T(8,128)(2,1)S(1)}, u32[]{:S(2)}, u32[]{:S(2)}) collective-permute-start(bf16[128,256]{1,0:T(8,128)(2,1)S(1)} %get-tuple-element.64), channel_id=1, source_target_pairs={{0,2},{1,3},{2,0},{3,1},{4,6},{5,7},{6,4},{7,5},{8,10},{9,11},{10,... | collective-permute-start | bytes 196616 | tf_op jit(solution)/shard_map/ppermute | solution.py:353
  30.1 17.7 %collective-permute-start.7 = (bf16[128,256]{1,0:T(8,128)(2,1)S(1)}, bf16[128,256]{1,0:T(8,128)(2,1)S(1)}, u32[]{:S(2)}, u32[]{:S(2)}) collective-permute-start(bf16[128,256]{1,0:T(8,128)(2,1)S(1)} %get-tuple-element.65), channel_id=1, source_target_pairs={{0,3},{1,0},{2,1},{3,2},{4,7},{5,4},{6,5},{7,6},{8,11},{9,8},{10,9... | collective-permute-start | bytes 196616 | tf_op jit(solution)/shard_map/ppermute | solution.py:353
  31.4 19.8 %copy-start.5 = (bf16[256,8192]{1,0:T(8,128)(2,1)S(1)}, bf16[256,8192]{1,0:T(8,128)(2,1)}, u32[]{:S(2)}) copy-start(bf16[256,8192]{1,0:T(8,128)(2,1)} %omega.15) | copy-start | bytes 12582916
  46.7 7.6 %collective-permute-start = (bf16[128,256]{1,0:T(8,128)(2,1)S(1)}, bf16[128,256]{1,0:T(8,128)(2,1)S(1)}, u32[]{:S(2)}, u32[]{:S(2)}) collective-permute-start(bf16[128,256]{1,0:T(8,128)(2,1)S(1)} %get-tuple-element.58), channel_id=1, source_target_pairs={{0,1},{1,2},{2,3},{3,0},{4,5},{5,6},{6,7},{7,4},{8,9},{9,10},{10,1... | collective-permute-start | bytes 196616 | tf_op jit(solution)/shard_map/ppermute | solution.py:353
  47.4 8.5 %collective-permute-start.1 = (bf16[128,256]{1,0:T(8,128)(2,1)S(1)}, bf16[128,256]{1,0:T(8,128)(2,1)S(1)}, u32[]{:S(2)}, u32[]{:S(2)}) collective-permute-start(bf16[128,256]{1,0:T(8,128)(2,1)S(1)} %get-tuple-element.59), channel_id=1, source_target_pairs={{0,2},{1,3},{2,0},{3,1},{4,6},{5,7},{6,4},{7,5},{8,10},{9,11},{10,... | collective-permute-start | bytes 196616 | tf_op jit(solution)/shard_map/ppermute | solution.py:353
  47.8 14.1 %collective-permute-start.2 = (bf16[128,256]{1,0:T(8,128)(2,1)S(1)}, bf16[128,256]{1,0:T(8,128)(2,1)S(1)}, u32[]{:S(2)}, u32[]{:S(2)}) collective-permute-start(bf16[128,256]{1,0:T(8,128)(2,1)S(1)} %get-tuple-element.60), channel_id=1, source_target_pairs={{0,3},{1,0},{2,1},{3,2},{4,7},{5,4},{6,5},{7,6},{8,11},{9,8},{10,9... | collective-permute-start | bytes 196616 | tf_op jit(solution)/shard_map/ppermute | solution.py:353
  50.7 11.8 %collective-permute-start.13 = (bf16[128,256]{1,0:T(8,128)(2,1)S(1)}, bf16[128,256]{1,0:T(8,128)(2,1)S(1)}, u32[]{:S(2)}, u32[]{:S(2)}) collective-permute-start(bf16[128,256]{1,0:T(8,128)(2,1)S(1)} %get-tuple-element.72.refs_0_), channel_id=1, source_target_pairs={{0,1},{1,2},{2,3},{3,0},{4,5},{5,6},{6,7},{7,4},{8,9},{9,10},{10,1... | collective-permute-start | bytes 196616 | tf_op jit(solution)/shard_map/ppermute | solution.py:353
  54.3 8.8 %collective-permute-start.14 = (bf16[128,256]{1,0:T(8,128)(2,1)S(1)}, bf16[128,256]{1,0:T(8,128)(2,1)S(1)}, u32[]{:S(2)}, u32[]{:S(2)}) collective-permute-start(bf16[128,256]{1,0:T(8,128)(2,1)S(1)} %get-tuple-element.72.refs_0_), channel_id=1, source_target_pairs={{0,2},{1,3},{2,0},{3,1},{4,6},{5,7},{6,4},{7,5},{8,10},{9,11},{10,... | collective-permute-start | bytes 196616 | tf_op jit(solution)/shard_map/ppermute | solution.py:353
  55.9 7.2 %collective-permute-start.15 = (bf16[128,256]{1,0:T(8,128)(2,1)S(1)}, bf16[128,256]{1,0:T(8,128)(2,1)S(1)}, u32[]{:S(2)}, u32[]{:S(2)}) collective-permute-start(bf16[128,256]{1,0:T(8,128)(2,1)S(1)} %get-tuple-element.72.refs_0_), channel_id=1, source_target_pairs={{0,3},{1,0},{2,1},{3,2},{4,7},{5,4},{6,5},{7,6},{8,11},{9,8},{10,9... | collective-permute-start | bytes 196616 | tf_op jit(solution)/shard_map/ppermute | solution.py:353
  58.8 6.3 %collective-permute-start.12 = (bf16[512,256]{1,0:T(8,128)(2,1)S(1)}, bf16[512,256]{1,0:T(8,128)(2,1)S(1)}, u32[]{:S(2)}, u32[]{:S(2)}) collective-permute-start(bf16[512,256]{1,0:T(8,128)(2,1)S(1)} %collective-permute-done.3.chosen), channel_id=1, source_target_pairs={{0,4},{4,0},{8,12},{12,8},{1,5},{5,1},{9,13},{13,9},{2,6},{6,2},{1... | collective-permute-start | bytes 786440 | tf_op jit(solution)/shard_map/ppermute | solution.py:357
  58.8 5.3 %copy-start.7 = (s32[2,512,256]{2,1,0:T(8,128)S(1)}, s32[2,512,256]{2,1,0:T(8,128)}, u32[]{:S(2)}) copy-start(s32[2,512,256]{2,1,0:T(8,128)} %refs_4_.3) | copy-start | bytes 3145732
  61.9 9.1 %collective-permute-start.11 = (bf16[512,256]{1,0:T(8,128)(2,1)S(1)}, bf16[512,256]{1,0:T(8,128)(2,1)S(1)}, u32[]{:S(2)}, u32[]{:S(2)}) collective-permute-start(bf16[512,256]{1,0:T(8,128)(2,1)S(1)} %get-tuple-element.71), channel_id=1, source_target_pairs={{0,4},{4,0},{8,12},{12,8},{1,5},{5,1},{9,13},{13,9},{2,6},{6,2},{1... | collective-permute-start | bytes 786440 | tf_op jit(solution)/shard_map/ppermute | solution.py:357
  62.5 13.2 %collective-permute-start.16 = (bf16[512,256]{1,0:T(8,128)(2,1)S(1)}, bf16[512,256]{1,0:T(8,128)(2,1)S(1)}, u32[]{:S(2)}, u32[]{:S(2)}) collective-permute-start(bf16[512,256]{1,0:T(8,128)(2,1)S(1)} %get-tuple-element.71), channel_id=1, source_target_pairs={{0,8},{4,12},{8,0},{12,4},{1,9},{5,13},{9,1},{13,5},{2,10},{6,14},... | collective-permute-start | bytes 786440 | tf_op jit(solution)/shard_map/ppermute | solution.py:353
  63.1 12.7 %collective-permute-start.8 = (bf16[128,256]{1,0:T(8,128)(2,1)S(1)}, bf16[128,256]{1,0:T(8,128)(2,1)S(1)}, u32[]{:S(2)}, u32[]{:S(2)}) collective-permute-start(bf16[128,256]{1,0:T(8,128)(2,1)S(1)} %get-tuple-element.70.refs_0_), channel_id=1, source_target_pairs={{0,1},{1,2},{2,3},{3,0},{4,5},{5,6},{6,7},{7,4},{8,9},{9,10},{10,1... | collective-permute-start | bytes 196616 | tf_op jit(solution)/shard_map/ppermute | solution.py:353
  63.1 13.2 %collective-permute-start.9 = (bf16[128,256]{1,0:T(8,128)(2,1)S(1)}, bf16[128,256]{1,0:T(8,128)(2,1)S(1)}, u32[]{:S(2)}, u32[]{:S(2)}) collective-permute-start(bf16[128,256]{1,0:T(8,128)(2,1)S(1)} %get-tuple-element.70.refs_0_), channel_id=1, source_target_pairs={{0,2},{1,3},{2,0},{3,1},{4,6},{5,7},{6,4},{7,5},{8,10},{9,11},{10,... | collective-permute-start | bytes 196616 | tf_op jit(solution)/shard_map/ppermute | solution.py:353
  65.0 11.2 %collective-permute-start.10 = (bf16[128,256]{1,0:T(8,128)(2,1)S(1)}, bf16[128,256]{1,0:T(8,128)(2,1)S(1)}, u32[]{:S(2)}, u32[]{:S(2)}) collective-permute-start(bf16[128,256]{1,0:T(8,128)(2,1)S(1)} %get-tuple-element.70.refs_0_), channel_id=1, source_target_pairs={{0,3},{1,0},{2,1},{3,2},{4,7},{5,4},{6,5},{7,6},{8,11},{9,8},{10,9... | collective-permute-start | bytes 196616 | tf_op jit(solution)/shard_map/ppermute | solution.py:353
  71.0 7.4 %collective-permute-start.19 = (bf16[256,512]{1,0:T(8,128)(2,1)S(1)}, bf16[256,512]{1,0:T(8,128)(2,1)S(1)}, u32[]{:S(2)}, u32[]{:S(2)}) collective-permute-start(bf16[256,512]{1,0:T(8,128)(2,1)S(1)} %get-tuple-element.89.refs_8_), channel_id=1, source_target_pairs={{0,8},{4,12},{8,0},{12,4},{1,9},{5,13},{9,1},{13,5},{2,10},{6,14},... | collective-permute-start | bytes 786440 | tf_op jit(solution)/shard_map/ppermute | solution.py:353
  75.7 14.0 %collective-permute-start.18 = (bf16[256,512]{1,0:T(8,128)(2,1)S(1)}, bf16[256,512]{1,0:T(8,128)(2,1)S(1)}, u32[]{:S(2)}, u32[]{:S(2)}) collective-permute-start(bf16[256,512]{1,0:T(8,128)(2,1)S(1)} %get-tuple-element.89.refs_8_), channel_id=1, source_target_pairs={{0,4},{4,0},{8,12},{12,8},{1,5},{5,1},{9,13},{13,9},{2,6},{6,2},{1... | collective-permute-start | bytes 786440 | tf_op jit(solution)/shard_map/ppermute | solution.py:357
  75.8 10.2 %collective-permute-start.17 = (bf16[512,256]{1,0:T(8,128)(2,1)S(1)}, bf16[512,256]{1,0:T(8,128)(2,1)S(1)}, u32[]{:S(2)}, u32[]{:S(2)}) collective-permute-start(bf16[512,256]{1,0:T(8,128)(2,1)S(1)} %collective-permute-done.16.chosen), channel_id=1, source_target_pairs={{0,4},{4,0},{8,12},{12,8},{1,5},{5,1},{9,13},{13,9},{2,6},{6,2},{1... | collective-permute-start | bytes 786440 | tf_op jit(solution)/shard_map/ppermute | solution.py:357
  77.2 12.5 %collective-permute-start.21 = (bf16[256,512]{1,0:T(8,128)(2,1)S(1)}, bf16[256,512]{1,0:T(8,128)(2,1)S(1)}, u32[]{:S(2)}, u32[]{:S(2)}) collective-permute-start(bf16[256,512]{1,0:T(8,128)(2,1)S(1)} %get-tuple-element.90.refs_12_), channel_id=1, source_target_pairs={{0,4},{4,0},{8,12},{12,8},{1,5},{5,1},{9,13},{13,9},{2,6},{6,2},{1... | collective-permute-start | bytes 786440 | tf_op jit(solution)/shard_map/ppermute | solution.py:357
  77.3 8.7 %collective-permute-start.22 = (bf16[256,512]{1,0:T(8,128)(2,1)S(1)}, bf16[256,512]{1,0:T(8,128)(2,1)S(1)}, u32[]{:S(2)}, u32[]{:S(2)}) collective-permute-start(bf16[256,512]{1,0:T(8,128)(2,1)S(1)} %get-tuple-element.90.refs_12_), channel_id=1, source_target_pairs={{0,8},{4,12},{8,0},{12,4},{1,9},{5,13},{9,1},{13,5},{2,10},{6,14},... | collective-permute-start | bytes 786440 | tf_op jit(solution)/shard_map/ppermute | solution.py:353
  78.4 11.3 %collective-permute-start.20 = (bf16[256,512]{1,0:T(8,128)(2,1)S(1)}, bf16[256,512]{1,0:T(8,128)(2,1)S(1)}, u32[]{:S(2)}, u32[]{:S(2)}) collective-permute-start(bf16[256,512]{1,0:T(8,128)(2,1)S(1)} %collective-permute-done.19.refs_10_), channel_id=1, source_target_pairs={{0,4},{4,0},{8,12},{12,8},{1,5},{5,1},{9,13},{13,9},{2,6},{6,2},{1... | collective-permute-start | bytes 786440 | tf_op jit(solution)/shard_map/ppermute | solution.py:357
  78.4 7.5 %copy-start.9 = (f32[8192]{0:T(1024)S(1)}, f32[8192]{0:T(1024)}, u32[]{:S(2)}) copy-start(f32[8192]{0:T(1024)} %param.13) | copy-start | bytes 98308
  86.0 3.7 %collective-permute-start.23 = (bf16[256,512]{1,0:T(8,128)(2,1)S(1)}, bf16[256,512]{1,0:T(8,128)(2,1)S(1)}, u32[]{:S(2)}, u32[]{:S(2)}) collective-permute-start(bf16[256,512]{1,0:T(8,128)(2,1)S(1)} %collective-permute-done.22.refs_14_), channel_id=1, source_target_pairs={{0,4},{4,0},{8,12},{12,8},{1,5},{5,1},{9,13},{13,9},{2,6},{6,2},{1... | collective-permute-start | bytes 786440 | tf_op jit(solution)/shard_map/ppermute | solution.py:357
  86.0 3.7 %copy-start = (f32[1,2048,256]{2,1,0:T(8,128)S(1)}, f32[1,2048,256]{2,1,0:T(8,128)}, u32[]{:S(2)}) copy-start(f32[1,2048,256]{2,1,0:T(8,128)} %refs_17_.7) | copy-start | bytes 6291460
  86.0 3.7 %copy-start.1 = (f32[1,2048,256]{2,1,0:T(8,128)S(1)}, f32[1,2048,256]{2,1,0:T(8,128)}, u32[]{:S(2)}) copy-start(f32[1,2048,256]{2,1,0:T(8,128)} %refs_18_.7) | copy-start | bytes 6291460
  86.0 3.7 %copy-start.2 = (bf16[256,256]{1,0:T(8,128)(2,1)S(1)}, bf16[256,256]{1,0:T(8,128)(2,1)}, u32[]{:S(2)}) copy-start(bf16[256,256]{1,0:T(8,128)(2,1)} %refs_16_.7) | copy-start | bytes 393220
  94.1 9.1 %collective-permute-start.24 = (bf16[512,256]{1,0:T(8,128)(2,1)S(1)}, bf16[512,256]{1,0:T(8,128)(2,1)S(1)}, u32[]{:S(2)}, u32[]{:S(2)}) collective-permute-start(bf16[512,256]{1,0:T(8,128)(2,1)S(1)} %get-tuple-element.97.refs_0_), channel_id=1, source_target_pairs={{0,8},{4,12},{8,0},{12,4},{1,9},{5,13},{9,1},{13,5},{2,10},{6,14},... | collective-permute-start | bytes 786440 | tf_op jit(solution)/shard_map/ppermute | solution.py:353
  98.9 9.5 %collective-permute-start.25 = (bf16[512,256]{1,0:T(8,128)(2,1)S(1)}, bf16[512,256]{1,0:T(8,128)(2,1)S(1)}, u32[]{:S(2)}, u32[]{:S(2)}) collective-permute-start(bf16[512,256]{1,0:T(8,128)(2,1)S(1)} %get-tuple-element.101.refs_0_), channel_id=1, source_target_pairs={{0,8},{4,12},{8,0},{12,4},{1,9},{5,13},{9,1},{13,5},{2,10},{6,14},... | collective-permute-start | bytes 786440 | tf_op jit(solution)/shard_map/ppermute | solution.py:353
  100.5 13.5 %collective-permute-start.32 = (bf16[512,256]{1,0:T(8,128)(2,1)S(1)}, bf16[512,256]{1,0:T(8,128)(2,1)S(1)}, u32[]{:S(2)}, u32[]{:S(2)}) collective-permute-start(bf16[512,256]{1,0:T(8,128)(2,1)S(1)} %get-tuple-element.101.refs_0_), channel_id=1, source_target_pairs={{0,4},{4,0},{8,12},{12,8},{1,5},{5,1},{9,13},{13,9},{2,6},{6,2},{1... | collective-permute-start | bytes 786440 | tf_op jit(solution)/shard_map/ppermute | solution.py:357
  100.5 14.0 %collective-permute-start.34 = (bf16[512,256]{1,0:T(8,128)(2,1)S(1)}, bf16[512,256]{1,0:T(8,128)(2,1)S(1)}, u32[]{:S(2)}, u32[]{:S(2)}) collective-permute-start(bf16[512,256]{1,0:T(8,128)(2,1)S(1)} %get-tuple-element.97.refs_0_), channel_id=1, source_target_pairs={{0,4},{4,0},{8,12},{12,8},{1,5},{5,1},{9,13},{13,9},{2,6},{6,2},{1... | collective-permute-start | bytes 786440 | tf_op jit(solution)/shard_map/ppermute | solution.py:357
  107.6 7.5 %collective-permute-start.30 = (bf16[512,256]{1,0:T(8,128)(2,1)S(1)}, bf16[512,256]{1,0:T(8,128)(2,1)S(1)}, u32[]{:S(2)}, u32[]{:S(2)}) collective-permute-start(bf16[512,256]{1,0:T(8,128)(2,1)S(1)} %get-tuple-element.106.refs_0_), channel_id=1, source_target_pairs={{0,8},{4,12},{8,0},{12,4},{1,9},{5,13},{9,1},{13,5},{2,10},{6,14},... | collective-permute-start | bytes 786440 | tf_op jit(solution)/shard_map/ppermute | solution.py:353
  112.7 7.9 %collective-permute-start.27 = (bf16[512,256]{1,0:T(8,128)(2,1)S(1)}, bf16[512,256]{1,0:T(8,128)(2,1)S(1)}, u32[]{:S(2)}, u32[]{:S(2)}) collective-permute-start(bf16[512,256]{1,0:T(8,128)(2,1)S(1)} %get-tuple-element.105.refs_0_), channel_id=1, source_target_pairs={{0,8},{4,12},{8,0},{12,4},{1,9},{5,13},{9,1},{13,5},{2,10},{6,14},... | collective-permute-start | bytes 786440 | tf_op jit(solution)/shard_map/ppermute | solution.py:353
  113.9 6.7 %collective-permute-start.35 = (bf16[512,256]{1,0:T(8,128)(2,1)S(1)}, bf16[512,256]{1,0:T(8,128)(2,1)S(1)}, u32[]{:S(2)}, u32[]{:S(2)}) collective-permute-start(bf16[512,256]{1,0:T(8,128)(2,1)S(1)} %collective-permute-done.24.refs_23_.refs_2_), channel_id=1, source_target_pairs={{0,4},{4,0},{8,12},{12,8},{1,5},{5,1},{9,13},{13,9},{2,6},{6,2},{1... | collective-permute-start | bytes 786440 | tf_op jit(solution)/shard_map/ppermute | solution.py:357
  113.9 8.2 %collective-permute-start.33 = (bf16[512,256]{1,0:T(8,128)(2,1)S(1)}, bf16[512,256]{1,0:T(8,128)(2,1)S(1)}, u32[]{:S(2)}, u32[]{:S(2)}) collective-permute-start(bf16[512,256]{1,0:T(8,128)(2,1)S(1)} %collective-permute-done.25.refs_23_.refs_2_), channel_id=1, source_target_pairs={{0,4},{4,0},{8,12},{12,8},{1,5},{5,1},{9,13},{13,9},{2,6},{6,2},{1... | collective-permute-start | bytes 786440 | tf_op jit(solution)/shard_map/ppermute | solution.py:357
  114.5 8.7 %collective-permute-start.29 = (bf16[512,256]{1,0:T(8,128)(2,1)S(1)}, bf16[512,256]{1,0:T(8,128)(2,1)S(1)}, u32[]{:S(2)}, u32[]{:S(2)}) collective-permute-start(bf16[512,256]{1,0:T(8,128)(2,1)S(1)} %get-tuple-element.106.refs_0_), channel_id=1, source_target_pairs={{0,4},{4,0},{8,12},{12,8},{1,5},{5,1},{9,13},{13,9},{2,6},{6,2},{1... | collective-permute-start | bytes 786440 | tf_op jit(solution)/shard_map/ppermute | solution.py:357
  115.0 8.2 %collective-permute-start.31 = (bf16[512,256]{1,0:T(8,128)(2,1)S(1)}, bf16[512,256]{1,0:T(8,128)(2,1)S(1)}, u32[]{:S(2)}, u32[]{:S(2)}) collective-permute-start(bf16[512,256]{1,0:T(8,128)(2,1)S(1)} %collective-permute-done.30.refs_2_), channel_id=1, source_target_pairs={{0,4},{4,0},{8,12},{12,8},{1,5},{5,1},{9,13},{13,9},{2,6},{6,2},{1... | collective-permute-start | bytes 786440 | tf_op jit(solution)/shard_map/ppermute | solution.py:357
  120.6 3.6 %collective-permute-start.26 = (bf16[512,256]{1,0:T(8,128)(2,1)S(1)}, bf16[512,256]{1,0:T(8,128)(2,1)S(1)}, u32[]{:S(2)}, u32[]{:S(2)}) collective-permute-start(bf16[512,256]{1,0:T(8,128)(2,1)S(1)} %get-tuple-element.105.refs_0_), channel_id=1, source_target_pairs={{0,4},{4,0},{8,12},{12,8},{1,5},{5,1},{9,13},{13,9},{2,6},{6,2},{1... | collective-permute-start | bytes 786440 | tf_op jit(solution)/shard_map/ppermute | solution.py:357
  120.7 3.6 %collective-permute-start.28 = (bf16[512,256]{1,0:T(8,128)(2,1)S(1)}, bf16[512,256]{1,0:T(8,128)(2,1)S(1)}, u32[]{:S(2)}, u32[]{:S(2)}) collective-permute-start(bf16[512,256]{1,0:T(8,128)(2,1)S(1)} %collective-permute-done.27.refs_2_), channel_id=1, source_target_pairs={{0,4},{4,0},{8,12},{12,8},{1,5},{5,1},{9,13},{13,9},{2,6},{6,2},{1... | collective-permute-start | bytes 786440 | tf_op jit(solution)/shard_map/ppermute | solution.py:357

commit v3 on v2

v3 whole, which is shorter than its diff:
```python
import functools
import math

import jax
import jax.numpy as jnp
from jax import lax
from jax.experimental import pallas as pl
from jax.experimental.pallas import tpu as pltpu
from jax.sharding import PartitionSpec as P

F = 32768
STEP = 20
CORES = 2

beta_one = 0.9
beta_two = 0.999
learn_rate = 0.2

SINE = tuple(
    c / 8.0
    for c in (3.141582022078924, -5.167142793540227, 2.541899000696469, -0.5546361258792201)
)
ROUNDER = 12582912.0
TURN = 1.0 / (2.0 * math.pi)
VMEM = 30 * 1024 * 1024
WIDE = 58 * 1024 * 1024

f32 = jnp.float32
bf16 = jnp.bfloat16
IN_VMEM = pl.BlockSpec(memory_space=pltpu.VMEM)
ANYWHERE = pl.BlockSpec(memory_space=pl.ANY)


def scaled_cos(product, phase_turns):
    turns = product * TURN + phase_turns
    r = turns - ((turns + ROUNDER) - ROUNDER)
    s = r * r
    w = ((SINE[3] * s + SINE[2]) * s + SINE[1]) * s + SINE[0]
    w = w * r
    return (math.sqrt(2.0 / F) - w * w).astype(bf16)


TOKEN = jax.ShapeDtypeStruct((8, 128), f32)


def cost(microseconds):
    return pl.CostEstimate(
        flops=int(microseconds * 1.0e9), bytes_accessed=1 << 10, transcendentals=0
    )


def params(limit=None):
    return pltpu.CompilerParams(vmem_limit_bytes=limit or VMEM)


def gather_kernel(picks, points, chosen, token):
    batch, pool = chosen.shape[0], points.shape[0]
    m = pl.program_id(0)
    wanted = jnp.broadcast_to(picks[pl.ds(m, 1), :], (128, batch)).T
    lane = lax.broadcasted_iota(jnp.int32, (batch, 128), 1)
    hot = [jnp.where(wanted == lane + 128 * j, 1.0, 0.0).astype(bf16) for j in range(pool // 128)]
    chosen[...] = jnp.dot(
        jnp.concatenate(hot, axis=1), points[...], preferred_element_type=f32
    ).astype(bf16)


def gather(picks, points):
    batch = picks.shape[1]
    pool, ins = points.shape
    return pl.pallas_call(
        gather_kernel,
        grid=(2,),
        in_specs=[
            pl.BlockSpec(picks.shape, lambda i: (0, 0)),
            pl.BlockSpec((pool, ins), lambda i: (0, 0)),
        ],
        out_specs=[pl.BlockSpec((batch, ins), lambda i: (i, 0)), ANYWHERE],
        out_shape=[jax.ShapeDtypeStruct((2 * batch, ins), bf16), TOKEN],
        compiler_params=params(WIDE),
        cost_estimate=cost(3),
        name="chosen_points",
    )(picks, points)


def rates_kernel(owned_blocks, f, p, chosen, omega, phase, weights, *refs):
    owned, *outs, token, feats, total = refs
    step = pl.program_id(0)
    width = omega.shape[1]
    tile = min(256, width)
    pair = min(512, width)

    @pl.when(step == 0)
    def _():
        total[...] = jnp.zeros_like(total)

    turns = phase[...] * TURN
    part = None
    for c in range(width // tile):
        cols = slice(c * tile, (c + 1) * tile)
        product = jnp.dot(chosen[...], omega[:, cols], preferred_element_type=f32)
        feats[:, cols] = scaled_cos(product, turns[:, cols])
        if (c + 1) * tile % pair == 0:
            rows = slice((c + 1) * tile - pair, (c + 1) * tile)
            term = jnp.dot(feats[:, rows], weights[rows, :], preferred_element_type=f32)
            part = term if part is None else part + term
    total[...] += part

    @pl.when(step < owned_blocks)
    def _():
        owned[...] = feats[...]

    @pl.when(step == pl.num_programs(0) - 1)
    def _():
        if len(outs) == 1:
            outs[0][...] = total[...].astype(bf16)
        else:
            split(total, f[0], 0, *outs)


def split(value, f, bit, kept, sent):
    rows = kept.shape[0]
    side = lax.rem(f // 2**bit, 2)
    kept[...] = value[pl.ds(pl.multiple_of(side * rows, rows), rows), :]
    sent[...] = value[pl.ds(pl.multiple_of((1 - side) * rows, rows), rows), :].astype(bf16)


def rates(f, p, chosen, omega, phase, weights, m, owned, halves, deps):
    ins, feat_dev = omega.shape
    k = weights.shape[1]
    batch = chosen.shape[0] // 2
    width = min(1024, owned)
    grid = feat_dev // width
    blocks = owned // width

    def turned(i, p):
        return lax.rem(i + p[0] * blocks, grid)

    if halves:
        outs = [
            jax.ShapeDtypeStruct((batch // 2, k), f32),
            jax.ShapeDtypeStruct((batch // 2, k), bf16),
        ]
    else:
        outs = [jax.ShapeDtypeStruct((batch, k), bf16)]
    n_refs = len(outs) + 4

    def kernel(f, p, chosen, omega, phase, weights, *refs):
        rates_kernel(blocks, f, p, chosen, omega, phase, weights, *refs[-n_refs:])

    return pl.pallas_call(
        kernel,
        grid_spec=pltpu.PrefetchScalarGridSpec(
            num_scalar_prefetch=2,
            grid=(grid,),
            in_specs=[
                pl.BlockSpec((batch, ins), lambda i, f, p: (m, 0)),
                pl.BlockSpec((ins, width), lambda i, f, p: (0, turned(i, p))),
                pl.BlockSpec((1, width), lambda i, f, p: (0, turned(i, p))),
                pl.BlockSpec((width, k), lambda i, f, p: (turned(i, p), 0)),
            ]
            + [ANYWHERE] * len(deps),
            out_specs=[pl.BlockSpec((batch, width), lambda i, f, p: (0, jnp.minimum(i, blocks - 1)))]
            + [IN_VMEM] * len(outs)
            + [ANYWHERE],
            scratch_shapes=[pltpu.VMEM((batch, width), bf16), pltpu.VMEM((batch, k), f32)],
        ),
        out_shape=[jax.ShapeDtypeStruct((batch, owned), bf16), *outs, TOKEN],
        compiler_params=params(WIDE),
        cost_estimate=cost(12),
        name="partial_log_rates",
    )(f, p, chosen, omega, phase, weights, *deps)


def features_kernel(tile, p, chosen, omega, phase, *refs):
    out, token = refs[-2:]
    turns = phase[...] * TURN
    for c in range(omega.shape[1] // tile):
        cols = slice(c * tile, (c + 1) * tile)
        product = jnp.dot(chosen[0], omega[:, cols], preferred_element_type=f32)
        out[:, cols] = scaled_cos(product, turns[:, cols])


def owned_features(p, everyone, omega, phase, owned, m, j, deps):
    n, points, ins = everyone.shape
    points //= 2
    width = min(512, owned)
    blocks = owned // width
    return pl.pallas_call(
        functools.partial(features_kernel, min(256, width)),
        grid_spec=pltpu.PrefetchScalarGridSpec(
            num_scalar_prefetch=1,
            grid=(blocks,),
            in_specs=[
                pl.BlockSpec((1, points, ins), lambda i, p: (lax.rem(p[0] + j, n), m, 0)),
                pl.BlockSpec((ins, width), lambda i, p: (0, p[0] * blocks + i)),
                pl.BlockSpec((1, width), lambda i, p: (0, p[0] * blocks + i)),
            ]
            + [ANYWHERE] * len(deps),
            out_specs=[pl.BlockSpec((points, width), lambda i, p: (0, i)), ANYWHERE],
        ),
        out_shape=[jax.ShapeDtypeStruct((points, owned), bf16), TOKEN],
        compiler_params=params(),
        cost_estimate=cost(4),
        name="owned_features",
    )(p, everyone, omega, phase, *deps)


def total_kernel(bit, halves, f, a, b, *refs):
    value = a[...].astype(f32) + b[...].astype(f32)
    if halves:
        kept, sent, token, held = refs[-4:]
        held[...] = value
        split(held, f[0], bit, kept, sent)
    else:
        out, token = refs[-2:]
        out[...] = value.astype(bf16)


def total(f, a, b, bit, halves, deps):
    rows, k = a.shape
    if halves:
        outs = [
            jax.ShapeDtypeStruct((rows // 2, k), f32),
            jax.ShapeDtypeStruct((rows // 2, k), bf16),
        ]
    else:
        outs = [jax.ShapeDtypeStruct((rows, k), bf16)]
    return pl.pallas_call(
        functools.partial(total_kernel, bit, halves),
        grid_spec=pltpu.PrefetchScalarGridSpec(
            num_scalar_prefetch=1,
            grid=(1,),
            in_specs=[IN_VMEM] * 2 + [ANYWHERE] * len(deps),
            out_specs=[IN_VMEM] * len(outs) + [ANYWHERE],
            scratch_shapes=[pltpu.VMEM((rows, k), f32)] if halves else [],
        ),
        out_shape=[*outs, TOKEN],
        compiler_params=params(),
        cost_estimate=cost(0.5),
        name="total_rates",
    )(f, a, b, *deps)


def residual_kernel(masks, m, f, *refs):
    chunks, observed = refs[: len(masks)], refs[len(masks)]
    rate_out, residual_out, token, held = refs[-4:]
    batch = held.shape[0]
    for j, mask in enumerate(masks):
        rows = chunks[j].shape[0]
        start, bit = 0, 0
        while batch >> (bit + 1) >= rows:
            side = lax.rem(f[0] // 2**bit, 2)
            side = 1 - side if mask >> bit & 1 else side
            start = start + side * (batch >> (bit + 1))
            bit += 1
        at = pl.ds(pl.multiple_of(start, rows), rows) if bit else slice(None)
        rate = chunks[j][...].astype(f32)
        rate_out[0, at, :] = rate
        held[at, :] = jnp.exp(rate) - observed[0, at, :].astype(f32)
    residual_out[...] = held[...].T.astype(bf16)


def residuals(f, chunks, masks, counts, m, before, deps):
    n = len(chunks)
    k = chunks[0].shape[1]
    batch = counts.shape[1]
    args = [f, *chunks, counts, *deps]
    specs = [IN_VMEM] * n + [pl.BlockSpec((1, batch, k), lambda i, _: (m, 0, 0))]
    specs += [ANYWHERE] * len(deps)
    aliases = {}
    if before is not None:
        aliases = {len(args): 0}
        args.append(before)
        specs.append(ANYWHERE)
    return pl.pallas_call(
        functools.partial(residual_kernel, masks, m),
        grid_spec=pltpu.PrefetchScalarGridSpec(
            num_scalar_prefetch=1,
            grid=(1,),
            in_specs=specs,
            out_specs=[pl.BlockSpec((1, batch, k), lambda i, _: (m, 0, 0)), IN_VMEM, ANYWHERE],
            scratch_shapes=[pltpu.VMEM((batch, k), f32)],
        ),
        out_shape=[
            jax.ShapeDtypeStruct(counts.shape, f32),
            jax.ShapeDtypeStruct((k, batch), bf16),
            TOKEN,
        ],
        input_output_aliases=aliases,
        compiler_params=params(),
        cost_estimate=cost(1),
        name="residuals",
    )(*args)


def gradient_part(n, p, features, residual):
    value = None
    for j in range(n):
        term = jnp.dot(
            residual[lax.rem(p[0] + j, n)], features[j][...], preferred_element_type=f32
        )
        value = term if value is None else value + term
    return value


def first_part_kernel(n, p, *refs):
    features, residual, master = refs[:n], refs[n], refs[n + 1]
    out, token = refs[-2:]
    out[...] = gradient_part(n, p, features, residual).T + master[0]


def first_part(p, features, residual, master, deps):
    n = len(features)
    owned, k = master.shape[1:]
    rows = min(512, owned)
    batch = features[0].shape[0]
    return pl.pallas_call(
        functools.partial(first_part_kernel, n),
        grid_spec=pltpu.PrefetchScalarGridSpec(
            num_scalar_prefetch=1,
            grid=(owned // rows,),
            in_specs=[pl.BlockSpec((batch, rows), lambda i, p: (0, i))] * n
            + [IN_VMEM, pl.BlockSpec((1, rows, k), lambda i, p: (0, i, 0))]
            + [ANYWHERE] * len(deps),
            out_specs=[pl.BlockSpec((rows, k), lambda i, p: (i, 0)), ANYWHERE],
        ),
        out_shape=[jax.ShapeDtypeStruct((owned, k), f32), TOKEN],
        compiler_params=params(),
        cost_estimate=cost(5),
        name="first_part",
    )(p, *features, residual, master, *deps)


def update_kernel(n, p, *refs):
    features, residual = refs[:n], refs[n]
    begun, cov, master, first, second = refs[n + 1 : n + 6]
    new_master, new_first, new_second, kept, sent = refs[-5:]
    rows = master.shape[1]
    gradient = gradient_part(n, p, features, residual).T + begun[...]
    conditioned = jnp.dot(gradient.astype(bf16), cov[...], preferred_element_type=f32)
    moved_first = beta_one * first[0] + (1.0 - beta_one) * conditioned
    moved_second = beta_two * second[0] + (1.0 - beta_two) * conditioned * conditioned
    correction_one = 1.0 - beta_one**STEP
    correction_two = 1.0 - beta_two**STEP
    moved = master[0] - learn_rate * (moved_first / correction_one) / (
        jnp.sqrt(moved_second / correction_two) + 1e-08
    )
    new_first[0] = moved_first
    new_second[0] = moved_second
    new_master[0] = moved
    rounded = moved.astype(bf16)
    kept[...] = rounded
    sent[pl.ds(pl.multiple_of(pl.program_id(0) * rows, rows), rows), :] = rounded


def update(p, features, residual, begun, cov, master, first, second, at, steps, before, deps):
    n = len(features)
    owned, k = master.shape[1:]
    rows = min(256, owned)
    batch = features[0].shape[0]
    state = pl.BlockSpec((1, rows, k), lambda i, p: (0, at + i, 0))
    flat = pl.BlockSpec((rows, k), lambda i, p: (at + i, 0))
    args = [p, *features, residual, begun, cov, master, first, second]
    specs = (
        [pl.BlockSpec((batch, rows), lambda i, p: (0, at + i))] * n
        + [IN_VMEM, flat]
        + [pl.BlockSpec(cov.shape, lambda i, p: (0, 0)), state, state, state]
    )
    aliases = {}
    if before is not None:
        aliases = {len(args) + j: j for j in range(4)}
        args += list(before)
        specs += [ANYWHERE] * 4
    args += deps
    specs += [ANYWHERE] * len(deps)
    return pl.pallas_call(
        functools.partial(update_kernel, n),
        grid_spec=pltpu.PrefetchScalarGridSpec(
            num_scalar_prefetch=1,
            grid=(steps,),
            in_specs=specs,
            out_specs=[state, state, state, flat, IN_VMEM],
        ),
        out_shape=[jax.ShapeDtypeStruct(master.shape, f32)] * 3
        + [
            jax.ShapeDtypeStruct((owned, k), bf16),
            jax.ShapeDtypeStruct((steps * rows, k), bf16),
        ],
        input_output_aliases=aliases,
        compiler_params=params(),
        cost_estimate=cost(4),
        name="update",
    )(*args)


def put_kernel(blocks, owned, n_pts, p, *refs):
    n = len(blocks)
    pieces, out, sems = refs[:n], refs[-2], refs[-1]
    me = p[0]
    copies = []
    for j, (distance, other, start) in enumerate(blocks):
        rows = pieces[j].shape[0]
        home = lax.rem(me + n_pts - distance * CORES, n_pts)
        home = home + other * (1 - 2 * lax.rem(home, 2))
        at = pl.ds(pl.multiple_of(home * owned + start, rows), rows)
        copies.append(pltpu.make_async_copy(pieces[j], out.at[at, :], sems.at[j]))
    for copy in copies:
        copy.start()
    for copy in copies:
        copy.wait()


def put(p, pieces, blocks, owned, n_pts):
    n = len(pieces)
    k = pieces[0].shape[1]
    return pl.pallas_call(
        functools.partial(put_kernel, blocks, owned, n_pts),
        grid_spec=pltpu.PrefetchScalarGridSpec(
            num_scalar_prefetch=1,
            grid=(1,),
            in_specs=[IN_VMEM] * n,
            out_specs=ANYWHERE,
            scratch_shapes=[pltpu.SemaphoreType.DMA((n,))],
        ),
        out_shape=jax.ShapeDtypeStruct((owned * n_pts, k), bf16),
        compiler_params=params(),
        cost_estimate=cost(2),
        name="put_rows",
    )(p, *pieces)


def ring(x, axis, n, distance):
    return lax.ppermute(x, axis, [(i, (i + distance) % n) for i in range(n)])


def mate(x, n):
    return lax.ppermute(x, "pts", [(i, i ^ 1) for i in range(n)])


def across(x, n, distance):
    return ring(x, "pts", n, distance * CORES)


def swap(x, n, bit):
    return lax.ppermute(x, "feat", [(i, i ^ 2**bit) for i in range(n)])


def body(n_feat, n_pts, points, picks, omega, phase, weights, counts, master, first, second, cov):
    f = lax.axis_index("feat").astype(jnp.int32).reshape(1)
    p = lax.axis_index("pts").astype(jnp.int32).reshape(1)
    owned, k = master.shape[1:]
    phase = phase[None, :]
    bits = n_feat.bit_length() - 1

    chosen, token = gather(picks, points)
    everyone = lax.all_gather(chosen, "pts")
    feats_zero, part, token = rates(
        f, p, chosen, omega, phase, weights, 0, owned, False, [token]
    )
    rate_zero = lax.psum(part, "feat")
    feats_one, kept, sent, token = rates(
        f, p, chosen, omega, phase, weights, 1, owned, True, [token]
    )
    features = [[feats_zero], [feats_one]]

    todo = [(m, j) for m in range(2) for j in range(1, n_pts)]
    share = len(todo) // 6

    def some(token, pieces):
        for _ in range(pieces * share):
            m, j = todo.pop(0)
            feats, token = owned_features(p, everyone, omega, phase, owned, m, j, [token])
            features[m].append(feats)
        return token

    got = swap(sent, n_feat, 0)
    token = some(token, 1)
    for bit in range(1, bits):
        *out, token = total(f, kept, got, bit, bit < bits - 1, [token])
        if bit < bits - 1:
            kept, sent = out
        else:
            kept = sent = out[0]
        got = swap(sent, n_feat, bit)
        if bit == 1:
            out_rates, res_zero, token = residuals(f, [rate_zero], [0], counts, 0, None, [token])
            res_zero = lax.all_gather(res_zero, "pts")
            token = some(token, 2)
    chunk, token = total(f, kept, got, 0, False, [token])
    rows, masks = [chunk], [0]
    for bit in reversed(range(bits - 1)):
        rows = rows + [swap(r, n_feat, bit) for r in rows]
        masks = masks + [q ^ 2**bit for q in masks]
    token = some(token, 1)
    out_rates, res_one, token = residuals(f, rows, masks, counts, 1, out_rates, [token])
    res_one = lax.all_gather(res_one, "pts")
    token = some(token, 2)
    begun, token = first_part(p, features[0], res_zero, master, [token])

    steps = max(1, owned // 256)
    sizes = [2, 3, 2, 1] if steps == 8 else [1] * steps
    chips = n_pts // CORES
    state = None
    pieces, blocks = [], []
    at = 0
    early = []
    for c, size in enumerate(sizes):
        deps = early if c == 2 else []
        *state, sent = update(
            p, features[1], res_one, begun, cov, master, first, second, at, size, state, deps
        )
        come = [across(sent, n_pts, d) for d in range(1, chips)]
        early = early or come[:1]
        pieces += come + [mate(x, n_pts) for x in come]
        start = at * (owned // steps)
        blocks += [(d, other, start) for other in (0, 1) for d in range(1, chips)]
        at += size
    *state, kept = state
    pieces += [kept, mate(kept, n_pts)]
    blocks += [(0, 0, 0), (0, 1, 0)]
    working = put(p, pieces, blocks, owned, n_pts)
    return out_rates, *state, working


def solution(mesh):
    placed = (
        P(("groups", "pts"), None),
        P(None, ("groups", "pts")),
        P(None, "feat"),
        P("feat"),
        P(("groups", "feat"), None),
        P(None, ("groups", "pts"), None),
        P(("groups", "feat"), "pts", None),
        P(("groups", "feat"), "pts", None),
        P(("groups", "feat"), "pts", None),
        P(),
    )
    return jax.shard_map(
        functools.partial(body, mesh.shape["feat"], mesh.shape["pts"]),
        mesh=mesh,
        in_specs=placed,
        out_specs=(
            P(None, ("groups", "pts"), None),
            P(("groups", "feat"), "pts", None),
            P(("groups", "feat"), "pts", None),
            P(("groups", "feat"), "pts", None),
            P(("groups", "feat"), None),
        ),
        check_vma=False,
    )
```

time: 126 us -> 186 us (1.48)
  local copies, waits for them, and re-layouts: 7.07 us -> 39.1 us
  waiting for transfers between devices: 14.3 us -> 45.4 us
  starting transfers between devices: 30.1 us -> 11.1 us
  between operations: 1.11 us -> 15.4 us
    unnamed x22 -> x68, local copies, waits for them, and re-layouts: 7.07 us -> 39.1 us
    psum x0 -> x1, waiting for transfers between devices: none -> 26.6 us  [body(): rate_zero = lax.psum(part, 'feat')]
    ppermute x20 -> x4, starting transfers between devices: 27.3 us -> 4.9 us  [ring(): return lax.ppermute(x, axis, [(i, (i + distance) % n) for i in range(n)])]
    ppermute x0 -> x3, starting transfers between devices: none -> 5.62 us  [swap(): return lax.ppermute(x, 'feat', [(i, i ^ 2 ** bit) for i in range(n)])]
    ppermute x20 -> x4, waiting for transfers between devices: 14.3 us -> 17.3 us  [ring(): return lax.ppermute(x, axis, [(i, (i + distance) % n) for i in range(n)])]
    ppermute x16 -> x5, starting transfers between devices: 2.8 us -> 0.24 us  [mate(): return lax.ppermute(x, 'pts', [(i, i ^ 1) for i in range(n)])]
    pallas_call x14 -> x13, Pallas kernels: 53.8 us -> 56.3 us  [the longest x2 33.1 us: rates(): pl.pallas_call(kernel, grid_spec=pltpu.PrefetchScalarGridSpec(num_scalar_...]
  transfers between devices with their start and end apart: 36 -> 16, of which waited for: 6 -> 6; matrix products, arithmetic and copies ran while one was open for 0% -> 0% of each run, Pallas kernels for 42% -> 33%
where the time goes in v3:
time: 186 us
  Pallas kernels  74.6 us (40%)
  waiting for transfers between devices  45.4 us (24%)
  local copies, waits for them, and re-layouts  39.1 us (21%)
  between operations  15.4 us (8%)
  starting transfers between devices  11.1 us (6%)
    unnamed x68, local copies, waits for them, and re-layouts  39.1 us
    pallas_call x2, Pallas kernels, rates(): pl.pallas_call(kernel, grid_spec=pltpu.PrefetchScalarGridSpec(num_scalar_...  33.1 us
    psum x1, waiting for transfers between devices, body(): rate_zero = lax.psum(part, 'feat')  26.6 us
    pallas_call x6, Pallas kernels, owned_features(): pl.pallas_call(functools.partial(features_kernel, min(256, width)), grid_...  18.4 us
    ppermute x4, waiting for transfers between devices, ring(): return lax.ppermute(x, axis, [(i, (i + distance) % n) for i in range(n)])  17.3 us
    pallas_call x4, Pallas kernels, update(): pl.pallas_call(functools.partial(update_kernel, n), grid_spec=pltpu.Prefe...  11.4 us
    ppermute x3, starting transfers between devices, swap(): return lax.ppermute(x, 'feat', [(i, i ^ 2 ** bit) for i in range(n)])  5.62 us
    ppermute x4, starting transfers between devices, ring(): return lax.ppermute(x, axis, [(i, (i + distance) % n) for i in range(n)])  4.9 us
  transfers between devices with their start and end apart: 16, of which 6 were waited for; matrix products, arithmetic and copies ran while one was open for 0% of the time, Pallas kernels for 33%

profile of v3, /device:TPU:0, one launch (start us, length us, event | category | flops | bytes accessed | tf_op | source)
XLA Modules:
  0.0 185.6 jit_solution(11926049076189370318)
XLA Ops:
  8.0 0.0 all-gather.7.cloned.1.call-start
  8.0 3.5 %chosen_points.1 = (bf16[1024,256]{1,0:T(8,128)(2,1)}, f32[8,128]{1,0:T(8,128)}) custom-call(s32[2,512]{1,0:T(2,128)} %picks.1, bf16[2048,256]{1,0:T(8,128)(2,1)} %points.1), custom_call_target="tpu_custom_call" | custom-call | flops 3000000000 | bytes 1024 | tf_op jit(solution)/shard_map/chosen_points/pallas_call | solution.py:70
  11.5 0.0 all-gather.7.cloned.1.call-update
  11.6 0.0 all-reduce.2.cloned.1.call-start
  11.6 16.5 %partial_log_rates.2 = (bf16[512,2048]{1,0:T(8,128)(2,1)}, bf16[512,256]{1,0:T(8,128)(2,1)}, f32[8,128]{1,0:T(8,128)}) custom-call(s32[1]{0:T(128)} %bitcast.f, s32[1]{0:T(128)} %bitcast.1.p, bf16[1024,256]{1,0:T(8,128)(2,1)} %get-tuple-element.57.chosen, bf16[256,8192]{1,0:T(8,128)(2,1)} %omega.15, f32[1,8192]{1,0:T(1,128)} %bitcast.17, ...), custom_call_target="tpu_custom_call" | custom-call | flops 12000000000 | bytes 1024 | tf_op jit(solution)/shard_map/partial_log_rates/pallas_call | solution.py:150
  28.1 16.6 %partial_log_rates.3 = (bf16[512,2048]{1,0:T(8,128)(2,1)}, f32[256,256]{1,0:T(8,128)}, bf16[256,256]{1,0:T(8,128)(2,1)}, f32[8,128]{1,0:T(8,128)}) custom-call(s32[1]{0:T(128)} %bitcast.f, s32[1]{0:T(128)} %bitcast.1.p, bf16[1024,256]{1,0:T(8,128)(2,1)} %get-tuple-element.57.chosen, bf16[256,8192]{1,0:T(8,128)(2,1)} %omega.15, f32[1,8192]{1,0:T(1,128)} %bitcast.18, ...), custom_call_target="tpu_custom_call" | custom-call | flops 12000000000 | bytes 1024 | tf_op jit(solution)/shard_map/partial_log_rates/pallas_call | solution.py:150
  44.8 3.0 %collective-permute-start = (bf16[256,256]{1,0:T(8,128)(2,1)}, bf16[256,256]{1,0:T(8,128)(2,1)S(1)}, u32[]{:S(2)}, u32[]{:S(2)}) collective-permute-start(bf16[256,256]{1,0:T(8,128)(2,1)} %get-tuple-element.61), channel_id=1, source_target_pairs={{0,1},{1,0},{2,3},{3,2},{4,5},{5,4},{6,7},{7,6},{8,9},{9,8},{10,11... | collective-permute-start | bytes 393224 | tf_op jit(solution)/shard_map/ppermute | solution.py:445
  47.8 0.0 all-reduce.2.cloned.1.call-update
  47.8 0.0 all-gather.11.cloned.1.call-start
  47.9 0.0 all-gather.7.cloned.1.call-done
  47.9 2.2 %copy-done.14 = bf16[256,8192]{1,0:T(8,128)(2,1)S(1)} copy-done((bf16[256,8192]{1,0:T(8,128)(2,1)S(1)}, bf16[256,8192]{1,0:T(8,128)(2,1)}, u32[]{:S(2)}) %copy-start.14) | copy-done | bytes 4194328
  50.1 1.6 copy-done.18
  51.7 0.7 copy-done.33
  52.4 3.1 %owned_features.6 = (bf16[512,2048]{1,0:T(8,128)(2,1)S(1)}, f32[8,128]{1,0:T(8,128)S(1)}) custom-call(s32[1]{0:T(128)} %bitcast.1.p, bf16[4,1024,256]{2,1,0:T(8,128)(2,1)S(1)} %bitcast.10, bf16[256,8192]{1,0:T(8,128)(2,1)S(1)} %copy-done.14, f32[1,8192]{1,0:T(1,128)S(1)} %bitcast.19, f32[8,128]{1,0:T(8,128)S(1)} %copy-done.33), custom_call_target="tpu_custom_call" | custom-call | flops 4000000000 | bytes 1024 | tf_op jit(solution)/shard_map/owned_features/pallas_call | solution.py:188
  55.4 1.3 copy-done.27
  56.8 26.6 %all-reduce.2.cloned.1.call-done.refs_0_ = bf16[512,256]{1,0:T(8,128)(2,1)} async-done(((bf16[512,256]{1,0:T(8,128)(2,1)}), bf16[512,256]{1,0:T(8,128)(2,1)}) %all-reduce.2.cloned.1.call-update) | async-done | bytes 262160 | tf_op jit(solution)/shard_map/psum | solution.py:460
  83.4 0.9 copy-done.23
  84.4 1.0 residuals.2
  85.4 0.2 all-gather.9.cloned.1.call-start
  85.6 1.9 %collective-permute-start.1 = (bf16[256,256]{1,0:T(8,128)(2,1)S(1)}, bf16[256,256]{1,0:T(8,128)(2,1)S(1)}, u32[]{:S(2)}, u32[]{:S(2)}) collective-permute-start(bf16[256,256]{1,0:T(8,128)(2,1)S(1)} %get-tuple-element.64.a), channel_id=1, source_target_pairs={{0,2},{1,3},{2,0},{3,1},{4,6},{5,7},{6,4},{7,5},{8,10},{9,11},{10,... | collective-permute-start | bytes 393224 | tf_op jit(solution)/shard_map/ppermute | solution.py:445
  87.5 2.2 %copy-done.15 = bf16[256,8192]{1,0:T(8,128)(2,1)S(1)} copy-done((bf16[256,8192]{1,0:T(8,128)(2,1)S(1)}, bf16[256,8192]{1,0:T(8,128)(2,1)}, u32[]{:S(2)}) %copy-start.15) | copy-done | bytes 4194328
  89.7 3.1 %owned_features.7 = (bf16[512,2048]{1,0:T(8,128)(2,1)S(1)}, f32[8,128]{1,0:T(8,128)S(1)}) custom-call(s32[1]{0:T(128)} %bitcast.1.p, bf16[4,1024,256]{2,1,0:T(8,128)(2,1)S(1)} %bitcast.11, bf16[256,8192]{1,0:T(8,128)(2,1)S(1)} %copy-done.15, f32[1,8192]{1,0:T(1,128)S(1)} %bitcast.20, f32[8,128]{1,0:T(8,128)S(1)} %get-tuple-element.67.refs_0_), custom_call_target="tpu_custom_call" | custom-call | flops 4000000000 | bytes 1024 | tf_op jit(solution)/shard_map/owned_features/pallas_call | solution.py:188
  92.8 1.3 copy-done.29
  94.1 3.1 %owned_features.8 = (bf16[512,2048]{1,0:T(8,128)(2,1)S(1)}, f32[8,128]{1,0:T(8,128)S(1)}) custom-call(s32[1]{0:T(128)} %bitcast.1.p, bf16[4,1024,256]{2,1,0:T(8,128)(2,1)S(1)} %bitcast.12, bf16[256,8192]{1,0:T(8,128)(2,1)S(1)} %copy-done.15, f32[1,8192]{1,0:T(1,128)S(1)} %bitcast.21, f32[8,128]{1,0:T(8,128)S(1)} %get-tuple-element.68.refs_0_), custom_call_target="tpu_custom_call" | custom-call | flops 4000000000 | bytes 1024 | tf_op jit(solution)/shard_map/owned_features/pallas_call | solution.py:188
  97.2 1.4 copy-done.31
  98.6 0.7 collective-permute-start.2
  99.3 3.1 %owned_features.9 = (bf16[512,2048]{1,0:T(8,128)(2,1)S(1)}, f32[8,128]{1,0:T(8,128)S(1)}) custom-call(s32[1]{0:T(128)} %bitcast.1.p, bf16[4,1024,256]{2,1,0:T(8,128)(2,1)S(1)} %bitcast.13, bf16[256,8192]{1,0:T(8,128)(2,1)S(1)} %copy-done.16, f32[1,8192]{1,0:T(1,128)S(1)} %bitcast.22, f32[8,128]{1,0:T(8,128)S(1)} %get-tuple-element.71.refs_0_), custom_call_target="tpu_custom_call" | custom-call | flops 4000000000 | bytes 1024 | tf_op jit(solution)/shard_map/owned_features/pallas_call | solution.py:188
  102.4 1.3 copy-done.4
  103.7 1.1 residuals.3
  104.8 2.2 %copy-done.17 = bf16[256,8192]{1,0:T(8,128)(2,1)S(1)} copy-done((bf16[256,8192]{1,0:T(8,128)(2,1)S(1)}, bf16[256,8192]{1,0:T(8,128)(2,1)}, u32[]{:S(2)}) %copy-start.17) | copy-done | bytes 4194328
  107.0 3.1 %owned_features.10 = (bf16[512,2048]{1,0:T(8,128)(2,1)S(1)}, f32[8,128]{1,0:T(8,128)S(1)}) custom-call(s32[1]{0:T(128)} %bitcast.1.p, bf16[4,1024,256]{2,1,0:T(8,128)(2,1)S(1)} %bitcast.14, bf16[256,8192]{1,0:T(8,128)(2,1)S(1)} %copy-done.17, f32[1,8192]{1,0:T(1,128)S(1)} %bitcast.23, f32[8,128]{1,0:T(8,128)S(1)} %get-tuple-element.77.refs_0_), custom_call_target="tpu_custom_call" | custom-call | flops 4000000000 | bytes 1024 | tf_op jit(solution)/shard_map/owned_features/pallas_call | solution.py:188
  110.1 1.3 copy-done.6
  111.4 3.1 %owned_features.11 = (bf16[512,2048]{1,0:T(8,128)(2,1)S(1)}, f32[8,128]{1,0:T(8,128)S(1)}) custom-call(s32[1]{0:T(128)} %bitcast.1.p, bf16[4,1024,256]{2,1,0:T(8,128)(2,1)S(1)} %bitcast.15, bf16[256,8192]{1,0:T(8,128)(2,1)S(1)} %copy-done.17, f32[1,8192]{1,0:T(1,128)S(1)} %bitcast.24, f32[8,128]{1,0:T(8,128)S(1)} %get-tuple-element.79.refs_0_), custom_call_target="tpu_custom_call" | custom-call | flops 4000000000 | bytes 1024 | tf_op jit(solution)/shard_map/owned_features/pallas_call | solution.py:188
  114.4 1.3 copy-done.8
  115.8 1.2 copy-done.22
  117.0 1.6 copy-done.26
  118.6 1.6 copy-done.28
  120.2 1.6 copy-done.30
  121.8 1.6 copy-done.32
  123.4 4.1 %first_part.1 = (f32[2048,256]{1,0:T(8,128)S(1)}, f32[8,128]{1,0:T(8,128)}) custom-call(s32[1]{0:T(128)} %bitcast.1.p, bf16[512,2048]{1,0:T(8,128)(2,1)S(1)} %copy-done.26, bf16[512,2048]{1,0:T(8,128)(2,1)S(1)} %copy-done.28, bf16[512,2048]{1,0:T(8,128)(2,1)S(1)} %copy-done.30, bf16[512,2048]{1,0:T(8,128)(2,1)S(1)} %copy-done.32, ...), custom_call_target="tpu_custom_call" | custom-call | flops 5000000000 | bytes 1024 | tf_op jit(solution)/shard_map/first_part/pallas_call | solution.py:317
  127.5 1.3 copy-done.10
  128.8 1.6 copy-done.1
  130.4 1.6 copy-done.2
  132.0 1.6 copy-done.3
  133.6 1.6 copy-done.5
  135.2 1.6 copy-done.7
  136.8 1.6 copy-done.9
  138.4 1.6 copy-done.11
  140.0 1.2 copy-done.12
  141.2 2.9 %update.4 = (f32[1,2048,256]{2,1,0:T(8,128)}, f32[1,2048,256]{2,1,0:T(8,128)}, f32[1,2048,256]{2,1,0:T(8,128)}, bf16[2048,256]{1,0:T(8,128)(2,1)S(1)}, bf16[512,256]{1,0:T(8,128)(2,1)S(1)}) custom-call(s32[1]{0:T(128)} %bitcast.1.p, bf16[512,2048]{1,0:T(8,128)(2,1)S(1)} %copy-done.3, bf16[512,2048]{1,0:T(8,128)(2,1)S(1)} %copy-done.5, ...), custom_call_target="tpu_custom_call" | custom-call | flops 4000000000 | bytes 1024 | tf_op jit(solution)/shard_map/update/pallas_call | solution.py:376
  144.1 1.4 collective-permute-start.3
  145.5 3.9 %update.5 = (f32[1,2048,256]{2,1,0:T(8,128)}, f32[1,2048,256]{2,1,0:T(8,128)}, f32[1,2048,256]{2,1,0:T(8,128)}, bf16[2048,256]{1,0:T(8,128)(2,1)S(1)}, bf16[768,256]{1,0:T(8,128)(2,1)S(1)}) custom-call(s32[1]{0:T(128)} %bitcast.1.p, bf16[512,2048]{1,0:T(8,128)(2,1)S(1)} %copy-done.3, ...), custom_call_target="tpu_custom_call", output_to_operand_aliasing={{0}: (11, {}), {1}: (12, {}), {2}: (13, {}), {3}: (14, {})} | custom-call | flops 4000000000 | bytes 1024 | tf_op jit(solution)/shard_map/update/pallas_call | solution.py:376
  149.4 1.0 collective-permute-done.3.refs_14_.refs_0_
  150.4 2.9 %update.6 = (f32[1,2048,256]{2,1,0:T(8,128)}, f32[1,2048,256]{2,1,0:T(8,128)}, f32[1,2048,256]{2,1,0:T(8,128)}, bf16[2048,256]{1,0:T(8,128)(2,1)S(1)}, bf16[512,256]{1,0:T(8,128)(2,1)S(1)}) custom-call(s32[1]{0:T(128)} %bitcast.1.p, bf16[512,2048]{1,0:T(8,128)(2,1)S(1)} %copy-done.3, ...), custom_call_target="tpu_custom_call", output_to_operand_aliasing={{0}: (11, {}), {1}: (12, {}), {2}: (13, {}), {3}: (14, {})} | custom-call | flops 4000000000 | bytes 1024 | tf_op jit(solution)/shard_map/update/pallas_call | solution.py:376
  153.3 1.7 update.7
  155.0 1.4 collective-permute-start.5
  156.5 0.6 collective-permute-start.7
  157.1 9.9 %collective-permute-done.5.refs_2_ = bf16[768,256]{1,0:T(8,128)(2,1)S(1)} collective-permute-done((bf16[768,256]{1,0:T(8,128)(2,1)S(1)}, bf16[768,256]{1,0:T(8,128)(2,1)S(1)}, u32[]{:S(2)}, u32[]{:S(2)}) %collective-permute-start.5) | collective-permute-done | bytes 393248 | tf_op jit(solution)/shard_map/ppermute | solution.py:433
  167.0 1.4 collective-permute-start.9
  168.4 0.2 collective-permute-start.4
  168.6 4.0 %collective-permute-done.7.refs_4_ = bf16[512,256]{1,0:T(8,128)(2,1)S(1)} collective-permute-done((bf16[512,256]{1,0:T(8,128)(2,1)S(1)}, bf16[512,256]{1,0:T(8,128)(2,1)S(1)}, u32[]{:S(2)}, u32[]{:S(2)}) %collective-permute-start.7) | collective-permute-done | bytes 262176 | tf_op jit(solution)/shard_map/ppermute | solution.py:433
  172.6 2.4 %collective-permute-done.9.refs_6_ = bf16[256,256]{1,0:T(8,128)(2,1)S(1)} collective-permute-done((bf16[256,256]{1,0:T(8,128)(2,1)S(1)}, bf16[256,256]{1,0:T(8,128)(2,1)S(1)}, u32[]{:S(2)}, u32[]{:S(2)}) %collective-permute-start.9) | collective-permute-done | bytes 131104 | tf_op jit(solution)/shard_map/ppermute | solution.py:433
  175.0 1.3 collective-permute-done.10.refs_7_
  176.4 2.1 %put_rows.1 = bf16[8192,256]{1,0:T(8,128)(2,1)} custom-call(s32[1]{0:T(128)} %bitcast.1.p, bf16[512,256]{1,0:T(8,128)(2,1)S(1)} %collective-permute-done.3.refs_14_.refs_0_, bf16[512,256]{1,0:T(8,128)(2,1)S(1)} %collective-permute-done.4.refs_1_, bf16[768,256]{1,0:T(8,128)(2,1)S(1)} %collective-permute-done.5.refs_2_, ...), custom_call_target="tpu_custom_call" | custom-call | flops 2000000000 | bytes 1024 | tf_op jit(solution)/shard_map/put_rows/pallas_call | solution.py:416
  (59 shorter events, 0.2 us)
Async XLA Ops:
  8.0 39.9 %all-gather.7.cloned.1.call-start = ((), (), s32[]{:S(2)}) async-start(), calls=%async_computation.1 | async-start | bytes 2621440 | tf_op jit(solution)/shard_map/all_gather | solution.py:456
  11.6 71.9 %all-reduce.2.cloned.1.call-start = ((), (), s32[]{:S(2)}) async-start(), calls=%async_computation | async-start | bytes 524288 | tf_op jit(solution)/shard_map/psum | solution.py:460
  28.1 19.7 %copy-start.24 = (f32[8192]{0:T(1024)S(1)}, f32[8192]{0:T(1024)}, u32[]{:S(2)}) copy-start(f32[8192]{0:T(1024)} %param.13) | copy-start | bytes 98308
  44.8 12.0 %collective-permute-start = (bf16[256,256]{1,0:T(8,128)(2,1)}, bf16[256,256]{1,0:T(8,128)(2,1)S(1)}, u32[]{:S(2)}, u32[]{:S(2)}) collective-permute-start(bf16[256,256]{1,0:T(8,128)(2,1)} %get-tuple-element.61), channel_id=1, source_target_pairs={{0,1},{1,0},{2,3},{3,2},{4,5},{5,4},{6,7},{7,6},{8,9},{9,8},{10,11... | collective-permute-start | bytes 393224 | tf_op jit(solution)/shard_map/ppermute | solution.py:445
  47.8 68.0 %all-gather.11.cloned.1.call-start = ((), (), s32[]{:S(2)}) async-start(), calls=%async_computation.3 | async-start | bytes 1310720 | tf_op jit(solution)/shard_map/all_gather | solution.py:487
  47.9 2.2 %copy-start.14 = (bf16[256,8192]{1,0:T(8,128)(2,1)S(1)}, bf16[256,8192]{1,0:T(8,128)(2,1)}, u32[]{:S(2)}) copy-start(bf16[256,8192]{1,0:T(8,128)(2,1)} %omega.15) | copy-start | bytes 12582916
  50.1 1.6 copy-start.18
  51.7 0.7 copy-start.33
  52.3 4.4 %copy-start.25 = (f32[256,256]{1,0:T(8,128)S(1)}, f32[256,256]{1,0:T(8,128)}, u32[]{:S(2)}) copy-start(f32[256,256]{1,0:T(8,128)} %get-tuple-element.60.a) | copy-start | bytes 786436
  52.4 31.1 %copy-start.21 = (s32[2,512,256]{2,1,0:T(8,128)S(1)}, s32[2,512,256]{2,1,0:T(8,128)}, u32[]{:S(2)}) copy-start(s32[2,512,256]{2,1,0:T(8,128)} %refs_2_.1) | copy-start | bytes 3145732
  55.4 1.3 copy-start.27
  56.8 30.7 %copy-start.19 = (bf16[4096,256]{1,0:T(8,128)(2,1)S(1)}, bf16[4096,256]{1,0:T(8,128)(2,1)}, u32[]{:S(2)}) copy-start(bf16[4096,256]{1,0:T(8,128)(2,1)} %all-gather.7.cloned.1.call-done) | copy-start | bytes 6291460
  83.4 1.0 copy-start.23
  85.4 43.4 %all-gather.9.cloned.1.call-start = ((), (), s32[]{:S(2)}) async-start(), calls=%async_computation.2 | async-start | bytes 1310720 | tf_op jit(solution)/shard_map/all_gather | solution.py:496
  85.6 13.0 %collective-permute-start.1 = (bf16[256,256]{1,0:T(8,128)(2,1)S(1)}, bf16[256,256]{1,0:T(8,128)(2,1)S(1)}, u32[]{:S(2)}, u32[]{:S(2)}) collective-permute-start(bf16[256,256]{1,0:T(8,128)(2,1)S(1)} %get-tuple-element.64.a), channel_id=1, source_target_pairs={{0,2},{1,3},{2,0},{3,1},{4,6},{5,7},{6,4},{7,5},{8,10},{9,11},{10,... | collective-permute-start | bytes 393224 | tf_op jit(solution)/shard_map/ppermute | solution.py:445
  87.5 2.2 %copy-start.15 = (bf16[256,8192]{1,0:T(8,128)(2,1)S(1)}, bf16[256,8192]{1,0:T(8,128)(2,1)}, u32[]{:S(2)}) copy-start(bf16[256,8192]{1,0:T(8,128)(2,1)} %omega.15) | copy-start | bytes 12582916
  92.8 1.3 copy-start.29
  94.1 5.2 %copy-start.16 = (bf16[256,8192]{1,0:T(8,128)(2,1)S(1)}, bf16[256,8192]{1,0:T(8,128)(2,1)}, u32[]{:S(2)}) copy-start(bf16[256,8192]{1,0:T(8,128)(2,1)} %omega.15) | copy-start | bytes 12582916
  97.2 1.4 copy-start.31
  98.6 5.1 %collective-permute-start.2 = (bf16[256,256]{1,0:T(8,128)(2,1)S(1)}, bf16[256,256]{1,0:T(8,128)(2,1)S(1)}, u32[]{:S(2)}, u32[]{:S(2)}) collective-permute-start(bf16[256,256]{1,0:T(8,128)(2,1)S(1)} %get-tuple-element.70.refs_0_), channel_id=1, source_target_pairs={{0,1},{1,0},{2,3},{3,2},{4,5},{5,4},{6,7},{7,6},{8,9},{9,8},{10,11... | collective-permute-start | bytes 393224 | tf_op jit(solution)/shard_map/ppermute | solution.py:445
  102.4 1.3 copy-start.4
  104.8 2.2 %copy-start.17 = (bf16[256,8192]{1,0:T(8,128)(2,1)S(1)}, bf16[256,8192]{1,0:T(8,128)(2,1)}, u32[]{:S(2)}) copy-start(bf16[256,8192]{1,0:T(8,128)(2,1)} %omega.15) | copy-start | bytes 12582916
  107.0 4.4 %copy-start.20 = (bf16[4096,256]{1,0:T(8,128)(2,1)S(1)}, bf16[4096,256]{1,0:T(8,128)(2,1)}, u32[]{:S(2)}) copy-start(bf16[4096,256]{1,0:T(8,128)(2,1)} %all-gather.7.cloned.1.call-done) | copy-start | bytes 6291460
  110.0 1.3 copy-start.6
  111.4 4.4 %copy-start = (f32[1,2048,256]{2,1,0:T(8,128)S(1)}, f32[1,2048,256]{2,1,0:T(8,128)}, u32[]{:S(2)}) copy-start(f32[1,2048,256]{2,1,0:T(8,128)} %refs_7_.7) | copy-start | bytes 6291460
  114.4 1.3 copy-start.8
  115.8 1.2 copy-start.22
  117.0 1.6 copy-start.26
  118.6 1.6 copy-start.28
  120.2 1.6 copy-start.30
  121.8 1.6 copy-start.32
  123.4 5.4 %copy-start.13 = (bf16[256,256]{1,0:T(8,128)(2,1)S(1)}, bf16[256,256]{1,0:T(8,128)(2,1)}, u32[]{:S(2)}) copy-start(bf16[256,256]{1,0:T(8,128)(2,1)} %refs_6_.7) | copy-start | bytes 393220
  127.5 1.3 copy-start.10
  128.8 1.6 copy-start.1
  130.4 1.6 copy-start.2
  132.0 1.6 copy-start.3
  133.6 1.6 copy-start.5
  135.2 1.6 copy-start.7
  136.8 1.6 copy-start.9
  138.4 1.6 copy-start.11
  140.0 1.2 copy-start.12
  144.1 6.4 %collective-permute-start.3 = (bf16[512,256]{1,0:T(8,128)(2,1)S(1)}, bf16[512,256]{1,0:T(8,128)(2,1)S(1)}, u32[]{:S(2)}, u32[]{:S(2)}) collective-permute-start(bf16[512,256]{1,0:T(8,128)(2,1)S(1)} %get-tuple-element.97), channel_id=1, source_target_pairs={{0,8},{4,12},{8,0},{12,4},{1,9},{5,13},{9,1},{13,5},{2,10},{6,14},... | collective-permute-start | bytes 786440 | tf_op jit(solution)/shard_map/ppermute | solution.py:433
  155.0 21.3 %collective-permute-start.11 = (bf16[2048,256]{1,0:T(8,128)(2,1)S(1)}, bf16[2048,256]{1,0:T(8,128)(2,1)S(1)}, u32[]{:S(2)}, u32[]{:S(2)}) collective-permute-start(bf16[2048,256]{1,0:T(8,128)(2,1)S(1)} %get-tuple-element.108.refs_8_), channel_id=1, source_target_pairs={{0,4},{4,0},{8,12},{12,8},{1,5},{5,1},{9,13},{13,9},{2,6},{6,2},{1... | collective-permute-start | bytes 3145736 | tf_op jit(solution)/shard_map/ppermute | solution.py:437
  155.0 11.9 %collective-permute-start.5 = (bf16[768,256]{1,0:T(8,128)(2,1)S(1)}, bf16[768,256]{1,0:T(8,128)(2,1)S(1)}, u32[]{:S(2)}, u32[]{:S(2)}) collective-permute-start(bf16[768,256]{1,0:T(8,128)(2,1)S(1)} %get-tuple-element.105), channel_id=1, source_target_pairs={{0,8},{4,12},{8,0},{12,4},{1,9},{5,13},{9,1},{13,5},{2,10},{6,14},... | collective-permute-start | bytes 1179656 | tf_op jit(solution)/shard_map/ppermute | solution.py:433
  156.5 16.1 %collective-permute-start.7 = (bf16[512,256]{1,0:T(8,128)(2,1)S(1)}, bf16[512,256]{1,0:T(8,128)(2,1)S(1)}, u32[]{:S(2)}, u32[]{:S(2)}) collective-permute-start(bf16[512,256]{1,0:T(8,128)(2,1)S(1)} %get-tuple-element.106), channel_id=1, source_target_pairs={{0,8},{4,12},{8,0},{12,4},{1,9},{5,13},{9,1},{13,5},{2,10},{6,14},... | collective-permute-start | bytes 786440 | tf_op jit(solution)/shard_map/ppermute | solution.py:433
  167.0 9.4 %collective-permute-start.6 = (bf16[768,256]{1,0:T(8,128)(2,1)S(1)}, bf16[768,256]{1,0:T(8,128)(2,1)S(1)}, u32[]{:S(2)}, u32[]{:S(2)}) collective-permute-start(bf16[768,256]{1,0:T(8,128)(2,1)S(1)} %collective-permute-done.5.refs_2_), channel_id=1, source_target_pairs={{0,4},{4,0},{8,12},{12,8},{1,5},{5,1},{9,13},{13,9},{2,6},{6,2},{1... | collective-permute-start | bytes 1179656 | tf_op jit(solution)/shard_map/ppermute | solution.py:437
  167.0 8.0 %collective-permute-start.9 = (bf16[256,256]{1,0:T(8,128)(2,1)S(1)}, bf16[256,256]{1,0:T(8,128)(2,1)S(1)}, u32[]{:S(2)}, u32[]{:S(2)}) collective-permute-start(bf16[256,256]{1,0:T(8,128)(2,1)S(1)} %get-tuple-element.107), channel_id=1, source_target_pairs={{0,8},{4,12},{8,0},{12,4},{1,9},{5,13},{9,1},{13,5},{2,10},{6,14},... | collective-permute-start | bytes 393224 | tf_op jit(solution)/shard_map/ppermute | solution.py:433
  168.4 6.6 %collective-permute-start.4 = (bf16[512,256]{1,0:T(8,128)(2,1)S(1)}, bf16[512,256]{1,0:T(8,128)(2,1)S(1)}, u32[]{:S(2)}, u32[]{:S(2)}) collective-permute-start(bf16[512,256]{1,0:T(8,128)(2,1)S(1)} %collective-permute-done.3.refs_14_.refs_0_), channel_id=1, source_target_pairs={{0,4},{4,0},{8,12},{12,8},{1,5},{5,1},{9,13},{13,9},{2,6},{6,2},{1... | collective-permute-start | bytes 786440 | tf_op jit(solution)/shard_map/ppermute | solution.py:437
  172.6 3.8 %collective-permute-start.8 = (bf16[512,256]{1,0:T(8,128)(2,1)S(1)}, bf16[512,256]{1,0:T(8,128)(2,1)S(1)}, u32[]{:S(2)}, u32[]{:S(2)}) collective-permute-start(bf16[512,256]{1,0:T(8,128)(2,1)S(1)} %collective-permute-done.7.refs_4_), channel_id=1, source_target_pairs={{0,4},{4,0},{8,12},{12,8},{1,5},{5,1},{9,13},{13,9},{2,6},{6,2},{1... | collective-permute-start | bytes 786440 | tf_op jit(solution)/shard_map/ppermute | solution.py:437
  175.0 1.3 collective-permute-start.10
Sparse Core Ops, SparseCore 0:
  11.7 25.2 all-gather.6
  85.5 16.1 all-gather.10
  104.9 16.2 all-gather.8
Sparse Core Ops, SparseCore 1:
  47.9 35.5 all-reduce.1

commit v4 on v3

v4 whole, which is shorter than its diff:
```python
import functools
import math

import jax
import jax.numpy as jnp
from jax import lax
from jax.experimental import pallas as pl
from jax.experimental.pallas import tpu as pltpu
from jax.sharding import PartitionSpec as P

F = 32768
STEP = 20
CORES = 2

beta_one = 0.9
beta_two = 0.999
learn_rate = 0.2

SINE = tuple(
    c / 8.0
    for c in (3.141582022078924, -5.167142793540227, 2.541899000696469, -0.5546361258792201)
)
ROUNDER = 12582912.0
TURN = 1.0 / (2.0 * math.pi)
VMEM = 24 * 1024 * 1024

f32 = jnp.float32
bf16 = jnp.bfloat16
IN_VMEM = pl.BlockSpec(memory_space=pltpu.VMEM)
ANYWHERE = pl.BlockSpec(memory_space=pl.ANY)


def scaled_cos(product, phase_turns):
    turns = product * TURN + phase_turns
    r = turns - ((turns + ROUNDER) - ROUNDER)
    s = r * r
    w = ((SINE[3] * s + SINE[2]) * s + SINE[1]) * s + SINE[0]
    w = w * r
    return (math.sqrt(2.0 / F) - w * w).astype(bf16)


TOKEN = jax.ShapeDtypeStruct((8, 128), f32)


def cost(microseconds):
    return pl.CostEstimate(
        flops=int(microseconds * 1.0e9), bytes_accessed=1 << 10, transcendentals=0
    )


def params():
    return pltpu.CompilerParams(vmem_limit_bytes=VMEM)


def in_hbm(x):
    return pltpu.with_memory_space_constraint(x, pltpu.HBM)


def gather_kernel(picks, points, chosen, token):
    batch, pool = chosen.shape[0], points.shape[0]
    m = pl.program_id(0)
    wanted = jnp.broadcast_to(picks[pl.ds(m, 1), :], (128, batch)).T
    lane = lax.broadcasted_iota(jnp.int32, (batch, 128), 1)
    hot = [jnp.where(wanted == lane + 128 * j, 1.0, 0.0).astype(bf16) for j in range(pool // 128)]
    chosen[...] = jnp.dot(
        jnp.concatenate(hot, axis=1), points[...], preferred_element_type=f32
    ).astype(bf16)


def gather(picks, points):
    batch = picks.shape[1]
    pool, ins = points.shape
    return pl.pallas_call(
        gather_kernel,
        grid=(2,),
        in_specs=[
            pl.BlockSpec(picks.shape, lambda i: (0, 0)),
            pl.BlockSpec((pool, ins), lambda i: (0, 0)),
        ],
        out_specs=[pl.BlockSpec((batch, ins), lambda i: (i, 0)), ANYWHERE],
        out_shape=[jax.ShapeDtypeStruct((2 * batch, ins), bf16), TOKEN],
        compiler_params=params(),
        cost_estimate=cost(3),
        name="chosen_points",
    )(picks, points)


def cosines(chosen, omega, turns, width, store, between=None):
    tile = min(256, width)
    count = width // tile

    def product(c):
        return jnp.dot(chosen, omega[:, c * tile : (c + 1) * tile], preferred_element_type=f32)

    ready = product(0)
    for c in range(count):
        coming = product(c + 1) if c + 1 < count else None
        if between is not None and c > 0:
            between(slice((c - 1) * tile, c * tile))
        cols = slice(c * tile, (c + 1) * tile)
        store(cols, scaled_cos(ready, turns[:, cols]))
        ready = coming
    if between is not None:
        between(slice((count - 1) * tile, count * tile))


def rates_kernel(start, size, begun, keep, ends, blocks, f, p, chosen, omega, phase, weights, *refs):
    refs = list(refs)
    total, feats = refs.pop(), refs.pop()
    before = refs.pop(0) if begun else None
    refs.pop()
    step = pl.program_id(0)
    width = omega.shape[1]

    @pl.when(step == 0)
    def _():
        total[...] = before[...] if begun else jnp.zeros_like(total)

    turns = phase[...] * TURN
    parts = []

    def store(cols, value):
        feats[:, cols] = value

    def between(cols):
        parts.append(jnp.dot(feats[:, cols], weights[cols, :], preferred_element_type=f32))

    cosines(chosen[start : start + size, :], omega, turns, width, store, between)
    part = parts[0]
    for q in parts[1:]:
        part = part + q
    total[...] += part

    if not begun:
        owned = refs.pop(0)

        @pl.when(step < blocks)
        def _():
            at = pl.ds(pl.multiple_of(step * width, width), width)
            owned[:, at] = feats[...]
            if keep:
                refs[0][:, at] = omega[...]
                refs[1][:, at] = turns

    @pl.when(step == pl.num_programs(0) - 1)
    def _():
        if ends:
            split(total, f[0], 0, *refs[-2:])
        else:
            refs[-1][...] = total[...]


def split(value, f, bit, kept, sent):
    rows = kept.shape[0]
    side = lax.rem(f // 2**bit, 2)
    kept[...] = value[pl.ds(pl.multiple_of(side * rows, rows), rows), :]
    sent[...] = value[pl.ds(pl.multiple_of((1 - side) * rows, rows), rows), :].astype(bf16)


def rates(f, p, chosen, omega, phase, weights, start, size, owned, blocks, before, keep, ends, deps):
    ins, feat_dev = omega.shape
    k = weights.shape[1]
    width = min(1024, owned)
    count = feat_dev // width
    own = owned // width
    low, high = blocks[0] * count // 2, blocks[1] * count // 2

    def turned(i, p):
        return lax.rem(i + low + p[0] * own, count)

    begun = before is not None
    outs = []
    if not begun:
        outs.append(jax.ShapeDtypeStruct((size, owned), bf16))
    if keep:
        outs += [jax.ShapeDtypeStruct((ins, owned), bf16), jax.ShapeDtypeStruct((1, owned), f32)]
    if ends:
        outs += [jax.ShapeDtypeStruct((size // 2, k), t) for t in (f32, bf16)]
    else:
        outs.append(jax.ShapeDtypeStruct((size, k), f32))
    args = [f, p, chosen, omega, phase, weights] + ([before] if begun else []) + deps

    def kernel(*refs):
        inputs = len(args) - len(deps)
        rates_kernel(
            start, size, begun, keep, ends, own, *refs[:inputs], *refs[inputs + len(deps) :]
        )

    return pl.pallas_call(
        kernel,
        grid_spec=pltpu.PrefetchScalarGridSpec(
            num_scalar_prefetch=2,
            grid=(high - low,),
            in_specs=[
                IN_VMEM,
                pl.BlockSpec((ins, width), lambda i, f, p: (0, turned(i, p))),
                pl.BlockSpec((1, width), lambda i, f, p: (0, turned(i, p))),
                pl.BlockSpec((width, k), lambda i, f, p: (turned(i, p), 0)),
            ]
            + [IN_VMEM] * begun
            + [ANYWHERE] * len(deps),
            out_specs=[IN_VMEM] * len(outs) + [ANYWHERE],
            scratch_shapes=[pltpu.VMEM((size, width), bf16), pltpu.VMEM((size, k), f32)],
        ),
        out_shape=[*outs, TOKEN],
        compiler_params=params(),
        cost_estimate=cost(12 * (high - low) / count),
        name="partial_log_rates",
    )(*args)


def features_kernel(start, size, chosen, omega, turns, *refs):
    out = refs[-2]

    def store(cols, value):
        out[:, cols] = value

    cosines(chosen[start : start + size, :], omega, turns, omega.shape[1], store)


def owned_features(chosen, omega, turns, start, size, deps):
    owned = omega.shape[1]
    return pl.pallas_call(
        functools.partial(features_kernel, start, size),
        in_specs=[IN_VMEM] * 3 + [ANYWHERE] * len(deps),
        out_specs=[IN_VMEM, ANYWHERE],
        out_shape=[jax.ShapeDtypeStruct((size, owned), bf16), TOKEN],
        compiler_params=params(),
        cost_estimate=cost(1),
        name="owned_features",
    )(chosen, omega, turns, *deps)


def total_kernel(bit, halves, f, a, b, *refs):
    value = a[...].astype(f32) + b[...].astype(f32)
    if halves:
        kept, sent, token, held = refs[-4:]
        held[...] = value
        split(held, f[0], bit, kept, sent)
    else:
        out, token = refs[-2:]
        out[...] = value.astype(bf16)


def total(f, a, b, bit, halves, deps):
    rows, k = a.shape
    if halves:
        outs = [
            jax.ShapeDtypeStruct((rows // 2, k), f32),
            jax.ShapeDtypeStruct((rows // 2, k), bf16),
        ]
    else:
        outs = [jax.ShapeDtypeStruct((rows, k), bf16)]
    return pl.pallas_call(
        functools.partial(total_kernel, bit, halves),
        grid_spec=pltpu.PrefetchScalarGridSpec(
            num_scalar_prefetch=1,
            grid=(1,),
            in_specs=[IN_VMEM] * 2 + [ANYWHERE] * len(deps),
            out_specs=[IN_VMEM] * len(outs) + [ANYWHERE],
            scratch_shapes=[pltpu.VMEM((rows, k), f32)] if halves else [],
        ),
        out_shape=[*outs, TOKEN],
        compiler_params=params(),
        cost_estimate=cost(0.5),
        name="total_rates",
    )(f, a, b, *deps)


def residual_kernel(masks, m, f, *refs):
    chunks, observed = refs[: len(masks)], refs[len(masks)]
    rate_out, residual_out, token, held = refs[-4:]
    batch = held.shape[0]
    for j, mask in enumerate(masks):
        rows = chunks[j].shape[0]
        start, bit = 0, 0
        while batch >> (bit + 1) >= rows:
            side = lax.rem(f[0] // 2**bit, 2)
            side = 1 - side if mask >> bit & 1 else side
            start = start + side * (batch >> (bit + 1))
            bit += 1
        at = pl.ds(pl.multiple_of(start, rows), rows) if bit else slice(None)
        rate = chunks[j][...].astype(f32)
        rate_out[0, at, :] = rate
        held[at, :] = jnp.exp(rate) - observed[0, at, :].astype(f32)
    residual_out[...] = held[...].T.astype(bf16)


def residuals(f, chunks, masks, counts, m, before, deps):
    n = len(chunks)
    k = chunks[0].shape[1]
    batch = counts.shape[1]
    args = [f, *chunks, counts, *deps]
    specs = [IN_VMEM] * n + [pl.BlockSpec((1, batch, k), lambda i, _: (m, 0, 0))]
    specs += [ANYWHERE] * len(deps)
    aliases = {}
    if before is not None:
        aliases = {len(args): 0}
        args.append(before)
        specs.append(ANYWHERE)
    return pl.pallas_call(
        functools.partial(residual_kernel, masks, m),
        grid_spec=pltpu.PrefetchScalarGridSpec(
            num_scalar_prefetch=1,
            grid=(1,),
            in_specs=specs,
            out_specs=[pl.BlockSpec((1, batch, k), lambda i, _: (m, 0, 0)), IN_VMEM, ANYWHERE],
            scratch_shapes=[pltpu.VMEM((batch, k), f32)],
        ),
        out_shape=[
            jax.ShapeDtypeStruct(counts.shape, f32),
            jax.ShapeDtypeStruct((k, batch), bf16),
            TOKEN,
        ],
        input_output_aliases=aliases,
        compiler_params=params(),
        cost_estimate=cost(1),
        name="residuals",
    )(*args)


def gradient_part(n, features, residual, start, rows):
    at = pl.ds(pl.multiple_of(start, rows), rows)
    value = None
    for j in range(n):
        term = jnp.dot(residual[j][...], features[j][:, at], preferred_element_type=f32)
        value = term if value is None else value + term
    return value


def first_part_kernel(n, *refs):
    features, residual, master = refs[:n], refs[n : 2 * n], refs[2 * n]
    out = refs[-2]
    rows = out.shape[0]
    out[...] = gradient_part(n, features, residual, pl.program_id(0) * rows, rows).T + master[0]


def first_part(features, residual, master, deps):
    n = len(features)
    owned, k = master.shape[1:]
    rows = min(512, owned)
    return pl.pallas_call(
        functools.partial(first_part_kernel, n),
        grid=(owned // rows,),
        in_specs=[IN_VMEM] * (2 * n)
        + [pl.BlockSpec((1, rows, k), lambda i: (0, i, 0))]
        + [ANYWHERE] * len(deps),
        out_specs=[pl.BlockSpec((rows, k), lambda i: (i, 0)), ANYWHERE],
        out_shape=[jax.ShapeDtypeStruct((owned, k), f32), TOKEN],
        compiler_params=params(),
        cost_estimate=cost(5),
        name="first_part",
    )(*features, *residual, master, *deps)


def update_kernel(n, begin, *refs):
    features, residual = refs[:n], refs[n : 2 * n]
    begun, cov, master, first, second = refs[2 * n : 2 * n + 5]
    new_master, new_first, new_second, sent = refs[-4:]
    rows = master.shape[1]
    step = pl.program_id(0)
    gradient = gradient_part(n, features, residual, (begin + step) * rows, rows).T + begun[...]
    conditioned = jnp.dot(gradient.astype(bf16), cov[...], preferred_element_type=f32)
    moved_first = beta_one * first[0] + (1.0 - beta_one) * conditioned
    moved_second = beta_two * second[0] + (1.0 - beta_two) * conditioned * conditioned
    correction_one = 1.0 - beta_one**STEP
    correction_two = 1.0 - beta_two**STEP
    moved = master[0] - learn_rate * (moved_first / correction_one) / (
        jnp.sqrt(moved_second / correction_two) + 1e-08
    )
    new_first[0] = moved_first
    new_second[0] = moved_second
    new_master[0] = moved
    sent[pl.ds(pl.multiple_of(step * rows, rows), rows), :] = moved.astype(bf16)


def update(features, residual, begun, cov, master, first, second, at, steps, before, deps):
    n = len(features)
    owned, k = master.shape[1:]
    rows = min(256, owned)
    state = pl.BlockSpec((1, rows, k), lambda i: (0, at + i, 0))
    flat = pl.BlockSpec((rows, k), lambda i: (at + i, 0))
    args = [*features, *residual, begun, cov, master, first, second]
    specs = [IN_VMEM] * (2 * n) + [flat, pl.BlockSpec(cov.shape, lambda i: (0, 0))] + [state] * 3
    aliases = {}
    if before is not None:
        aliases = {len(args) + j: j for j in range(3)}
        args += list(before)
        specs += [ANYWHERE] * 3
    args += deps
    specs += [ANYWHERE] * len(deps)
    return pl.pallas_call(
        functools.partial(update_kernel, n, at),
        grid=(steps,),
        in_specs=specs,
        out_specs=[state, state, state, IN_VMEM],
        out_shape=[jax.ShapeDtypeStruct(master.shape, f32)] * 3
        + [jax.ShapeDtypeStruct((steps * rows, k), bf16)],
        input_output_aliases=aliases,
        compiler_params=params(),
        cost_estimate=cost(1),
        name="update",
    )(*args)


def put_kernel(blocks, owned, n_pts, p, *refs):
    n = len(blocks)
    pieces, out, sems = refs[:n], refs[-2], refs[-1]
    me = p[0]
    copies = []
    for j, (distance, other, start) in enumerate(blocks):
        rows = pieces[j].shape[0]
        home = lax.rem(me + n_pts - distance * CORES, n_pts)
        home = home + other * (1 - 2 * lax.rem(home, 2))
        at = pl.ds(pl.multiple_of(home * owned + start, rows), rows)
        copies.append(pltpu.make_async_copy(pieces[j], out.at[at, :], sems.at[j]))
    for copy in copies:
        copy.start()
    for copy in copies:
        copy.wait()


def put(p, pieces, blocks, owned, n_pts):
    n = len(pieces)
    k = pieces[0].shape[1]
    return pl.pallas_call(
        functools.partial(put_kernel, blocks, owned, n_pts),
        grid_spec=pltpu.PrefetchScalarGridSpec(
            num_scalar_prefetch=1,
            grid=(1,),
            in_specs=[IN_VMEM] * n,
            out_specs=ANYWHERE,
            scratch_shapes=[pltpu.SemaphoreType.DMA((n,))],
        ),
        out_shape=jax.ShapeDtypeStruct((owned * n_pts, k), bf16),
        compiler_params=params(),
        cost_estimate=cost(2),
        name="put_rows",
    )(p, *pieces)


def ring(x, axis, n, distance):
    return lax.ppermute(x, axis, [(i, (i + distance) % n) for i in range(n)])


def mate(x, n):
    return lax.ppermute(x, "pts", [(i, i ^ 1) for i in range(n)])


def across(x, n, distance):
    return ring(x, "pts", n, distance * CORES)


def swap(x, n, bit):
    return lax.ppermute(x, "feat", [(i, i ^ 2**bit) for i in range(n)])


def spread(x, n):
    got = [x if d == 0 else across(x, n, d) for d in range(n // CORES)]
    return [y for g in got for y in (g, mate(g, n))]


def body(n_feat, n_pts, points, picks, omega, phase, weights, counts, master, first, second, cov):
    f = lax.axis_index("feat").astype(jnp.int32).reshape(1)
    p = lax.axis_index("pts").astype(jnp.int32).reshape(1)
    owned, k = master.shape[1:]
    batch = picks.shape[1]
    bits = n_feat.bit_length() - 1
    points, picks, omega, weights = map(in_hbm, (points, picks, omega, weights))
    phase, counts, cov = map(in_hbm, (phase[None, :], counts, cov))
    master, first, second = map(in_hbm, (master, first, second))

    chosen, token = gather(picks, points)
    everyone = spread(chosen, n_pts)

    def some_rates(m, blocks, before, keep, ends, token):
        return rates(
            f, p, chosen, omega, phase, weights, m * batch, batch, owned, blocks, before, keep, ends, [token]
        )

    def add_up(kept, got, bit, token):
        last = bit == bits - 1
        *out, token = total(f, kept, got, bit, not last, [token])
        kept, sent = (out[0], out[0]) if last else out
        return kept, swap(sent, n_feat, bit), token

    def give_back(chunk):
        rows, masks = [chunk], [0]
        for bit in reversed(range(bits - 1)):
            rows = rows + [swap(r, n_feat, bit) for r in rows]
            masks = masks + [q ^ 2**bit for q in masks]
        return rows, masks

    feats_zero, own_omega, own_turns, kept_zero, sent, token = some_rates(
        0, (0, 2), None, True, True, token
    )
    got_zero = swap(sent, n_feat, 0)
    feats_one, begun, token = some_rates(1, (0, 1), None, False, False, token)
    for bit in range(1, bits):
        kept_zero, got_zero, token = add_up(kept_zero, got_zero, bit, token)
    kept_one, sent, token = some_rates(1, (1, 2), begun, False, True, token)
    got_one = swap(sent, n_feat, 0)
    features = [[feats_zero], [feats_one]]

    todo = [(m, j) for m in range(2) for j in range(1, n_pts)]
    share = len(todo) // 6

    def some(token, pieces):
        for _ in range(pieces * share):
            m, j = todo.pop(0)
            feats, token = owned_features(
                everyone[j], own_omega, own_turns, m * batch, batch, [token]
            )
            features[m].append(feats)
        return token

    chunk, token = total(f, kept_zero, got_zero, 0, False, [token])
    rows_zero, masks = give_back(chunk)
    token = some(token, 1)
    for bit in range(1, bits):
        kept_one, got_one, token = add_up(kept_one, got_one, bit, token)
    token = some(token, 1)
    out_rates, res, token = residuals(f, rows_zero, masks, counts, 0, None, [token])
    res_zero = spread(res, n_pts)
    token = some(token, 1)
    chunk, token = total(f, kept_one, got_one, 0, False, [token])
    rows_one, masks = give_back(chunk)
    token = some(token, 1)
    out_rates, res, token = residuals(f, rows_one, masks, counts, 1, out_rates, [token])
    res_one = spread(res, n_pts)
    token = some(token, 2)
    begun, token = first_part(features[0], res_zero, master, [token])

    steps = max(1, owned // 256)
    sizes = [2, 3, 2, 1] if steps == 8 else [1] * steps
    chips = n_pts // CORES
    state = None
    pieces, blocks = [], []
    at = 0
    early = []
    for c, size in enumerate(sizes):
        *state, sent = update(
            features[1], res_one, begun, cov, master, first, second, at, size, state, [token]
        )
        come = [sent]
        if chips > 1:
            if c >= 2:
                sent, _ = lax.optimization_barrier((sent, early[c - 2]))
            come += [across(sent, n_pts, d) for d in range(1, chips)]
            early.append(come[1])
        pieces += come + [mate(x, n_pts) for x in come]
        start = at * (owned // steps)
        blocks += [(d, other, start) for other in (0, 1) for d in range(chips)]
        at += size
    working = put(p, pieces, blocks, owned, n_pts)
    return out_rates, *state, working


def solution(mesh):
    placed = (
        P(("groups", "pts"), None),
        P(None, ("groups", "pts")),
        P(None, "feat"),
        P("feat"),
        P(("groups", "feat"), None),
        P(None, ("groups", "pts"), None),
        P(("groups", "feat"), "pts", None),
        P(("groups", "feat"), "pts", None),
        P(("groups", "feat"), "pts", None),
        P(),
    )
    return jax.shard_map(
        functools.partial(body, mesh.shape["feat"], mesh.shape["pts"]),
        mesh=mesh,
        in_specs=placed,
        out_specs=(
            P(None, ("groups", "pts"), None),
            P(("groups", "feat"), "pts", None),
            P(("groups", "feat"), "pts", None),
            P(("groups", "feat"), "pts", None),
            P(("groups", "feat"), None),
        ),
        check_vma=False,
    )
```

time: 186 us -> 108 us (0.58)
  local copies, waits for them, and re-layouts: 39.1 us -> 0 us
  waiting for transfers between devices: 45.4 us -> 16.7 us
  between operations: 15.4 us -> 0.96 us
  starting transfers between devices: 11.1 us -> 16.9 us
    unnamed x68 -> x0, local copies, waits for them, and re-layouts: 39.1 us -> none
    psum x1 -> x0, waiting for transfers between devices: 26.6 us -> none  [body(): rate_zero = lax.psum(part, 'feat')]
    ppermute x4 -> x7, waiting for transfers between devices: 17.3 us -> 9.47 us  [ring(): return lax.ppermute(x, axis, [(i, (i + distance) % n) for i in range(n)])]
    ppermute x3 -> x6, waiting for transfers between devices: 0.01 us -> 5.45 us  [swap(): return lax.ppermute(x, 'feat', [(i, i ^ 2 ** bit) for i in range(n)])]
    pallas_call x2 -> x3, Pallas kernels: 33.1 us -> 29.5 us  [rates(): pl.pallas_call(kernel, grid_spec=pltpu.PrefetchScalarGridSpec(num_scalar_...]
    ppermute x4 -> x7, starting transfers between devices: 4.9 us -> 7.81 us  [ring(): return lax.ppermute(x, axis, [(i, (i + distance) % n) for i in range(n)])]
    pallas_call x2, Pallas kernels: 2.02 us -> 4.01 us  [residuals(): pl.pallas_call(functools.partial(residual_kernel, masks, m), grid_spec=pl...]
    ppermute x5 -> x14, starting transfers between devices: 0.24 us -> 2.21 us  [mate(): return lax.ppermute(x, 'pts', [(i, i ^ 1) for i in range(n)])]
  transfers between devices with their start and end apart: 16 -> 27, of which waited for: 6 -> 9; matrix products, arithmetic and copies ran while one was open for 0% -> 0% of each run, Pallas kernels for 33% -> 60%
where the time goes in v4:
time: 108 us
  Pallas kernels  73.3 us (68%)
  starting transfers between devices  16.9 us (16%)
  waiting for transfers between devices  16.7 us (15%)
    pallas_call x3, Pallas kernels, rates(): pl.pallas_call(kernel, grid_spec=pltpu.PrefetchScalarGridSpec(num_scalar_...  29.5 us
    pallas_call x4, Pallas kernels, update(): pl.pallas_call(functools.partial(update_kernel, n, at), grid=(steps,), in...  15.7 us
    pallas_call x6, Pallas kernels, owned_features(): pl.pallas_call(functools.partial(features_kernel, start, size), in_specs=...  14.3 us
    ppermute x7, waiting for transfers between devices, ring(): return lax.ppermute(x, axis, [(i, (i + distance) % n) for i in range(n)])  9.47 us
    ppermute x7, starting transfers between devices, ring(): return lax.ppermute(x, axis, [(i, (i + distance) % n) for i in range(n)])  7.81 us
    ppermute x6, starting transfers between devices, swap(): return lax.ppermute(x, 'feat', [(i, i ^ 2 ** bit) for i in range(n)])  6.92 us
    ppermute x6, waiting for transfers between devices, swap(): return lax.ppermute(x, 'feat', [(i, i ^ 2 ** bit) for i in range(n)])  5.45 us
    pallas_call x1, Pallas kernels, first_part(): pl.pallas_call(functools.partial(first_part_kernel, n), grid=(owned // ro...  4.74 us
  transfers between devices with their start and end apart: 27, of which 9 were waited for; matrix products, arithmetic and copies ran while one was open for 0% of the time, Pallas kernels for 60%

profile of v4, /device:TPU:0, one launch (start us, length us, event | category | flops | bytes accessed | tf_op | source)
XLA Modules:
  0.0 108.0 jit_solution(1018372404719710952)
XLA Ops:
  0.6 2.8 %chosen_points.1 = (bf16[1024,256]{1,0:T(8,128)(2,1)S(1)}, f32[8,128]{1,0:T(8,128)S(1)}) custom-call(s32[2,512]{1,0:T(2,128)} %picks.1, bf16[2048,256]{1,0:T(8,128)(2,1)} %points.1), custom_call_target="tpu_custom_call" | custom-call | flops 3000000000 | bytes 1024 | tf_op jit(solution)/shard_map/chosen_points/pallas_call | solution.py:73
  3.4 0.5 collective-permute-start.2
  3.9 2.6 %collective-permute-start.5 = (bf16[1024,256]{1,0:T(8,128)(2,1)S(1)}, bf16[1024,256]{1,0:T(8,128)(2,1)S(1)}, u32[]{:S(2)}, u32[]{:S(2)}) collective-permute-start(bf16[1024,256]{1,0:T(8,128)(2,1)S(1)} %get-tuple-element.65.refs_2_), channel_id=1, source_target_pairs={{0,8},{4,12},{8,0},{12,4},{1,9},{5,13},{9,1},{13,5},{2,10},{6,14},... | collective-permute-start | bytes 1572872 | tf_op jit(solution)/shard_map/ppermute | solution.py:443
  6.5 14.4 %partial_log_rates.3 = (bf16[512,2048]{1,0:T(8,128)(2,1)S(1)}, bf16[256,2048]{1,0:T(8,128)(2,1)S(1)}, f32[1,2048]{1,0:T(1,128)S(1)}, f32[256,256]{1,0:T(8,128)S(...) custom-call(s32[1]{0:T(128)} %bitcast.refs_0_.f, s32[1]{0:T(128)} %bitcast.1.refs_1_.p, ...), custom_call_target="tpu_custom_call" | custom-call | flops 12000000000 | bytes 1024 | tf_op jit(solution)/shard_map/partial_log_rates/pallas_call | solution.py:189
  21.0 1.6 %collective-permute-start = (bf16[256,256]{1,0:T(8,128)(2,1)S(1)}, bf16[256,256]{1,0:T(8,128)(2,1)S(1)}, u32[]{:S(2)}, u32[]{:S(2)}) collective-permute-start(bf16[256,256]{1,0:T(8,128)(2,1)S(1)} %get-tuple-element.70), channel_id=1, source_target_pairs={{0,1},{1,0},{2,3},{3,2},{4,5},{5,4},{6,7},{7,6},{8,9},{9,8},{10,11... | collective-permute-start | bytes 393224 | tf_op jit(solution)/shard_map/ppermute | solution.py:455
  22.6 7.9 %partial_log_rates.4 = (bf16[512,2048]{1,0:T(8,128)(2,1)S(1)}, f32[512,256]{1,0:T(8,128)S(1)}, f32[8,128]{1,0:T(8,128)S(1)}) custom-call(s32[1]{0:T(128)} %bitcast.refs_0_.f, s32[1]{0:T(128)} %bitcast.1.refs_1_.p, bf16[1024,256]{1,0:T(8,128)(2,1)S(1)} %get-tuple-element.65.refs_2_, bf16[256,8192]{1,0:T(8,128)(2,1)} %refs_3_.5, f32[1,8192]{1,0:T(1,128)} %bitcast.4, ...), custom_call_target="tpu_custom_call" | custom-call | flops 6000000000 | bytes 1024 | tf_op jit(solution)/shard_map/partial_log_rates/pallas_call | solution.py:189
  30.5 0.0 collective-permute-done.b
  30.5 2.7 %collective-permute-start.3 = (bf16[256,256]{1,0:T(8,128)(2,1)S(1)}, bf16[256,256]{1,0:T(8,128)(2,1)S(1)}, u32[]{:S(2)}, u32[]{:S(2)}) collective-permute-start(bf16[256,256]{1,0:T(8,128)(2,1)S(1)} %get-tuple-element.77.a), channel_id=1, source_target_pairs={{0,2},{1,3},{2,0},{3,1},{4,6},{5,7},{6,4},{7,5},{8,10},{9,11},{10,... | collective-permute-start | bytes 393224 | tf_op jit(solution)/shard_map/ppermute | solution.py:455
  33.2 0.0 collective-permute-done.5.chosen
  33.2 0.0 collective-permute-start.6
  33.2 7.2 %partial_log_rates.5 = (f32[256,256]{1,0:T(8,128)S(1)}, bf16[256,256]{1,0:T(8,128)(2,1)S(1)}, f32[8,128]{1,0:T(8,128)S(1)}) custom-call(s32[1]{0:T(128)} %bitcast.refs_0_.f, s32[1]{0:T(128)} %bitcast.1.refs_1_.p, bf16[1024,256]{1,0:T(8,128)(2,1)S(1)} %get-tuple-element.65.refs_2_, bf16[256,8192]{1,0:T(8,128)(2,1)} %refs_3_.5, f32[1,8192]{1,0:T(1,128)} %bitcast.5, ...), custom_call_target="tpu_custom_call" | custom-call | flops 6000000000 | bytes 1024 | tf_op jit(solution)/shard_map/partial_log_rates/pallas_call | solution.py:189
  40.4 0.5 collective-permute-start.1
  40.9 0.0 collective-permute-done.3.b
  40.9 1.6 %collective-permute-start.7 = (bf16[256,256]{1,0:T(8,128)(2,1)S(1)}, bf16[256,256]{1,0:T(8,128)(2,1)S(1)}, u32[]{:S(2)}, u32[]{:S(2)}) collective-permute-start(bf16[256,256]{1,0:T(8,128)(2,1)S(1)} %get-tuple-element.82.refs_0_), channel_id=1, source_target_pairs={{0,1},{1,0},{2,3},{3,2},{4,5},{5,4},{6,7},{7,6},{8,9},{9,8},{10,11... | collective-permute-start | bytes 393224 | tf_op jit(solution)/shard_map/ppermute | solution.py:455
  42.6 0.0 collective-permute-done.2.chosen
  42.6 2.3 %owned_features.6 = (bf16[512,2048]{1,0:T(8,128)(2,1)S(1)}, f32[8,128]{1,0:T(8,128)S(1)}) custom-call(bf16[1024,256]{1,0:T(8,128)(2,1)S(1)} %collective-permute-done.2.chosen, bf16[256,2048]{1,0:T(8,128)(2,1)S(1)} %get-tuple-element.75.omega, f32[1,2048]{1,0:T(1,128)S(1)} %get-tuple-element.76.turns, f32[8,128]{1,0:T(8,128)S(1)} %get-tuple-element.79.refs_0_), custom_call_target="tpu_custom_call" | custom-call | flops 1000000000 | bytes 1024 | tf_op jit(solution)/shard_map/owned_features/pallas_call | solution.py:223
  44.9 1.8 %collective-permute-done.1.b = bf16[256,256]{1,0:T(8,128)(2,1)S(1)} collective-permute-done((bf16[256,256]{1,0:T(8,128)(2,1)S(1)}, bf16[256,256]{1,0:T(8,128)(2,1)S(1)}, u32[]{:S(2)}, u32[]{:S(2)}) %collective-permute-start.1) | collective-permute-done | bytes 131104 | tf_op jit(solution)/shard_map/ppermute | solution.py:455
  46.8 0.4 collective-permute-start.4
  47.2 2.3 %owned_features.7 = (bf16[512,2048]{1,0:T(8,128)(2,1)S(1)}, f32[8,128]{1,0:T(8,128)S(1)}) custom-call(bf16[1024,256]{1,0:T(8,128)(2,1)S(1)} %collective-permute-done.5.chosen, bf16[256,2048]{1,0:T(8,128)(2,1)S(1)} %get-tuple-element.75.omega, f32[1,2048]{1,0:T(1,128)S(1)} %get-tuple-element.76.turns, f32[8,128]{1,0:T(8,128)S(1)} %get-tuple-element.83.refs_0_), custom_call_target="tpu_custom_call" | custom-call | flops 1000000000 | bytes 1024 | tf_op jit(solution)/shard_map/owned_features/pallas_call | solution.py:223
  49.5 0.0 collective-permute-done.7.refs_1_
  49.5 2.0 %residuals.2 = (f32[2,512,256]{2,1,0:T(8,128)}, bf16[256,512]{1,0:T(8,128)(2,1)S(1)}, f32[8,128]{1,0:T(8,128)S(1)}) custom-call(s32[1]{0:T(128)} %bitcast.refs_0_.f, bf16[256,256]{1,0:T(8,128)(2,1)S(1)} %get-tuple-element.82.refs_0_, bf16[256,256]{1,0:T(8,128)(2,1)S(1)} %collective-permute-done.7.refs_1_, s32[2,512,256]{2,1,0:T(8,128)} %refs_2_.3, ...), custom_call_target="tpu_custom_call" | custom-call | flops 1000000000 | bytes 1024 | tf_op jit(solution)/shard_map/residuals/pallas_call | solution.py:301
  51.5 0.5 collective-permute-start.13
  52.0 2.4 %owned_features.8 = (bf16[512,2048]{1,0:T(8,128)(2,1)S(1)}, f32[8,128]{1,0:T(8,128)S(1)}) custom-call(bf16[1024,256]{1,0:T(8,128)(2,1)S(1)} %collective-permute-done.6.chosen, bf16[256,2048]{1,0:T(8,128)(2,1)S(1)} %get-tuple-element.75.omega, f32[1,2048]{1,0:T(1,128)S(1)} %get-tuple-element.76.turns, f32[8,128]{1,0:T(8,128)S(1)} %get-tuple-element.85.refs_0_), custom_call_target="tpu_custom_call" | custom-call | flops 1000000000 | bytes 1024 | tf_op jit(solution)/shard_map/owned_features/pallas_call | solution.py:223
  54.4 0.7 collective-permute-done.4.b
  55.2 0.1 collective-permute-start.8
  55.2 2.3 %owned_features.9 = (bf16[512,2048]{1,0:T(8,128)(2,1)S(1)}, f32[8,128]{1,0:T(8,128)S(1)}) custom-call(bf16[1024,256]{1,0:T(8,128)(2,1)S(1)} %collective-permute-done.2.chosen, bf16[256,2048]{1,0:T(8,128)(2,1)S(1)} %get-tuple-element.75.omega, f32[1,2048]{1,0:T(1,128)S(1)} %get-tuple-element.76.turns, f32[8,128]{1,0:T(8,128)S(1)} %get-tuple-element.88.refs_0_), custom_call_target="tpu_custom_call" | custom-call | flops 1000000000 | bytes 1024 | tf_op jit(solution)/shard_map/owned_features/pallas_call | solution.py:223
  57.6 2.9 %collective-permute-done.8.refs_1_ = bf16[256,256]{1,0:T(8,128)(2,1)S(1)} collective-permute-done((bf16[256,256]{1,0:T(8,128)(2,1)S(1)}, bf16[256,256]{1,0:T(8,128)(2,1)S(1)}, u32[]{:S(2)}, u32[]{:S(2)}) %collective-permute-start.8) | collective-permute-done | bytes 131104 | tf_op jit(solution)/shard_map/ppermute | solution.py:455
  60.5 2.0 %residuals.3 = (f32[2,512,256]{2,1,0:T(8,128)}, bf16[256,512]{1,0:T(8,128)(2,1)S(1)}, f32[8,128]{1,0:T(8,128)S(1)}) custom-call(s32[1]{0:T(128)} %bitcast.refs_0_.f, bf16[256,256]{1,0:T(8,128)(2,1)S(1)} %get-tuple-element.87.refs_0_, bf16[256,256]{1,0:T(8,128)(2,1)S(1)} %collective-permute-done.8.refs_1_, ...), custom_call_target="tpu_custom_call", output_to_operand_aliasing={{0}: (5, {})} | custom-call | flops 1000000000 | bytes 1024 | tf_op jit(solution)/shard_map/residuals/pallas_call | solution.py:301
  62.5 0.5 collective-permute-start.10
  63.0 0.0 collective-permute-start.12
  63.0 0.0 collective-permute-done.13.refs_6_
  63.0 0.5 collective-permute-start.14
  63.5 0.0 collective-permute-start.9
  63.5 2.6 %owned_features.10 = (bf16[512,2048]{1,0:T(8,128)(2,1)S(1)}, f32[8,128]{1,0:T(8,128)S(1)}) custom-call(bf16[1024,256]{1,0:T(8,128)(2,1)S(1)} %collective-permute-done.5.chosen, bf16[256,2048]{1,0:T(8,128)(2,1)S(1)} %get-tuple-element.75.omega, f32[1,2048]{1,0:T(1,128)S(1)} %get-tuple-element.76.turns, f32[8,128]{1,0:T(8,128)S(1)} %get-tuple-element.94.refs_0_), custom_call_target="tpu_custom_call" | custom-call | flops 1000000000 | bytes 1024 | tf_op jit(solution)/shard_map/owned_features/pallas_call | solution.py:223
  66.1 2.4 %owned_features.11 = (bf16[512,2048]{1,0:T(8,128)(2,1)S(1)}, f32[8,128]{1,0:T(8,128)S(1)}) custom-call(bf16[1024,256]{1,0:T(8,128)(2,1)S(1)} %collective-permute-done.6.chosen, bf16[256,2048]{1,0:T(8,128)(2,1)S(1)} %get-tuple-element.75.omega, f32[1,2048]{1,0:T(1,128)S(1)} %get-tuple-element.76.turns, f32[8,128]{1,0:T(8,128)S(1)} %get-tuple-element.96.refs_0_), custom_call_target="tpu_custom_call" | custom-call | flops 1000000000 | bytes 1024 | tf_op jit(solution)/shard_map/owned_features/pallas_call | solution.py:223
  68.4 1.3 %collective-permute-done.10.refs_6_ = bf16[256,512]{1,0:T(8,128)(2,1)S(1)} collective-permute-done((bf16[256,512]{1,0:T(8,128)(2,1)S(1)}, bf16[256,512]{1,0:T(8,128)(2,1)S(1)}, u32[]{:S(2)}, u32[]{:S(2)}) %collective-permute-start.10) | collective-permute-done | bytes 262176 | tf_op jit(solution)/shard_map/ppermute | solution.py:443
  69.7 0.0 collective-permute-done.12.refs_5_
  69.7 0.0 collective-permute-done.14.refs_7_
  69.7 4.7 %first_part.1 = (f32[2048,256]{1,0:T(8,128)S(1)}, f32[8,128]{1,0:T(8,128)S(1)}) custom-call(bf16[512,2048]{1,0:T(8,128)(2,1)S(1)} %get-tuple-element.99.refs_0_, bf16[512,2048]{1,0:T(8,128)(2,1)S(1)} %get-tuple-element.100.refs_1_, bf16[512,2048]{1,0:T(8,128)(2,1)S(1)} %get-tuple-element.101.refs_2_, bf16[512,2048]{1,0:T(8,128)(2,1)S(1)} %get-tuple-element.102.refs_3_, ...), custom_call_target="tpu_custom_call" | custom-call | flops 5000000000 | bytes 1024 | tf_op jit(solution)/shard_map/first_part/pallas_call | solution.py:342
  74.5 0.0 collective-permute-done.11.refs_7_
  74.5 3.9 %update.4 = (f32[1,2048,256]{2,1,0:T(8,128)}, f32[1,2048,256]{2,1,0:T(8,128)}, f32[1,2048,256]{2,1,0:T(8,128)}, bf16[512,256]{1,0:T(8,128)(2,1)S(1)}) custom-call(bf16[512,2048]{1,0:T(8,128)(2,1)S(1)} %get-tuple-element.92.refs_0_, bf16[512,2048]{1,0:T(8,128)(2,1)S(1)} %get-tuple-element.93.refs_1_, bf16[512,2048]{1,0:T(8,128)(2,1)S(1)} %get-tuple-element.95.refs_2_, ...), custom_call_target="tpu_custom_call" | custom-call | flops 1000000000 | bytes 1024 | tf_op jit(solution)/shard_map/update/pallas_call | solution.py:392
  78.3 0.8 collective-permute-start.15
  79.2 5.2 %update.5 = (f32[1,2048,256]{2,1,0:T(8,128)}, f32[1,2048,256]{2,1,0:T(8,128)}, f32[1,2048,256]{2,1,0:T(8,128)}, bf16[768,256]{1,0:T(8,128)(2,1)S(1)}) custom-call(bf16[512,2048]{1,0:T(8,128)(2,1)S(1)} %get-tuple-element.92.refs_0_, bf16[512,2048]{1,0:T(8,128)(2,1)S(1)} %get-tuple-element.93.refs_1_, ...), custom_call_target="tpu_custom_call", output_to_operand_aliasing={{0}: (13, {}), {1}: (14, {}), {2}: (15, {})} | custom-call | flops 1000000000 | bytes 1024 | tf_op jit(solution)/shard_map/update/pallas_call | solution.py:392
  84.3 1.2 %collective-permute-start.18 = (bf16[768,256]{1,0:T(8,128)(2,1)S(1)}, bf16[768,256]{1,0:T(8,128)(2,1)S(1)}, u32[]{:S(2)}, u32[]{:S(2)}) collective-permute-start(bf16[768,256]{1,0:T(8,128)(2,1)S(1)} %get-tuple-element.120.refs_4_), channel_id=1, source_target_pairs={{0,8},{4,12},{8,0},{12,4},{1,9},{5,13},{9,1},{13,5},{2,10},{6,14},... | collective-permute-start | bytes 1179656 | tf_op jit(solution)/shard_map/ppermute | solution.py:443
  85.5 3.8 %update.6 = (f32[1,2048,256]{2,1,0:T(8,128)}, f32[1,2048,256]{2,1,0:T(8,128)}, f32[1,2048,256]{2,1,0:T(8,128)}, bf16[512,256]{1,0:T(8,128)(2,1)S(1)}) custom-call(bf16[512,2048]{1,0:T(8,128)(2,1)S(1)} %get-tuple-element.92.refs_0_, bf16[512,2048]{1,0:T(8,128)(2,1)S(1)} %get-tuple-element.93.refs_1_, ...), custom_call_target="tpu_custom_call", output_to_operand_aliasing={{0}: (13, {}), {1}: (14, {}), {2}: (15, {})} | custom-call | flops 1000000000 | bytes 1024 | tf_op jit(solution)/shard_map/update/pallas_call | solution.py:392
  89.4 0.5 collective-permute-start.22
  89.9 2.9 %update.7 = (f32[1,2048,256]{2,1,0:T(8,128)}, f32[1,2048,256]{2,1,0:T(8,128)}, f32[1,2048,256]{2,1,0:T(8,128)}, bf16[256,256]{1,0:T(8,128)(2,1)S(1)}) custom-call(bf16[512,2048]{1,0:T(8,128)(2,1)S(1)} %get-tuple-element.92.refs_0_, bf16[512,2048]{1,0:T(8,128)(2,1)S(1)} %get-tuple-element.93.refs_1_, ...), custom_call_target="tpu_custom_call", output_to_operand_aliasing={{0}: (13, {}), {1}: (14, {}), {2}: (15, {})} | custom-call | flops 1000000000 | bytes 1024 | tf_op jit(solution)/shard_map/update/pallas_call | solution.py:392
  92.8 0.0 collective-permute-start.25
  92.8 0.0 collective-permute-done.15.refs_1_
  92.8 0.9 collective-permute-start.21
  93.7 0.5 collective-permute-done.25.refs_14_
  94.1 0.1 collective-permute-start.19
  94.3 1.2 %collective-permute-done.18.refs_5_ = bf16[768,256]{1,0:T(8,128)(2,1)S(1)} collective-permute-done((bf16[768,256]{1,0:T(8,128)(2,1)S(1)}, bf16[768,256]{1,0:T(8,128)(2,1)S(1)}, u32[]{:S(2)}, u32[]{:S(2)}) %collective-permute-start.18) | collective-permute-done | bytes 393248 | tf_op jit(solution)/shard_map/ppermute | solution.py:443
  95.5 0.0 collective-permute-start.20
  95.5 0.0 collective-permute-done.16.refs_2_
  95.5 0.5 collective-permute-start.17
  96.0 0.0 collective-permute-done.22.refs_10_
  96.0 1.3 %collective-permute-start.24 = (bf16[256,256]{1,0:T(8,128)(2,1)S(1)}, bf16[256,256]{1,0:T(8,128)(2,1)S(1)}, u32[]{:S(2)}, u32[]{:S(2)}) collective-permute-start(bf16[256,256]{1,0:T(8,128)(2,1)S(1)} %get-tuple-element.124.refs_12_), channel_id=1, source_target_pairs={{0,8},{4,12},{8,0},{12,4},{1,9},{5,13},{9,1},{13,5},{2,10},{6,14},... | collective-permute-start | bytes 393224 | tf_op jit(solution)/shard_map/ppermute | solution.py:443
  97.3 4.6 %collective-permute-done.21.refs_9_ = bf16[512,256]{1,0:T(8,128)(2,1)S(1)} collective-permute-done((bf16[512,256]{1,0:T(8,128)(2,1)S(1)}, bf16[512,256]{1,0:T(8,128)(2,1)S(1)}, u32[]{:S(2)}, u32[]{:S(2)}) %collective-permute-start.21) | collective-permute-done | bytes 262176 | tf_op jit(solution)/shard_map/ppermute | solution.py:443
  101.9 2.3 %collective-permute-done.24.refs_13_ = bf16[256,256]{1,0:T(8,128)(2,1)S(1)} collective-permute-done((bf16[256,256]{1,0:T(8,128)(2,1)S(1)}, bf16[256,256]{1,0:T(8,128)(2,1)S(1)}, u32[]{:S(2)}, u32[]{:S(2)}) %collective-permute-start.24) | collective-permute-done | bytes 131104 | tf_op jit(solution)/shard_map/ppermute | solution.py:443
  104.3 0.0 collective-permute-done.17.refs_3_
  104.3 1.3 %collective-permute-done.26.refs_15_ = bf16[256,256]{1,0:T(8,128)(2,1)S(1)} collective-permute-done((bf16[256,256]{1,0:T(8,128)(2,1)S(1)}, bf16[256,256]{1,0:T(8,128)(2,1)S(1)}, u32[]{:S(2)}, u32[]{:S(2)}) %collective-permute-start.26) | collective-permute-done | bytes 131104 | tf_op jit(solution)/shard_map/ppermute | solution.py:447
  105.6 0.0 collective-permute-done.23.refs_11_
  105.6 2.1 %put_rows.1 = bf16[8192,256]{1,0:T(8,128)(2,1)} custom-call(s32[1]{0:T(128)} %bitcast.1.refs_1_.p, bf16[512,256]{1,0:T(8,128)(2,1)S(1)} %get-tuple-element.119.refs_0_, bf16[512,256]{1,0:T(8,128)(2,1)S(1)} %collective-permute-done.15.refs_1_, bf16[512,256]{1,0:T(8,128)(2,1)S(1)} %collective-permute-done.16.refs_2_, ...), custom_call_target="tpu_custom_call" | custom-call | flops 2000000000 | bytes 1024 | tf_op jit(solution)/shard_map/put_rows/pallas_call | solution.py:426
  (12 shorter events, 0.2 us)
Async XLA Ops:
  3.4 39.1 %collective-permute-start.2 = (bf16[1024,256]{1,0:T(8,128)(2,1)S(1)}, bf16[1024,256]{1,0:T(8,128)(2,1)S(1)}, u32[]{:S(2)}, u32[]{:S(2)}) collective-permute-start(bf16[1024,256]{1,0:T(8,128)(2,1)S(1)} %get-tuple-element.65.refs_2_), channel_id=1, source_target_pairs={{0,4},{4,0},{8,12},{12,8},{1,5},{5,1},{9,13},{13,9},{2,6},{6,2},{1... | collective-permute-start | bytes 1572872 | tf_op jit(solution)/shard_map/ppermute | solution.py:447
  3.9 29.3 %collective-permute-start.5 = (bf16[1024,256]{1,0:T(8,128)(2,1)S(1)}, bf16[1024,256]{1,0:T(8,128)(2,1)S(1)}, u32[]{:S(2)}, u32[]{:S(2)}) collective-permute-start(bf16[1024,256]{1,0:T(8,128)(2,1)S(1)} %get-tuple-element.65.refs_2_), channel_id=1, source_target_pairs={{0,8},{4,12},{8,0},{12,4},{1,9},{5,13},{9,1},{13,5},{2,10},{6,14},... | collective-permute-start | bytes 1572872 | tf_op jit(solution)/shard_map/ppermute | solution.py:443
  21.0 9.5 %collective-permute-start = (bf16[256,256]{1,0:T(8,128)(2,1)S(1)}, bf16[256,256]{1,0:T(8,128)(2,1)S(1)}, u32[]{:S(2)}, u32[]{:S(2)}) collective-permute-start(bf16[256,256]{1,0:T(8,128)(2,1)S(1)} %get-tuple-element.70), channel_id=1, source_target_pairs={{0,1},{1,0},{2,3},{3,2},{4,5},{5,4},{6,7},{7,6},{8,9},{9,8},{10,11... | collective-permute-start | bytes 393224 | tf_op jit(solution)/shard_map/ppermute | solution.py:455
  30.5 10.3 %collective-permute-start.3 = (bf16[256,256]{1,0:T(8,128)(2,1)S(1)}, bf16[256,256]{1,0:T(8,128)(2,1)S(1)}, u32[]{:S(2)}, u32[]{:S(2)}) collective-permute-start(bf16[256,256]{1,0:T(8,128)(2,1)S(1)} %get-tuple-element.77.a), channel_id=1, source_target_pairs={{0,2},{1,3},{2,0},{3,1},{4,6},{5,7},{6,4},{7,5},{8,10},{9,11},{10,... | collective-permute-start | bytes 393224 | tf_op jit(solution)/shard_map/ppermute | solution.py:455
  33.2 18.8 %collective-permute-start.6 = (bf16[1024,256]{1,0:T(8,128)(2,1)S(1)}, bf16[1024,256]{1,0:T(8,128)(2,1)S(1)}, u32[]{:S(2)}, u32[]{:S(2)}) collective-permute-start(bf16[1024,256]{1,0:T(8,128)(2,1)S(1)} %collective-permute-done.5.chosen), channel_id=1, source_target_pairs={{0,4},{4,0},{8,12},{12,8},{1,5},{5,1},{9,13},{13,9},{2,6},{6,2},{1... | collective-permute-start | bytes 1572872 | tf_op jit(solution)/shard_map/ppermute | solution.py:447
  40.4 6.4 %collective-permute-start.1 = (bf16[256,256]{1,0:T(8,128)(2,1)S(1)}, bf16[256,256]{1,0:T(8,128)(2,1)S(1)}, u32[]{:S(2)}, u32[]{:S(2)}) collective-permute-start(bf16[256,256]{1,0:T(8,128)(2,1)S(1)} %get-tuple-element.74), channel_id=1, source_target_pairs={{0,1},{1,0},{2,3},{3,2},{4,5},{5,4},{6,7},{7,6},{8,9},{9,8},{10,11... | collective-permute-start | bytes 393224 | tf_op jit(solution)/shard_map/ppermute | solution.py:455
  40.9 8.6 %collective-permute-start.7 = (bf16[256,256]{1,0:T(8,128)(2,1)S(1)}, bf16[256,256]{1,0:T(8,128)(2,1)S(1)}, u32[]{:S(2)}, u32[]{:S(2)}) collective-permute-start(bf16[256,256]{1,0:T(8,128)(2,1)S(1)} %get-tuple-element.82.refs_0_), channel_id=1, source_target_pairs={{0,1},{1,0},{2,3},{3,2},{4,5},{5,4},{6,7},{7,6},{8,9},{9,8},{10,11... | collective-permute-start | bytes 393224 | tf_op jit(solution)/shard_map/ppermute | solution.py:455
  46.8 8.4 %collective-permute-start.4 = (bf16[256,256]{1,0:T(8,128)(2,1)S(1)}, bf16[256,256]{1,0:T(8,128)(2,1)S(1)}, u32[]{:S(2)}, u32[]{:S(2)}) collective-permute-start(bf16[256,256]{1,0:T(8,128)(2,1)S(1)} %get-tuple-element.81.a), channel_id=1, source_target_pairs={{0,2},{1,3},{2,0},{3,1},{4,6},{5,7},{6,4},{7,5},{8,10},{9,11},{10,... | collective-permute-start | bytes 393224 | tf_op jit(solution)/shard_map/ppermute | solution.py:455
  51.5 11.5 %collective-permute-start.13 = (bf16[256,512]{1,0:T(8,128)(2,1)S(1)}, bf16[256,512]{1,0:T(8,128)(2,1)S(1)}, u32[]{:S(2)}, u32[]{:S(2)}) collective-permute-start(bf16[256,512]{1,0:T(8,128)(2,1)S(1)} %get-tuple-element.103.refs_4_), channel_id=1, source_target_pairs={{0,8},{4,12},{8,0},{12,4},{1,9},{5,13},{9,1},{13,5},{2,10},{6,14},... | collective-permute-start | bytes 786440 | tf_op jit(solution)/shard_map/ppermute | solution.py:443
  55.2 5.3 %collective-permute-start.8 = (bf16[256,256]{1,0:T(8,128)(2,1)S(1)}, bf16[256,256]{1,0:T(8,128)(2,1)S(1)}, u32[]{:S(2)}, u32[]{:S(2)}) collective-permute-start(bf16[256,256]{1,0:T(8,128)(2,1)S(1)} %get-tuple-element.87.refs_0_), channel_id=1, source_target_pairs={{0,1},{1,0},{2,3},{3,2},{4,5},{5,4},{6,7},{7,6},{8,9},{9,8},{10,11... | collective-permute-start | bytes 393224 | tf_op jit(solution)/shard_map/ppermute | solution.py:455
  62.5 7.2 %collective-permute-start.10 = (bf16[256,512]{1,0:T(8,128)(2,1)S(1)}, bf16[256,512]{1,0:T(8,128)(2,1)S(1)}, u32[]{:S(2)}, u32[]{:S(2)}) collective-permute-start(bf16[256,512]{1,0:T(8,128)(2,1)S(1)} %get-tuple-element.98.refs_4_), channel_id=1, source_target_pairs={{0,8},{4,12},{8,0},{12,4},{1,9},{5,13},{9,1},{13,5},{2,10},{6,14},... | collective-permute-start | bytes 786440 | tf_op jit(solution)/shard_map/ppermute | solution.py:443
  63.0 6.7 %collective-permute-start.12 = (bf16[256,512]{1,0:T(8,128)(2,1)S(1)}, bf16[256,512]{1,0:T(8,128)(2,1)S(1)}, u32[]{:S(2)}, u32[]{:S(2)}) collective-permute-start(bf16[256,512]{1,0:T(8,128)(2,1)S(1)} %get-tuple-element.103.refs_4_), channel_id=1, source_target_pairs={{0,4},{4,0},{8,12},{12,8},{1,5},{5,1},{9,13},{13,9},{2,6},{6,2},{1... | collective-permute-start | bytes 786440 | tf_op jit(solution)/shard_map/ppermute | solution.py:447
  63.0 6.7 %collective-permute-start.14 = (bf16[256,512]{1,0:T(8,128)(2,1)S(1)}, bf16[256,512]{1,0:T(8,128)(2,1)S(1)}, u32[]{:S(2)}, u32[]{:S(2)}) collective-permute-start(bf16[256,512]{1,0:T(8,128)(2,1)S(1)} %collective-permute-done.13.refs_6_), channel_id=1, source_target_pairs={{0,4},{4,0},{8,12},{12,8},{1,5},{5,1},{9,13},{13,9},{2,6},{6,2},{1... | collective-permute-start | bytes 786440 | tf_op jit(solution)/shard_map/ppermute | solution.py:447
  63.5 10.9 %collective-permute-start.9 = (bf16[256,512]{1,0:T(8,128)(2,1)S(1)}, bf16[256,512]{1,0:T(8,128)(2,1)S(1)}, u32[]{:S(2)}, u32[]{:S(2)}) collective-permute-start(bf16[256,512]{1,0:T(8,128)(2,1)S(1)} %get-tuple-element.98.refs_4_), channel_id=1, source_target_pairs={{0,4},{4,0},{8,12},{12,8},{1,5},{5,1},{9,13},{13,9},{2,6},{6,2},{1... | collective-permute-start | bytes 786440 | tf_op jit(solution)/shard_map/ppermute | solution.py:447
  69.7 4.8 %collective-permute-start.11 = (bf16[256,512]{1,0:T(8,128)(2,1)S(1)}, bf16[256,512]{1,0:T(8,128)(2,1)S(1)}, u32[]{:S(2)}, u32[]{:S(2)}) collective-permute-start(bf16[256,512]{1,0:T(8,128)(2,1)S(1)} %collective-permute-done.10.refs_6_), channel_id=1, source_target_pairs={{0,4},{4,0},{8,12},{12,8},{1,5},{5,1},{9,13},{13,9},{2,6},{6,2},{1... | collective-permute-start | bytes 786440 | tf_op jit(solution)/shard_map/ppermute | solution.py:447
  78.3 14.4 %collective-permute-start.15 = (bf16[512,256]{1,0:T(8,128)(2,1)S(1)}, bf16[512,256]{1,0:T(8,128)(2,1)S(1)}, u32[]{:S(2)}, u32[]{:S(2)}) collective-permute-start(bf16[512,256]{1,0:T(8,128)(2,1)S(1)} %get-tuple-element.119.refs_0_), channel_id=1, source_target_pairs={{0,8},{4,12},{8,0},{12,4},{1,9},{5,13},{9,1},{13,5},{2,10},{6,14},... | collective-permute-start | bytes 786440 | tf_op jit(solution)/shard_map/ppermute | solution.py:443
  84.3 11.1 %collective-permute-start.18 = (bf16[768,256]{1,0:T(8,128)(2,1)S(1)}, bf16[768,256]{1,0:T(8,128)(2,1)S(1)}, u32[]{:S(2)}, u32[]{:S(2)}) collective-permute-start(bf16[768,256]{1,0:T(8,128)(2,1)S(1)} %get-tuple-element.120.refs_4_), channel_id=1, source_target_pairs={{0,8},{4,12},{8,0},{12,4},{1,9},{5,13},{9,1},{13,5},{2,10},{6,14},... | collective-permute-start | bytes 1179656 | tf_op jit(solution)/shard_map/ppermute | solution.py:443
  85.5 9.9 %collective-permute-start.16 = (bf16[512,256]{1,0:T(8,128)(2,1)S(1)}, bf16[512,256]{1,0:T(8,128)(2,1)S(1)}, u32[]{:S(2)}, u32[]{:S(2)}) collective-permute-start(bf16[512,256]{1,0:T(8,128)(2,1)S(1)} %get-tuple-element.119.refs_0_), channel_id=1, source_target_pairs={{0,4},{4,0},{8,12},{12,8},{1,5},{5,1},{9,13},{13,9},{2,6},{6,2},{1... | collective-permute-start | bytes 786440 | tf_op jit(solution)/shard_map/ppermute | solution.py:447
  89.4 6.6 %collective-permute-start.22 = (bf16[512,256]{1,0:T(8,128)(2,1)S(1)}, bf16[512,256]{1,0:T(8,128)(2,1)S(1)}, u32[]{:S(2)}, u32[]{:S(2)}) collective-permute-start(bf16[512,256]{1,0:T(8,128)(2,1)S(1)} %get-tuple-element.122.refs_8_), channel_id=1, source_target_pairs={{0,4},{4,0},{8,12},{12,8},{1,5},{5,1},{9,13},{13,9},{2,6},{6,2},{1... | collective-permute-start | bytes 786440 | tf_op jit(solution)/shard_map/ppermute | solution.py:447
  92.8 1.3 %collective-permute-start.25 = (bf16[256,256]{1,0:T(8,128)(2,1)S(1)}, bf16[256,256]{1,0:T(8,128)(2,1)S(1)}, u32[]{:S(2)}, u32[]{:S(2)}) collective-permute-start(bf16[256,256]{1,0:T(8,128)(2,1)S(1)} %get-tuple-element.124.refs_12_), channel_id=1, source_target_pairs={{0,4},{4,0},{8,12},{12,8},{1,5},{5,1},{9,13},{13,9},{2,6},{6,2},{1... | collective-permute-start | bytes 393224 | tf_op jit(solution)/shard_map/ppermute | solution.py:447
  92.8 9.2 %collective-permute-start.21 = (bf16[512,256]{1,0:T(8,128)(2,1)S(1)}, bf16[512,256]{1,0:T(8,128)(2,1)S(1)}, u32[]{:S(2)}, u32[]{:S(2)}) collective-permute-start(bf16[512,256]{1,0:T(8,128)(2,1)S(1)} %get-tuple-element.122.refs_8_), channel_id=1, source_target_pairs={{0,8},{4,12},{8,0},{12,4},{1,9},{5,13},{9,1},{13,5},{2,10},{6,14},... | collective-permute-start | bytes 786440 | tf_op jit(solution)/shard_map/ppermute | solution.py:443
  94.1 10.2 %collective-permute-start.19 = (bf16[768,256]{1,0:T(8,128)(2,1)S(1)}, bf16[768,256]{1,0:T(8,128)(2,1)S(1)}, u32[]{:S(2)}, u32[]{:S(2)}) collective-permute-start(bf16[768,256]{1,0:T(8,128)(2,1)S(1)} %get-tuple-element.120.refs_4_), channel_id=1, source_target_pairs={{0,4},{4,0},{8,12},{12,8},{1,5},{5,1},{9,13},{13,9},{2,6},{6,2},{1... | collective-permute-start | bytes 1179656 | tf_op jit(solution)/shard_map/ppermute | solution.py:447
  95.5 10.2 %collective-permute-start.20 = (bf16[768,256]{1,0:T(8,128)(2,1)S(1)}, bf16[768,256]{1,0:T(8,128)(2,1)S(1)}, u32[]{:S(2)}, u32[]{:S(2)}) collective-permute-start(bf16[768,256]{1,0:T(8,128)(2,1)S(1)} %collective-permute-done.18.refs_5_), channel_id=1, source_target_pairs={{0,4},{4,0},{8,12},{12,8},{1,5},{5,1},{9,13},{13,9},{2,6},{6,2},{1... | collective-permute-start | bytes 1179656 | tf_op jit(solution)/shard_map/ppermute | solution.py:447
  95.5 8.8 %collective-permute-start.17 = (bf16[512,256]{1,0:T(8,128)(2,1)S(1)}, bf16[512,256]{1,0:T(8,128)(2,1)S(1)}, u32[]{:S(2)}, u32[]{:S(2)}) collective-permute-start(bf16[512,256]{1,0:T(8,128)(2,1)S(1)} %collective-permute-done.15.refs_1_), channel_id=1, source_target_pairs={{0,4},{4,0},{8,12},{12,8},{1,5},{5,1},{9,13},{13,9},{2,6},{6,2},{1... | collective-permute-start | bytes 786440 | tf_op jit(solution)/shard_map/ppermute | solution.py:447
  96.0 8.3 %collective-permute-start.24 = (bf16[256,256]{1,0:T(8,128)(2,1)S(1)}, bf16[256,256]{1,0:T(8,128)(2,1)S(1)}, u32[]{:S(2)}, u32[]{:S(2)}) collective-permute-start(bf16[256,256]{1,0:T(8,128)(2,1)S(1)} %get-tuple-element.124.refs_12_), channel_id=1, source_target_pairs={{0,8},{4,12},{8,0},{12,4},{1,9},{5,13},{9,1},{13,5},{2,10},{6,14},... | collective-permute-start | bytes 393224 | tf_op jit(solution)/shard_map/ppermute | solution.py:443
  101.9 3.7 %collective-permute-start.23 = (bf16[512,256]{1,0:T(8,128)(2,1)S(1)}, bf16[512,256]{1,0:T(8,128)(2,1)S(1)}, u32[]{:S(2)}, u32[]{:S(2)}) collective-permute-start(bf16[512,256]{1,0:T(8,128)(2,1)S(1)} %collective-permute-done.21.refs_9_), channel_id=1, source_target_pairs={{0,4},{4,0},{8,12},{12,8},{1,5},{5,1},{9,13},{13,9},{2,6},{6,2},{1... | collective-permute-start | bytes 786440 | tf_op jit(solution)/shard_map/ppermute | solution.py:447
  104.3 1.3 %collective-permute-start.26 = (bf16[256,256]{1,0:T(8,128)(2,1)S(1)}, bf16[256,256]{1,0:T(8,128)(2,1)S(1)}, u32[]{:S(2)}, u32[]{:S(2)}) collective-permute-start(bf16[256,256]{1,0:T(8,128)(2,1)S(1)} %collective-permute-done.24.refs_13_), channel_id=1, source_target_pairs={{0,4},{4,0},{8,12},{12,8},{1,5},{5,1},{9,13},{13,9},{2,6},{6,2},{1... | collective-permute-start | bytes 393224 | tf_op jit(solution)/shard_map/ppermute | solution.py:447

commit v5 on v4

--- a/solution.py
+++ b/solution.py
@@ -17,8 +17,7 @@
 learn_rate = 0.2
 
 SINE = tuple(
-    c / 8.0
-    for c in (3.141582022078924, -5.167142793540227, 2.541899000696469, -0.5546361258792201)
+    c * math.sqrt(2.0 / F) for c in (6.2825055774072665, -41.16644056159234, 74.4523919857074)
 )
 ROUNDER = 12582912.0
 TURN = 1.0 / (2.0 * math.pi)
@@ -28,18 +27,14 @@
 bf16 = jnp.bfloat16
 IN_VMEM = pl.BlockSpec(memory_space=pltpu.VMEM)
 ANYWHERE = pl.BlockSpec(memory_space=pl.ANY)
+TOKEN = jax.ShapeDtypeStruct((8, 128), f32)
 
 
 def scaled_cos(product, phase_turns):
     turns = product * TURN + phase_turns
-    r = turns - ((turns + ROUNDER) - ROUNDER)
-    s = r * r
-    w = ((SINE[3] * s + SINE[2]) * s + SINE[1]) * s + SINE[0]
-    w = w * r
-    return (math.sqrt(2.0 / F) - w * w).astype(bf16)
-
-
-TOKEN = jax.ShapeDtypeStruct((8, 128), f32)
+    v = 0.25 - jnp.abs(turns - ((turns + ROUNDER) - ROUNDER))
+    s = v * v
+    return (((SINE[2] * s + SINE[1]) * s + SINE[0]) * v).astype(bf16)
 
 
 def cost(microseconds):
@@ -88,6 +83,7 @@
 def cosines(chosen, omega, turns, width, store, between=None):
     tile = min(256, width)
     count = width // tile
+    group = min(512, width)
 
     def product(c):
         return jnp.dot(chosen, omega[:, c * tile : (c + 1) * tile], preferred_element_type=f32)
@@ -95,13 +91,13 @@
     ready = product(0)
     for c in range(count):
         coming = product(c + 1) if c + 1 < count else None
-        if between is not None and c > 0:
-            between(slice((c - 1) * tile, c * tile))
+        if between is not None and c > 0 and c * tile % group == 0:
+            between(slice(c * tile - group, c * tile))
         cols = slice(c * tile, (c + 1) * tile)
         store(cols, scaled_cos(ready, turns[:, cols]))
         ready = coming
     if between is not None:
-        between(slice((count - 1) * tile, count * tile))
+        between(slice(width - group, width))
 
 
 def rates_kernel(start, size, begun, keep, ends, blocks, f, p, chosen, omega, phase, weights, *refs):
@@ -160,7 +156,7 @@
 def rates(f, p, chosen, omega, phase, weights, start, size, owned, blocks, before, keep, ends, deps):
     ins, feat_dev = omega.shape
     k = weights.shape[1]
-    width = min(1024, owned)
+    width = min(2048, owned)
     count = feat_dev // width
     own = owned // width
     low, high = blocks[0] * count // 2, blocks[1] * count // 2
@@ -282,7 +278,7 @@
         at = pl.ds(pl.multiple_of(start, rows), rows) if bit else slice(None)
         rate = chunks[j][...].astype(f32)
         rate_out[0, at, :] = rate
-        held[at, :] = jnp.exp(rate) - observed[0, at, :].astype(f32)
+        held[at, :] = jnp.exp(rate) - observed[m, at, :].astype(f32)
     residual_out[...] = held[...].T.astype(bf16)
 
 
@@ -291,8 +287,7 @@
     k = chunks[0].shape[1]
     batch = counts.shape[1]
     args = [f, *chunks, counts, *deps]
-    specs = [IN_VMEM] * n + [pl.BlockSpec((1, batch, k), lambda i, _: (m, 0, 0))]
-    specs += [ANYWHERE] * len(deps)
+    specs = [IN_VMEM] * (n + 1) + [ANYWHERE] * len(deps)
     aliases = {}
     if before is not None:
         aliases = {len(args): 0}
@@ -365,8 +360,8 @@
     moved_second = beta_two * second[0] + (1.0 - beta_two) * conditioned * conditioned
     correction_one = 1.0 - beta_one**STEP
     correction_two = 1.0 - beta_two**STEP
-    moved = master[0] - learn_rate * (moved_first / correction_one) / (
-        jnp.sqrt(moved_second / correction_two) + 1e-08
+    moved = master[0] - (learn_rate / correction_one) * moved_first / (
+        jnp.sqrt(moved_second * (1.0 / correction_two)) + 1e-08
     )
     new_first[0] = moved_first
     new_second[0] = moved_second
@@ -420,7 +415,7 @@
         copy.wait()
 
 
-def put(p, pieces, blocks, owned, n_pts):
+def put(p, pieces, blocks, owned, n_pts, before):
     n = len(pieces)
     k = pieces[0].shape[1]
     return pl.pallas_call(
@@ -428,15 +423,16 @@
         grid_spec=pltpu.PrefetchScalarGridSpec(
             num_scalar_prefetch=1,
             grid=(1,),
-            in_specs=[IN_VMEM] * n,
+            in_specs=[IN_VMEM] * n + [ANYWHERE] * (before is not None),
             out_specs=ANYWHERE,
             scratch_shapes=[pltpu.SemaphoreType.DMA((n,))],
         ),
         out_shape=jax.ShapeDtypeStruct((owned * n_pts, k), bf16),
+        input_output_aliases={} if before is None else {n + 1: 0},
         compiler_params=params(),
         cost_estimate=cost(2),
         name="put_rows",
-    )(p, *pieces)
+    )(p, *pieces, *([] if before is None else [before]))
 
 
 def ring(x, axis, n, distance):
@@ -467,7 +463,7 @@
     batch = picks.shape[1]
     bits = n_feat.bit_length() - 1
     points, picks, omega, weights = map(in_hbm, (points, picks, omega, weights))
-    phase, counts, cov = map(in_hbm, (phase[None, :], counts, cov))
+    phase, cov = map(in_hbm, (phase[None, :], cov))
     master, first, second = map(in_hbm, (master, first, second))
 
     chosen, token = gather(picks, points)
@@ -535,24 +531,32 @@
     sizes = [2, 3, 2, 1] if steps == 8 else [1] * steps
     chips = n_pts // CORES
     state = None
-    pieces, blocks = [], []
     at = 0
-    early = []
+    sent, come, starts = [], [], []
     for c, size in enumerate(sizes):
-        *state, sent = update(
+        *state, rows = update(
             features[1], res_one, begun, cov, master, first, second, at, size, state, [token]
         )
-        come = [sent]
-        if chips > 1:
-            if c >= 2:
-                sent, _ = lax.optimization_barrier((sent, early[c - 2]))
-            come += [across(sent, n_pts, d) for d in range(1, chips)]
-            early.append(come[1])
-        pieces += come + [mate(x, n_pts) for x in come]
-        start = at * (owned // steps)
-        blocks += [(d, other, start) for other in (0, 1) for d in range(chips)]
+        if c >= 2 and chips > 1:
+            rows, _ = lax.optimization_barrier((rows, come[c - 2][0]))
+        sent.append(rows)
+        come.append([across(rows, n_pts, d) for d in range(1, chips)])
+        starts.append(at * (owned // steps))
         at += size
-    working = put(p, pieces, blocks, owned, n_pts)
+    working = None
+    for group in [range(len(sizes) - 1), [len(sizes) - 1]]:
+        pieces, blocks = [], []
+        for c in group:
+            got = come[c]
+            if c and got:
+                fence = sent[-1] if working is None else working
+                *got, fence = lax.optimization_barrier((*got, fence))
+                working = None if working is None else fence
+            pieces += [sent[c], mate(sent[c], n_pts)] + got + [mate(y, n_pts) for y in got]
+            blocks += [(0, other, starts[c]) for other in (0, 1)]
+            blocks += [(d, other, starts[c]) for other in (0, 1) for d in range(1, chips)]
+        if pieces:
+            working = put(p, pieces, blocks, owned, n_pts, working)
     return out_rates, *state, working
 
 

time: 108 us -> 106 us (0.981)
  Pallas kernels: 73.3 us -> 66.2 us
  waiting for transfers between devices: 16.7 us -> 21 us
    pallas_call x3, Pallas kernels: 29.5 us -> 25.2 us  [rates(): pl.pallas_call(kernel, grid_spec=pltpu.PrefetchScalarGridSpec(num_scalar_...]
    pallas_call x2, Pallas kernels: 4.01 us -> 1.94 us  [residuals(): pl.pallas_call(functools.partial(residual_kernel, masks, m), grid_spec=pl...]
    ppermute x6, waiting for transfers between devices: 5.45 us -> 7.41 us  [swap(): return lax.ppermute(x, 'feat', [(i, i ^ 2 ** bit) for i in range(n)])]
    ppermute x7, waiting for transfers between devices: 9.47 us -> 11.3 us  [ring(): return lax.ppermute(x, axis, [(i, (i + distance) % n) for i in range(n)])]
    pallas_call x6, Pallas kernels: 14.3 us -> 13 us  [owned_features(): pl.pallas_call(functools.partial(features_kernel, start, size), in_specs=...]
    pallas_call x1 -> x2, Pallas kernels: 2.13 us -> 2.75 us  [put(): pl.pallas_call(functools.partial(put_kernel, blocks, owned, n_pts), grid_...]
  transfers between devices with their start and end apart: 27 -> 27, of which waited for: 9 -> 9; matrix products, arithmetic and copies ran while one was open for 0% -> 0% of each run, Pallas kernels for 60% -> 56%
where the time goes in v5:
time: 106 us; the launch traced here: 105 us
  Pallas kernels  66.2 us (62%)
  waiting for transfers between devices  21 us (20%)
  starting transfers between devices  17 us (16%)
    pallas_call x3, Pallas kernels, rates(): pl.pallas_call(kernel, grid_spec=pltpu.PrefetchScalarGridSpec(num_scalar_...  25.2 us
    pallas_call x4, Pallas kernels, update(): pl.pallas_call(functools.partial(update_kernel, n, at), grid=(steps,), in...  15.7 us
    pallas_call x6, Pallas kernels, owned_features(): pl.pallas_call(functools.partial(features_kernel, start, size), in_specs=...  13 us
    ppermute x7, waiting for transfers between devices, ring(): return lax.ppermute(x, axis, [(i, (i + distance) % n) for i in range(n)])  11.3 us
    ppermute x7, starting transfers between devices, ring(): return lax.ppermute(x, axis, [(i, (i + distance) % n) for i in range(n)])  7.49 us
    ppermute x6, waiting for transfers between devices, swap(): return lax.ppermute(x, 'feat', [(i, i ^ 2 ** bit) for i in range(n)])  7.41 us
    ppermute x6, starting transfers between devices, swap(): return lax.ppermute(x, 'feat', [(i, i ^ 2 ** bit) for i in range(n)])  6.92 us
    pallas_call x1, Pallas kernels, first_part(): pl.pallas_call(functools.partial(first_part_kernel, n), grid=(owned // ro...  4.75 us
  transfers between devices with their start and end apart: 27, of which 9 were waited for; matrix products, arithmetic and copies ran while one was open for 0% of the time, Pallas kernels for 56%

profile of v5, /device:TPU:0, one launch (start us, length us, event | category | flops | bytes accessed | tf_op | source)
XLA Modules:
  0.0 105.3 jit_solution(16986301257826082644)
XLA Ops:
  0.6 2.8 %chosen_points.1 = (bf16[1024,256]{1,0:T(8,128)(2,1)S(1)}, f32[8,128]{1,0:T(8,128)S(1)}) custom-call(s32[2,512]{1,0:T(2,128)} %picks.1, bf16[2048,256]{1,0:T(8,128)(2,1)} %points.1), custom_call_target="tpu_custom_call" | custom-call | flops 3000000000 | bytes 1024 | tf_op jit(solution)/shard_map/chosen_points/pallas_call | solution.py:68
  3.4 0.5 collective-permute-start.2
  3.9 2.6 %collective-permute-start.5 = (bf16[1024,256]{1,0:T(8,128)(2,1)S(1)}, bf16[1024,256]{1,0:T(8,128)(2,1)S(1)}, u32[]{:S(2)}, u32[]{:S(2)}) collective-permute-start(bf16[1024,256]{1,0:T(8,128)(2,1)S(1)} %get-tuple-element.69.refs_2_), channel_id=1, source_target_pairs={{0,8},{4,12},{8,0},{12,4},{1,9},{5,13},{9,1},{13,5},{2,10},{6,14},... | collective-permute-start | bytes 1572872 | tf_op jit(solution)/shard_map/ppermute | solution.py:439
  6.5 12.0 %partial_log_rates.3 = (bf16[512,2048]{1,0:T(8,128)(2,1)S(1)}, bf16[256,2048]{1,0:T(8,128)(2,1)S(1)}, f32[1,2048]{1,0:T(1,128)S(1)}, f32[256,256]{1,0:T(8,128)S(...) custom-call(s32[1]{0:T(128)} %bitcast.refs_0_.f, s32[1]{0:T(128)} %bitcast.1.refs_1_.p, ...), custom_call_target="tpu_custom_call" | custom-call | flops 12000000000 | bytes 1024 | tf_op jit(solution)/shard_map/partial_log_rates/pallas_call | solution.py:185
  18.5 1.6 %collective-permute-start = (bf16[256,256]{1,0:T(8,128)(2,1)S(1)}, bf16[256,256]{1,0:T(8,128)(2,1)S(1)}, u32[]{:S(2)}, u32[]{:S(2)}) collective-permute-start(bf16[256,256]{1,0:T(8,128)(2,1)S(1)} %get-tuple-element.74), channel_id=1, source_target_pairs={{0,1},{1,0},{2,3},{3,2},{4,5},{5,4},{6,7},{7,6},{8,9},{9,8},{10,11... | collective-permute-start | bytes 393224 | tf_op jit(solution)/shard_map/ppermute | solution.py:451
  20.2 6.8 %partial_log_rates.4 = (bf16[512,2048]{1,0:T(8,128)(2,1)S(1)}, f32[512,256]{1,0:T(8,128)S(1)}, f32[8,128]{1,0:T(8,128)S(1)}) custom-call(s32[1]{0:T(128)} %bitcast.refs_0_.f, s32[1]{0:T(128)} %bitcast.1.refs_1_.p, bf16[1024,256]{1,0:T(8,128)(2,1)S(1)} %get-tuple-element.69.refs_2_, bf16[256,8192]{1,0:T(8,128)(2,1)} %refs_3_.5, f32[1,8192]{1,0:T(1,128)} %bitcast.4, ...), custom_call_target="tpu_custom_call" | custom-call | flops 6000000000 | bytes 1024 | tf_op jit(solution)/shard_map/partial_log_rates/pallas_call | solution.py:185
  27.0 0.0 collective-permute-done.b
  27.1 2.7 %collective-permute-start.3 = (bf16[256,256]{1,0:T(8,128)(2,1)S(1)}, bf16[256,256]{1,0:T(8,128)(2,1)S(1)}, u32[]{:S(2)}, u32[]{:S(2)}) collective-permute-start(bf16[256,256]{1,0:T(8,128)(2,1)S(1)} %get-tuple-element.81.a), channel_id=1, source_target_pairs={{0,2},{1,3},{2,0},{3,1},{4,6},{5,7},{6,4},{7,5},{8,10},{9,11},{10,... | collective-permute-start | bytes 393224 | tf_op jit(solution)/shard_map/ppermute | solution.py:451
  29.7 6.4 %partial_log_rates.5 = (f32[256,256]{1,0:T(8,128)S(1)}, bf16[256,256]{1,0:T(8,128)(2,1)S(1)}, f32[8,128]{1,0:T(8,128)S(1)}) custom-call(s32[1]{0:T(128)} %bitcast.refs_0_.f, s32[1]{0:T(128)} %bitcast.1.refs_1_.p, bf16[1024,256]{1,0:T(8,128)(2,1)S(1)} %get-tuple-element.69.refs_2_, bf16[256,8192]{1,0:T(8,128)(2,1)} %refs_3_.5, f32[1,8192]{1,0:T(1,128)} %bitcast.5, ...), custom_call_target="tpu_custom_call" | custom-call | flops 6000000000 | bytes 1024 | tf_op jit(solution)/shard_map/partial_log_rates/pallas_call | solution.py:185
  36.1 0.5 collective-permute-start.1
  36.7 0.0 collective-permute-done.3.b
  36.7 1.6 %collective-permute-start.7 = (bf16[256,256]{1,0:T(8,128)(2,1)S(1)}, bf16[256,256]{1,0:T(8,128)(2,1)S(1)}, u32[]{:S(2)}, u32[]{:S(2)}) collective-permute-start(bf16[256,256]{1,0:T(8,128)(2,1)S(1)} %get-tuple-element.86.refs_0_), channel_id=1, source_target_pairs={{0,1},{1,0},{2,3},{3,2},{4,5},{5,4},{6,7},{7,6},{8,9},{9,8},{10,11... | collective-permute-start | bytes 393224 | tf_op jit(solution)/shard_map/ppermute | solution.py:451
  38.3 0.0 collective-permute-done.2.chosen
  38.3 2.1 %owned_features.6 = (bf16[512,2048]{1,0:T(8,128)(2,1)S(1)}, f32[8,128]{1,0:T(8,128)S(1)}) custom-call(bf16[1024,256]{1,0:T(8,128)(2,1)S(1)} %collective-permute-done.2.chosen, bf16[256,2048]{1,0:T(8,128)(2,1)S(1)} %get-tuple-element.79.omega, f32[1,2048]{1,0:T(1,128)S(1)} %get-tuple-element.80.turns, f32[8,128]{1,0:T(8,128)S(1)} %get-tuple-element.83.refs_0_), custom_call_target="tpu_custom_call" | custom-call | flops 1000000000 | bytes 1024 | tf_op jit(solution)/shard_map/owned_features/pallas_call | solution.py:219
  40.5 2.0 %collective-permute-done.1.b = bf16[256,256]{1,0:T(8,128)(2,1)S(1)} collective-permute-done((bf16[256,256]{1,0:T(8,128)(2,1)S(1)}, bf16[256,256]{1,0:T(8,128)(2,1)S(1)}, u32[]{:S(2)}, u32[]{:S(2)}) %collective-permute-start.1) | collective-permute-done | bytes 131104 | tf_op jit(solution)/shard_map/ppermute | solution.py:451
  42.5 0.0 copy-start
  42.6 0.4 collective-permute-start.4
  43.0 2.1 %owned_features.7 = (bf16[512,2048]{1,0:T(8,128)(2,1)S(1)}, f32[8,128]{1,0:T(8,128)S(1)}) custom-call(bf16[1024,256]{1,0:T(8,128)(2,1)S(1)} %collective-permute-done.5.chosen, bf16[256,2048]{1,0:T(8,128)(2,1)S(1)} %get-tuple-element.79.omega, f32[1,2048]{1,0:T(1,128)S(1)} %get-tuple-element.80.turns, f32[8,128]{1,0:T(8,128)S(1)} %get-tuple-element.87.refs_0_), custom_call_target="tpu_custom_call" | custom-call | flops 1000000000 | bytes 1024 | tf_op jit(solution)/shard_map/owned_features/pallas_call | solution.py:219
  45.1 0.0 collective-permute-done.7.refs_1_
  45.1 1.0 residuals.2
  46.1 0.5 collective-permute-start.13
  46.6 2.1 %owned_features.8 = (bf16[512,2048]{1,0:T(8,128)(2,1)S(1)}, f32[8,128]{1,0:T(8,128)S(1)}) custom-call(bf16[1024,256]{1,0:T(8,128)(2,1)S(1)} %collective-permute-done.6.chosen, bf16[256,2048]{1,0:T(8,128)(2,1)S(1)} %get-tuple-element.79.omega, f32[1,2048]{1,0:T(1,128)S(1)} %get-tuple-element.80.turns, f32[8,128]{1,0:T(8,128)S(1)} %get-tuple-element.89.refs_0_), custom_call_target="tpu_custom_call" | custom-call | flops 1000000000 | bytes 1024 | tf_op jit(solution)/shard_map/owned_features/pallas_call | solution.py:219
  48.7 2.2 %collective-permute-done.4.b = bf16[256,256]{1,0:T(8,128)(2,1)S(1)} collective-permute-done((bf16[256,256]{1,0:T(8,128)(2,1)S(1)}, bf16[256,256]{1,0:T(8,128)(2,1)S(1)}, u32[]{:S(2)}, u32[]{:S(2)}) %collective-permute-start.4) | collective-permute-done | bytes 131104 | tf_op jit(solution)/shard_map/ppermute | solution.py:451
  51.0 0.1 collective-permute-start.8
  51.0 2.1 %owned_features.9 = (bf16[512,2048]{1,0:T(8,128)(2,1)S(1)}, f32[8,128]{1,0:T(8,128)S(1)}) custom-call(bf16[1024,256]{1,0:T(8,128)(2,1)S(1)} %collective-permute-done.2.chosen, bf16[256,2048]{1,0:T(8,128)(2,1)S(1)} %get-tuple-element.79.omega, f32[1,2048]{1,0:T(1,128)S(1)} %get-tuple-element.80.turns, f32[8,128]{1,0:T(8,128)S(1)} %get-tuple-element.92.refs_0_), custom_call_target="tpu_custom_call" | custom-call | flops 1000000000 | bytes 1024 | tf_op jit(solution)/shard_map/owned_features/pallas_call | solution.py:219
  53.2 3.1 %collective-permute-done.8.refs_1_ = bf16[256,256]{1,0:T(8,128)(2,1)S(1)} collective-permute-done((bf16[256,256]{1,0:T(8,128)(2,1)S(1)}, bf16[256,256]{1,0:T(8,128)(2,1)S(1)}, u32[]{:S(2)}, u32[]{:S(2)}) %collective-permute-start.8) | collective-permute-done | bytes 131104 | tf_op jit(solution)/shard_map/ppermute | solution.py:451
  56.3 1.0 residuals.3
  57.3 0.5 collective-permute-start.10
  57.8 0.5 collective-permute-start.14
  58.3 0.0 collective-permute-start.9
  58.3 2.1 %owned_features.10 = (bf16[512,2048]{1,0:T(8,128)(2,1)S(1)}, f32[8,128]{1,0:T(8,128)S(1)}) custom-call(bf16[1024,256]{1,0:T(8,128)(2,1)S(1)} %collective-permute-done.5.chosen, bf16[256,2048]{1,0:T(8,128)(2,1)S(1)} %get-tuple-element.79.omega, f32[1,2048]{1,0:T(1,128)S(1)} %get-tuple-element.80.turns, f32[8,128]{1,0:T(8,128)S(1)} %get-tuple-element.98.refs_0_), custom_call_target="tpu_custom_call" | custom-call | flops 1000000000 | bytes 1024 | tf_op jit(solution)/shard_map/owned_features/pallas_call | solution.py:219
  60.4 2.4 %owned_features.11 = (bf16[512,2048]{1,0:T(8,128)(2,1)S(1)}, f32[8,128]{1,0:T(8,128)S(1)}) custom-call(bf16[1024,256]{1,0:T(8,128)(2,1)S(1)} %collective-permute-done.6.chosen, bf16[256,2048]{1,0:T(8,128)(2,1)S(1)} %get-tuple-element.79.omega, f32[1,2048]{1,0:T(1,128)S(1)} %get-tuple-element.80.turns, f32[8,128]{1,0:T(8,128)S(1)} %get-tuple-element.100.refs_0_), custom_call_target="tpu_custom_call" | custom-call | flops 1000000000 | bytes 1024 | tf_op jit(solution)/shard_map/owned_features/pallas_call | solution.py:219
  62.8 1.7 %collective-permute-done.10.refs_6_ = bf16[256,512]{1,0:T(8,128)(2,1)S(1)} collective-permute-done((bf16[256,512]{1,0:T(8,128)(2,1)S(1)}, bf16[256,512]{1,0:T(8,128)(2,1)S(1)}, u32[]{:S(2)}, u32[]{:S(2)}) %collective-permute-start.10) | collective-permute-done | bytes 262176 | tf_op jit(solution)/shard_map/ppermute | solution.py:439
  64.5 0.0 collective-permute-done.12.refs_5_
  64.5 0.0 collective-permute-done.14.refs_7_
  64.5 4.7 %first_part.1 = (f32[2048,256]{1,0:T(8,128)S(1)}, f32[8,128]{1,0:T(8,128)S(1)}) custom-call(bf16[512,2048]{1,0:T(8,128)(2,1)S(1)} %get-tuple-element.103.refs_0_, bf16[512,2048]{1,0:T(8,128)(2,1)S(1)} %get-tuple-element.104.refs_1_, bf16[512,2048]{1,0:T(8,128)(2,1)S(1)} %get-tuple-element.105.refs_2_, bf16[512,2048]{1,0:T(8,128)(2,1)S(1)} %get-tuple-element.106.refs_3_, ...), custom_call_target="tpu_custom_call" | custom-call | flops 5000000000 | bytes 1024 | tf_op jit(solution)/shard_map/first_part/pallas_call | solution.py:337
  69.3 0.0 collective-permute-done.9.refs_5_
  69.3 0.0 collective-permute-done.11.refs_7_
  69.3 3.8 %update.4 = (f32[1,2048,256]{2,1,0:T(8,128)}, f32[1,2048,256]{2,1,0:T(8,128)}, f32[1,2048,256]{2,1,0:T(8,128)}, bf16[512,256]{1,0:T(8,128)(2,1)S(1)}) custom-call(bf16[512,2048]{1,0:T(8,128)(2,1)S(1)} %get-tuple-element.96.refs_0_, bf16[512,2048]{1,0:T(8,128)(2,1)S(1)} %get-tuple-element.97.refs_1_, bf16[512,2048]{1,0:T(8,128)(2,1)S(1)} %get-tuple-element.99.refs_2_, ...), custom_call_target="tpu_custom_call" | custom-call | flops 1000000000 | bytes 1024 | tf_op jit(solution)/shard_map/update/pallas_call | solution.py:387
  73.1 0.5 collective-permute-start.19
  73.6 5.1 %update.5 = (f32[1,2048,256]{2,1,0:T(8,128)}, f32[1,2048,256]{2,1,0:T(8,128)}, f32[1,2048,256]{2,1,0:T(8,128)}, bf16[768,256]{1,0:T(8,128)(2,1)S(1)}) custom-call(bf16[512,2048]{1,0:T(8,128)(2,1)S(1)} %get-tuple-element.96.refs_0_, bf16[512,2048]{1,0:T(8,128)(2,1)S(1)} %get-tuple-element.97.refs_1_, ...), custom_call_target="tpu_custom_call", output_to_operand_aliasing={{0}: (13, {}), {1}: (14, {}), {2}: (15, {})} | custom-call | flops 1000000000 | bytes 1024 | tf_op jit(solution)/shard_map/update/pallas_call | solution.py:387
  78.8 1.5 %collective-permute-start.15 = (bf16[768,256]{1,0:T(8,128)(2,1)S(1)}, bf16[768,256]{1,0:T(8,128)(2,1)S(1)}, u32[]{:S(2)}, u32[]{:S(2)}) collective-permute-start(bf16[768,256]{1,0:T(8,128)(2,1)S(1)} %get-tuple-element.124.refs_4_), channel_id=1, source_target_pairs={{0,8},{4,12},{8,0},{12,4},{1,9},{5,13},{9,1},{13,5},{2,10},{6,14},... | collective-permute-start | bytes 1179656 | tf_op jit(solution)/shard_map/ppermute | solution.py:439
  80.3 3.8 %update.6 = (f32[1,2048,256]{2,1,0:T(8,128)}, f32[1,2048,256]{2,1,0:T(8,128)}, f32[1,2048,256]{2,1,0:T(8,128)}, bf16[512,256]{1,0:T(8,128)(2,1)S(1)}) custom-call(bf16[512,2048]{1,0:T(8,128)(2,1)S(1)} %get-tuple-element.96.refs_0_, bf16[512,2048]{1,0:T(8,128)(2,1)S(1)} %get-tuple-element.97.refs_1_, ...), custom_call_target="tpu_custom_call", output_to_operand_aliasing={{0}: (13, {}), {1}: (14, {}), {2}: (15, {})} | custom-call | flops 1000000000 | bytes 1024 | tf_op jit(solution)/shard_map/update/pallas_call | solution.py:387
  84.1 0.0 collective-permute-done.19.refs_2_
  84.1 0.6 collective-permute-start.24
  84.7 0.5 collective-permute-start.21
  85.2 2.9 %update.7 = (f32[1,2048,256]{2,1,0:T(8,128)}, f32[1,2048,256]{2,1,0:T(8,128)}, f32[1,2048,256]{2,1,0:T(8,128)}, bf16[256,256]{1,0:T(8,128)(2,1)S(1)}) custom-call(bf16[512,2048]{1,0:T(8,128)(2,1)S(1)} %get-tuple-element.96.refs_0_, bf16[512,2048]{1,0:T(8,128)(2,1)S(1)} %get-tuple-element.97.refs_1_, ...), custom_call_target="tpu_custom_call", output_to_operand_aliasing={{0}: (13, {}), {1}: (14, {}), {2}: (15, {})} | custom-call | flops 1000000000 | bytes 1024 | tf_op jit(solution)/shard_map/update/pallas_call | solution.py:387
  88.1 2.7 %collective-permute-done.15.refs_6_ = bf16[768,256]{1,0:T(8,128)(2,1)S(1)} collective-permute-done((bf16[768,256]{1,0:T(8,128)(2,1)S(1)}, bf16[768,256]{1,0:T(8,128)(2,1)S(1)}, u32[]{:S(2)}, u32[]{:S(2)}) %collective-permute-start.15) | collective-permute-done | bytes 393248 | tf_op jit(solution)/shard_map/ppermute | solution.py:439
  90.7 0.0 collective-permute-start.22
  90.7 0.5 collective-permute-start.23
  91.3 4.6 %collective-permute-done.24.refs_10_ = bf16[512,256]{1,0:T(8,128)(2,1)S(1)} collective-permute-done((bf16[512,256]{1,0:T(8,128)(2,1)S(1)}, bf16[512,256]{1,0:T(8,128)(2,1)S(1)}, u32[]{:S(2)}, u32[]{:S(2)}) %collective-permute-start.24) | collective-permute-done | bytes 262176 | tf_op jit(solution)/shard_map/ppermute | solution.py:439
  95.9 0.0 collective-permute-start.20
  95.9 0.5 collective-permute-start.25
  96.4 0.1 collective-permute-start.16
  96.5 0.9 collective-permute-done.20.refs_3_
  97.4 1.3 %collective-permute-start.17 = (bf16[256,256]{1,0:T(8,128)(2,1)S(1)}, bf16[256,256]{1,0:T(8,128)(2,1)S(1)}, u32[]{:S(2)}, u32[]{:S(2)}) collective-permute-start(bf16[256,256]{1,0:T(8,128)(2,1)S(1)} %get-tuple-element.125.refs_0_), channel_id=1, source_target_pairs={{0,8},{4,12},{8,0},{12,4},{1,9},{5,13},{9,1},{13,5},{2,10},{6,14},... | collective-permute-start | bytes 393224 | tf_op jit(solution)/shard_map/ppermute | solution.py:439
  98.7 0.0 collective-permute-done.23.refs_9_
  98.7 0.0 collective-permute-done.25.refs_11_
  98.7 0.0 collective-permute-done.22.refs_7_
  98.7 1.9 %put_rows.2.refs_4_ = bf16[8192,256]{1,0:T(8,128)(2,1)} custom-call(s32[1]{0:T(128)} %bitcast.1.refs_1_.p, bf16[512,256]{1,0:T(8,128)(2,1)S(1)} %get-tuple-element.126.refs_0_, bf16[512,256]{1,0:T(8,128)(2,1)S(1)} %collective-permute-done.18.refs_1_, bf16[512,256]{1,0:T(8,128)(2,1)S(1)} %collective-permute-done.19.refs_2_, ...), custom_call_target="tpu_custom_call" | custom-call | flops 2000000000 | bytes 1024 | tf_op jit(solution)/shard_map/put_rows/pallas_call | solution.py:421
  100.6 2.3 %collective-permute-done.17.refs_2_ = bf16[256,256]{1,0:T(8,128)(2,1)S(1)} collective-permute-done((bf16[256,256]{1,0:T(8,128)(2,1)S(1)}, bf16[256,256]{1,0:T(8,128)(2,1)S(1)}, u32[]{:S(2)}, u32[]{:S(2)}) %collective-permute-start.17) | collective-permute-done | bytes 131104 | tf_op jit(solution)/shard_map/ppermute | solution.py:439
  103.0 0.0 collective-permute-start.26
  103.0 1.3 %collective-permute-done.26.refs_3_ = bf16[256,256]{1,0:T(8,128)(2,1)S(1)} collective-permute-done((bf16[256,256]{1,0:T(8,128)(2,1)S(1)}, bf16[256,256]{1,0:T(8,128)(2,1)S(1)}, u32[]{:S(2)}, u32[]{:S(2)}) %collective-permute-start.26) | collective-permute-done | bytes 131104 | tf_op jit(solution)/shard_map/ppermute | solution.py:443
  104.3 0.8 put_rows.3
  (15 shorter events, 0.2 us)
Async XLA Ops:
  3.4 34.9 %collective-permute-start.2 = (bf16[1024,256]{1,0:T(8,128)(2,1)S(1)}, bf16[1024,256]{1,0:T(8,128)(2,1)S(1)}, u32[]{:S(2)}, u32[]{:S(2)}) collective-permute-start(bf16[1024,256]{1,0:T(8,128)(2,1)S(1)} %get-tuple-element.69.refs_2_), channel_id=1, source_target_pairs={{0,4},{4,0},{8,12},{12,8},{1,5},{5,1},{9,13},{13,9},{2,6},{6,2},{1... | collective-permute-start | bytes 1572872 | tf_op jit(solution)/shard_map/ppermute | solution.py:443
  3.9 25.8 %collective-permute-start.5 = (bf16[1024,256]{1,0:T(8,128)(2,1)S(1)}, bf16[1024,256]{1,0:T(8,128)(2,1)S(1)}, u32[]{:S(2)}, u32[]{:S(2)}) collective-permute-start(bf16[1024,256]{1,0:T(8,128)(2,1)S(1)} %get-tuple-element.69.refs_2_), channel_id=1, source_target_pairs={{0,8},{4,12},{8,0},{12,4},{1,9},{5,13},{9,1},{13,5},{2,10},{6,14},... | collective-permute-start | bytes 1572872 | tf_op jit(solution)/shard_map/ppermute | solution.py:439
  18.5 8.5 %collective-permute-start = (bf16[256,256]{1,0:T(8,128)(2,1)S(1)}, bf16[256,256]{1,0:T(8,128)(2,1)S(1)}, u32[]{:S(2)}, u32[]{:S(2)}) collective-permute-start(bf16[256,256]{1,0:T(8,128)(2,1)S(1)} %get-tuple-element.74), channel_id=1, source_target_pairs={{0,1},{1,0},{2,3},{3,2},{4,5},{5,4},{6,7},{7,6},{8,9},{9,8},{10,11... | collective-permute-start | bytes 393224 | tf_op jit(solution)/shard_map/ppermute | solution.py:451
  27.1 9.6 %collective-permute-start.3 = (bf16[256,256]{1,0:T(8,128)(2,1)S(1)}, bf16[256,256]{1,0:T(8,128)(2,1)S(1)}, u32[]{:S(2)}, u32[]{:S(2)}) collective-permute-start(bf16[256,256]{1,0:T(8,128)(2,1)S(1)} %get-tuple-element.81.a), channel_id=1, source_target_pairs={{0,2},{1,3},{2,0},{3,1},{4,6},{5,7},{6,4},{7,5},{8,10},{9,11},{10,... | collective-permute-start | bytes 393224 | tf_op jit(solution)/shard_map/ppermute | solution.py:451
  29.7 16.9 %collective-permute-start.6 = (bf16[1024,256]{1,0:T(8,128)(2,1)S(1)}, bf16[1024,256]{1,0:T(8,128)(2,1)S(1)}, u32[]{:S(2)}, u32[]{:S(2)}) collective-permute-start(bf16[1024,256]{1,0:T(8,128)(2,1)S(1)} %collective-permute-done.5.chosen), channel_id=1, source_target_pairs={{0,4},{4,0},{8,12},{12,8},{1,5},{5,1},{9,13},{13,9},{2,6},{6,2},{1... | collective-permute-start | bytes 1572872 | tf_op jit(solution)/shard_map/ppermute | solution.py:443
  36.1 6.4 %collective-permute-start.1 = (bf16[256,256]{1,0:T(8,128)(2,1)S(1)}, bf16[256,256]{1,0:T(8,128)(2,1)S(1)}, u32[]{:S(2)}, u32[]{:S(2)}) collective-permute-start(bf16[256,256]{1,0:T(8,128)(2,1)S(1)} %get-tuple-element.78), channel_id=1, source_target_pairs={{0,1},{1,0},{2,3},{3,2},{4,5},{5,4},{6,7},{7,6},{8,9},{9,8},{10,11... | collective-permute-start | bytes 393224 | tf_op jit(solution)/shard_map/ppermute | solution.py:451
  36.7 8.4 %collective-permute-start.7 = (bf16[256,256]{1,0:T(8,128)(2,1)S(1)}, bf16[256,256]{1,0:T(8,128)(2,1)S(1)}, u32[]{:S(2)}, u32[]{:S(2)}) collective-permute-start(bf16[256,256]{1,0:T(8,128)(2,1)S(1)} %get-tuple-element.86.refs_0_), channel_id=1, source_target_pairs={{0,1},{1,0},{2,3},{3,2},{4,5},{5,4},{6,7},{7,6},{8,9},{9,8},{10,11... | collective-permute-start | bytes 393224 | tf_op jit(solution)/shard_map/ppermute | solution.py:451
  42.5 2.6 %copy-start = (s32[2,512,256]{2,1,0:T(8,128)S(1)}, s32[2,512,256]{2,1,0:T(8,128)}, u32[]{:S(2)}) copy-start(s32[2,512,256]{2,1,0:T(8,128)} %refs_2_.3) | copy-start | bytes 3145732
  42.6 8.4 %collective-permute-start.4 = (bf16[256,256]{1,0:T(8,128)(2,1)S(1)}, bf16[256,256]{1,0:T(8,128)(2,1)S(1)}, u32[]{:S(2)}, u32[]{:S(2)}) collective-permute-start(bf16[256,256]{1,0:T(8,128)(2,1)S(1)} %get-tuple-element.85.a), channel_id=1, source_target_pairs={{0,2},{1,3},{2,0},{3,1},{4,6},{5,7},{6,4},{7,5},{8,10},{9,11},{10,... | collective-permute-start | bytes 393224 | tf_op jit(solution)/shard_map/ppermute | solution.py:451
  46.1 11.7 %collective-permute-start.13 = (bf16[256,512]{1,0:T(8,128)(2,1)S(1)}, bf16[256,512]{1,0:T(8,128)(2,1)S(1)}, u32[]{:S(2)}, u32[]{:S(2)}) collective-permute-start(bf16[256,512]{1,0:T(8,128)(2,1)S(1)} %get-tuple-element.107.refs_4_), channel_id=1, source_target_pairs={{0,8},{4,12},{8,0},{12,4},{1,9},{5,13},{9,1},{13,5},{2,10},{6,14},... | collective-permute-start | bytes 786440 | tf_op jit(solution)/shard_map/ppermute | solution.py:439
  51.0 5.3 %collective-permute-start.8 = (bf16[256,256]{1,0:T(8,128)(2,1)S(1)}, bf16[256,256]{1,0:T(8,128)(2,1)S(1)}, u32[]{:S(2)}, u32[]{:S(2)}) collective-permute-start(bf16[256,256]{1,0:T(8,128)(2,1)S(1)} %get-tuple-element.91.refs_0_), channel_id=1, source_target_pairs={{0,1},{1,0},{2,3},{3,2},{4,5},{5,4},{6,7},{7,6},{8,9},{9,8},{10,11... | collective-permute-start | bytes 393224 | tf_op jit(solution)/shard_map/ppermute | solution.py:451
  57.3 7.2 %collective-permute-start.10 = (bf16[256,512]{1,0:T(8,128)(2,1)S(1)}, bf16[256,512]{1,0:T(8,128)(2,1)S(1)}, u32[]{:S(2)}, u32[]{:S(2)}) collective-permute-start(bf16[256,512]{1,0:T(8,128)(2,1)S(1)} %get-tuple-element.102.refs_4_), channel_id=1, source_target_pairs={{0,8},{4,12},{8,0},{12,4},{1,9},{5,13},{9,1},{13,5},{2,10},{6,14},... | collective-permute-start | bytes 786440 | tf_op jit(solution)/shard_map/ppermute | solution.py:439
  57.8 6.7 %collective-permute-start.12 = (bf16[256,512]{1,0:T(8,128)(2,1)S(1)}, bf16[256,512]{1,0:T(8,128)(2,1)S(1)}, u32[]{:S(2)}, u32[]{:S(2)}) collective-permute-start(bf16[256,512]{1,0:T(8,128)(2,1)S(1)} %get-tuple-element.107.refs_4_), channel_id=1, source_target_pairs={{0,4},{4,0},{8,12},{12,8},{1,5},{5,1},{9,13},{13,9},{2,6},{6,2},{1... | collective-permute-start | bytes 786440 | tf_op jit(solution)/shard_map/ppermute | solution.py:443
  57.8 6.7 %collective-permute-start.14 = (bf16[256,512]{1,0:T(8,128)(2,1)S(1)}, bf16[256,512]{1,0:T(8,128)(2,1)S(1)}, u32[]{:S(2)}, u32[]{:S(2)}) collective-permute-start(bf16[256,512]{1,0:T(8,128)(2,1)S(1)} %collective-permute-done.13.refs_6_), channel_id=1, source_target_pairs={{0,4},{4,0},{8,12},{12,8},{1,5},{5,1},{9,13},{13,9},{2,6},{6,2},{1... | collective-permute-start | bytes 786440 | tf_op jit(solution)/shard_map/ppermute | solution.py:443
  58.3 11.0 %collective-permute-start.9 = (bf16[256,512]{1,0:T(8,128)(2,1)S(1)}, bf16[256,512]{1,0:T(8,128)(2,1)S(1)}, u32[]{:S(2)}, u32[]{:S(2)}) collective-permute-start(bf16[256,512]{1,0:T(8,128)(2,1)S(1)} %get-tuple-element.102.refs_4_), channel_id=1, source_target_pairs={{0,4},{4,0},{8,12},{12,8},{1,5},{5,1},{9,13},{13,9},{2,6},{6,2},{1... | collective-permute-start | bytes 786440 | tf_op jit(solution)/shard_map/ppermute | solution.py:443
  64.5 4.8 %collective-permute-start.11 = (bf16[256,512]{1,0:T(8,128)(2,1)S(1)}, bf16[256,512]{1,0:T(8,128)(2,1)S(1)}, u32[]{:S(2)}, u32[]{:S(2)}) collective-permute-start(bf16[256,512]{1,0:T(8,128)(2,1)S(1)} %collective-permute-done.10.refs_6_), channel_id=1, source_target_pairs={{0,4},{4,0},{8,12},{12,8},{1,5},{5,1},{9,13},{13,9},{2,6},{6,2},{1... | collective-permute-start | bytes 786440 | tf_op jit(solution)/shard_map/ppermute | solution.py:443
  73.1 11.0 %collective-permute-start.19 = (bf16[512,256]{1,0:T(8,128)(2,1)S(1)}, bf16[512,256]{1,0:T(8,128)(2,1)S(1)}, u32[]{:S(2)}, u32[]{:S(2)}) collective-permute-start(bf16[512,256]{1,0:T(8,128)(2,1)S(1)} %get-tuple-element.126.refs_0_), channel_id=1, source_target_pairs={{0,8},{4,12},{8,0},{12,4},{1,9},{5,13},{9,1},{13,5},{2,10},{6,14},... | collective-permute-start | bytes 786440 | tf_op jit(solution)/shard_map/ppermute | solution.py:439
  78.8 12.0 %collective-permute-start.15 = (bf16[768,256]{1,0:T(8,128)(2,1)S(1)}, bf16[768,256]{1,0:T(8,128)(2,1)S(1)}, u32[]{:S(2)}, u32[]{:S(2)}) collective-permute-start(bf16[768,256]{1,0:T(8,128)(2,1)S(1)} %get-tuple-element.124.refs_4_), channel_id=1, source_target_pairs={{0,8},{4,12},{8,0},{12,4},{1,9},{5,13},{9,1},{13,5},{2,10},{6,14},... | collective-permute-start | bytes 1179656 | tf_op jit(solution)/shard_map/ppermute | solution.py:439
  84.1 11.8 %collective-permute-start.24 = (bf16[512,256]{1,0:T(8,128)(2,1)S(1)}, bf16[512,256]{1,0:T(8,128)(2,1)S(1)}, u32[]{:S(2)}, u32[]{:S(2)}) collective-permute-start(bf16[512,256]{1,0:T(8,128)(2,1)S(1)} %get-tuple-element.129.refs_8_), channel_id=1, source_target_pairs={{0,8},{4,12},{8,0},{12,4},{1,9},{5,13},{9,1},{13,5},{2,10},{6,14},... | collective-permute-start | bytes 786440 | tf_op jit(solution)/shard_map/ppermute | solution.py:439
  84.7 11.2 %collective-permute-start.18 = (bf16[512,256]{1,0:T(8,128)(2,1)S(1)}, bf16[512,256]{1,0:T(8,128)(2,1)S(1)}, u32[]{:S(2)}, u32[]{:S(2)}) collective-permute-start(bf16[512,256]{1,0:T(8,128)(2,1)S(1)} %get-tuple-element.126.refs_0_), channel_id=1, source_target_pairs={{0,4},{4,0},{8,12},{12,8},{1,5},{5,1},{9,13},{13,9},{2,6},{6,2},{1... | collective-permute-start | bytes 786440 | tf_op jit(solution)/shard_map/ppermute | solution.py:443
  84.7 11.7 %collective-permute-start.21 = (bf16[768,256]{1,0:T(8,128)(2,1)S(1)}, bf16[768,256]{1,0:T(8,128)(2,1)S(1)}, u32[]{:S(2)}, u32[]{:S(2)}) collective-permute-start(bf16[768,256]{1,0:T(8,128)(2,1)S(1)} %get-tuple-element.124.refs_4_), channel_id=1, source_target_pairs={{0,4},{4,0},{8,12},{12,8},{1,5},{5,1},{9,13},{13,9},{2,6},{6,2},{1... | collective-permute-start | bytes 1179656 | tf_op jit(solution)/shard_map/ppermute | solution.py:443
  90.7 8.0 %collective-permute-start.22 = (bf16[768,256]{1,0:T(8,128)(2,1)S(1)}, bf16[768,256]{1,0:T(8,128)(2,1)S(1)}, u32[]{:S(2)}, u32[]{:S(2)}) collective-permute-start(bf16[768,256]{1,0:T(8,128)(2,1)S(1)} %collective-permute-done.15.refs_6_), channel_id=1, source_target_pairs={{0,4},{4,0},{8,12},{12,8},{1,5},{5,1},{9,13},{13,9},{2,6},{6,2},{1... | collective-permute-start | bytes 1179656 | tf_op jit(solution)/shard_map/ppermute | solution.py:443
  90.7 7.9 %collective-permute-start.23 = (bf16[512,256]{1,0:T(8,128)(2,1)S(1)}, bf16[512,256]{1,0:T(8,128)(2,1)S(1)}, u32[]{:S(2)}, u32[]{:S(2)}) collective-permute-start(bf16[512,256]{1,0:T(8,128)(2,1)S(1)} %get-tuple-element.129.refs_8_), channel_id=1, source_target_pairs={{0,4},{4,0},{8,12},{12,8},{1,5},{5,1},{9,13},{13,9},{2,6},{6,2},{1... | collective-permute-start | bytes 786440 | tf_op jit(solution)/shard_map/ppermute | solution.py:443
  95.9 1.5 %collective-permute-start.20 = (bf16[512,256]{1,0:T(8,128)(2,1)S(1)}, bf16[512,256]{1,0:T(8,128)(2,1)S(1)}, u32[]{:S(2)}, u32[]{:S(2)}) collective-permute-start(bf16[512,256]{1,0:T(8,128)(2,1)S(1)} %collective-permute-done.19.refs_2_), channel_id=1, source_target_pairs={{0,4},{4,0},{8,12},{12,8},{1,5},{5,1},{9,13},{13,9},{2,6},{6,2},{1... | collective-permute-start | bytes 786440 | tf_op jit(solution)/shard_map/ppermute | solution.py:443
  95.9 2.8 %collective-permute-start.25 = (bf16[512,256]{1,0:T(8,128)(2,1)S(1)}, bf16[512,256]{1,0:T(8,128)(2,1)S(1)}, u32[]{:S(2)}, u32[]{:S(2)}) collective-permute-start(bf16[512,256]{1,0:T(8,128)(2,1)S(1)} %collective-permute-done.24.refs_10_), channel_id=1, source_target_pairs={{0,4},{4,0},{8,12},{12,8},{1,5},{5,1},{9,13},{13,9},{2,6},{6,2},{1... | collective-permute-start | bytes 786440 | tf_op jit(solution)/shard_map/ppermute | solution.py:443
  96.4 6.6 %collective-permute-start.16 = (bf16[256,256]{1,0:T(8,128)(2,1)S(1)}, bf16[256,256]{1,0:T(8,128)(2,1)S(1)}, u32[]{:S(2)}, u32[]{:S(2)}) collective-permute-start(bf16[256,256]{1,0:T(8,128)(2,1)S(1)} %get-tuple-element.125.refs_0_), channel_id=1, source_target_pairs={{0,4},{4,0},{8,12},{12,8},{1,5},{5,1},{9,13},{13,9},{2,6},{6,2},{1... | collective-permute-start | bytes 393224 | tf_op jit(solution)/shard_map/ppermute | solution.py:443
  97.4 5.5 %collective-permute-start.17 = (bf16[256,256]{1,0:T(8,128)(2,1)S(1)}, bf16[256,256]{1,0:T(8,128)(2,1)S(1)}, u32[]{:S(2)}, u32[]{:S(2)}) collective-permute-start(bf16[256,256]{1,0:T(8,128)(2,1)S(1)} %get-tuple-element.125.refs_0_), channel_id=1, source_target_pairs={{0,8},{4,12},{8,0},{12,4},{1,9},{5,13},{9,1},{13,5},{2,10},{6,14},... | collective-permute-start | bytes 393224 | tf_op jit(solution)/shard_map/ppermute | solution.py:439
  103.0 1.3 %collective-permute-start.26 = (bf16[256,256]{1,0:T(8,128)(2,1)S(1)}, bf16[256,256]{1,0:T(8,128)(2,1)S(1)}, u32[]{:S(2)}, u32[]{:S(2)}) collective-permute-start(bf16[256,256]{1,0:T(8,128)(2,1)S(1)} %collective-permute-done.17.refs_2_), channel_id=1, source_target_pairs={{0,4},{4,0},{8,12},{12,8},{1,5},{5,1},{9,13},{13,9},{2,6},{6,2},{1... | collective-permute-start | bytes 393224 | tf_op jit(solution)/shard_map/ppermute | solution.py:443

commit v6 on v5

--- a/solution.py
+++ b/solution.py
@@ -263,29 +263,30 @@
     )(f, a, b, *deps)
 
 
-def residual_kernel(masks, m, f, *refs):
+def residual_kernel(masks, start, f, *refs):
     chunks, observed = refs[: len(masks)], refs[len(masks)]
-    rate_out, residual_out, token, held = refs[-4:]
-    batch = held.shape[0]
+    rate_out, residual_out, token, rates, held, sem = refs[-6:]
+    size = held.shape[0]
     for j, mask in enumerate(masks):
         rows = chunks[j].shape[0]
-        start, bit = 0, 0
-        while batch >> (bit + 1) >= rows:
+        first, bit = 0, 0
+        while size >> (bit + 1) >= rows:
             side = lax.rem(f[0] // 2**bit, 2)
             side = 1 - side if mask >> bit & 1 else side
-            start = start + side * (batch >> (bit + 1))
+            first = first + side * (size >> (bit + 1))
             bit += 1
-        at = pl.ds(pl.multiple_of(start, rows), rows) if bit else slice(None)
-        rate = chunks[j][...].astype(f32)
-        rate_out[0, at, :] = rate
-        held[at, :] = jnp.exp(rate) - observed[m, at, :].astype(f32)
+        at = pl.ds(pl.multiple_of(first, rows), rows) if bit else slice(None)
+        rates[at, :] = chunks[j][...].astype(f32)
+    copy = pltpu.make_async_copy(rates, rate_out.at[pl.ds(start, size), :], sem)
+    copy.start()
+    held[...] = jnp.exp(rates[...]) - observed[start : start + size, :].astype(f32)
     residual_out[...] = held[...].T.astype(bf16)
-
-
-def residuals(f, chunks, masks, counts, m, before, deps):
+    copy.wait()
+
+
+def residuals(f, chunks, masks, counts, start, size, before, deps):
     n = len(chunks)
-    k = chunks[0].shape[1]
-    batch = counts.shape[1]
+    k = counts.shape[1]
     args = [f, *chunks, counts, *deps]
     specs = [IN_VMEM] * (n + 1) + [ANYWHERE] * len(deps)
     aliases = {}
@@ -294,17 +295,17 @@
         args.append(before)
         specs.append(ANYWHERE)
     return pl.pallas_call(
-        functools.partial(residual_kernel, masks, m),
+        functools.partial(residual_kernel, masks, start),
         grid_spec=pltpu.PrefetchScalarGridSpec(
             num_scalar_prefetch=1,
             grid=(1,),
             in_specs=specs,
-            out_specs=[pl.BlockSpec((1, batch, k), lambda i, _: (m, 0, 0)), IN_VMEM, ANYWHERE],
-            scratch_shapes=[pltpu.VMEM((batch, k), f32)],
+            out_specs=[ANYWHERE, IN_VMEM, ANYWHERE],
+            scratch_shapes=[pltpu.VMEM((size, k), f32)] * 2 + [pltpu.SemaphoreType.DMA],
         ),
         out_shape=[
             jax.ShapeDtypeStruct(counts.shape, f32),
-            jax.ShapeDtypeStruct((k, batch), bf16),
+            jax.ShapeDtypeStruct((k, size), bf16),
             TOKEN,
         ],
         input_output_aliases=aliases,
@@ -315,7 +316,7 @@
 
 
 def gradient_part(n, features, residual, start, rows):
-    at = pl.ds(pl.multiple_of(start, rows), rows)
+    at = slice(start, start + rows) if isinstance(start, int) else pl.ds(pl.multiple_of(start, rows), rows)
     value = None
     for j in range(n):
         term = jnp.dot(residual[j][...], features[j][:, at], preferred_element_type=f32)
@@ -326,21 +327,19 @@
 def first_part_kernel(n, *refs):
     features, residual, master = refs[:n], refs[n : 2 * n], refs[2 * n]
     out = refs[-2]
-    rows = out.shape[0]
-    out[...] = gradient_part(n, features, residual, pl.program_id(0) * rows, rows).T + master[0]
+    rows = min(512, out.shape[0])
+    for start in range(0, out.shape[0], rows):
+        value = gradient_part(n, features, residual, start, rows).T
+        out[start : start + rows, :] = value + master[0, start : start + rows, :]
 
 
 def first_part(features, residual, master, deps):
     n = len(features)
     owned, k = master.shape[1:]
-    rows = min(512, owned)
     return pl.pallas_call(
         functools.partial(first_part_kernel, n),
-        grid=(owned // rows,),
-        in_specs=[IN_VMEM] * (2 * n)
-        + [pl.BlockSpec((1, rows, k), lambda i: (0, i, 0))]
-        + [ANYWHERE] * len(deps),
-        out_specs=[pl.BlockSpec((rows, k), lambda i: (i, 0)), ANYWHERE],
+        in_specs=[IN_VMEM] * (2 * n + 1) + [ANYWHERE] * len(deps),
+        out_specs=[IN_VMEM, ANYWHERE],
         out_shape=[jax.ShapeDtypeStruct((owned, k), f32), TOKEN],
         compiler_params=params(),
         cost_estimate=cost(5),
@@ -352,15 +351,17 @@
     features, residual = refs[:n], refs[n : 2 * n]
     begun, cov, master, first, second = refs[2 * n : 2 * n + 5]
     new_master, new_first, new_second, sent = refs[-4:]
-    rows = master.shape[1]
+    rows = new_master.shape[1]
     step = pl.program_id(0)
-    gradient = gradient_part(n, features, residual, (begin + step) * rows, rows).T + begun[...]
+    start = pl.multiple_of((begin + step) * rows, rows)
+    at = pl.ds(start, rows)
+    gradient = gradient_part(n, features, residual, start, rows).T + begun[at, :]
     conditioned = jnp.dot(gradient.astype(bf16), cov[...], preferred_element_type=f32)
-    moved_first = beta_one * first[0] + (1.0 - beta_one) * conditioned
-    moved_second = beta_two * second[0] + (1.0 - beta_two) * conditioned * conditioned
+    moved_first = beta_one * first[0, at, :] + (1.0 - beta_one) * conditioned
+    moved_second = beta_two * second[0, at, :] + (1.0 - beta_two) * conditioned * conditioned
     correction_one = 1.0 - beta_one**STEP
     correction_two = 1.0 - beta_two**STEP
-    moved = master[0] - (learn_rate / correction_one) * moved_first / (
+    moved = master[0, at, :] - (learn_rate / correction_one) * moved_first / (
         jnp.sqrt(moved_second * (1.0 / correction_two)) + 1e-08
     )
     new_first[0] = moved_first
@@ -374,9 +375,8 @@
     owned, k = master.shape[1:]
     rows = min(256, owned)
     state = pl.BlockSpec((1, rows, k), lambda i: (0, at + i, 0))
-    flat = pl.BlockSpec((rows, k), lambda i: (at + i, 0))
     args = [*features, *residual, begun, cov, master, first, second]
-    specs = [IN_VMEM] * (2 * n) + [flat, pl.BlockSpec(cov.shape, lambda i: (0, 0))] + [state] * 3
+    specs = [IN_VMEM] * (2 * n + 5)
     aliases = {}
     if before is not None:
         aliases = {len(args) + j: j for j in range(3)}
@@ -430,7 +430,7 @@
         out_shape=jax.ShapeDtypeStruct((owned * n_pts, k), bf16),
         input_output_aliases={} if before is None else {n + 1: 0},
         compiler_params=params(),
-        cost_estimate=cost(2),
+        cost_estimate=cost(0.01),
         name="put_rows",
     )(p, *pieces, *([] if before is None else [before]))
 
@@ -460,18 +460,21 @@
     f = lax.axis_index("feat").astype(jnp.int32).reshape(1)
     p = lax.axis_index("pts").astype(jnp.int32).reshape(1)
     owned, k = master.shape[1:]
-    batch = picks.shape[1]
+    points_here = 2 * picks.shape[1]
+    size_one = points_here * 3 // 8
+    parts = [(0, points_here - size_one), (points_here - size_one, size_one)]
     bits = n_feat.bit_length() - 1
     points, picks, omega, weights = map(in_hbm, (points, picks, omega, weights))
-    phase, cov = map(in_hbm, (phase[None, :], cov))
-    master, first, second = map(in_hbm, (master, first, second))
+    phase = in_hbm(phase[None, :])
+    outer = counts.shape
+    counts = counts.reshape(points_here, k)
 
     chosen, token = gather(picks, points)
     everyone = spread(chosen, n_pts)
 
     def some_rates(m, blocks, before, keep, ends, token):
         return rates(
-            f, p, chosen, omega, phase, weights, m * batch, batch, owned, blocks, before, keep, ends, [token]
+            f, p, chosen, omega, phase, weights, *parts[m], owned, blocks, before, keep, ends, [token]
         )
 
     def add_up(kept, got, bit, token):
@@ -505,7 +508,7 @@
         for _ in range(pieces * share):
             m, j = todo.pop(0)
             feats, token = owned_features(
-                everyone[j], own_omega, own_turns, m * batch, batch, [token]
+                everyone[j], own_omega, own_turns, *parts[m], [token]
             )
             features[m].append(feats)
         return token
@@ -515,20 +518,21 @@
     token = some(token, 1)
     for bit in range(1, bits):
         kept_one, got_one, token = add_up(kept_one, got_one, bit, token)
-    token = some(token, 1)
-    out_rates, res, token = residuals(f, rows_zero, masks, counts, 0, None, [token])
+    out_rates, res, token = residuals(f, rows_zero, masks, counts, *parts[0], None, [token])
     res_zero = spread(res, n_pts)
     token = some(token, 1)
     chunk, token = total(f, kept_one, got_one, 0, False, [token])
     rows_one, masks = give_back(chunk)
     token = some(token, 1)
-    out_rates, res, token = residuals(f, rows_one, masks, counts, 1, out_rates, [token])
+    out_rates, res, token = residuals(
+        f, rows_one, masks, counts, *parts[1], out_rates, [token]
+    )
     res_one = spread(res, n_pts)
-    token = some(token, 2)
+    token = some(token, 3)
     begun, token = first_part(features[0], res_zero, master, [token])
 
     steps = max(1, owned // 256)
-    sizes = [2, 3, 2, 1] if steps == 8 else [1] * steps
+    sizes = [1, 3, 4] if steps == 8 else [1] * steps
     chips = n_pts // CORES
     state = None
     at = 0
@@ -537,9 +541,9 @@
         *state, rows = update(
             features[1], res_one, begun, cov, master, first, second, at, size, state, [token]
         )
-        if c >= 2 and chips > 1:
-            rows, _ = lax.optimization_barrier((rows, come[c - 2][0]))
-        sent.append(rows)
+        if c and chips > 1:
+            rows, _ = lax.optimization_barrier((rows, come[max(0, c - 2)][0]))
+        sent.append([rows, mate(rows, n_pts)])
         come.append([across(rows, n_pts, d) for d in range(1, chips)])
         starts.append(at * (owned // steps))
         at += size
@@ -549,15 +553,15 @@
         for c in group:
             got = come[c]
             if c and got:
-                fence = sent[-1] if working is None else working
+                fence = sent[-1][0] if working is None else working
                 *got, fence = lax.optimization_barrier((*got, fence))
                 working = None if working is None else fence
-            pieces += [sent[c], mate(sent[c], n_pts)] + got + [mate(y, n_pts) for y in got]
+            pieces += sent[c] + got + [mate(y, n_pts) for y in got]
             blocks += [(0, other, starts[c]) for other in (0, 1)]
             blocks += [(d, other, starts[c]) for other in (0, 1) for d in range(1, chips)]
         if pieces:
             working = put(p, pieces, blocks, owned, n_pts, working)
-    return out_rates, *state, working
+    return out_rates.reshape(outer), *state, working
 
 
 def solution(mesh):

time: 106 us -> 105 us (level)
  Pallas kernels: 66.2 us -> 58.7 us
  waiting for transfers between devices: 21 us -> 28.5 us
    pallas_call x4 -> x3, Pallas kernels: 15.7 us -> 9.14 us  [update(): pl.pallas_call(functools.partial(update_kernel, n, at), grid=(steps,), in...]
    ppermute x7 -> x6, waiting for transfers between devices: 11.3 us -> 15.3 us  [ring(): return lax.ppermute(x, axis, [(i, (i + distance) % n) for i in range(n)])]
    ppermute x6, waiting for transfers between devices: 7.41 us -> 9.8 us  [swap(): return lax.ppermute(x, 'feat', [(i, i ^ 2 ** bit) for i in range(n)])]
    ppermute x14 -> x12, starting transfers between devices: 2.64 us -> 1.49 us  [mate(): return lax.ppermute(x, 'pts', [(i, i ^ 1) for i in range(n)])]
    pallas_call x3, Pallas kernels: 6.69 us -> 5.59 us  [the longest x1 3.64 us: first_part(): pl.pallas_call(functools.partial(first_part_kernel, n), in_specs=[IN_VMEM...]
    ppermute x14 -> x12, waiting for transfers between devices: 2.32 us -> 3.37 us  [mate(): return lax.ppermute(x, 'pts', [(i, i ^ 1) for i in range(n)])]
    ppermute x7 -> x6, starting transfers between devices: 7.49 us -> 8.2 us  [ring(): return lax.ppermute(x, axis, [(i, (i + distance) % n) for i in range(n)])]
  transfers between devices with their start and end apart: 27 -> 24, of which waited for: 9 -> 11; matrix products, arithmetic and copies ran while one was open for 0% -> 0% of each run, Pallas kernels for 56% -> 50%
where the time goes in v6:
time: 105 us
  Pallas kernels  58.7 us (56%)
  waiting for transfers between devices  28.5 us (27%)
  starting transfers between devices  16.6 us (16%)
  between operations  1.07 us (1%)
    pallas_call x3, Pallas kernels, rates(): pl.pallas_call(kernel, grid_spec=pltpu.PrefetchScalarGridSpec(num_scalar_...  25.3 us
    ppermute x6, waiting for transfers between devices, ring(): return lax.ppermute(x, axis, [(i, (i + distance) % n) for i in range(n)])  15.3 us
    pallas_call x6, Pallas kernels, owned_features(): pl.pallas_call(functools.partial(features_kernel, start, size), in_specs=...  13 us
    ppermute x6, waiting for transfers between devices, swap(): return lax.ppermute(x, 'feat', [(i, i ^ 2 ** bit) for i in range(n)])  9.8 us
    pallas_call x3, Pallas kernels, update(): pl.pallas_call(functools.partial(update_kernel, n, at), grid=(steps,), in...  9.14 us
    ppermute x6, starting transfers between devices, ring(): return lax.ppermute(x, axis, [(i, (i + distance) % n) for i in range(n)])  8.2 us
    ppermute x6, starting transfers between devices, swap(): return lax.ppermute(x, 'feat', [(i, i ^ 2 ** bit) for i in range(n)])  6.88 us
    pallas_call x1, Pallas kernels, first_part(): pl.pallas_call(functools.partial(first_part_kernel, n), in_specs=[IN_VMEM...  3.64 us
  transfers between devices with their start and end apart: 24, of which 11 were waited for; matrix products, arithmetic and copies ran while one was open for 0% of the time, Pallas kernels for 50%

profile of v6, /device:TPU:0, one launch (start us, length us, event | category | flops | bytes accessed | tf_op | source)
XLA Modules:
  0.0 104.9 jit_solution(3147926945044587966)
XLA Ops:
  0.6 2.8 %chosen_points.1 = (bf16[1024,256]{1,0:T(8,128)(2,1)S(1)}, f32[8,128]{1,0:T(8,128)S(1)}) custom-call(s32[2,512]{1,0:T(2,128)} %picks.1, bf16[2048,256]{1,0:T(8,128)(2,1)} %points.1), custom_call_target="tpu_custom_call" | custom-call | flops 3000000000 | bytes 1024 | tf_op jit(solution)/shard_map/chosen_points/pallas_call | solution.py:68
  3.4 0.5 collective-permute-start.2
  3.9 2.6 %collective-permute-start.5 = (bf16[1024,256]{1,0:T(8,128)(2,1)S(1)}, bf16[1024,256]{1,0:T(8,128)(2,1)S(1)}, u32[]{:S(2)}, u32[]{:S(2)}) collective-permute-start(bf16[1024,256]{1,0:T(8,128)(2,1)S(1)} %get-tuple-element.64.refs_2_), channel_id=1, source_target_pairs={{0,8},{4,12},{8,0},{12,4},{1,9},{5,13},{9,1},{13,5},{2,10},{6,14},... | collective-permute-start | bytes 1572872 | tf_op jit(solution)/shard_map/ppermute | solution.py:439
  6.5 14.2 %partial_log_rates.3 = (bf16[640,2048]{1,0:T(8,128)(2,1)S(1)}, bf16[256,2048]{1,0:T(8,128)(2,1)S(1)}, f32[1,2048]{1,0:T(1,128)S(1)}, f32[320,256]{1,0:T(8,128)S(...) custom-call(s32[1]{0:T(128)} %bitcast.refs_0_.f, s32[1]{0:T(128)} %bitcast.1.refs_1_.p, ...), custom_call_target="tpu_custom_call" | custom-call | flops 12000000000 | bytes 1024 | tf_op jit(solution)/shard_map/partial_log_rates/pallas_call | solution.py:185
  20.8 1.6 %collective-permute-start = (bf16[320,256]{1,0:T(8,128)(2,1)S(1)}, bf16[320,256]{1,0:T(8,128)(2,1)S(1)}, u32[]{:S(2)}, u32[]{:S(2)}) collective-permute-start(bf16[320,256]{1,0:T(8,128)(2,1)S(1)} %get-tuple-element.69), channel_id=1, source_target_pairs={{0,1},{1,0},{2,3},{3,2},{4,5},{5,4},{6,7},{7,6},{8,9},{9,8},{10,11... | collective-permute-start | bytes 491528 | tf_op jit(solution)/shard_map/ppermute | solution.py:451
  22.4 5.7 %partial_log_rates.4 = (bf16[384,2048]{1,0:T(8,128)(2,1)S(1)}, f32[384,256]{1,0:T(8,128)S(1)}, f32[8,128]{1,0:T(8,128)S(1)}) custom-call(s32[1]{0:T(128)} %bitcast.refs_0_.f, s32[1]{0:T(128)} %bitcast.1.refs_1_.p, bf16[1024,256]{1,0:T(8,128)(2,1)S(1)} %get-tuple-element.64.refs_2_, bf16[256,8192]{1,0:T(8,128)(2,1)} %refs_3_.5, f32[1,8192]{1,0:T(1,128)} %bitcast.8, ...), custom_call_target="tpu_custom_call" | custom-call | flops 6000000000 | bytes 1024 | tf_op jit(solution)/shard_map/partial_log_rates/pallas_call | solution.py:185
  28.1 0.0 collective-permute-done.b
  28.2 2.7 %collective-permute-start.3 = (bf16[320,256]{1,0:T(8,128)(2,1)S(1)}, bf16[320,256]{1,0:T(8,128)(2,1)S(1)}, u32[]{:S(2)}, u32[]{:S(2)}) collective-permute-start(bf16[320,256]{1,0:T(8,128)(2,1)S(1)} %get-tuple-element.76.a), channel_id=1, source_target_pairs={{0,2},{1,3},{2,0},{3,1},{4,6},{5,7},{6,4},{7,5},{8,10},{9,11},{10,... | collective-permute-start | bytes 491528 | tf_op jit(solution)/shard_map/ppermute | solution.py:451
  30.9 5.4 %partial_log_rates.5 = (f32[192,256]{1,0:T(8,128)S(1)}, bf16[192,256]{1,0:T(8,128)(2,1)S(1)}, f32[8,128]{1,0:T(8,128)S(1)}) custom-call(s32[1]{0:T(128)} %bitcast.refs_0_.f, s32[1]{0:T(128)} %bitcast.1.refs_1_.p, bf16[1024,256]{1,0:T(8,128)(2,1)S(1)} %get-tuple-element.64.refs_2_, bf16[256,8192]{1,0:T(8,128)(2,1)} %refs_3_.5, f32[1,8192]{1,0:T(1,128)} %bitcast.9, ...), custom_call_target="tpu_custom_call" | custom-call | flops 6000000000 | bytes 1024 | tf_op jit(solution)/shard_map/partial_log_rates/pallas_call | solution.py:185
  36.2 2.3 %collective-permute-done.3.b = bf16[320,256]{1,0:T(8,128)(2,1)S(1)} collective-permute-done((bf16[320,256]{1,0:T(8,128)(2,1)S(1)}, bf16[320,256]{1,0:T(8,128)(2,1)S(1)}, u32[]{:S(2)}, u32[]{:S(2)}) %collective-permute-start.3) | collective-permute-done | bytes 163872 | tf_op jit(solution)/shard_map/ppermute | solution.py:451
  38.6 0.1 collective-permute-start.6
  38.7 2.0 %collective-permute-start.1 = (bf16[192,256]{1,0:T(8,128)(2,1)S(1)}, bf16[192,256]{1,0:T(8,128)(2,1)S(1)}, u32[]{:S(2)}, u32[]{:S(2)}) collective-permute-start(bf16[192,256]{1,0:T(8,128)(2,1)S(1)} %get-tuple-element.73), channel_id=1, source_target_pairs={{0,1},{1,0},{2,3},{3,2},{4,5},{5,4},{6,7},{7,6},{8,9},{9,8},{10,11... | collective-permute-start | bytes 294920 | tf_op jit(solution)/shard_map/ppermute | solution.py:451
  40.7 0.0 copy-start.4
  40.7 2.6 %owned_features.6 = (bf16[640,2048]{1,0:T(8,128)(2,1)S(1)}, f32[8,128]{1,0:T(8,128)S(1)}) custom-call(bf16[1024,256]{1,0:T(8,128)(2,1)S(1)} %collective-permute-done.2.chosen, bf16[256,2048]{1,0:T(8,128)(2,1)S(1)} %get-tuple-element.74.omega, f32[1,2048]{1,0:T(1,128)S(1)} %get-tuple-element.75.turns, f32[8,128]{1,0:T(8,128)S(1)} %get-tuple-element.78.refs_0_), custom_call_target="tpu_custom_call" | custom-call | flops 1000000000 | bytes 1024 | tf_op jit(solution)/shard_map/owned_features/pallas_call | solution.py:219
  43.3 3.6 %collective-permute-done.1.b = bf16[192,256]{1,0:T(8,128)(2,1)S(1)} collective-permute-done((bf16[192,256]{1,0:T(8,128)(2,1)S(1)}, bf16[192,256]{1,0:T(8,128)(2,1)S(1)}, u32[]{:S(2)}, u32[]{:S(2)}) %collective-permute-start.1) | collective-permute-done | bytes 98336 | tf_op jit(solution)/shard_map/ppermute | solution.py:451
  46.9 1.1 %residuals.2 = (f32[1024,256]{1,0:T(8,128)}, bf16[256,640]{1,0:T(8,128)(2,1)S(1)}, f32[8,128]{1,0:T(8,128)S(1)}) custom-call(s32[1]{0:T(128)} %bitcast.refs_0_.f, bf16[320,256]{1,0:T(8,128)(2,1)S(1)} %get-tuple-element.81.refs_0_, bf16[320,256]{1,0:T(8,128)(2,1)S(1)} %collective-permute-done.6.refs_1_, s32[1024,256]{1,0:T(8,128)S(1)} %bitcast.5, ...), custom_call_target="tpu_custom_call" | custom-call | flops 1000000000 | bytes 1024 | tf_op jit(solution)/shard_map/residuals/pallas_call | solution.py:297
  48.0 0.5 collective-permute-start.13
  48.5 0.4 collective-permute-start.4
  49.0 2.6 %owned_features.7 = (bf16[640,2048]{1,0:T(8,128)(2,1)S(1)}, f32[8,128]{1,0:T(8,128)S(1)}) custom-call(bf16[1024,256]{1,0:T(8,128)(2,1)S(1)} %collective-permute-done.5.chosen, bf16[256,2048]{1,0:T(8,128)(2,1)S(1)} %get-tuple-element.74.omega, f32[1,2048]{1,0:T(1,128)S(1)} %get-tuple-element.75.turns, f32[8,128]{1,0:T(8,128)S(1)} %get-tuple-element.83.refs_0_), custom_call_target="tpu_custom_call" | custom-call | flops 1000000000 | bytes 1024 | tf_op jit(solution)/shard_map/owned_features/pallas_call | solution.py:219
  51.6 3.6 %collective-permute-done.4.b = bf16[192,256]{1,0:T(8,128)(2,1)S(1)} collective-permute-done((bf16[192,256]{1,0:T(8,128)(2,1)S(1)}, bf16[192,256]{1,0:T(8,128)(2,1)S(1)}, u32[]{:S(2)}, u32[]{:S(2)}) %collective-permute-start.4) | collective-permute-done | bytes 98336 | tf_op jit(solution)/shard_map/ppermute | solution.py:451
  55.2 0.1 collective-permute-start.7
  55.2 0.1 collective-permute-start.12
  55.3 1.5 %collective-permute-done.13.refs_6_ = bf16[256,640]{1,0:T(8,128)(2,1)S(1)} collective-permute-done((bf16[256,640]{1,0:T(8,128)(2,1)S(1)}, bf16[256,640]{1,0:T(8,128)(2,1)S(1)}, u32[]{:S(2)}, u32[]{:S(2)}) %collective-permute-start.13) | collective-permute-done | bytes 327712 | tf_op jit(solution)/shard_map/ppermute | solution.py:439
  56.9 0.0 collective-permute-start.14
  56.9 0.0 collective-permute-done.8.chosen
  56.9 2.6 %owned_features.8 = (bf16[640,2048]{1,0:T(8,128)(2,1)S(1)}, f32[8,128]{1,0:T(8,128)S(1)}) custom-call(bf16[1024,256]{1,0:T(8,128)(2,1)S(1)} %collective-permute-done.8.chosen, bf16[256,2048]{1,0:T(8,128)(2,1)S(1)} %get-tuple-element.74.omega, f32[1,2048]{1,0:T(1,128)S(1)} %get-tuple-element.75.turns, f32[8,128]{1,0:T(8,128)S(1)} %get-tuple-element.86.refs_0_), custom_call_target="tpu_custom_call" | custom-call | flops 1000000000 | bytes 1024 | tf_op jit(solution)/shard_map/owned_features/pallas_call | solution.py:219
  59.5 0.4 collective-permute-done.7.refs_1_
  59.8 0.9 residuals.3
  60.7 0.2 collective-permute-start.9
  61.0 1.5 %collective-permute-start.10 = (bf16[256,384]{1,0:T(8,128)(2,1)S(1)}, bf16[256,384]{1,0:T(8,128)(2,1)S(1)}, u32[]{:S(2)}, u32[]{:S(2)}) collective-permute-start(bf16[256,384]{1,0:T(8,128)(2,1)S(1)} %get-tuple-element.97.refs_4_), channel_id=1, source_target_pairs={{0,8},{4,12},{8,0},{12,4},{1,9},{5,13},{9,1},{13,5},{2,10},{6,14},... | collective-permute-start | bytes 589832 | tf_op jit(solution)/shard_map/ppermute | solution.py:439
  62.5 1.7 %owned_features.9 = (bf16[384,2048]{1,0:T(8,128)(2,1)S(1)}, f32[8,128]{1,0:T(8,128)S(1)}) custom-call(bf16[1024,256]{1,0:T(8,128)(2,1)S(1)} %collective-permute-done.2.chosen, bf16[256,2048]{1,0:T(8,128)(2,1)S(1)} %get-tuple-element.74.omega, f32[1,2048]{1,0:T(1,128)S(1)} %get-tuple-element.75.turns, f32[8,128]{1,0:T(8,128)S(1)} %get-tuple-element.91.refs_0_), custom_call_target="tpu_custom_call" | custom-call | flops 1000000000 | bytes 1024 | tf_op jit(solution)/shard_map/owned_features/pallas_call | solution.py:219
  64.1 1.9 %owned_features.10 = (bf16[384,2048]{1,0:T(8,128)(2,1)S(1)}, f32[8,128]{1,0:T(8,128)S(1)}) custom-call(bf16[1024,256]{1,0:T(8,128)(2,1)S(1)} %collective-permute-done.5.chosen, bf16[256,2048]{1,0:T(8,128)(2,1)S(1)} %get-tuple-element.74.omega, f32[1,2048]{1,0:T(1,128)S(1)} %get-tuple-element.75.turns, f32[8,128]{1,0:T(8,128)S(1)} %get-tuple-element.93.refs_0_), custom_call_target="tpu_custom_call" | custom-call | flops 1000000000 | bytes 1024 | tf_op jit(solution)/shard_map/owned_features/pallas_call | solution.py:219
  66.0 0.0 copy-start
  66.0 1.6 %owned_features.11 = (bf16[384,2048]{1,0:T(8,128)(2,1)S(1)}, f32[8,128]{1,0:T(8,128)S(1)}) custom-call(bf16[1024,256]{1,0:T(8,128)(2,1)S(1)} %collective-permute-done.8.chosen, bf16[256,2048]{1,0:T(8,128)(2,1)S(1)} %get-tuple-element.74.omega, f32[1,2048]{1,0:T(1,128)S(1)} %get-tuple-element.75.turns, f32[8,128]{1,0:T(8,128)S(1)} %get-tuple-element.95.refs_0_), custom_call_target="tpu_custom_call" | custom-call | flops 1000000000 | bytes 1024 | tf_op jit(solution)/shard_map/owned_features/pallas_call | solution.py:219
  67.7 0.5 collective-permute-done.10.refs_6_
  68.1 0.0 collective-permute-start.11
  68.1 0.0 collective-permute-done.12.refs_5_
  68.1 0.0 collective-permute-done.14.refs_7_
  68.2 0.0 copy-start.1
  68.2 0.0 copy-start.2
  68.2 0.0 copy-start.3
  68.2 3.6 %first_part.1 = (f32[2048,256]{1,0:T(8,128)S(1)}, f32[8,128]{1,0:T(8,128)S(1)}) custom-call(bf16[640,2048]{1,0:T(8,128)(2,1)S(1)} %get-tuple-element.98.refs_0_, bf16[640,2048]{1,0:T(8,128)(2,1)S(1)} %get-tuple-element.99.refs_1_, bf16[640,2048]{1,0:T(8,128)(2,1)S(1)} %get-tuple-element.100.refs_2_, bf16[640,2048]{1,0:T(8,128)(2,1)S(1)} %get-tuple-element.101.refs_3_, ...), custom_call_target="tpu_custom_call" | custom-call | flops 5000000000 | bytes 1024 | tf_op jit(solution)/shard_map/first_part/pallas_call | solution.py:339
  71.8 0.0 collective-permute-done.9.refs_5_
  71.8 0.0 collective-permute-done.11.refs_7_
  71.9 1.7 %update.3 = (f32[1,2048,256]{2,1,0:T(8,128)}, f32[1,2048,256]{2,1,0:T(8,128)}, f32[1,2048,256]{2,1,0:T(8,128)}, bf16[256,256]{1,0:T(8,128)(2,1)S(1)}) custom-call(bf16[384,2048]{1,0:T(8,128)(2,1)S(1)} %get-tuple-element.90.refs_0_, bf16[384,2048]{1,0:T(8,128)(2,1)S(1)} %get-tuple-element.92.refs_1_, bf16[384,2048]{1,0:T(8,128)(2,1)S(1)} %get-tuple-element.94.refs_2_, ...), custom_call_target="tpu_custom_call" | custom-call | flops 1000000000 | bytes 1024 | tf_op jit(solution)/shard_map/update/pallas_call | solution.py:387
  73.5 1.6 %collective-permute-start.15 = (bf16[256,256]{1,0:T(8,128)(2,1)S(1)}, bf16[256,256]{1,0:T(8,128)(2,1)S(1)}, u32[]{:S(2)}, u32[]{:S(2)}) collective-permute-start(bf16[256,256]{1,0:T(8,128)(2,1)S(1)} %get-tuple-element.116.refs_0_), channel_id=1, source_target_pairs={{0,8},{4,12},{8,0},{12,4},{1,9},{5,13},{9,1},{13,5},{2,10},{6,14},... | collective-permute-start | bytes 393224 | tf_op jit(solution)/shard_map/ppermute | solution.py:439
  75.1 3.3 %update.4 = (f32[1,2048,256]{2,1,0:T(8,128)}, f32[1,2048,256]{2,1,0:T(8,128)}, f32[1,2048,256]{2,1,0:T(8,128)}, bf16[768,256]{1,0:T(8,128)(2,1)S(1)}) custom-call(bf16[384,2048]{1,0:T(8,128)(2,1)S(1)} %get-tuple-element.90.refs_0_, bf16[384,2048]{1,0:T(8,128)(2,1)S(1)} %get-tuple-element.92.refs_1_, ...), custom_call_target="tpu_custom_call", output_to_operand_aliasing={{0}: (13, {}), {1}: (14, {}), {2}: (15, {})} | custom-call | flops 1000000000 | bytes 1024 | tf_op jit(solution)/shard_map/update/pallas_call | solution.py:387
  78.5 1.0 collective-permute-done.15.refs_2_
  79.4 1.6 %collective-permute-start.21 = (bf16[768,256]{1,0:T(8,128)(2,1)S(1)}, bf16[768,256]{1,0:T(8,128)(2,1)S(1)}, u32[]{:S(2)}, u32[]{:S(2)}) collective-permute-start(bf16[768,256]{1,0:T(8,128)(2,1)S(1)} %get-tuple-element.119.refs_4_), channel_id=1, source_target_pairs={{0,8},{4,12},{8,0},{12,4},{1,9},{5,13},{9,1},{13,5},{2,10},{6,14},... | collective-permute-start | bytes 1179656 | tf_op jit(solution)/shard_map/ppermute | solution.py:439
  81.0 4.2 %update.5 = (f32[1,2048,256]{2,1,0:T(8,128)}, f32[1,2048,256]{2,1,0:T(8,128)}, f32[1,2048,256]{2,1,0:T(8,128)}, bf16[1024,256]{1,0:T(8,128)(2,1)S(1)}) custom-call(bf16[384,2048]{1,0:T(8,128)(2,1)S(1)} %get-tuple-element.90.refs_0_, bf16[384,2048]{1,0:T(8,128)(2,1)S(1)} %get-tuple-element.92.refs_1_, ...), custom_call_target="tpu_custom_call", output_to_operand_aliasing={{0}: (13, {}), {1}: (14, {}), {2}: (15, {})} | custom-call | flops 1000000000 | bytes 1024 | tf_op jit(solution)/shard_map/update/pallas_call | solution.py:387
  85.2 0.4 collective-permute-start.17
  85.6 0.0 collective-permute-start.20
  85.6 5.8 %collective-permute-done.21.refs_6_ = bf16[768,256]{1,0:T(8,128)(2,1)S(1)} collective-permute-done((bf16[768,256]{1,0:T(8,128)(2,1)S(1)}, bf16[768,256]{1,0:T(8,128)(2,1)S(1)}, u32[]{:S(2)}, u32[]{:S(2)}) %collective-permute-start.21) | collective-permute-done | bytes 393248 | tf_op jit(solution)/shard_map/ppermute | solution.py:439
  91.5 0.0 collective-permute-start.22
  91.5 0.5 collective-permute-start.18
  92.0 0.0 collective-permute-start.19
  92.0 1.4 %collective-permute-done.18.refs_1_ = bf16[256,256]{1,0:T(8,128)(2,1)S(1)} collective-permute-done((bf16[256,256]{1,0:T(8,128)(2,1)S(1)}, bf16[256,256]{1,0:T(8,128)(2,1)S(1)}, u32[]{:S(2)}, u32[]{:S(2)}) %collective-permute-start.18) | collective-permute-done | bytes 131104 | tf_op jit(solution)/shard_map/ppermute | solution.py:443
  93.4 0.1 collective-permute-start.16
  93.5 0.0 collective-permute-done.19.refs_3_
  93.6 0.0 collective-permute-done.20.refs_5_
  93.6 1.4 %put_rows.2.refs_4_ = bf16[8192,256]{1,0:T(8,128)(2,1)} custom-call(s32[1]{0:T(128)} %bitcast.1.refs_1_.p, bf16[256,256]{1,0:T(8,128)(2,1)S(1)} %get-tuple-element.116.refs_0_, bf16[256,256]{1,0:T(8,128)(2,1)S(1)} %collective-permute-done.18.refs_1_, bf16[256,256]{1,0:T(8,128)(2,1)S(1)} %collective-permute-done.15.refs_2_, ...), custom_call_target="tpu_custom_call" | custom-call | flops 10000000 | bytes 1024 | tf_op jit(solution)/shard_map/put_rows/pallas_call | solution.py:421
  95.0 6.5 %collective-permute-done.17.refs_2_ = bf16[1024,256]{1,0:T(8,128)(2,1)S(1)} collective-permute-done((bf16[1024,256]{1,0:T(8,128)(2,1)S(1)}, bf16[1024,256]{1,0:T(8,128)(2,1)S(1)}, u32[]{:S(2)}, u32[]{:S(2)}) %collective-permute-start.17) | collective-permute-done | bytes 524320 | tf_op jit(solution)/shard_map/ppermute | solution.py:439
  101.4 1.9 %collective-permute-done.23.refs_3_ = bf16[1024,256]{1,0:T(8,128)(2,1)S(1)} collective-permute-done((bf16[1024,256]{1,0:T(8,128)(2,1)S(1)}, bf16[1024,256]{1,0:T(8,128)(2,1)S(1)}, u32[]{:S(2)}, u32[]{:S(2)}) %collective-permute-start.23) | collective-permute-done | bytes 524320 | tf_op jit(solution)/shard_map/ppermute | solution.py:443
  103.3 1.3 %put_rows.3 = bf16[8192,256]{1,0:T(8,128)(2,1)} custom-call(s32[1]{0:T(128)} %bitcast.1.refs_1_.p, bf16[1024,256]{1,0:T(8,128)(2,1)S(1)} %get-tuple-element.117.refs_0_, bf16[1024,256]{1,0:T(8,128)(2,1)S(1)} %collective-permute-done.16.refs_1_, bf16[1024,256]{1,0:T(8,128)(2,1)S(1)} %collective-permute-done.17.refs_2_, ...), custom_call_target="tpu_custom_call", output_to_operand_aliasing={{}: (5, {})} | custom-call | flops 10000000 | bytes 1024 | tf_op jit(solution)/shard_map/put_rows/pallas_call | solution.py:421
  (16 shorter events, 0.2 us)
Async XLA Ops:
  3.4 37.3 %collective-permute-start.2 = (bf16[1024,256]{1,0:T(8,128)(2,1)S(1)}, bf16[1024,256]{1,0:T(8,128)(2,1)S(1)}, u32[]{:S(2)}, u32[]{:S(2)}) collective-permute-start(bf16[1024,256]{1,0:T(8,128)(2,1)S(1)} %get-tuple-element.64.refs_2_), channel_id=1, source_target_pairs={{0,4},{4,0},{8,12},{12,8},{1,5},{5,1},{9,13},{13,9},{2,6},{6,2},{1... | collective-permute-start | bytes 1572872 | tf_op jit(solution)/shard_map/ppermute | solution.py:443
  3.9 36.7 %collective-permute-start.5 = (bf16[1024,256]{1,0:T(8,128)(2,1)S(1)}, bf16[1024,256]{1,0:T(8,128)(2,1)S(1)}, u32[]{:S(2)}, u32[]{:S(2)}) collective-permute-start(bf16[1024,256]{1,0:T(8,128)(2,1)S(1)} %get-tuple-element.64.refs_2_), channel_id=1, source_target_pairs={{0,8},{4,12},{8,0},{12,4},{1,9},{5,13},{9,1},{13,5},{2,10},{6,14},... | collective-permute-start | bytes 1572872 | tf_op jit(solution)/shard_map/ppermute | solution.py:439
  20.8 7.4 %collective-permute-start = (bf16[320,256]{1,0:T(8,128)(2,1)S(1)}, bf16[320,256]{1,0:T(8,128)(2,1)S(1)}, u32[]{:S(2)}, u32[]{:S(2)}) collective-permute-start(bf16[320,256]{1,0:T(8,128)(2,1)S(1)} %get-tuple-element.69), channel_id=1, source_target_pairs={{0,1},{1,0},{2,3},{3,2},{4,5},{5,4},{6,7},{7,6},{8,9},{9,8},{10,11... | collective-permute-start | bytes 491528 | tf_op jit(solution)/shard_map/ppermute | solution.py:451
  28.2 10.4 %collective-permute-start.3 = (bf16[320,256]{1,0:T(8,128)(2,1)S(1)}, bf16[320,256]{1,0:T(8,128)(2,1)S(1)}, u32[]{:S(2)}, u32[]{:S(2)}) collective-permute-start(bf16[320,256]{1,0:T(8,128)(2,1)S(1)} %get-tuple-element.76.a), channel_id=1, source_target_pairs={{0,2},{1,3},{2,0},{3,1},{4,6},{5,7},{6,4},{7,5},{8,10},{9,11},{10,... | collective-permute-start | bytes 491528 | tf_op jit(solution)/shard_map/ppermute | solution.py:451
  38.6 8.3 %collective-permute-start.6 = (bf16[320,256]{1,0:T(8,128)(2,1)S(1)}, bf16[320,256]{1,0:T(8,128)(2,1)S(1)}, u32[]{:S(2)}, u32[]{:S(2)}) collective-permute-start(bf16[320,256]{1,0:T(8,128)(2,1)S(1)} %get-tuple-element.81.refs_0_), channel_id=1, source_target_pairs={{0,1},{1,0},{2,3},{3,2},{4,5},{5,4},{6,7},{7,6},{8,9},{9,8},{10,11... | collective-permute-start | bytes 491528 | tf_op jit(solution)/shard_map/ppermute | solution.py:451
  38.7 8.2 %collective-permute-start.1 = (bf16[192,256]{1,0:T(8,128)(2,1)S(1)}, bf16[192,256]{1,0:T(8,128)(2,1)S(1)}, u32[]{:S(2)}, u32[]{:S(2)}) collective-permute-start(bf16[192,256]{1,0:T(8,128)(2,1)S(1)} %get-tuple-element.73), channel_id=1, source_target_pairs={{0,1},{1,0},{2,3},{3,2},{4,5},{5,4},{6,7},{7,6},{8,9},{9,8},{10,11... | collective-permute-start | bytes 294920 | tf_op jit(solution)/shard_map/ppermute | solution.py:451
  40.7 16.2 %collective-permute-start.8 = (bf16[1024,256]{1,0:T(8,128)(2,1)S(1)}, bf16[1024,256]{1,0:T(8,128)(2,1)S(1)}, u32[]{:S(2)}, u32[]{:S(2)}) collective-permute-start(bf16[1024,256]{1,0:T(8,128)(2,1)S(1)} %collective-permute-done.5.chosen), channel_id=1, source_target_pairs={{0,4},{4,0},{8,12},{12,8},{1,5},{5,1},{9,13},{13,9},{2,6},{6,2},{1... | collective-permute-start | bytes 1572872 | tf_op jit(solution)/shard_map/ppermute | solution.py:443
  40.7 6.2 %copy-start.4 = (s32[2,512,256]{2,1,0:T(8,128)S(1)}, s32[2,512,256]{2,1,0:T(8,128)}, u32[]{:S(2)}) copy-start(s32[2,512,256]{2,1,0:T(8,128)} %param.15) | copy-start | bytes 3145732
  48.0 8.9 %collective-permute-start.13 = (bf16[256,640]{1,0:T(8,128)(2,1)S(1)}, bf16[256,640]{1,0:T(8,128)(2,1)S(1)}, u32[]{:S(2)}, u32[]{:S(2)}) collective-permute-start(bf16[256,640]{1,0:T(8,128)(2,1)S(1)} %get-tuple-element.102.refs_4_), channel_id=1, source_target_pairs={{0,8},{4,12},{8,0},{12,4},{1,9},{5,13},{9,1},{13,5},{2,10},{6,14},... | collective-permute-start | bytes 983048 | tf_op jit(solution)/shard_map/ppermute | solution.py:439
  48.5 6.6 %collective-permute-start.4 = (bf16[192,256]{1,0:T(8,128)(2,1)S(1)}, bf16[192,256]{1,0:T(8,128)(2,1)S(1)}, u32[]{:S(2)}, u32[]{:S(2)}) collective-permute-start(bf16[192,256]{1,0:T(8,128)(2,1)S(1)} %get-tuple-element.80.a), channel_id=1, source_target_pairs={{0,2},{1,3},{2,0},{3,1},{4,6},{5,7},{6,4},{7,5},{8,10},{9,11},{10,... | collective-permute-start | bytes 294920 | tf_op jit(solution)/shard_map/ppermute | solution.py:451
  55.2 4.7 %collective-permute-start.7 = (bf16[192,256]{1,0:T(8,128)(2,1)S(1)}, bf16[192,256]{1,0:T(8,128)(2,1)S(1)}, u32[]{:S(2)}, u32[]{:S(2)}) collective-permute-start(bf16[192,256]{1,0:T(8,128)(2,1)S(1)} %get-tuple-element.85.refs_0_), channel_id=1, source_target_pairs={{0,1},{1,0},{2,3},{3,2},{4,5},{5,4},{6,7},{7,6},{8,9},{9,8},{10,11... | collective-permute-start | bytes 294920 | tf_op jit(solution)/shard_map/ppermute | solution.py:451
  55.2 12.9 %collective-permute-start.12 = (bf16[256,640]{1,0:T(8,128)(2,1)S(1)}, bf16[256,640]{1,0:T(8,128)(2,1)S(1)}, u32[]{:S(2)}, u32[]{:S(2)}) collective-permute-start(bf16[256,640]{1,0:T(8,128)(2,1)S(1)} %get-tuple-element.102.refs_4_), channel_id=1, source_target_pairs={{0,4},{4,0},{8,12},{12,8},{1,5},{5,1},{9,13},{13,9},{2,6},{6,2},{1... | collective-permute-start | bytes 983048 | tf_op jit(solution)/shard_map/ppermute | solution.py:443
  56.9 11.3 %collective-permute-start.14 = (bf16[256,640]{1,0:T(8,128)(2,1)S(1)}, bf16[256,640]{1,0:T(8,128)(2,1)S(1)}, u32[]{:S(2)}, u32[]{:S(2)}) collective-permute-start(bf16[256,640]{1,0:T(8,128)(2,1)S(1)} %collective-permute-done.13.refs_6_), channel_id=1, source_target_pairs={{0,4},{4,0},{8,12},{12,8},{1,5},{5,1},{9,13},{13,9},{2,6},{6,2},{1... | collective-permute-start | bytes 983048 | tf_op jit(solution)/shard_map/ppermute | solution.py:443
  60.7 11.1 %collective-permute-start.9 = (bf16[256,384]{1,0:T(8,128)(2,1)S(1)}, bf16[256,384]{1,0:T(8,128)(2,1)S(1)}, u32[]{:S(2)}, u32[]{:S(2)}) collective-permute-start(bf16[256,384]{1,0:T(8,128)(2,1)S(1)} %get-tuple-element.97.refs_4_), channel_id=1, source_target_pairs={{0,4},{4,0},{8,12},{12,8},{1,5},{5,1},{9,13},{13,9},{2,6},{6,2},{1... | collective-permute-start | bytes 589832 | tf_op jit(solution)/shard_map/ppermute | solution.py:443
  61.0 7.1 %collective-permute-start.10 = (bf16[256,384]{1,0:T(8,128)(2,1)S(1)}, bf16[256,384]{1,0:T(8,128)(2,1)S(1)}, u32[]{:S(2)}, u32[]{:S(2)}) collective-permute-start(bf16[256,384]{1,0:T(8,128)(2,1)S(1)} %get-tuple-element.97.refs_4_), channel_id=1, source_target_pairs={{0,8},{4,12},{8,0},{12,4},{1,9},{5,13},{9,1},{13,5},{2,10},{6,14},... | collective-permute-start | bytes 589832 | tf_op jit(solution)/shard_map/ppermute | solution.py:439
  66.0 2.1 %copy-start = (f32[1,2048,256]{2,1,0:T(8,128)S(1)}, f32[1,2048,256]{2,1,0:T(8,128)}, u32[]{:S(2)}) copy-start(f32[1,2048,256]{2,1,0:T(8,128)} %refs_10_.5) | copy-start | bytes 6291460
  68.1 3.7 %collective-permute-start.11 = (bf16[256,384]{1,0:T(8,128)(2,1)S(1)}, bf16[256,384]{1,0:T(8,128)(2,1)S(1)}, u32[]{:S(2)}, u32[]{:S(2)}) collective-permute-start(bf16[256,384]{1,0:T(8,128)(2,1)S(1)} %collective-permute-done.10.refs_6_), channel_id=1, source_target_pairs={{0,4},{4,0},{8,12},{12,8},{1,5},{5,1},{9,13},{13,9},{2,6},{6,2},{1... | collective-permute-start | bytes 589832 | tf_op jit(solution)/shard_map/ppermute | solution.py:443
  68.2 3.7 %copy-start.1 = (f32[1,2048,256]{2,1,0:T(8,128)S(1)}, f32[1,2048,256]{2,1,0:T(8,128)}, u32[]{:S(2)}) copy-start(f32[1,2048,256]{2,1,0:T(8,128)} %refs_11_.5) | copy-start | bytes 6291460
  68.2 3.7 %copy-start.2 = (f32[1,2048,256]{2,1,0:T(8,128)S(1)}, f32[1,2048,256]{2,1,0:T(8,128)}, u32[]{:S(2)}) copy-start(f32[1,2048,256]{2,1,0:T(8,128)} %refs_12_.5) | copy-start | bytes 6291460
  68.2 3.7 %copy-start.3 = (bf16[256,256]{1,0:T(8,128)(2,1)S(1)}, bf16[256,256]{1,0:T(8,128)(2,1)}, u32[]{:S(2)}) copy-start(bf16[256,256]{1,0:T(8,128)(2,1)} %refs_9_.5) | copy-start | bytes 393220
  73.5 5.9 %collective-permute-start.15 = (bf16[256,256]{1,0:T(8,128)(2,1)S(1)}, bf16[256,256]{1,0:T(8,128)(2,1)S(1)}, u32[]{:S(2)}, u32[]{:S(2)}) collective-permute-start(bf16[256,256]{1,0:T(8,128)(2,1)S(1)} %get-tuple-element.116.refs_0_), channel_id=1, source_target_pairs={{0,8},{4,12},{8,0},{12,4},{1,9},{5,13},{9,1},{13,5},{2,10},{6,14},... | collective-permute-start | bytes 393224 | tf_op jit(solution)/shard_map/ppermute | solution.py:439
  79.4 12.0 %collective-permute-start.21 = (bf16[768,256]{1,0:T(8,128)(2,1)S(1)}, bf16[768,256]{1,0:T(8,128)(2,1)S(1)}, u32[]{:S(2)}, u32[]{:S(2)}) collective-permute-start(bf16[768,256]{1,0:T(8,128)(2,1)S(1)} %get-tuple-element.119.refs_4_), channel_id=1, source_target_pairs={{0,8},{4,12},{8,0},{12,4},{1,9},{5,13},{9,1},{13,5},{2,10},{6,14},... | collective-permute-start | bytes 1179656 | tf_op jit(solution)/shard_map/ppermute | solution.py:439
  85.2 16.2 %collective-permute-start.17 = (bf16[1024,256]{1,0:T(8,128)(2,1)S(1)}, bf16[1024,256]{1,0:T(8,128)(2,1)S(1)}, u32[]{:S(2)}, u32[]{:S(2)}) collective-permute-start(bf16[1024,256]{1,0:T(8,128)(2,1)S(1)} %get-tuple-element.117.refs_0_), channel_id=1, source_target_pairs={{0,8},{4,12},{8,0},{12,4},{1,9},{5,13},{9,1},{13,5},{2,10},{6,14},... | collective-permute-start | bytes 1572872 | tf_op jit(solution)/shard_map/ppermute | solution.py:439
  85.6 7.9 %collective-permute-start.20 = (bf16[768,256]{1,0:T(8,128)(2,1)S(1)}, bf16[768,256]{1,0:T(8,128)(2,1)S(1)}, u32[]{:S(2)}, u32[]{:S(2)}) collective-permute-start(bf16[768,256]{1,0:T(8,128)(2,1)S(1)} %get-tuple-element.119.refs_4_), channel_id=1, source_target_pairs={{0,4},{4,0},{8,12},{12,8},{1,5},{5,1},{9,13},{13,9},{2,6},{6,2},{1... | collective-permute-start | bytes 1179656 | tf_op jit(solution)/shard_map/ppermute | solution.py:443
  91.5 2.1 %collective-permute-start.22 = (bf16[768,256]{1,0:T(8,128)(2,1)S(1)}, bf16[768,256]{1,0:T(8,128)(2,1)S(1)}, u32[]{:S(2)}, u32[]{:S(2)}) collective-permute-start(bf16[768,256]{1,0:T(8,128)(2,1)S(1)} %collective-permute-done.21.refs_6_), channel_id=1, source_target_pairs={{0,4},{4,0},{8,12},{12,8},{1,5},{5,1},{9,13},{13,9},{2,6},{6,2},{1... | collective-permute-start | bytes 1179656 | tf_op jit(solution)/shard_map/ppermute | solution.py:443
  91.5 1.9 %collective-permute-start.18 = (bf16[256,256]{1,0:T(8,128)(2,1)S(1)}, bf16[256,256]{1,0:T(8,128)(2,1)S(1)}, u32[]{:S(2)}, u32[]{:S(2)}) collective-permute-start(bf16[256,256]{1,0:T(8,128)(2,1)S(1)} %get-tuple-element.116.refs_0_), channel_id=1, source_target_pairs={{0,4},{4,0},{8,12},{12,8},{1,5},{5,1},{9,13},{13,9},{2,6},{6,2},{1... | collective-permute-start | bytes 393224 | tf_op jit(solution)/shard_map/ppermute | solution.py:443
  92.0 1.6 %collective-permute-start.19 = (bf16[256,256]{1,0:T(8,128)(2,1)S(1)}, bf16[256,256]{1,0:T(8,128)(2,1)S(1)}, u32[]{:S(2)}, u32[]{:S(2)}) collective-permute-start(bf16[256,256]{1,0:T(8,128)(2,1)S(1)} %collective-permute-done.15.refs_2_), channel_id=1, source_target_pairs={{0,4},{4,0},{8,12},{12,8},{1,5},{5,1},{9,13},{13,9},{2,6},{6,2},{1... | collective-permute-start | bytes 393224 | tf_op jit(solution)/shard_map/ppermute | solution.py:443
  93.4 8.1 %collective-permute-start.16 = (bf16[1024,256]{1,0:T(8,128)(2,1)S(1)}, bf16[1024,256]{1,0:T(8,128)(2,1)S(1)}, u32[]{:S(2)}, u32[]{:S(2)}) collective-permute-start(bf16[1024,256]{1,0:T(8,128)(2,1)S(1)} %get-tuple-element.117.refs_0_), channel_id=1, source_target_pairs={{0,4},{4,0},{8,12},{12,8},{1,5},{5,1},{9,13},{13,9},{2,6},{6,2},{1... | collective-permute-start | bytes 1572872 | tf_op jit(solution)/shard_map/ppermute | solution.py:443
  101.4 1.9 %collective-permute-start.23 = (bf16[1024,256]{1,0:T(8,128)(2,1)S(1)}, bf16[1024,256]{1,0:T(8,128)(2,1)S(1)}, u32[]{:S(2)}, u32[]{:S(2)}) collective-permute-start(bf16[1024,256]{1,0:T(8,128)(2,1)S(1)} %collective-permute-done.17.refs_2_), channel_id=1, source_target_pairs={{0,4},{4,0},{8,12},{12,8},{1,5},{5,1},{9,13},{13,9},{2,6},{6,2},{1... | collective-permute-start | bytes 1572872 | tf_op jit(solution)/shard_map/ppermute | solution.py:443

commit v7 on v6

--- a/solution.py
+++ b/solution.py
@@ -214,7 +214,7 @@
     cosines(chosen[start : start + size, :], omega, turns, omega.shape[1], store)
 
 
-def owned_features(chosen, omega, turns, start, size, deps):
+def owned_features(chosen, omega, turns, start, size, weight, deps):
     owned = omega.shape[1]
     return pl.pallas_call(
         functools.partial(features_kernel, start, size),
@@ -222,7 +222,7 @@
         out_specs=[IN_VMEM, ANYWHERE],
         out_shape=[jax.ShapeDtypeStruct((size, owned), bf16), TOKEN],
         compiler_params=params(),
-        cost_estimate=cost(1),
+        cost_estimate=cost(weight),
         name="owned_features",
     )(chosen, omega, turns, *deps)
 
@@ -342,7 +342,7 @@
         out_specs=[IN_VMEM, ANYWHERE],
         out_shape=[jax.ShapeDtypeStruct((owned, k), f32), TOKEN],
         compiler_params=params(),
-        cost_estimate=cost(5),
+        cost_estimate=cost(0.3),
         name="first_part",
     )(*features, *residual, master, *deps)
 
@@ -393,7 +393,7 @@
         + [jax.ShapeDtypeStruct((steps * rows, k), bf16)],
         input_output_aliases=aliases,
         compiler_params=params(),
-        cost_estimate=cost(1),
+        cost_estimate=cost(4),
         name="update",
     )(*args)
 
@@ -504,45 +504,48 @@
     todo = [(m, j) for m in range(2) for j in range(1, n_pts)]
     share = len(todo) // 6
 
-    def some(token, pieces):
+    def some(token, pieces, weight=1.0):
         for _ in range(pieces * share):
             m, j = todo.pop(0)
             feats, token = owned_features(
-                everyone[j], own_omega, own_turns, *parts[m], [token]
+                everyone[j], own_omega, own_turns, *parts[m], weight, [token]
             )
             features[m].append(feats)
         return token
 
+    token = some(token, 1)
+    for bit in range(1, bits):
+        kept_one, got_one, token = add_up(kept_one, got_one, bit, token)
     chunk, token = total(f, kept_zero, got_zero, 0, False, [token])
     rows_zero, masks = give_back(chunk)
     token = some(token, 1)
-    for bit in range(1, bits):
-        kept_one, got_one, token = add_up(kept_one, got_one, bit, token)
-    out_rates, res, token = residuals(f, rows_zero, masks, counts, *parts[0], None, [token])
-    res_zero = spread(res, n_pts)
-    token = some(token, 1)
     chunk, token = total(f, kept_one, got_one, 0, False, [token])
     rows_one, masks = give_back(chunk)
+    out_rates, res_zero, token = residuals(f, rows_zero, masks, counts, *parts[0], None, [token])
+    far_zero = [across(res_zero, n_pts, d) for d in range(1, n_pts // CORES)]
     token = some(token, 1)
-    out_rates, res, token = residuals(
+    out_rates, res_one, token = residuals(
         f, rows_one, masks, counts, *parts[1], out_rates, [token]
     )
-    res_one = spread(res, n_pts)
-    token = some(token, 3)
+    far_one = [across(res_one, n_pts, d) for d in range(1, n_pts // CORES)]
+    token = some(token, 2, 0.1)
+    *far_zero, token = lax.optimization_barrier((*far_zero, token))
+    res_zero = [y for g in [res_zero] + far_zero for y in (g, mate(g, n_pts))]
+    token = some(token, 1, 0.1)
+    *far_one, token = lax.optimization_barrier((*far_one, token))
+    res_one = [y for g in [res_one] + far_one for y in (g, mate(g, n_pts))]
     begun, token = first_part(features[0], res_zero, master, [token])
 
     steps = max(1, owned // 256)
-    sizes = [1, 3, 4] if steps == 8 else [1] * steps
+    sizes = [1, 2, 2, 3] if steps == 8 else [1] * steps
     chips = n_pts // CORES
     state = None
     at = 0
     sent, come, starts = [], [], []
     for c, size in enumerate(sizes):
         *state, rows = update(
-            features[1], res_one, begun, cov, master, first, second, at, size, state, [token]
+            features[1], res_one, begun, cov, master, first, second, at, size, state, [token] + (come[c - 2] if c > 1 else [])
         )
-        if c and chips > 1:
-            rows, _ = lax.optimization_barrier((rows, come[max(0, c - 2)][0]))
         sent.append([rows, mate(rows, n_pts)])
         come.append([across(rows, n_pts, d) for d in range(1, chips)])
         starts.append(at * (owned // steps))

time: 105 us -> 98 us (0.933)
  waiting for transfers between devices: 28.5 us -> 16.2 us
  starting transfers between devices: 16.6 us -> 21 us
    ppermute x6, waiting for transfers between devices: 9.8 us -> 3.43 us  [swap(): return lax.ppermute(x, 'feat', [(i, i ^ 2 ** bit) for i in range(n)])]
    ppermute x6 -> x7, waiting for transfers between devices: 15.3 us -> 9.54 us  [ring(): return lax.ppermute(x, axis, [(i, (i + distance) % n) for i in range(n)])]
    ppermute x6, starting transfers between devices: 6.88 us -> 9.76 us  [swap(): return lax.ppermute(x, 'feat', [(i, i ^ 2 ** bit) for i in range(n)])]
    ppermute x12 -> x14, starting transfers between devices: 1.49 us -> 2.48 us  [mate(): return lax.ppermute(x, 'pts', [(i, i ^ 1) for i in range(n)])]
    pallas_call x3 -> x4, Pallas kernels: 9.14 us -> 9.97 us  [update(): pl.pallas_call(functools.partial(update_kernel, n, at), grid=(steps,), in...]
    ppermute x6 -> x7, starting transfers between devices: 8.2 us -> 8.8 us  [ring(): return lax.ppermute(x, axis, [(i, (i + distance) % n) for i in range(n)])]
    ppermute x12 -> x14, waiting for transfers between devices: 3.37 us -> 3.23 us  [mate(): return lax.ppermute(x, 'pts', [(i, i ^ 1) for i in range(n)])]
  transfers between devices with their start and end apart: 24 -> 27, of which waited for: 11 -> 13; matrix products, arithmetic and copies ran while one was open for 0% -> 0% of each run, Pallas kernels for 50% -> 55%
where the time goes in v7:
time: 98 us; the launch traced here: 97.8 us
  Pallas kernels  59.5 us (61%)
  starting transfers between devices  21 us (21%)
  waiting for transfers between devices  16.2 us (17%)
  between operations  1.05 us (1%)
    pallas_call x3, Pallas kernels, rates(): pl.pallas_call(kernel, grid_spec=pltpu.PrefetchScalarGridSpec(num_scalar_...  25.3 us
    pallas_call x6, Pallas kernels, owned_features(): pl.pallas_call(functools.partial(features_kernel, start, size), in_specs=...  13 us
    pallas_call x4, Pallas kernels, update(): pl.pallas_call(functools.partial(update_kernel, n, at), grid=(steps,), in...  9.97 us
    ppermute x6, starting transfers between devices, swap(): return lax.ppermute(x, 'feat', [(i, i ^ 2 ** bit) for i in range(n)])  9.76 us
    ppermute x7, waiting for transfers between devices, ring(): return lax.ppermute(x, axis, [(i, (i + distance) % n) for i in range(n)])  9.54 us
    ppermute x7, starting transfers between devices, ring(): return lax.ppermute(x, axis, [(i, (i + distance) % n) for i in range(n)])  8.8 us
    pallas_call x1, Pallas kernels, first_part(): pl.pallas_call(functools.partial(first_part_kernel, n), in_specs=[IN_VMEM...  3.61 us
    ppermute x6, waiting for transfers between devices, swap(): return lax.ppermute(x, 'feat', [(i, i ^ 2 ** bit) for i in range(n)])  3.43 us
  transfers between devices with their start and end apart: 27, of which 13 were waited for; matrix products, arithmetic and copies ran while one was open for 0% of the time, Pallas kernels for 55%

profile of v7, /device:TPU:0, one launch (start us, length us, event | category | flops | bytes accessed | tf_op | source)
XLA Modules:
  0.0 97.8 jit_solution(13003140373676436611)
XLA Ops:
  0.6 2.8 %chosen_points.1 = (bf16[1024,256]{1,0:T(8,128)(2,1)S(1)}, f32[8,128]{1,0:T(8,128)S(1)}) custom-call(s32[2,512]{1,0:T(2,128)} %picks.1, bf16[2048,256]{1,0:T(8,128)(2,1)} %points.1), custom_call_target="tpu_custom_call" | custom-call | flops 3000000000 | bytes 1024 | tf_op jit(solution)/shard_map/chosen_points/pallas_call | solution.py:68
  3.4 0.5 collective-permute-start.2
  3.9 2.6 %collective-permute-start.4 = (bf16[1024,256]{1,0:T(8,128)(2,1)S(1)}, bf16[1024,256]{1,0:T(8,128)(2,1)S(1)}, u32[]{:S(2)}, u32[]{:S(2)}) collective-permute-start(bf16[1024,256]{1,0:T(8,128)(2,1)S(1)} %get-tuple-element.71.refs_2_), channel_id=1, source_target_pairs={{0,8},{4,12},{8,0},{12,4},{1,9},{5,13},{9,1},{13,5},{2,10},{6,14},... | collective-permute-start | bytes 1572872 | tf_op jit(solution)/shard_map/ppermute | solution.py:439
  6.5 14.2 %partial_log_rates.3 = (bf16[640,2048]{1,0:T(8,128)(2,1)S(1)}, bf16[256,2048]{1,0:T(8,128)(2,1)S(1)}, f32[1,2048]{1,0:T(1,128)S(1)}, f32[320,256]{1,0:T(8,128)S(...) custom-call(s32[1]{0:T(128)} %bitcast.refs_0_.f, s32[1]{0:T(128)} %bitcast.1.refs_1_.p, ...), custom_call_target="tpu_custom_call" | custom-call | flops 12000000000 | bytes 1024 | tf_op jit(solution)/shard_map/partial_log_rates/pallas_call | solution.py:185
  20.8 1.6 %collective-permute-start = (bf16[320,256]{1,0:T(8,128)(2,1)S(1)}, bf16[320,256]{1,0:T(8,128)(2,1)S(1)}, u32[]{:S(2)}, u32[]{:S(2)}) collective-permute-start(bf16[320,256]{1,0:T(8,128)(2,1)S(1)} %get-tuple-element.76), channel_id=1, source_target_pairs={{0,1},{1,0},{2,3},{3,2},{4,5},{5,4},{6,7},{7,6},{8,9},{9,8},{10,11... | collective-permute-start | bytes 491528 | tf_op jit(solution)/shard_map/ppermute | solution.py:451
  22.4 5.7 %partial_log_rates.4 = (bf16[384,2048]{1,0:T(8,128)(2,1)S(1)}, f32[384,256]{1,0:T(8,128)S(1)}, f32[8,128]{1,0:T(8,128)S(1)}) custom-call(s32[1]{0:T(128)} %bitcast.refs_0_.f, s32[1]{0:T(128)} %bitcast.1.refs_1_.p, bf16[1024,256]{1,0:T(8,128)(2,1)S(1)} %get-tuple-element.71.refs_2_, bf16[256,8192]{1,0:T(8,128)(2,1)} %refs_3_.5, f32[1,8192]{1,0:T(1,128)} %bitcast.8, ...), custom_call_target="tpu_custom_call" | custom-call | flops 6000000000 | bytes 1024 | tf_op jit(solution)/shard_map/partial_log_rates/pallas_call | solution.py:185
  28.1 0.0 collective-permute-done.b
  28.2 2.7 %collective-permute-start.5 = (bf16[320,256]{1,0:T(8,128)(2,1)S(1)}, bf16[320,256]{1,0:T(8,128)(2,1)S(1)}, u32[]{:S(2)}, u32[]{:S(2)}) collective-permute-start(bf16[320,256]{1,0:T(8,128)(2,1)S(1)} %get-tuple-element.86.a), channel_id=1, source_target_pairs={{0,2},{1,3},{2,0},{3,1},{4,6},{5,7},{6,4},{7,5},{8,10},{9,11},{10,... | collective-permute-start | bytes 491528 | tf_op jit(solution)/shard_map/ppermute | solution.py:451
  30.8 5.4 %partial_log_rates.5 = (f32[192,256]{1,0:T(8,128)S(1)}, bf16[192,256]{1,0:T(8,128)(2,1)S(1)}, f32[8,128]{1,0:T(8,128)S(1)}) custom-call(s32[1]{0:T(128)} %bitcast.refs_0_.f, s32[1]{0:T(128)} %bitcast.1.refs_1_.p, bf16[1024,256]{1,0:T(8,128)(2,1)S(1)} %get-tuple-element.71.refs_2_, bf16[256,8192]{1,0:T(8,128)(2,1)} %refs_3_.5, f32[1,8192]{1,0:T(1,128)} %bitcast.9, ...), custom_call_target="tpu_custom_call" | custom-call | flops 6000000000 | bytes 1024 | tf_op jit(solution)/shard_map/partial_log_rates/pallas_call | solution.py:185
  36.2 0.6 collective-permute-start.1
  36.8 0.0 collective-permute-done.2.chosen
  36.8 2.6 %owned_features.6 = (bf16[640,2048]{1,0:T(8,128)(2,1)S(1)}, f32[8,128]{1,0:T(8,128)S(1)}) custom-call(bf16[1024,256]{1,0:T(8,128)(2,1)S(1)} %collective-permute-done.2.chosen, bf16[256,2048]{1,0:T(8,128)(2,1)S(1)} %get-tuple-element.81.omega, f32[1,2048]{1,0:T(1,128)S(1)} %get-tuple-element.82.turns, f32[8,128]{1,0:T(8,128)S(1)} %get-tuple-element.83.refs_0_), custom_call_target="tpu_custom_call" | custom-call | flops 1000000000 | bytes 1024 | tf_op jit(solution)/shard_map/owned_features/pallas_call | solution.py:219
  39.5 1.5 %collective-permute-done.1.b = bf16[192,256]{1,0:T(8,128)(2,1)S(1)} collective-permute-done((bf16[192,256]{1,0:T(8,128)(2,1)S(1)}, bf16[192,256]{1,0:T(8,128)(2,1)S(1)}, u32[]{:S(2)}, u32[]{:S(2)}) %collective-permute-start.1) | collective-permute-done | bytes 98336 | tf_op jit(solution)/shard_map/ppermute | solution.py:451
  40.9 0.0 collective-permute-done.5.b
  41.0 0.6 collective-permute-start.8
  41.6 2.3 %collective-permute-start.3 = (bf16[192,256]{1,0:T(8,128)(2,1)S(1)}, bf16[192,256]{1,0:T(8,128)(2,1)S(1)}, u32[]{:S(2)}, u32[]{:S(2)}) collective-permute-start(bf16[192,256]{1,0:T(8,128)(2,1)S(1)} %get-tuple-element.85.a), channel_id=1, source_target_pairs={{0,2},{1,3},{2,0},{3,1},{4,6},{5,7},{6,4},{7,5},{8,10},{9,11},{10,... | collective-permute-start | bytes 294920 | tf_op jit(solution)/shard_map/ppermute | solution.py:451
  43.9 2.6 %owned_features.7 = (bf16[640,2048]{1,0:T(8,128)(2,1)S(1)}, f32[8,128]{1,0:T(8,128)S(1)}) custom-call(bf16[1024,256]{1,0:T(8,128)(2,1)S(1)} %collective-permute-done.4.chosen, bf16[256,2048]{1,0:T(8,128)(2,1)S(1)} %get-tuple-element.81.omega, f32[1,2048]{1,0:T(1,128)S(1)} %get-tuple-element.82.turns, f32[8,128]{1,0:T(8,128)S(1)} %get-tuple-element.88.refs_0_), custom_call_target="tpu_custom_call" | custom-call | flops 1000000000 | bytes 1024 | tf_op jit(solution)/shard_map/owned_features/pallas_call | solution.py:219
  46.5 0.8 collective-permute-done.3.b
  47.4 1.1 %collective-permute-done.8.refs_1_ = bf16[320,256]{1,0:T(8,128)(2,1)S(1)} collective-permute-done((bf16[320,256]{1,0:T(8,128)(2,1)S(1)}, bf16[320,256]{1,0:T(8,128)(2,1)S(1)}, u32[]{:S(2)}, u32[]{:S(2)}) %collective-permute-start.8) | collective-permute-done | bytes 163872 | tf_op jit(solution)/shard_map/ppermute | solution.py:451
  48.5 1.0 %residuals.2 = (f32[1024,256]{1,0:T(8,128)}, bf16[256,640]{1,0:T(8,128)(2,1)S(1)}, f32[8,128]{1,0:T(8,128)S(1)}) custom-call(s32[1]{0:T(128)} %bitcast.refs_0_.f, bf16[320,256]{1,0:T(8,128)(2,1)S(1)} %get-tuple-element.91.refs_0_, bf16[320,256]{1,0:T(8,128)(2,1)S(1)} %collective-permute-done.8.refs_1_, s32[1024,256]{1,0:T(8,128)S(1)} %bitcast.5, ...), custom_call_target="tpu_custom_call" | custom-call | flops 1000000000 | bytes 1024 | tf_op jit(solution)/shard_map/residuals/pallas_call | solution.py:297
  49.5 0.6 collective-permute-start.9
  50.1 1.9 %collective-permute-start.6 = (bf16[192,256]{1,0:T(8,128)(2,1)S(1)}, bf16[192,256]{1,0:T(8,128)(2,1)S(1)}, u32[]{:S(2)}, u32[]{:S(2)}) collective-permute-start(bf16[192,256]{1,0:T(8,128)(2,1)S(1)} %get-tuple-element.90.refs_0_), channel_id=1, source_target_pairs={{0,1},{1,0},{2,3},{3,2},{4,5},{5,4},{6,7},{7,6},{8,9},{9,8},{10,11... | collective-permute-start | bytes 294920 | tf_op jit(solution)/shard_map/ppermute | solution.py:451
  52.1 0.0 collective-permute-done.7.chosen
  52.1 2.6 %owned_features.8 = (bf16[640,2048]{1,0:T(8,128)(2,1)S(1)}, f32[8,128]{1,0:T(8,128)S(1)}) custom-call(bf16[1024,256]{1,0:T(8,128)(2,1)S(1)} %collective-permute-done.7.chosen, bf16[256,2048]{1,0:T(8,128)(2,1)S(1)} %get-tuple-element.81.omega, f32[1,2048]{1,0:T(1,128)S(1)} %get-tuple-element.82.turns, f32[8,128]{1,0:T(8,128)S(1)} %get-tuple-element.93.refs_0_), custom_call_target="tpu_custom_call" | custom-call | flops 1000000000 | bytes 1024 | tf_op jit(solution)/shard_map/owned_features/pallas_call | solution.py:219
  54.7 0.1 collective-permute-done.6.refs_1_
  54.7 0.9 residuals.3
  55.7 1.6 %collective-permute-start.11 = (bf16[256,384]{1,0:T(8,128)(2,1)S(1)}, bf16[256,384]{1,0:T(8,128)(2,1)S(1)}, u32[]{:S(2)}, u32[]{:S(2)}) collective-permute-start(bf16[256,384]{1,0:T(8,128)(2,1)S(1)} %get-tuple-element.106.refs_4_), channel_id=1, source_target_pairs={{0,8},{4,12},{8,0},{12,4},{1,9},{5,13},{9,1},{13,5},{2,10},{6,14},... | collective-permute-start | bytes 589832 | tf_op jit(solution)/shard_map/ppermute | solution.py:439
  57.2 0.0 collective-permute-start.13
  57.2 1.7 %owned_features.9 = (bf16[384,2048]{1,0:T(8,128)(2,1)S(1)}, f32[8,128]{1,0:T(8,128)S(1)}) custom-call(bf16[1024,256]{1,0:T(8,128)(2,1)S(1)} %collective-permute-done.2.chosen, bf16[256,2048]{1,0:T(8,128)(2,1)S(1)} %get-tuple-element.81.omega, f32[1,2048]{1,0:T(1,128)S(1)} %get-tuple-element.82.turns, f32[8,128]{1,0:T(8,128)S(1)} %get-tuple-element.98.refs_0_), custom_call_target="tpu_custom_call" | custom-call | flops 100000000 | bytes 1024 | tf_op jit(solution)/shard_map/owned_features/pallas_call | solution.py:219
  58.9 1.9 %owned_features.10 = (bf16[384,2048]{1,0:T(8,128)(2,1)S(1)}, f32[8,128]{1,0:T(8,128)S(1)}) custom-call(bf16[1024,256]{1,0:T(8,128)(2,1)S(1)} %collective-permute-done.4.chosen, bf16[256,2048]{1,0:T(8,128)(2,1)S(1)} %get-tuple-element.81.omega, f32[1,2048]{1,0:T(1,128)S(1)} %get-tuple-element.82.turns, f32[8,128]{1,0:T(8,128)S(1)} %get-tuple-element.100.refs_0_), custom_call_target="tpu_custom_call" | custom-call | flops 100000000 | bytes 1024 | tf_op jit(solution)/shard_map/owned_features/pallas_call | solution.py:219
  60.8 0.0 collective-permute-done.9.refs_6_
  60.8 0.6 collective-permute-start.14
  61.4 0.1 collective-permute-start.10
  61.4 1.6 %owned_features.11 = (bf16[384,2048]{1,0:T(8,128)(2,1)S(1)}, f32[8,128]{1,0:T(8,128)S(1)}) custom-call(bf16[1024,256]{1,0:T(8,128)(2,1)S(1)} %collective-permute-done.7.chosen, bf16[256,2048]{1,0:T(8,128)(2,1)S(1)} %get-tuple-element.81.omega, f32[1,2048]{1,0:T(1,128)S(1)} %get-tuple-element.82.turns, f32[8,128]{1,0:T(8,128)S(1)} %get-tuple-element.104.refs_0_), custom_call_target="tpu_custom_call" | custom-call | flops 100000000 | bytes 1024 | tf_op jit(solution)/shard_map/owned_features/pallas_call | solution.py:219
  63.1 0.0 collective-permute-done.11.refs_6_
  63.1 0.5 collective-permute-start.12
  63.6 0.0 collective-permute-done.13.refs_5_
  63.6 0.0 copy-start.1
  63.6 0.0 copy-start.2
  63.6 0.0 copy-start.3
  63.7 3.6 %first_part.1 = (f32[2048,256]{1,0:T(8,128)S(1)}, f32[8,128]{1,0:T(8,128)S(1)}) custom-call(bf16[640,2048]{1,0:T(8,128)(2,1)S(1)} %get-tuple-element.109.refs_0_, bf16[640,2048]{1,0:T(8,128)(2,1)S(1)} %get-tuple-element.110.refs_1_, bf16[640,2048]{1,0:T(8,128)(2,1)S(1)} %get-tuple-element.111.refs_2_, bf16[640,2048]{1,0:T(8,128)(2,1)S(1)} %get-tuple-element.112.refs_3_, ...), custom_call_target="tpu_custom_call" | custom-call | flops 300000000 | bytes 1024 | tf_op jit(solution)/shard_map/first_part/pallas_call | solution.py:339
  67.3 1.7 %update.4 = (f32[1,2048,256]{2,1,0:T(8,128)}, f32[1,2048,256]{2,1,0:T(8,128)}, f32[1,2048,256]{2,1,0:T(8,128)}, bf16[256,256]{1,0:T(8,128)(2,1)S(1)}) custom-call(bf16[384,2048]{1,0:T(8,128)(2,1)S(1)} %get-tuple-element.97.refs_0_, bf16[384,2048]{1,0:T(8,128)(2,1)S(1)} %get-tuple-element.99.refs_1_, bf16[384,2048]{1,0:T(8,128)(2,1)S(1)} %get-tuple-element.101.refs_2_, ...), custom_call_target="tpu_custom_call" | custom-call | flops 4000000000 | bytes 1024 | tf_op jit(solution)/shard_map/update/pallas_call | solution.py:387
  69.0 0.5 collective-permute-start.15
  69.5 2.5 %update.5 = (f32[1,2048,256]{2,1,0:T(8,128)}, f32[1,2048,256]{2,1,0:T(8,128)}, f32[1,2048,256]{2,1,0:T(8,128)}, bf16[512,256]{1,0:T(8,128)(2,1)S(1)}) custom-call(bf16[384,2048]{1,0:T(8,128)(2,1)S(1)} %get-tuple-element.97.refs_0_, bf16[384,2048]{1,0:T(8,128)(2,1)S(1)} %get-tuple-element.99.refs_1_, ...), custom_call_target="tpu_custom_call", output_to_operand_aliasing={{0}: (13, {}), {1}: (14, {}), {2}: (15, {})} | custom-call | flops 4000000000 | bytes 1024 | tf_op jit(solution)/shard_map/update/pallas_call | solution.py:387
  72.0 1.5 %collective-permute-start.16 = (bf16[512,256]{1,0:T(8,128)(2,1)S(1)}, bf16[512,256]{1,0:T(8,128)(2,1)S(1)}, u32[]{:S(2)}, u32[]{:S(2)}) collective-permute-start(bf16[512,256]{1,0:T(8,128)(2,1)S(1)} %get-tuple-element.127.refs_4_), channel_id=1, source_target_pairs={{0,8},{4,12},{8,0},{12,4},{1,9},{5,13},{9,1},{13,5},{2,10},{6,14},... | collective-permute-start | bytes 786440 | tf_op jit(solution)/shard_map/ppermute | solution.py:439
  73.5 1.0 collective-permute-done.15.refs_17_.refs_2_
  74.5 2.5 %update.6 = (f32[1,2048,256]{2,1,0:T(8,128)}, f32[1,2048,256]{2,1,0:T(8,128)}, f32[1,2048,256]{2,1,0:T(8,128)}, bf16[512,256]{1,0:T(8,128)(2,1)S(1)}) custom-call(bf16[384,2048]{1,0:T(8,128)(2,1)S(1)} %get-tuple-element.97.refs_0_, bf16[384,2048]{1,0:T(8,128)(2,1)S(1)} %get-tuple-element.99.refs_1_, ...), custom_call_target="tpu_custom_call", output_to_operand_aliasing={{0}: (13, {}), {1}: (14, {}), {2}: (15, {})} | custom-call | flops 4000000000 | bytes 1024 | tf_op jit(solution)/shard_map/update/pallas_call | solution.py:387
  76.9 0.5 collective-permute-start.24
  77.4 3.6 %collective-permute-done.16.refs_17_.refs_6_ = bf16[512,256]{1,0:T(8,128)(2,1)S(1)} collective-permute-done((bf16[512,256]{1,0:T(8,128)(2,1)S(1)}, bf16[512,256]{1,0:T(8,128)(2,1)S(1)}, u32[]{:S(2)}, u32[]{:S(2)}) %collective-permute-start.16) | collective-permute-done | bytes 262176 | tf_op jit(solution)/shard_map/ppermute | solution.py:439
  81.1 3.3 %update.7 = (f32[1,2048,256]{2,1,0:T(8,128)}, f32[1,2048,256]{2,1,0:T(8,128)}, f32[1,2048,256]{2,1,0:T(8,128)}, bf16[768,256]{1,0:T(8,128)(2,1)S(1)}) custom-call(bf16[384,2048]{1,0:T(8,128)(2,1)S(1)} %get-tuple-element.97.refs_0_, bf16[384,2048]{1,0:T(8,128)(2,1)S(1)} %get-tuple-element.99.refs_1_, ...), custom_call_target="tpu_custom_call", output_to_operand_aliasing={{0}: (13, {}), {1}: (14, {}), {2}: (15, {})} | custom-call | flops 4000000000 | bytes 1024 | tf_op jit(solution)/shard_map/update/pallas_call | solution.py:387
  84.4 1.5 %collective-permute-start.18 = (bf16[768,256]{1,0:T(8,128)(2,1)S(1)}, bf16[768,256]{1,0:T(8,128)(2,1)S(1)}, u32[]{:S(2)}, u32[]{:S(2)}) collective-permute-start(bf16[768,256]{1,0:T(8,128)(2,1)S(1)} %get-tuple-element.131.refs_0_), channel_id=1, source_target_pairs={{0,8},{4,12},{8,0},{12,4},{1,9},{5,13},{9,1},{13,5},{2,10},{6,14},... | collective-permute-start | bytes 1179656 | tf_op jit(solution)/shard_map/ppermute | solution.py:439
  85.9 0.4 collective-permute-done.24.refs_10_
  86.3 0.1 collective-permute-start.23
  86.5 0.4 collective-permute-start.22
  86.8 0.1 collective-permute-start.25
  87.0 0.5 collective-permute-done.21.refs_5_
  87.5 0.1 collective-permute-start.17
  87.6 0.2 collective-permute-done.23.refs_9_
  87.8 0.4 collective-permute-done.22.refs_7_
  88.2 0.4 collective-permute-done.25.refs_11_
  88.6 1.6 %put_rows.2.refs_4_ = bf16[8192,256]{1,0:T(8,128)(2,1)} custom-call(s32[1]{0:T(128)} %bitcast.1.refs_1_.p, bf16[256,256]{1,0:T(8,128)(2,1)S(1)} %get-tuple-element.123.refs_0_, bf16[256,256]{1,0:T(8,128)(2,1)S(1)} %collective-permute-done.19.refs_1_, bf16[256,256]{1,0:T(8,128)(2,1)S(1)} %collective-permute-done.15.refs_17_.refs_2_, ...), custom_call_target="tpu_custom_call" | custom-call | flops 10000000 | bytes 1024 | tf_op jit(solution)/shard_map/put_rows/pallas_call | solution.py:421
  90.2 4.6 %collective-permute-done.18.refs_2_ = bf16[768,256]{1,0:T(8,128)(2,1)S(1)} collective-permute-done((bf16[768,256]{1,0:T(8,128)(2,1)S(1)}, bf16[768,256]{1,0:T(8,128)(2,1)S(1)}, u32[]{:S(2)}, u32[]{:S(2)}) %collective-permute-start.18) | collective-permute-done | bytes 393248 | tf_op jit(solution)/shard_map/ppermute | solution.py:439
  94.8 1.7 %collective-permute-done.26.refs_3_ = bf16[768,256]{1,0:T(8,128)(2,1)S(1)} collective-permute-done((bf16[768,256]{1,0:T(8,128)(2,1)S(1)}, bf16[768,256]{1,0:T(8,128)(2,1)S(1)}, u32[]{:S(2)}, u32[]{:S(2)}) %collective-permute-start.26) | collective-permute-done | bytes 393248 | tf_op jit(solution)/shard_map/ppermute | solution.py:443
  96.5 1.2 %put_rows.3 = bf16[8192,256]{1,0:T(8,128)(2,1)} custom-call(s32[1]{0:T(128)} %bitcast.1.refs_1_.p, bf16[768,256]{1,0:T(8,128)(2,1)S(1)} %get-tuple-element.131.refs_0_, bf16[768,256]{1,0:T(8,128)(2,1)S(1)} %collective-permute-done.17.refs_1_, bf16[768,256]{1,0:T(8,128)(2,1)S(1)} %collective-permute-done.18.refs_2_, ...), custom_call_target="tpu_custom_call", output_to_operand_aliasing={{}: (5, {})} | custom-call | flops 10000000 | bytes 1024 | tf_op jit(solution)/shard_map/put_rows/pallas_call | solution.py:421
  (23 shorter events, 0.2 us)
Async XLA Ops:
  3.4 33.4 %collective-permute-start.2 = (bf16[1024,256]{1,0:T(8,128)(2,1)S(1)}, bf16[1024,256]{1,0:T(8,128)(2,1)S(1)}, u32[]{:S(2)}, u32[]{:S(2)}) collective-permute-start(bf16[1024,256]{1,0:T(8,128)(2,1)S(1)} %get-tuple-element.71.refs_2_), channel_id=1, source_target_pairs={{0,4},{4,0},{8,12},{12,8},{1,5},{5,1},{9,13},{13,9},{2,6},{6,2},{1... | collective-permute-start | bytes 1572872 | tf_op jit(solution)/shard_map/ppermute | solution.py:443
  3.9 32.9 %collective-permute-start.4 = (bf16[1024,256]{1,0:T(8,128)(2,1)S(1)}, bf16[1024,256]{1,0:T(8,128)(2,1)S(1)}, u32[]{:S(2)}, u32[]{:S(2)}) collective-permute-start(bf16[1024,256]{1,0:T(8,128)(2,1)S(1)} %get-tuple-element.71.refs_2_), channel_id=1, source_target_pairs={{0,8},{4,12},{8,0},{12,4},{1,9},{5,13},{9,1},{13,5},{2,10},{6,14},... | collective-permute-start | bytes 1572872 | tf_op jit(solution)/shard_map/ppermute | solution.py:439
  20.8 7.4 %collective-permute-start = (bf16[320,256]{1,0:T(8,128)(2,1)S(1)}, bf16[320,256]{1,0:T(8,128)(2,1)S(1)}, u32[]{:S(2)}, u32[]{:S(2)}) collective-permute-start(bf16[320,256]{1,0:T(8,128)(2,1)S(1)} %get-tuple-element.76), channel_id=1, source_target_pairs={{0,1},{1,0},{2,3},{3,2},{4,5},{5,4},{6,7},{7,6},{8,9},{9,8},{10,11... | collective-permute-start | bytes 491528 | tf_op jit(solution)/shard_map/ppermute | solution.py:451
  28.2 12.8 %collective-permute-start.5 = (bf16[320,256]{1,0:T(8,128)(2,1)S(1)}, bf16[320,256]{1,0:T(8,128)(2,1)S(1)}, u32[]{:S(2)}, u32[]{:S(2)}) collective-permute-start(bf16[320,256]{1,0:T(8,128)(2,1)S(1)} %get-tuple-element.86.a), channel_id=1, source_target_pairs={{0,2},{1,3},{2,0},{3,1},{4,6},{5,7},{6,4},{7,5},{8,10},{9,11},{10,... | collective-permute-start | bytes 491528 | tf_op jit(solution)/shard_map/ppermute | solution.py:451
  36.2 4.7 %collective-permute-start.1 = (bf16[192,256]{1,0:T(8,128)(2,1)S(1)}, bf16[192,256]{1,0:T(8,128)(2,1)S(1)}, u32[]{:S(2)}, u32[]{:S(2)}) collective-permute-start(bf16[192,256]{1,0:T(8,128)(2,1)S(1)} %get-tuple-element.80), channel_id=1, source_target_pairs={{0,1},{1,0},{2,3},{3,2},{4,5},{5,4},{6,7},{7,6},{8,9},{9,8},{10,11... | collective-permute-start | bytes 294920 | tf_op jit(solution)/shard_map/ppermute | solution.py:451
  36.8 15.2 %collective-permute-start.7 = (bf16[1024,256]{1,0:T(8,128)(2,1)S(1)}, bf16[1024,256]{1,0:T(8,128)(2,1)S(1)}, u32[]{:S(2)}, u32[]{:S(2)}) collective-permute-start(bf16[1024,256]{1,0:T(8,128)(2,1)S(1)} %collective-permute-done.4.chosen), channel_id=1, source_target_pairs={{0,4},{4,0},{8,12},{12,8},{1,5},{5,1},{9,13},{13,9},{2,6},{6,2},{1... | collective-permute-start | bytes 1572872 | tf_op jit(solution)/shard_map/ppermute | solution.py:443
  41.0 7.5 %collective-permute-start.8 = (bf16[320,256]{1,0:T(8,128)(2,1)S(1)}, bf16[320,256]{1,0:T(8,128)(2,1)S(1)}, u32[]{:S(2)}, u32[]{:S(2)}) collective-permute-start(bf16[320,256]{1,0:T(8,128)(2,1)S(1)} %get-tuple-element.91.refs_0_), channel_id=1, source_target_pairs={{0,1},{1,0},{2,3},{3,2},{4,5},{5,4},{6,7},{7,6},{8,9},{9,8},{10,11... | collective-permute-start | bytes 491528 | tf_op jit(solution)/shard_map/ppermute | solution.py:451
  41.6 5.8 %collective-permute-start.3 = (bf16[192,256]{1,0:T(8,128)(2,1)S(1)}, bf16[192,256]{1,0:T(8,128)(2,1)S(1)}, u32[]{:S(2)}, u32[]{:S(2)}) collective-permute-start(bf16[192,256]{1,0:T(8,128)(2,1)S(1)} %get-tuple-element.85.a), channel_id=1, source_target_pairs={{0,2},{1,3},{2,0},{3,1},{4,6},{5,7},{6,4},{7,5},{8,10},{9,11},{10,... | collective-permute-start | bytes 294920 | tf_op jit(solution)/shard_map/ppermute | solution.py:451
  43.9 4.6 %copy-start.4 = (s32[2,512,256]{2,1,0:T(8,128)S(1)}, s32[2,512,256]{2,1,0:T(8,128)}, u32[]{:S(2)}) copy-start(s32[2,512,256]{2,1,0:T(8,128)} %param.15) | copy-start | bytes 3145732
  49.5 11.2 %collective-permute-start.9 = (bf16[256,640]{1,0:T(8,128)(2,1)S(1)}, bf16[256,640]{1,0:T(8,128)(2,1)S(1)}, u32[]{:S(2)}, u32[]{:S(2)}) collective-permute-start(bf16[256,640]{1,0:T(8,128)(2,1)S(1)} %get-tuple-element.102.refs_4_), channel_id=1, source_target_pairs={{0,8},{4,12},{8,0},{12,4},{1,9},{5,13},{9,1},{13,5},{2,10},{6,14},... | collective-permute-start | bytes 983048 | tf_op jit(solution)/shard_map/ppermute | solution.py:439
  50.1 4.6 %collective-permute-start.6 = (bf16[192,256]{1,0:T(8,128)(2,1)S(1)}, bf16[192,256]{1,0:T(8,128)(2,1)S(1)}, u32[]{:S(2)}, u32[]{:S(2)}) collective-permute-start(bf16[192,256]{1,0:T(8,128)(2,1)S(1)} %get-tuple-element.90.refs_0_), channel_id=1, source_target_pairs={{0,1},{1,0},{2,3},{3,2},{4,5},{5,4},{6,7},{7,6},{8,9},{9,8},{10,11... | collective-permute-start | bytes 294920 | tf_op jit(solution)/shard_map/ppermute | solution.py:451
  55.7 7.5 %collective-permute-start.11 = (bf16[256,384]{1,0:T(8,128)(2,1)S(1)}, bf16[256,384]{1,0:T(8,128)(2,1)S(1)}, u32[]{:S(2)}, u32[]{:S(2)}) collective-permute-start(bf16[256,384]{1,0:T(8,128)(2,1)S(1)} %get-tuple-element.106.refs_4_), channel_id=1, source_target_pairs={{0,8},{4,12},{8,0},{12,4},{1,9},{5,13},{9,1},{13,5},{2,10},{6,14},... | collective-permute-start | bytes 589832 | tf_op jit(solution)/shard_map/ppermute | solution.py:439
  57.2 6.4 %collective-permute-start.13 = (bf16[256,640]{1,0:T(8,128)(2,1)S(1)}, bf16[256,640]{1,0:T(8,128)(2,1)S(1)}, u32[]{:S(2)}, u32[]{:S(2)}) collective-permute-start(bf16[256,640]{1,0:T(8,128)(2,1)S(1)} %get-tuple-element.102.refs_4_), channel_id=1, source_target_pairs={{0,4},{4,0},{8,12},{12,8},{1,5},{5,1},{9,13},{13,9},{2,6},{6,2},{1... | collective-permute-start | bytes 983048 | tf_op jit(solution)/shard_map/ppermute | solution.py:443
  57.2 6.4 %copy-start = (f32[1,2048,256]{2,1,0:T(8,128)S(1)}, f32[1,2048,256]{2,1,0:T(8,128)}, u32[]{:S(2)}) copy-start(f32[1,2048,256]{2,1,0:T(8,128)} %refs_10_.7) | copy-start | bytes 6291460
  60.8 2.8 %collective-permute-start.14 = (bf16[256,640]{1,0:T(8,128)(2,1)S(1)}, bf16[256,640]{1,0:T(8,128)(2,1)S(1)}, u32[]{:S(2)}, u32[]{:S(2)}) collective-permute-start(bf16[256,640]{1,0:T(8,128)(2,1)S(1)} %collective-permute-done.9.refs_6_), channel_id=1, source_target_pairs={{0,4},{4,0},{8,12},{12,8},{1,5},{5,1},{9,13},{13,9},{2,6},{6,2},{1... | collective-permute-start | bytes 983048 | tf_op jit(solution)/shard_map/ppermute | solution.py:443
  61.4 5.9 %collective-permute-start.10 = (bf16[256,384]{1,0:T(8,128)(2,1)S(1)}, bf16[256,384]{1,0:T(8,128)(2,1)S(1)}, u32[]{:S(2)}, u32[]{:S(2)}) collective-permute-start(bf16[256,384]{1,0:T(8,128)(2,1)S(1)} %get-tuple-element.106.refs_4_), channel_id=1, source_target_pairs={{0,4},{4,0},{8,12},{12,8},{1,5},{5,1},{9,13},{13,9},{2,6},{6,2},{1... | collective-permute-start | bytes 589832 | tf_op jit(solution)/shard_map/ppermute | solution.py:443
  63.1 4.2 %collective-permute-start.12 = (bf16[256,384]{1,0:T(8,128)(2,1)S(1)}, bf16[256,384]{1,0:T(8,128)(2,1)S(1)}, u32[]{:S(2)}, u32[]{:S(2)}) collective-permute-start(bf16[256,384]{1,0:T(8,128)(2,1)S(1)} %collective-permute-done.11.refs_6_), channel_id=1, source_target_pairs={{0,4},{4,0},{8,12},{12,8},{1,5},{5,1},{9,13},{13,9},{2,6},{6,2},{1... | collective-permute-start | bytes 589832 | tf_op jit(solution)/shard_map/ppermute | solution.py:443
  63.6 3.7 %copy-start.1 = (f32[1,2048,256]{2,1,0:T(8,128)S(1)}, f32[1,2048,256]{2,1,0:T(8,128)}, u32[]{:S(2)}) copy-start(f32[1,2048,256]{2,1,0:T(8,128)} %refs_11_.7) | copy-start | bytes 6291460
  63.6 3.7 %copy-start.2 = (f32[1,2048,256]{2,1,0:T(8,128)S(1)}, f32[1,2048,256]{2,1,0:T(8,128)}, u32[]{:S(2)}) copy-start(f32[1,2048,256]{2,1,0:T(8,128)} %refs_12_.7) | copy-start | bytes 6291460
  63.6 3.7 %copy-start.3 = (bf16[256,256]{1,0:T(8,128)(2,1)S(1)}, bf16[256,256]{1,0:T(8,128)(2,1)}, u32[]{:S(2)}) copy-start(bf16[256,256]{1,0:T(8,128)(2,1)} %refs_9_.7) | copy-start | bytes 393220
  69.0 5.5 %collective-permute-start.15 = (bf16[256,256]{1,0:T(8,128)(2,1)S(1)}, bf16[256,256]{1,0:T(8,128)(2,1)S(1)}, u32[]{:S(2)}, u32[]{:S(2)}) collective-permute-start(bf16[256,256]{1,0:T(8,128)(2,1)S(1)} %get-tuple-element.123.refs_0_), channel_id=1, source_target_pairs={{0,8},{4,12},{8,0},{12,4},{1,9},{5,13},{9,1},{13,5},{2,10},{6,14},... | collective-permute-start | bytes 393224 | tf_op jit(solution)/shard_map/ppermute | solution.py:439
  69.5 17.0 %collective-permute-start.19 = (bf16[256,256]{1,0:T(8,128)(2,1)S(1)}, bf16[256,256]{1,0:T(8,128)(2,1)S(1)}, u32[]{:S(2)}, u32[]{:S(2)}) collective-permute-start(bf16[256,256]{1,0:T(8,128)(2,1)S(1)} %get-tuple-element.123.refs_0_), channel_id=1, source_target_pairs={{0,4},{4,0},{8,12},{12,8},{1,5},{5,1},{9,13},{13,9},{2,6},{6,2},{1... | collective-permute-start | bytes 393224 | tf_op jit(solution)/shard_map/ppermute | solution.py:443
  72.0 9.1 %collective-permute-start.16 = (bf16[512,256]{1,0:T(8,128)(2,1)S(1)}, bf16[512,256]{1,0:T(8,128)(2,1)S(1)}, u32[]{:S(2)}, u32[]{:S(2)}) collective-permute-start(bf16[512,256]{1,0:T(8,128)(2,1)S(1)} %get-tuple-element.127.refs_4_), channel_id=1, source_target_pairs={{0,8},{4,12},{8,0},{12,4},{1,9},{5,13},{9,1},{13,5},{2,10},{6,14},... | collective-permute-start | bytes 786440 | tf_op jit(solution)/shard_map/ppermute | solution.py:439
  76.9 9.4 %collective-permute-start.24 = (bf16[512,256]{1,0:T(8,128)(2,1)S(1)}, bf16[512,256]{1,0:T(8,128)(2,1)S(1)}, u32[]{:S(2)}, u32[]{:S(2)}) collective-permute-start(bf16[512,256]{1,0:T(8,128)(2,1)S(1)} %get-tuple-element.133.refs_8_), channel_id=1, source_target_pairs={{0,8},{4,12},{8,0},{12,4},{1,9},{5,13},{9,1},{13,5},{2,10},{6,14},... | collective-permute-start | bytes 786440 | tf_op jit(solution)/shard_map/ppermute | solution.py:439
  77.4 9.4 %collective-permute-start.20 = (bf16[256,256]{1,0:T(8,128)(2,1)S(1)}, bf16[256,256]{1,0:T(8,128)(2,1)S(1)}, u32[]{:S(2)}, u32[]{:S(2)}) collective-permute-start(bf16[256,256]{1,0:T(8,128)(2,1)S(1)} %collective-permute-done.15.refs_17_.refs_2_), channel_id=1, source_target_pairs={{0,4},{4,0},{8,12},{12,8},{1,5},{5,1},{9,13},{13,9},{2,6},{6,2},{1... | collective-permute-start | bytes 393224 | tf_op jit(solution)/shard_map/ppermute | solution.py:443
  84.4 10.4 %collective-permute-start.18 = (bf16[768,256]{1,0:T(8,128)(2,1)S(1)}, bf16[768,256]{1,0:T(8,128)(2,1)S(1)}, u32[]{:S(2)}, u32[]{:S(2)}) collective-permute-start(bf16[768,256]{1,0:T(8,128)(2,1)S(1)} %get-tuple-element.131.refs_0_), channel_id=1, source_target_pairs={{0,8},{4,12},{8,0},{12,4},{1,9},{5,13},{9,1},{13,5},{2,10},{6,14},... | collective-permute-start | bytes 1179656 | tf_op jit(solution)/shard_map/ppermute | solution.py:439
  85.9 1.5 %collective-permute-start.21 = (bf16[512,256]{1,0:T(8,128)(2,1)S(1)}, bf16[512,256]{1,0:T(8,128)(2,1)S(1)}, u32[]{:S(2)}, u32[]{:S(2)}) collective-permute-start(bf16[512,256]{1,0:T(8,128)(2,1)S(1)} %get-tuple-element.127.refs_4_), channel_id=1, source_target_pairs={{0,4},{4,0},{8,12},{12,8},{1,5},{5,1},{9,13},{13,9},{2,6},{6,2},{1... | collective-permute-start | bytes 786440 | tf_op jit(solution)/shard_map/ppermute | solution.py:443
  86.3 1.5 %collective-permute-start.23 = (bf16[512,256]{1,0:T(8,128)(2,1)S(1)}, bf16[512,256]{1,0:T(8,128)(2,1)S(1)}, u32[]{:S(2)}, u32[]{:S(2)}) collective-permute-start(bf16[512,256]{1,0:T(8,128)(2,1)S(1)} %get-tuple-element.133.refs_8_), channel_id=1, source_target_pairs={{0,4},{4,0},{8,12},{12,8},{1,5},{5,1},{9,13},{13,9},{2,6},{6,2},{1... | collective-permute-start | bytes 786440 | tf_op jit(solution)/shard_map/ppermute | solution.py:443
  86.5 1.8 %collective-permute-start.22 = (bf16[512,256]{1,0:T(8,128)(2,1)S(1)}, bf16[512,256]{1,0:T(8,128)(2,1)S(1)}, u32[]{:S(2)}, u32[]{:S(2)}) collective-permute-start(bf16[512,256]{1,0:T(8,128)(2,1)S(1)} %collective-permute-done.16.refs_17_.refs_6_), channel_id=1, source_target_pairs={{0,4},{4,0},{8,12},{12,8},{1,5},{5,1},{9,13},{13,9},{2,6},{6,2},{1... | collective-permute-start | bytes 786440 | tf_op jit(solution)/shard_map/ppermute | solution.py:443
  86.8 1.8 %collective-permute-start.25 = (bf16[512,256]{1,0:T(8,128)(2,1)S(1)}, bf16[512,256]{1,0:T(8,128)(2,1)S(1)}, u32[]{:S(2)}, u32[]{:S(2)}) collective-permute-start(bf16[512,256]{1,0:T(8,128)(2,1)S(1)} %collective-permute-done.24.refs_10_), channel_id=1, source_target_pairs={{0,4},{4,0},{8,12},{12,8},{1,5},{5,1},{9,13},{13,9},{2,6},{6,2},{1... | collective-permute-start | bytes 786440 | tf_op jit(solution)/shard_map/ppermute | solution.py:443
  87.5 7.3 %collective-permute-start.17 = (bf16[768,256]{1,0:T(8,128)(2,1)S(1)}, bf16[768,256]{1,0:T(8,128)(2,1)S(1)}, u32[]{:S(2)}, u32[]{:S(2)}) collective-permute-start(bf16[768,256]{1,0:T(8,128)(2,1)S(1)} %get-tuple-element.131.refs_0_), channel_id=1, source_target_pairs={{0,4},{4,0},{8,12},{12,8},{1,5},{5,1},{9,13},{13,9},{2,6},{6,2},{1... | collective-permute-start | bytes 1179656 | tf_op jit(solution)/shard_map/ppermute | solution.py:443
  94.8 1.7 %collective-permute-start.26 = (bf16[768,256]{1,0:T(8,128)(2,1)S(1)}, bf16[768,256]{1,0:T(8,128)(2,1)S(1)}, u32[]{:S(2)}, u32[]{:S(2)}) collective-permute-start(bf16[768,256]{1,0:T(8,128)(2,1)S(1)} %collective-permute-done.18.refs_2_), channel_id=1, source_target_pairs={{0,4},{4,0},{8,12},{12,8},{1,5},{5,1},{9,13},{13,9},{2,6},{6,2},{1... | collective-permute-start | bytes 1179656 | tf_op jit(solution)/shard_map/ppermute | solution.py:443

commit v8 on v7

--- a/solution.py
+++ b/solution.py
@@ -52,14 +52,16 @@
 
 
 def gather_kernel(picks, points, chosen, token):
-    batch, pool = chosen.shape[0], points.shape[0]
-    m = pl.program_id(0)
-    wanted = jnp.broadcast_to(picks[pl.ds(m, 1), :], (128, batch)).T
+    batch, pool = picks.shape[1], points.shape[0]
     lane = lax.broadcasted_iota(jnp.int32, (batch, 128), 1)
-    hot = [jnp.where(wanted == lane + 128 * j, 1.0, 0.0).astype(bf16) for j in range(pool // 128)]
-    chosen[...] = jnp.dot(
-        jnp.concatenate(hot, axis=1), points[...], preferred_element_type=f32
-    ).astype(bf16)
+    for m in range(2):
+        wanted = jnp.broadcast_to(picks[m : m + 1, :], (128, batch)).T
+        hot = [
+            jnp.where(wanted == lane + 128 * j, 1.0, 0.0).astype(bf16) for j in range(pool // 128)
+        ]
+        chosen[m * batch : (m + 1) * batch, :] = jnp.dot(
+            jnp.concatenate(hot, axis=1), points[...], preferred_element_type=f32
+        ).astype(bf16)
 
 
 def gather(picks, points):
@@ -67,12 +69,12 @@
     pool, ins = points.shape
     return pl.pallas_call(
         gather_kernel,
-        grid=(2,),
+        grid=(1,),
         in_specs=[
             pl.BlockSpec(picks.shape, lambda i: (0, 0)),
             pl.BlockSpec((pool, ins), lambda i: (0, 0)),
         ],
-        out_specs=[pl.BlockSpec((batch, ins), lambda i: (i, 0)), ANYWHERE],
+        out_specs=[IN_VMEM, ANYWHERE],
         out_shape=[jax.ShapeDtypeStruct((2 * batch, ins), bf16), TOKEN],
         compiler_params=params(),
         cost_estimate=cost(3),
@@ -80,70 +82,75 @@
     )(picks, points)
 
 
-def cosines(chosen, omega, turns, width, store, between=None):
+def cosines(chosen, omega, phase, base, width, store, between=None):
     tile = min(256, width)
     count = width // tile
     group = min(512, width)
 
+    def part(start, size):
+        if isinstance(base, int):
+            return slice(base + start, base + start + size)
+        return pl.ds(pl.multiple_of(base + start, tile), size)
+
     def product(c):
-        return jnp.dot(chosen, omega[:, c * tile : (c + 1) * tile], preferred_element_type=f32)
+        return jnp.dot(chosen, omega[:, part(c * tile, tile)], preferred_element_type=f32)
 
     ready = product(0)
     for c in range(count):
         coming = product(c + 1) if c + 1 < count else None
         if between is not None and c > 0 and c * tile % group == 0:
-            between(slice(c * tile - group, c * tile))
-        cols = slice(c * tile, (c + 1) * tile)
-        store(cols, scaled_cos(ready, turns[:, cols]))
+            between(c * tile - group, part(c * tile - group, group), group)
+        turns = phase[:, part(c * tile, tile)] * TURN
+        store(slice(c * tile, (c + 1) * tile), scaled_cos(ready, turns))
         ready = coming
     if between is not None:
-        between(slice(width - group, width))
-
-
-def rates_kernel(start, size, begun, keep, ends, blocks, f, p, chosen, omega, phase, weights, *refs):
+        between(width - group, part(width - group, group), group)
+
+
+def rates_kernel(start, size, low, high, width, own, begun, keep, ends, f, p, chosen, omega, phase, weights, *refs):
     refs = list(refs)
     total, feats = refs.pop(), refs.pop()
     before = refs.pop(0) if begun else None
     refs.pop()
-    step = pl.program_id(0)
-    width = omega.shape[1]
-
-    @pl.when(step == 0)
-    def _():
-        total[...] = before[...] if begun else jnp.zeros_like(total)
-
-    turns = phase[...] * TURN
-    parts = []
-
-    def store(cols, value):
-        feats[:, cols] = value
-
-    def between(cols):
-        parts.append(jnp.dot(feats[:, cols], weights[cols, :], preferred_element_type=f32))
-
-    cosines(chosen[start : start + size, :], omega, turns, width, store, between)
-    part = parts[0]
-    for q in parts[1:]:
-        part = part + q
-    total[...] += part
+    owned = None if begun else refs.pop(0)
+    count = omega.shape[1] // width
+    total[...] = before[...] if begun else jnp.zeros_like(total)
+
+    def block(place, into, offset):
+        parts = []
+
+        def store(cols, value):
+            into[:, offset + cols.start : offset + cols.stop] = value
+
+        def between(at, rows, group):
+            done = into[:, offset + at : offset + at + group]
+            parts.append(jnp.dot(done, weights[rows, :], preferred_element_type=f32))
+
+        cosines(
+            chosen[start : start + size, :], omega, phase, place * width, width, store, between
+        )
+        part = parts[0]
+        for q in parts[1:]:
+            part = part + q
+        total[...] += part
 
     if not begun:
-        owned = refs.pop(0)
-
-        @pl.when(step < blocks)
-        def _():
-            at = pl.ds(pl.multiple_of(step * width, width), width)
-            owned[:, at] = feats[...]
-            if keep:
-                refs[0][:, at] = omega[...]
-                refs[1][:, at] = turns
-
-    @pl.when(step == pl.num_programs(0) - 1)
-    def _():
-        if ends:
-            split(total, f[0], 0, *refs[-2:])
-        else:
-            refs[-1][...] = total[...]
+        for step in range(own):
+            block(p[0] * own + step, owned, step * width)
+
+    def turn(step, _):
+        block(lax.rem(step + p[0] * own, count), feats, 0)
+        return _
+
+    lax.fori_loop(low if begun else own, high, turn, 0)
+    if keep:
+        at = pl.ds(pl.multiple_of(p[0] * own * width, width), own * width)
+        refs[0][...] = omega[:, at]
+        refs[1][...] = phase[:, at]
+    if ends:
+        split(total, f[0], 0, *refs[-2:])
+    else:
+        refs[-1][...] = total[...]
 
 
 def split(value, f, bit, kept, sent):
@@ -160,9 +167,6 @@
     count = feat_dev // width
     own = owned // width
     low, high = blocks[0] * count // 2, blocks[1] * count // 2
-
-    def turned(i, p):
-        return lax.rem(i + low + p[0] * own, count)
 
     begun = before is not None
     outs = []
@@ -179,22 +183,15 @@
     def kernel(*refs):
         inputs = len(args) - len(deps)
         rates_kernel(
-            start, size, begun, keep, ends, own, *refs[:inputs], *refs[inputs + len(deps) :]
+            start, size, low, high, width, own, begun, keep, ends, *refs[:inputs], *refs[inputs + len(deps) :]
         )
 
     return pl.pallas_call(
         kernel,
         grid_spec=pltpu.PrefetchScalarGridSpec(
             num_scalar_prefetch=2,
-            grid=(high - low,),
-            in_specs=[
-                IN_VMEM,
-                pl.BlockSpec((ins, width), lambda i, f, p: (0, turned(i, p))),
-                pl.BlockSpec((1, width), lambda i, f, p: (0, turned(i, p))),
-                pl.BlockSpec((width, k), lambda i, f, p: (turned(i, p), 0)),
-            ]
-            + [IN_VMEM] * begun
-            + [ANYWHERE] * len(deps),
+            grid=(1,),
+            in_specs=[IN_VMEM] * (4 + begun) + [ANYWHERE] * len(deps),
             out_specs=[IN_VMEM] * len(outs) + [ANYWHERE],
             scratch_shapes=[pltpu.VMEM((size, width), bf16), pltpu.VMEM((size, k), f32)],
         ),
@@ -205,16 +202,16 @@
     )(*args)
 
 
-def features_kernel(start, size, chosen, omega, turns, *refs):
+def features_kernel(start, size, chosen, omega, phase, *refs):
     out = refs[-2]
 
     def store(cols, value):
         out[:, cols] = value
 
-    cosines(chosen[start : start + size, :], omega, turns, omega.shape[1], store)
-
-
-def owned_features(chosen, omega, turns, start, size, weight, deps):
+    cosines(chosen[start : start + size, :], omega, phase, 0, omega.shape[1], store)
+
+
+def owned_features(chosen, omega, phase, start, size, weight, deps):
     owned = omega.shape[1]
     return pl.pallas_call(
         functools.partial(features_kernel, start, size),
@@ -224,7 +221,7 @@
         compiler_params=params(),
         cost_estimate=cost(weight),
         name="owned_features",
-    )(chosen, omega, turns, *deps)
+    )(chosen, omega, phase, *deps)
 
 
 def total_kernel(bit, halves, f, a, b, *refs):
@@ -464,8 +461,7 @@
     size_one = points_here * 3 // 8
     parts = [(0, points_here - size_one), (points_here - size_one, size_one)]
     bits = n_feat.bit_length() - 1
-    points, picks, omega, weights = map(in_hbm, (points, picks, omega, weights))
-    phase = in_hbm(phase[None, :])
+    points, picks, phase = in_hbm(points), in_hbm(picks), phase[None, :]
     outer = counts.shape
     counts = counts.reshape(points_here, k)
 
@@ -490,7 +486,7 @@
             masks = masks + [q ^ 2**bit for q in masks]
         return rows, masks
 
-    feats_zero, own_omega, own_turns, kept_zero, sent, token = some_rates(
+    feats_zero, own_omega, own_phase, kept_zero, sent, token = some_rates(
         0, (0, 2), None, True, True, token
     )
     got_zero = swap(sent, n_feat, 0)
@@ -508,7 +504,7 @@
         for _ in range(pieces * share):
             m, j = todo.pop(0)
             feats, token = owned_features(
-                everyone[j], own_omega, own_turns, *parts[m], weight, [token]
+                everyone[j], own_omega, own_phase, *parts[m], weight, [token]
             )
             features[m].append(feats)
         return token

time: 98 us -> 98.7 us (level)
  Pallas kernels: 59.5 us -> 52.5 us
  local copies, waits for them, and re-layouts: 0.03 us -> 4.41 us
  waiting for transfers between devices: 16.2 us -> 18.5 us
  starting transfers between devices: 21 us -> 22 us
    pallas_call x3, Pallas kernels: 25.3 us -> 18.6 us  [rates(): pl.pallas_call(kernel, grid_spec=pltpu.PrefetchScalarGridSpec(num_scalar_...]
    unnamed x10 -> x20, local copies, waits for them, and re-layouts: 0.03 us -> 4.41 us
    ppermute x6, waiting for transfers between devices: 3.43 us -> 5.47 us  [swap(): return lax.ppermute(x, 'feat', [(i, i ^ 2 ** bit) for i in range(n)])]
    ppermute x6, starting transfers between devices: 9.76 us -> 10.8 us  [swap(): return lax.ppermute(x, 'feat', [(i, i ^ 2 ** bit) for i in range(n)])]
  transfers between devices with their start and end apart: 27 -> 27, of which waited for: 13 -> 14; matrix products, arithmetic and copies ran while one was open for 0% -> 0% of each run, Pallas kernels for 55% -> 48%
where the time goes in v8:
time: 98.7 us; the launch traced here: 98.5 us
  Pallas kernels  52.5 us (53%)
  starting transfers between devices  22 us (22%)
  waiting for transfers between devices  18.5 us (19%)
  local copies, waits for them, and re-layouts  4.41 us (4%)
  between operations  1.09 us (1%)
    pallas_call x3, Pallas kernels, rates(): pl.pallas_call(kernel, grid_spec=pltpu.PrefetchScalarGridSpec(num_scalar_...  18.6 us
    pallas_call x6, Pallas kernels, owned_features(): pl.pallas_call(functools.partial(features_kernel, start, size), in_specs=...  12.9 us
    ppermute x6, starting transfers between devices, swap(): return lax.ppermute(x, 'feat', [(i, i ^ 2 ** bit) for i in range(n)])  10.8 us
    pallas_call x4, Pallas kernels, update(): pl.pallas_call(functools.partial(update_kernel, n, at), grid=(steps,), in...  9.96 us
    ppermute x7, waiting for transfers between devices, ring(): return lax.ppermute(x, axis, [(i, (i + distance) % n) for i in range(n)])  9.76 us
    ppermute x7, starting transfers between devices, ring(): return lax.ppermute(x, axis, [(i, (i + distance) % n) for i in range(n)])  8.81 us
    ppermute x6, waiting for transfers between devices, swap(): return lax.ppermute(x, 'feat', [(i, i ^ 2 ** bit) for i in range(n)])  5.47 us
    unnamed x20, local copies, waits for them, and re-layouts  4.41 us
  transfers between devices with their start and end apart: 27, of which 14 were waited for; matrix products, arithmetic and copies ran while one was open for 0% of the time, Pallas kernels for 48%

profile of v8, /device:TPU:0, one launch (start us, length us, event | category | flops | bytes accessed | tf_op | source)
XLA Modules:
  0.0 98.5 jit_solution(9775360512582943493)
XLA Ops:
  0.6 2.5 %chosen_points.1 = (bf16[1024,256]{1,0:T(8,128)(2,1)S(1)}, f32[8,128]{1,0:T(8,128)S(1)}) custom-call(s32[2,512]{1,0:T(2,128)} %picks.1, bf16[2048,256]{1,0:T(8,128)(2,1)} %points.1), custom_call_target="tpu_custom_call" | custom-call | flops 3000000000 | bytes 1024 | tf_op jit(solution)/shard_map/chosen_points/pallas_call | solution.py:70
  3.2 0.5 collective-permute-start.2
  3.7 2.6 %collective-permute-start.4 = (bf16[1024,256]{1,0:T(8,128)(2,1)S(1)}, bf16[1024,256]{1,0:T(8,128)(2,1)S(1)}, u32[]{:S(2)}, u32[]{:S(2)}) collective-permute-start(bf16[1024,256]{1,0:T(8,128)(2,1)S(1)} %get-tuple-element.71.refs_2_), channel_id=1, source_target_pairs={{0,8},{4,12},{8,0},{12,4},{1,9},{5,13},{9,1},{13,5},{2,10},{6,14},... | collective-permute-start | bytes 1572872 | tf_op jit(solution)/shard_map/ppermute | solution.py:436
  6.3 2.2 %copy-done.4 = bf16[256,8192]{1,0:T(8,128)(2,1)S(1)} copy-done((bf16[256,8192]{1,0:T(8,128)(2,1)S(1)}, bf16[256,8192]{1,0:T(8,128)(2,1)}, u32[]{:S(2)}) %copy-start.4) | copy-done | bytes 4194328
  8.5 2.2 %copy-done.6 = bf16[8192,256]{1,0:T(8,128)(2,1)S(1)} copy-done((bf16[8192,256]{1,0:T(8,128)(2,1)S(1)}, bf16[8192,256]{1,0:T(8,128)(2,1)}, u32[]{:S(2)}) %copy-start.6) | copy-done | bytes 4194328
  10.7 11.5 %partial_log_rates.3 = (bf16[640,2048]{1,0:T(8,128)(2,1)S(1)}, bf16[256,2048]{1,0:T(8,128)(2,1)S(1)}, f32[1,2048]{1,0:T(1,128)S(1)}, f32[320,256]{1,0:T(8,128)S(...) custom-call(s32[1]{0:T(128)} %bitcast.refs_0_.f, s32[1]{0:T(128)} %bitcast.1.refs_1_.p, ...), custom_call_target="tpu_custom_call" | custom-call | flops 12000000000 | bytes 1024 | tf_op jit(solution)/shard_map/partial_log_rates/pallas_call | solution.py:189
  22.2 1.6 %collective-permute-start = (bf16[320,256]{1,0:T(8,128)(2,1)S(1)}, bf16[320,256]{1,0:T(8,128)(2,1)S(1)}, u32[]{:S(2)}, u32[]{:S(2)}) collective-permute-start(bf16[320,256]{1,0:T(8,128)(2,1)S(1)} %get-tuple-element.76), channel_id=1, source_target_pairs={{0,1},{1,0},{2,3},{3,2},{4,5},{5,4},{6,7},{7,6},{8,9},{9,8},{10,11... | collective-permute-start | bytes 491528 | tf_op jit(solution)/shard_map/ppermute | solution.py:448
  23.9 3.3 %partial_log_rates.4 = (bf16[384,2048]{1,0:T(8,128)(2,1)S(1)}, f32[384,256]{1,0:T(8,128)S(1)}, f32[8,128]{1,0:T(8,128)S(1)}) custom-call(s32[1]{0:T(128)} %bitcast.refs_0_.f, s32[1]{0:T(128)} %bitcast.1.refs_1_.p, bf16[1024,256]{1,0:T(8,128)(2,1)S(1)} %get-tuple-element.71.refs_2_, bf16[256,8192]{1,0:T(8,128)(2,1)S(1)} %copy-done.5, f32[1,8192]{1,0:T(1,128)S(1)} %bitcast.8, ...), custom_call_target="tpu_custom_call" | custom-call | flops 6000000000 | bytes 1024 | tf_op jit(solution)/shard_map/partial_log_rates/pallas_call | solution.py:189
  27.2 1.4 %collective-permute-done.b = bf16[320,256]{1,0:T(8,128)(2,1)S(1)} collective-permute-done((bf16[320,256]{1,0:T(8,128)(2,1)S(1)}, bf16[320,256]{1,0:T(8,128)(2,1)S(1)}, u32[]{:S(2)}, u32[]{:S(2)}) %collective-permute-start) | collective-permute-done | bytes 163872 | tf_op jit(solution)/shard_map/ppermute | solution.py:448
  28.6 2.7 %collective-permute-start.5 = (bf16[320,256]{1,0:T(8,128)(2,1)S(1)}, bf16[320,256]{1,0:T(8,128)(2,1)S(1)}, u32[]{:S(2)}, u32[]{:S(2)}) collective-permute-start(bf16[320,256]{1,0:T(8,128)(2,1)S(1)} %get-tuple-element.86.a), channel_id=1, source_target_pairs={{0,2},{1,3},{2,0},{3,1},{4,6},{5,7},{6,4},{7,5},{8,10},{9,11},{10,... | collective-permute-start | bytes 491528 | tf_op jit(solution)/shard_map/ppermute | solution.py:448
  31.2 3.8 %partial_log_rates.5 = (f32[192,256]{1,0:T(8,128)S(1)}, bf16[192,256]{1,0:T(8,128)(2,1)S(1)}, f32[8,128]{1,0:T(8,128)S(1)}) custom-call(s32[1]{0:T(128)} %bitcast.refs_0_.f, s32[1]{0:T(128)} %bitcast.1.refs_1_.p, bf16[1024,256]{1,0:T(8,128)(2,1)S(1)} %get-tuple-element.71.refs_2_, bf16[256,8192]{1,0:T(8,128)(2,1)S(1)} %copy-done.5, f32[1,8192]{1,0:T(1,128)S(1)} %bitcast.9, ...), custom_call_target="tpu_custom_call" | custom-call | flops 6000000000 | bytes 1024 | tf_op jit(solution)/shard_map/partial_log_rates/pallas_call | solution.py:189
  35.1 1.6 %collective-permute-start.1 = (bf16[192,256]{1,0:T(8,128)(2,1)S(1)}, bf16[192,256]{1,0:T(8,128)(2,1)S(1)}, u32[]{:S(2)}, u32[]{:S(2)}) collective-permute-start(bf16[192,256]{1,0:T(8,128)(2,1)S(1)} %get-tuple-element.80), channel_id=1, source_target_pairs={{0,1},{1,0},{2,3},{3,2},{4,5},{5,4},{6,7},{7,6},{8,9},{9,8},{10,11... | collective-permute-start | bytes 294920 | tf_op jit(solution)/shard_map/ppermute | solution.py:448
  36.7 2.6 %owned_features.6 = (bf16[640,2048]{1,0:T(8,128)(2,1)S(1)}, f32[8,128]{1,0:T(8,128)S(1)}) custom-call(bf16[1024,256]{1,0:T(8,128)(2,1)S(1)} %collective-permute-done.2.chosen, bf16[256,2048]{1,0:T(8,128)(2,1)S(1)} %get-tuple-element.81.omega, f32[1,2048]{1,0:T(1,128)S(1)} %get-tuple-element.82.phase, f32[8,128]{1,0:T(8,128)S(1)} %get-tuple-element.83.refs_0_), custom_call_target="tpu_custom_call" | custom-call | flops 1000000000 | bytes 1024 | tf_op jit(solution)/shard_map/owned_features/pallas_call | solution.py:216
  39.3 1.3 %collective-permute-done.1.b = bf16[192,256]{1,0:T(8,128)(2,1)S(1)} collective-permute-done((bf16[192,256]{1,0:T(8,128)(2,1)S(1)}, bf16[192,256]{1,0:T(8,128)(2,1)S(1)}, u32[]{:S(2)}, u32[]{:S(2)}) %collective-permute-start.1) | collective-permute-done | bytes 98336 | tf_op jit(solution)/shard_map/ppermute | solution.py:448
  40.6 0.0 collective-permute-done.5.b
  40.7 0.8 collective-permute-start.8
  41.5 2.9 %collective-permute-start.3 = (bf16[192,256]{1,0:T(8,128)(2,1)S(1)}, bf16[192,256]{1,0:T(8,128)(2,1)S(1)}, u32[]{:S(2)}, u32[]{:S(2)}) collective-permute-start(bf16[192,256]{1,0:T(8,128)(2,1)S(1)} %get-tuple-element.85.a), channel_id=1, source_target_pairs={{0,2},{1,3},{2,0},{3,1},{4,6},{5,7},{6,4},{7,5},{8,10},{9,11},{10,... | collective-permute-start | bytes 294920 | tf_op jit(solution)/shard_map/ppermute | solution.py:448
  44.4 2.6 %owned_features.7 = (bf16[640,2048]{1,0:T(8,128)(2,1)S(1)}, f32[8,128]{1,0:T(8,128)S(1)}) custom-call(bf16[1024,256]{1,0:T(8,128)(2,1)S(1)} %collective-permute-done.4.chosen, bf16[256,2048]{1,0:T(8,128)(2,1)S(1)} %get-tuple-element.81.omega, f32[1,2048]{1,0:T(1,128)S(1)} %get-tuple-element.82.phase, f32[8,128]{1,0:T(8,128)S(1)} %get-tuple-element.88.refs_0_), custom_call_target="tpu_custom_call" | custom-call | flops 1000000000 | bytes 1024 | tf_op jit(solution)/shard_map/owned_features/pallas_call | solution.py:216
  46.9 0.6 collective-permute-done.3.b
  47.6 1.3 %collective-permute-done.8.refs_1_ = bf16[320,256]{1,0:T(8,128)(2,1)S(1)} collective-permute-done((bf16[320,256]{1,0:T(8,128)(2,1)S(1)}, bf16[320,256]{1,0:T(8,128)(2,1)S(1)}, u32[]{:S(2)}, u32[]{:S(2)}) %collective-permute-start.8) | collective-permute-done | bytes 163872 | tf_op jit(solution)/shard_map/ppermute | solution.py:448
  48.9 1.0 %residuals.2 = (f32[1024,256]{1,0:T(8,128)}, bf16[256,640]{1,0:T(8,128)(2,1)S(1)}, f32[8,128]{1,0:T(8,128)S(1)}) custom-call(s32[1]{0:T(128)} %bitcast.refs_0_.f, bf16[320,256]{1,0:T(8,128)(2,1)S(1)} %get-tuple-element.91.refs_0_, bf16[320,256]{1,0:T(8,128)(2,1)S(1)} %collective-permute-done.8.refs_1_, s32[1024,256]{1,0:T(8,128)S(1)} %bitcast.5, ...), custom_call_target="tpu_custom_call" | custom-call | flops 1000000000 | bytes 1024 | tf_op jit(solution)/shard_map/residuals/pallas_call | solution.py:294
  50.0 0.8 collective-permute-start.9
  50.8 1.2 %collective-permute-start.6 = (bf16[192,256]{1,0:T(8,128)(2,1)S(1)}, bf16[192,256]{1,0:T(8,128)(2,1)S(1)}, u32[]{:S(2)}, u32[]{:S(2)}) collective-permute-start(bf16[192,256]{1,0:T(8,128)(2,1)S(1)} %get-tuple-element.90.refs_0_), channel_id=1, source_target_pairs={{0,1},{1,0},{2,3},{3,2},{4,5},{5,4},{6,7},{7,6},{8,9},{9,8},{10,11... | collective-permute-start | bytes 294920 | tf_op jit(solution)/shard_map/ppermute | solution.py:448
  52.0 0.0 collective-permute-done.7.chosen
  52.0 2.6 %owned_features.8 = (bf16[640,2048]{1,0:T(8,128)(2,1)S(1)}, f32[8,128]{1,0:T(8,128)S(1)}) custom-call(bf16[1024,256]{1,0:T(8,128)(2,1)S(1)} %collective-permute-done.7.chosen, bf16[256,2048]{1,0:T(8,128)(2,1)S(1)} %get-tuple-element.81.omega, f32[1,2048]{1,0:T(1,128)S(1)} %get-tuple-element.82.phase, f32[8,128]{1,0:T(8,128)S(1)} %get-tuple-element.93.refs_0_), custom_call_target="tpu_custom_call" | custom-call | flops 1000000000 | bytes 1024 | tf_op jit(solution)/shard_map/owned_features/pallas_call | solution.py:216
  54.6 0.8 collective-permute-done.6.refs_1_
  55.4 0.9 residuals.3
  56.3 1.4 %collective-permute-start.11 = (bf16[256,384]{1,0:T(8,128)(2,1)S(1)}, bf16[256,384]{1,0:T(8,128)(2,1)S(1)}, u32[]{:S(2)}, u32[]{:S(2)}) collective-permute-start(bf16[256,384]{1,0:T(8,128)(2,1)S(1)} %get-tuple-element.106.refs_4_), channel_id=1, source_target_pairs={{0,8},{4,12},{8,0},{12,4},{1,9},{5,13},{9,1},{13,5},{2,10},{6,14},... | collective-permute-start | bytes 589832 | tf_op jit(solution)/shard_map/ppermute | solution.py:436
  57.7 0.0 collective-permute-start.13
  57.7 1.6 %owned_features.9 = (bf16[384,2048]{1,0:T(8,128)(2,1)S(1)}, f32[8,128]{1,0:T(8,128)S(1)}) custom-call(bf16[1024,256]{1,0:T(8,128)(2,1)S(1)} %collective-permute-done.2.chosen, bf16[256,2048]{1,0:T(8,128)(2,1)S(1)} %get-tuple-element.81.omega, f32[1,2048]{1,0:T(1,128)S(1)} %get-tuple-element.82.phase, f32[8,128]{1,0:T(8,128)S(1)} %get-tuple-element.98.refs_0_), custom_call_target="tpu_custom_call" | custom-call | flops 100000000 | bytes 1024 | tf_op jit(solution)/shard_map/owned_features/pallas_call | solution.py:216
  59.3 1.9 %owned_features.10 = (bf16[384,2048]{1,0:T(8,128)(2,1)S(1)}, f32[8,128]{1,0:T(8,128)S(1)}) custom-call(bf16[1024,256]{1,0:T(8,128)(2,1)S(1)} %collective-permute-done.4.chosen, bf16[256,2048]{1,0:T(8,128)(2,1)S(1)} %get-tuple-element.81.omega, f32[1,2048]{1,0:T(1,128)S(1)} %get-tuple-element.82.phase, f32[8,128]{1,0:T(8,128)S(1)} %get-tuple-element.100.refs_0_), custom_call_target="tpu_custom_call" | custom-call | flops 100000000 | bytes 1024 | tf_op jit(solution)/shard_map/owned_features/pallas_call | solution.py:216
  61.2 0.0 collective-permute-done.9.refs_6_
  61.2 0.6 collective-permute-start.14
  61.8 0.1 collective-permute-start.10
  61.9 1.6 %owned_features.11 = (bf16[384,2048]{1,0:T(8,128)(2,1)S(1)}, f32[8,128]{1,0:T(8,128)S(1)}) custom-call(bf16[1024,256]{1,0:T(8,128)(2,1)S(1)} %collective-permute-done.7.chosen, bf16[256,2048]{1,0:T(8,128)(2,1)S(1)} %get-tuple-element.81.omega, f32[1,2048]{1,0:T(1,128)S(1)} %get-tuple-element.82.phase, f32[8,128]{1,0:T(8,128)S(1)} %get-tuple-element.104.refs_0_), custom_call_target="tpu_custom_call" | custom-call | flops 100000000 | bytes 1024 | tf_op jit(solution)/shard_map/owned_features/pallas_call | solution.py:216
  63.5 0.0 collective-permute-done.11.refs_6_
  63.5 0.5 collective-permute-start.12
  64.0 0.0 copy-start.1
  64.1 0.0 copy-start.2
  64.1 0.0 copy-start.3
  64.1 3.6 %first_part.1 = (f32[2048,256]{1,0:T(8,128)S(1)}, f32[8,128]{1,0:T(8,128)S(1)}) custom-call(bf16[640,2048]{1,0:T(8,128)(2,1)S(1)} %get-tuple-element.109.refs_0_, bf16[640,2048]{1,0:T(8,128)(2,1)S(1)} %get-tuple-element.110.refs_1_, bf16[640,2048]{1,0:T(8,128)(2,1)S(1)} %get-tuple-element.111.refs_2_, bf16[640,2048]{1,0:T(8,128)(2,1)S(1)} %get-tuple-element.112.refs_3_, ...), custom_call_target="tpu_custom_call" | custom-call | flops 300000000 | bytes 1024 | tf_op jit(solution)/shard_map/first_part/pallas_call | solution.py:336
  67.7 0.0 collective-permute-done.10.refs_5_
  67.7 1.7 %update.4 = (f32[1,2048,256]{2,1,0:T(8,128)}, f32[1,2048,256]{2,1,0:T(8,128)}, f32[1,2048,256]{2,1,0:T(8,128)}, bf16[256,256]{1,0:T(8,128)(2,1)S(1)}) custom-call(bf16[384,2048]{1,0:T(8,128)(2,1)S(1)} %get-tuple-element.97.refs_0_, bf16[384,2048]{1,0:T(8,128)(2,1)S(1)} %get-tuple-element.99.refs_1_, bf16[384,2048]{1,0:T(8,128)(2,1)S(1)} %get-tuple-element.101.refs_2_, ...), custom_call_target="tpu_custom_call" | custom-call | flops 4000000000 | bytes 1024 | tf_op jit(solution)/shard_map/update/pallas_call | solution.py:384
  69.4 0.7 collective-permute-start.15
  70.1 2.5 %update.5 = (f32[1,2048,256]{2,1,0:T(8,128)}, f32[1,2048,256]{2,1,0:T(8,128)}, f32[1,2048,256]{2,1,0:T(8,128)}, bf16[512,256]{1,0:T(8,128)(2,1)S(1)}) custom-call(bf16[384,2048]{1,0:T(8,128)(2,1)S(1)} %get-tuple-element.97.refs_0_, bf16[384,2048]{1,0:T(8,128)(2,1)S(1)} %get-tuple-element.99.refs_1_, ...), custom_call_target="tpu_custom_call", output_to_operand_aliasing={{0}: (13, {}), {1}: (14, {}), {2}: (15, {})} | custom-call | flops 4000000000 | bytes 1024 | tf_op jit(solution)/shard_map/update/pallas_call | solution.py:384
  72.6 1.3 %collective-permute-start.16 = (bf16[512,256]{1,0:T(8,128)(2,1)S(1)}, bf16[512,256]{1,0:T(8,128)(2,1)S(1)}, u32[]{:S(2)}, u32[]{:S(2)}) collective-permute-start(bf16[512,256]{1,0:T(8,128)(2,1)S(1)} %get-tuple-element.127.refs_4_), channel_id=1, source_target_pairs={{0,8},{4,12},{8,0},{12,4},{1,9},{5,13},{9,1},{13,5},{2,10},{6,14},... | collective-permute-start | bytes 786440 | tf_op jit(solution)/shard_map/ppermute | solution.py:436
  73.9 1.0 collective-permute-done.15.refs_17_.refs_2_
  74.9 2.5 %update.6 = (f32[1,2048,256]{2,1,0:T(8,128)}, f32[1,2048,256]{2,1,0:T(8,128)}, f32[1,2048,256]{2,1,0:T(8,128)}, bf16[512,256]{1,0:T(8,128)(2,1)S(1)}) custom-call(bf16[384,2048]{1,0:T(8,128)(2,1)S(1)} %get-tuple-element.97.refs_0_, bf16[384,2048]{1,0:T(8,128)(2,1)S(1)} %get-tuple-element.99.refs_1_, ...), custom_call_target="tpu_custom_call", output_to_operand_aliasing={{0}: (13, {}), {1}: (14, {}), {2}: (15, {})} | custom-call | flops 4000000000 | bytes 1024 | tf_op jit(solution)/shard_map/update/pallas_call | solution.py:384
  77.4 0.7 collective-permute-start.24
  78.1 3.6 %collective-permute-done.16.refs_17_.refs_6_ = bf16[512,256]{1,0:T(8,128)(2,1)S(1)} collective-permute-done((bf16[512,256]{1,0:T(8,128)(2,1)S(1)}, bf16[512,256]{1,0:T(8,128)(2,1)S(1)}, u32[]{:S(2)}, u32[]{:S(2)}) %collective-permute-start.16) | collective-permute-done | bytes 262176 | tf_op jit(solution)/shard_map/ppermute | solution.py:436
  81.7 3.3 %update.7 = (f32[1,2048,256]{2,1,0:T(8,128)}, f32[1,2048,256]{2,1,0:T(8,128)}, f32[1,2048,256]{2,1,0:T(8,128)}, bf16[768,256]{1,0:T(8,128)(2,1)S(1)}) custom-call(bf16[384,2048]{1,0:T(8,128)(2,1)S(1)} %get-tuple-element.97.refs_0_, bf16[384,2048]{1,0:T(8,128)(2,1)S(1)} %get-tuple-element.99.refs_1_, ...), custom_call_target="tpu_custom_call", output_to_operand_aliasing={{0}: (13, {}), {1}: (14, {}), {2}: (15, {})} | custom-call | flops 4000000000 | bytes 1024 | tf_op jit(solution)/shard_map/update/pallas_call | solution.py:384
  85.0 1.3 %collective-permute-start.18 = (bf16[768,256]{1,0:T(8,128)(2,1)S(1)}, bf16[768,256]{1,0:T(8,128)(2,1)S(1)}, u32[]{:S(2)}, u32[]{:S(2)}) collective-permute-start(bf16[768,256]{1,0:T(8,128)(2,1)S(1)} %get-tuple-element.131.refs_0_), channel_id=1, source_target_pairs={{0,8},{4,12},{8,0},{12,4},{1,9},{5,13},{9,1},{13,5},{2,10},{6,14},... | collective-permute-start | bytes 1179656 | tf_op jit(solution)/shard_map/ppermute | solution.py:436
  86.3 0.6 collective-permute-done.24.refs_10_
  86.9 0.5 collective-permute-start.22
  87.5 0.1 collective-permute-start.25
  87.5 0.4 collective-permute-done.21.refs_5_
  87.9 0.1 collective-permute-start.17
  88.0 0.5 collective-permute-done.23.refs_9_
  88.5 0.4 collective-permute-done.22.refs_7_
  88.9 0.4 collective-permute-done.25.refs_11_
  89.2 1.6 %put_rows.2.refs_4_ = bf16[8192,256]{1,0:T(8,128)(2,1)} custom-call(s32[1]{0:T(128)} %bitcast.1.refs_1_.p, bf16[256,256]{1,0:T(8,128)(2,1)S(1)} %get-tuple-element.123.refs_0_, bf16[256,256]{1,0:T(8,128)(2,1)S(1)} %collective-permute-done.19.refs_1_, bf16[256,256]{1,0:T(8,128)(2,1)S(1)} %collective-permute-done.15.refs_17_.refs_2_, ...), custom_call_target="tpu_custom_call" | custom-call | flops 10000000 | bytes 1024 | tf_op jit(solution)/shard_map/put_rows/pallas_call | solution.py:418
  90.8 4.6 %collective-permute-done.18.refs_2_ = bf16[768,256]{1,0:T(8,128)(2,1)S(1)} collective-permute-done((bf16[768,256]{1,0:T(8,128)(2,1)S(1)}, bf16[768,256]{1,0:T(8,128)(2,1)S(1)}, u32[]{:S(2)}, u32[]{:S(2)}) %collective-permute-start.18) | collective-permute-done | bytes 393248 | tf_op jit(solution)/shard_map/ppermute | solution.py:436
  95.4 1.7 %collective-permute-done.26.refs_3_ = bf16[768,256]{1,0:T(8,128)(2,1)S(1)} collective-permute-done((bf16[768,256]{1,0:T(8,128)(2,1)S(1)}, bf16[768,256]{1,0:T(8,128)(2,1)S(1)}, u32[]{:S(2)}, u32[]{:S(2)}) %collective-permute-start.26) | collective-permute-done | bytes 393248 | tf_op jit(solution)/shard_map/ppermute | solution.py:440
  97.1 1.2 %put_rows.3 = bf16[8192,256]{1,0:T(8,128)(2,1)} custom-call(s32[1]{0:T(128)} %bitcast.1.refs_1_.p, bf16[768,256]{1,0:T(8,128)(2,1)S(1)} %get-tuple-element.131.refs_0_, bf16[768,256]{1,0:T(8,128)(2,1)S(1)} %collective-permute-done.17.refs_1_, bf16[768,256]{1,0:T(8,128)(2,1)S(1)} %collective-permute-done.18.refs_2_, ...), custom_call_target="tpu_custom_call", output_to_operand_aliasing={{}: (5, {})} | custom-call | flops 10000000 | bytes 1024 | tf_op jit(solution)/shard_map/put_rows/pallas_call | solution.py:418
  (33 shorter events, 0.2 us)
Async XLA Ops:
  0.6 5.7 %copy-start.9 = (f32[8192]{0:T(1024)S(1)}, f32[8192]{0:T(1024)}, u32[]{:S(2)}) copy-start(f32[8192]{0:T(1024)} %param.13) | copy-start | bytes 98308
  3.2 33.5 %collective-permute-start.2 = (bf16[1024,256]{1,0:T(8,128)(2,1)S(1)}, bf16[1024,256]{1,0:T(8,128)(2,1)S(1)}, u32[]{:S(2)}, u32[]{:S(2)}) collective-permute-start(bf16[1024,256]{1,0:T(8,128)(2,1)S(1)} %get-tuple-element.71.refs_2_), channel_id=1, source_target_pairs={{0,4},{4,0},{8,12},{12,8},{1,5},{5,1},{9,13},{13,9},{2,6},{6,2},{1... | collective-permute-start | bytes 1572872 | tf_op jit(solution)/shard_map/ppermute | solution.py:440
  3.7 33.0 %collective-permute-start.4 = (bf16[1024,256]{1,0:T(8,128)(2,1)S(1)}, bf16[1024,256]{1,0:T(8,128)(2,1)S(1)}, u32[]{:S(2)}, u32[]{:S(2)}) collective-permute-start(bf16[1024,256]{1,0:T(8,128)(2,1)S(1)} %get-tuple-element.71.refs_2_), channel_id=1, source_target_pairs={{0,8},{4,12},{8,0},{12,4},{1,9},{5,13},{9,1},{13,5},{2,10},{6,14},... | collective-permute-start | bytes 1572872 | tf_op jit(solution)/shard_map/ppermute | solution.py:436
  6.3 2.2 %copy-start.4 = (bf16[256,8192]{1,0:T(8,128)(2,1)S(1)}, bf16[256,8192]{1,0:T(8,128)(2,1)}, u32[]{:S(2)}) copy-start(bf16[256,8192]{1,0:T(8,128)(2,1)} %refs_3_.5) | copy-start | bytes 12582916
  8.5 2.2 %copy-start.6 = (bf16[8192,256]{1,0:T(8,128)(2,1)S(1)}, bf16[8192,256]{1,0:T(8,128)(2,1)}, u32[]{:S(2)}) copy-start(bf16[8192,256]{1,0:T(8,128)(2,1)} %refs_5_.5) | copy-start | bytes 12582916
  10.7 13.2 %copy-start.5 = (bf16[256,8192]{1,0:T(8,128)(2,1)S(1)}, bf16[256,8192]{1,0:T(8,128)(2,1)}, u32[]{:S(2)}) copy-start(bf16[256,8192]{1,0:T(8,128)(2,1)} %refs_3_.5) | copy-start | bytes 12582916
  10.7 13.2 %copy-start.7 = (bf16[8192,256]{1,0:T(8,128)(2,1)S(1)}, bf16[8192,256]{1,0:T(8,128)(2,1)}, u32[]{:S(2)}) copy-start(bf16[8192,256]{1,0:T(8,128)(2,1)} %refs_5_.5) | copy-start | bytes 12582916
  22.2 6.3 %collective-permute-start = (bf16[320,256]{1,0:T(8,128)(2,1)S(1)}, bf16[320,256]{1,0:T(8,128)(2,1)S(1)}, u32[]{:S(2)}, u32[]{:S(2)}) collective-permute-start(bf16[320,256]{1,0:T(8,128)(2,1)S(1)} %get-tuple-element.76), channel_id=1, source_target_pairs={{0,1},{1,0},{2,3},{3,2},{4,5},{5,4},{6,7},{7,6},{8,9},{9,8},{10,11... | collective-permute-start | bytes 491528 | tf_op jit(solution)/shard_map/ppermute | solution.py:448
  28.6 12.1 %collective-permute-start.5 = (bf16[320,256]{1,0:T(8,128)(2,1)S(1)}, bf16[320,256]{1,0:T(8,128)(2,1)S(1)}, u32[]{:S(2)}, u32[]{:S(2)}) collective-permute-start(bf16[320,256]{1,0:T(8,128)(2,1)S(1)} %get-tuple-element.86.a), channel_id=1, source_target_pairs={{0,2},{1,3},{2,0},{3,1},{4,6},{5,7},{6,4},{7,5},{8,10},{9,11},{10,... | collective-permute-start | bytes 491528 | tf_op jit(solution)/shard_map/ppermute | solution.py:448
  35.1 5.6 %collective-permute-start.1 = (bf16[192,256]{1,0:T(8,128)(2,1)S(1)}, bf16[192,256]{1,0:T(8,128)(2,1)S(1)}, u32[]{:S(2)}, u32[]{:S(2)}) collective-permute-start(bf16[192,256]{1,0:T(8,128)(2,1)S(1)} %get-tuple-element.80), channel_id=1, source_target_pairs={{0,1},{1,0},{2,3},{3,2},{4,5},{5,4},{6,7},{7,6},{8,9},{9,8},{10,11... | collective-permute-start | bytes 294920 | tf_op jit(solution)/shard_map/ppermute | solution.py:448
  36.7 15.3 %collective-permute-start.7 = (bf16[1024,256]{1,0:T(8,128)(2,1)S(1)}, bf16[1024,256]{1,0:T(8,128)(2,1)S(1)}, u32[]{:S(2)}, u32[]{:S(2)}) collective-permute-start(bf16[1024,256]{1,0:T(8,128)(2,1)S(1)} %collective-permute-done.4.chosen), channel_id=1, source_target_pairs={{0,4},{4,0},{8,12},{12,8},{1,5},{5,1},{9,13},{13,9},{2,6},{6,2},{1... | collective-permute-start | bytes 1572872 | tf_op jit(solution)/shard_map/ppermute | solution.py:440
  40.7 8.2 %collective-permute-start.8 = (bf16[320,256]{1,0:T(8,128)(2,1)S(1)}, bf16[320,256]{1,0:T(8,128)(2,1)S(1)}, u32[]{:S(2)}, u32[]{:S(2)}) collective-permute-start(bf16[320,256]{1,0:T(8,128)(2,1)S(1)} %get-tuple-element.91.refs_0_), channel_id=1, source_target_pairs={{0,1},{1,0},{2,3},{3,2},{4,5},{5,4},{6,7},{7,6},{8,9},{9,8},{10,11... | collective-permute-start | bytes 491528 | tf_op jit(solution)/shard_map/ppermute | solution.py:448
  41.5 6.1 %collective-permute-start.3 = (bf16[192,256]{1,0:T(8,128)(2,1)S(1)}, bf16[192,256]{1,0:T(8,128)(2,1)S(1)}, u32[]{:S(2)}, u32[]{:S(2)}) collective-permute-start(bf16[192,256]{1,0:T(8,128)(2,1)S(1)} %get-tuple-element.85.a), channel_id=1, source_target_pairs={{0,2},{1,3},{2,0},{3,1},{4,6},{5,7},{6,4},{7,5},{8,10},{9,11},{10,... | collective-permute-start | bytes 294920 | tf_op jit(solution)/shard_map/ppermute | solution.py:448
  44.3 4.6 %copy-start.8 = (s32[2,512,256]{2,1,0:T(8,128)S(1)}, s32[2,512,256]{2,1,0:T(8,128)}, u32[]{:S(2)}) copy-start(s32[2,512,256]{2,1,0:T(8,128)} %param.15) | copy-start | bytes 3145732
  50.0 11.2 %collective-permute-start.9 = (bf16[256,640]{1,0:T(8,128)(2,1)S(1)}, bf16[256,640]{1,0:T(8,128)(2,1)S(1)}, u32[]{:S(2)}, u32[]{:S(2)}) collective-permute-start(bf16[256,640]{1,0:T(8,128)(2,1)S(1)} %get-tuple-element.102.refs_4_), channel_id=1, source_target_pairs={{0,8},{4,12},{8,0},{12,4},{1,9},{5,13},{9,1},{13,5},{2,10},{6,14},... | collective-permute-start | bytes 983048 | tf_op jit(solution)/shard_map/ppermute | solution.py:436
  50.8 4.6 %collective-permute-start.6 = (bf16[192,256]{1,0:T(8,128)(2,1)S(1)}, bf16[192,256]{1,0:T(8,128)(2,1)S(1)}, u32[]{:S(2)}, u32[]{:S(2)}) collective-permute-start(bf16[192,256]{1,0:T(8,128)(2,1)S(1)} %get-tuple-element.90.refs_0_), channel_id=1, source_target_pairs={{0,1},{1,0},{2,3},{3,2},{4,5},{5,4},{6,7},{7,6},{8,9},{9,8},{10,11... | collective-permute-start | bytes 294920 | tf_op jit(solution)/shard_map/ppermute | solution.py:448
  56.3 7.2 %collective-permute-start.11 = (bf16[256,384]{1,0:T(8,128)(2,1)S(1)}, bf16[256,384]{1,0:T(8,128)(2,1)S(1)}, u32[]{:S(2)}, u32[]{:S(2)}) collective-permute-start(bf16[256,384]{1,0:T(8,128)(2,1)S(1)} %get-tuple-element.106.refs_4_), channel_id=1, source_target_pairs={{0,8},{4,12},{8,0},{12,4},{1,9},{5,13},{9,1},{13,5},{2,10},{6,14},... | collective-permute-start | bytes 589832 | tf_op jit(solution)/shard_map/ppermute | solution.py:436
  57.7 6.4 %collective-permute-start.13 = (bf16[256,640]{1,0:T(8,128)(2,1)S(1)}, bf16[256,640]{1,0:T(8,128)(2,1)S(1)}, u32[]{:S(2)}, u32[]{:S(2)}) collective-permute-start(bf16[256,640]{1,0:T(8,128)(2,1)S(1)} %get-tuple-element.102.refs_4_), channel_id=1, source_target_pairs={{0,4},{4,0},{8,12},{12,8},{1,5},{5,1},{9,13},{13,9},{2,6},{6,2},{1... | collective-permute-start | bytes 983048 | tf_op jit(solution)/shard_map/ppermute | solution.py:440
  57.7 6.4 %copy-start = (f32[1,2048,256]{2,1,0:T(8,128)S(1)}, f32[1,2048,256]{2,1,0:T(8,128)}, u32[]{:S(2)}) copy-start(f32[1,2048,256]{2,1,0:T(8,128)} %refs_10_.7) | copy-start | bytes 6291460
  61.2 2.8 %collective-permute-start.14 = (bf16[256,640]{1,0:T(8,128)(2,1)S(1)}, bf16[256,640]{1,0:T(8,128)(2,1)S(1)}, u32[]{:S(2)}, u32[]{:S(2)}) collective-permute-start(bf16[256,640]{1,0:T(8,128)(2,1)S(1)} %collective-permute-done.9.refs_6_), channel_id=1, source_target_pairs={{0,4},{4,0},{8,12},{12,8},{1,5},{5,1},{9,13},{13,9},{2,6},{6,2},{1... | collective-permute-start | bytes 983048 | tf_op jit(solution)/shard_map/ppermute | solution.py:440
  61.8 5.9 %collective-permute-start.10 = (bf16[256,384]{1,0:T(8,128)(2,1)S(1)}, bf16[256,384]{1,0:T(8,128)(2,1)S(1)}, u32[]{:S(2)}, u32[]{:S(2)}) collective-permute-start(bf16[256,384]{1,0:T(8,128)(2,1)S(1)} %get-tuple-element.106.refs_4_), channel_id=1, source_target_pairs={{0,4},{4,0},{8,12},{12,8},{1,5},{5,1},{9,13},{13,9},{2,6},{6,2},{1... | collective-permute-start | bytes 589832 | tf_op jit(solution)/shard_map/ppermute | solution.py:440
  63.5 4.2 %collective-permute-start.12 = (bf16[256,384]{1,0:T(8,128)(2,1)S(1)}, bf16[256,384]{1,0:T(8,128)(2,1)S(1)}, u32[]{:S(2)}, u32[]{:S(2)}) collective-permute-start(bf16[256,384]{1,0:T(8,128)(2,1)S(1)} %collective-permute-done.11.refs_6_), channel_id=1, source_target_pairs={{0,4},{4,0},{8,12},{12,8},{1,5},{5,1},{9,13},{13,9},{2,6},{6,2},{1... | collective-permute-start | bytes 589832 | tf_op jit(solution)/shard_map/ppermute | solution.py:440
  64.0 3.7 %copy-start.1 = (f32[1,2048,256]{2,1,0:T(8,128)S(1)}, f32[1,2048,256]{2,1,0:T(8,128)}, u32[]{:S(2)}) copy-start(f32[1,2048,256]{2,1,0:T(8,128)} %refs_11_.7) | copy-start | bytes 6291460
  64.1 3.7 %copy-start.2 = (f32[1,2048,256]{2,1,0:T(8,128)S(1)}, f32[1,2048,256]{2,1,0:T(8,128)}, u32[]{:S(2)}) copy-start(f32[1,2048,256]{2,1,0:T(8,128)} %refs_12_.7) | copy-start | bytes 6291460
  64.1 3.7 %copy-start.3 = (bf16[256,256]{1,0:T(8,128)(2,1)S(1)}, bf16[256,256]{1,0:T(8,128)(2,1)}, u32[]{:S(2)}) copy-start(bf16[256,256]{1,0:T(8,128)(2,1)} %refs_9_.7) | copy-start | bytes 393220
  69.4 5.5 %collective-permute-start.15 = (bf16[256,256]{1,0:T(8,128)(2,1)S(1)}, bf16[256,256]{1,0:T(8,128)(2,1)S(1)}, u32[]{:S(2)}, u32[]{:S(2)}) collective-permute-start(bf16[256,256]{1,0:T(8,128)(2,1)S(1)} %get-tuple-element.123.refs_0_), channel_id=1, source_target_pairs={{0,8},{4,12},{8,0},{12,4},{1,9},{5,13},{9,1},{13,5},{2,10},{6,14},... | collective-permute-start | bytes 393224 | tf_op jit(solution)/shard_map/ppermute | solution.py:436
  70.1 16.8 %collective-permute-start.19 = (bf16[256,256]{1,0:T(8,128)(2,1)S(1)}, bf16[256,256]{1,0:T(8,128)(2,1)S(1)}, u32[]{:S(2)}, u32[]{:S(2)}) collective-permute-start(bf16[256,256]{1,0:T(8,128)(2,1)S(1)} %get-tuple-element.123.refs_0_), channel_id=1, source_target_pairs={{0,4},{4,0},{8,12},{12,8},{1,5},{5,1},{9,13},{13,9},{2,6},{6,2},{1... | collective-permute-start | bytes 393224 | tf_op jit(solution)/shard_map/ppermute | solution.py:440
  72.6 9.1 %collective-permute-start.16 = (bf16[512,256]{1,0:T(8,128)(2,1)S(1)}, bf16[512,256]{1,0:T(8,128)(2,1)S(1)}, u32[]{:S(2)}, u32[]{:S(2)}) collective-permute-start(bf16[512,256]{1,0:T(8,128)(2,1)S(1)} %get-tuple-element.127.refs_4_), channel_id=1, source_target_pairs={{0,8},{4,12},{8,0},{12,4},{1,9},{5,13},{9,1},{13,5},{2,10},{6,14},... | collective-permute-start | bytes 786440 | tf_op jit(solution)/shard_map/ppermute | solution.py:436
  77.4 9.6 %collective-permute-start.24 = (bf16[512,256]{1,0:T(8,128)(2,1)S(1)}, bf16[512,256]{1,0:T(8,128)(2,1)S(1)}, u32[]{:S(2)}, u32[]{:S(2)}) collective-permute-start(bf16[512,256]{1,0:T(8,128)(2,1)S(1)} %get-tuple-element.133.refs_8_), channel_id=1, source_target_pairs={{0,8},{4,12},{8,0},{12,4},{1,9},{5,13},{9,1},{13,5},{2,10},{6,14},... | collective-permute-start | bytes 786440 | tf_op jit(solution)/shard_map/ppermute | solution.py:436
  78.1 9.4 %collective-permute-start.20 = (bf16[256,256]{1,0:T(8,128)(2,1)S(1)}, bf16[256,256]{1,0:T(8,128)(2,1)S(1)}, u32[]{:S(2)}, u32[]{:S(2)}) collective-permute-start(bf16[256,256]{1,0:T(8,128)(2,1)S(1)} %collective-permute-done.15.refs_17_.refs_2_), channel_id=1, source_target_pairs={{0,4},{4,0},{8,12},{12,8},{1,5},{5,1},{9,13},{13,9},{2,6},{6,2},{1... | collective-permute-start | bytes 393224 | tf_op jit(solution)/shard_map/ppermute | solution.py:440
  85.0 10.4 %collective-permute-start.18 = (bf16[768,256]{1,0:T(8,128)(2,1)S(1)}, bf16[768,256]{1,0:T(8,128)(2,1)S(1)}, u32[]{:S(2)}, u32[]{:S(2)}) collective-permute-start(bf16[768,256]{1,0:T(8,128)(2,1)S(1)} %get-tuple-element.131.refs_0_), channel_id=1, source_target_pairs={{0,8},{4,12},{8,0},{12,4},{1,9},{5,13},{9,1},{13,5},{2,10},{6,14},... | collective-permute-start | bytes 1179656 | tf_op jit(solution)/shard_map/ppermute | solution.py:436
  86.3 1.5 %collective-permute-start.21 = (bf16[512,256]{1,0:T(8,128)(2,1)S(1)}, bf16[512,256]{1,0:T(8,128)(2,1)S(1)}, u32[]{:S(2)}, u32[]{:S(2)}) collective-permute-start(bf16[512,256]{1,0:T(8,128)(2,1)S(1)} %get-tuple-element.127.refs_4_), channel_id=1, source_target_pairs={{0,4},{4,0},{8,12},{12,8},{1,5},{5,1},{9,13},{13,9},{2,6},{6,2},{1... | collective-permute-start | bytes 786440 | tf_op jit(solution)/shard_map/ppermute | solution.py:440
  86.9 1.5 %collective-permute-start.23 = (bf16[512,256]{1,0:T(8,128)(2,1)S(1)}, bf16[512,256]{1,0:T(8,128)(2,1)S(1)}, u32[]{:S(2)}, u32[]{:S(2)}) collective-permute-start(bf16[512,256]{1,0:T(8,128)(2,1)S(1)} %get-tuple-element.133.refs_8_), channel_id=1, source_target_pairs={{0,4},{4,0},{8,12},{12,8},{1,5},{5,1},{9,13},{13,9},{2,6},{6,2},{1... | collective-permute-start | bytes 786440 | tf_op jit(solution)/shard_map/ppermute | solution.py:440
  86.9 1.9 %collective-permute-start.22 = (bf16[512,256]{1,0:T(8,128)(2,1)S(1)}, bf16[512,256]{1,0:T(8,128)(2,1)S(1)}, u32[]{:S(2)}, u32[]{:S(2)}) collective-permute-start(bf16[512,256]{1,0:T(8,128)(2,1)S(1)} %collective-permute-done.16.refs_17_.refs_6_), channel_id=1, source_target_pairs={{0,4},{4,0},{8,12},{12,8},{1,5},{5,1},{9,13},{13,9},{2,6},{6,2},{1... | collective-permute-start | bytes 786440 | tf_op jit(solution)/shard_map/ppermute | solution.py:440
  87.5 1.8 %collective-permute-start.25 = (bf16[512,256]{1,0:T(8,128)(2,1)S(1)}, bf16[512,256]{1,0:T(8,128)(2,1)S(1)}, u32[]{:S(2)}, u32[]{:S(2)}) collective-permute-start(bf16[512,256]{1,0:T(8,128)(2,1)S(1)} %collective-permute-done.24.refs_10_), channel_id=1, source_target_pairs={{0,4},{4,0},{8,12},{12,8},{1,5},{5,1},{9,13},{13,9},{2,6},{6,2},{1... | collective-permute-start | bytes 786440 | tf_op jit(solution)/shard_map/ppermute | solution.py:440
  87.9 7.5 %collective-permute-start.17 = (bf16[768,256]{1,0:T(8,128)(2,1)S(1)}, bf16[768,256]{1,0:T(8,128)(2,1)S(1)}, u32[]{:S(2)}, u32[]{:S(2)}) collective-permute-start(bf16[768,256]{1,0:T(8,128)(2,1)S(1)} %get-tuple-element.131.refs_0_), channel_id=1, source_target_pairs={{0,4},{4,0},{8,12},{12,8},{1,5},{5,1},{9,13},{13,9},{2,6},{6,2},{1... | collective-permute-start | bytes 1179656 | tf_op jit(solution)/shard_map/ppermute | solution.py:440
  95.4 1.7 %collective-permute-start.26 = (bf16[768,256]{1,0:T(8,128)(2,1)S(1)}, bf16[768,256]{1,0:T(8,128)(2,1)S(1)}, u32[]{:S(2)}, u32[]{:S(2)}) collective-permute-start(bf16[768,256]{1,0:T(8,128)(2,1)S(1)} %collective-permute-done.18.refs_2_), channel_id=1, source_target_pairs={{0,4},{4,0},{8,12},{12,8},{1,5},{5,1},{9,13},{13,9},{2,6},{6,2},{1... | collective-permute-start | bytes 1179656 | tf_op jit(solution)/shard_map/ppermute | solution.py:440

commit v9 on v8

--- a/solution.py
+++ b/solution.py
@@ -51,8 +51,15 @@
     return pltpu.with_memory_space_constraint(x, pltpu.HBM)
 
 
-def gather_kernel(picks, points, chosen, token):
+def gather_kernel(picks, points, omega, chosen, omega_here, token, sems):
     batch, pool = picks.shape[1], points.shape[0]
+    rows = omega.shape[0] // sems.shape[0]
+    copies = [
+        pltpu.make_async_copy(omega.at[at, :], omega_here.at[at, :], sems.at[j])
+        for j, at in enumerate(pl.ds(j * rows, rows) for j in range(sems.shape[0]))
+    ]
+    for copy in copies:
+        copy.start()
     lane = lax.broadcasted_iota(jnp.int32, (batch, 128), 1)
     for m in range(2):
         wanted = jnp.broadcast_to(picks[m : m + 1, :], (128, batch)).T
@@ -62,9 +69,11 @@
         chosen[m * batch : (m + 1) * batch, :] = jnp.dot(
             jnp.concatenate(hot, axis=1), points[...], preferred_element_type=f32
         ).astype(bf16)
-
-
-def gather(picks, points):
+    for copy in copies:
+        copy.wait()
+
+
+def gather(picks, points, omega):
     batch = picks.shape[1]
     pool, ins = points.shape
     return pl.pallas_call(
@@ -73,13 +82,19 @@
         in_specs=[
             pl.BlockSpec(picks.shape, lambda i: (0, 0)),
             pl.BlockSpec((pool, ins), lambda i: (0, 0)),
+            ANYWHERE,
         ],
-        out_specs=[IN_VMEM, ANYWHERE],
-        out_shape=[jax.ShapeDtypeStruct((2 * batch, ins), bf16), TOKEN],
+        out_specs=[IN_VMEM, IN_VMEM, ANYWHERE],
+        out_shape=[
+            jax.ShapeDtypeStruct((2 * batch, ins), bf16),
+            jax.ShapeDtypeStruct(omega.shape, bf16),
+            TOKEN,
+        ],
+        scratch_shapes=[pltpu.SemaphoreType.DMA((4,))],
         compiler_params=params(),
         cost_estimate=cost(3),
         name="chosen_points",
-    )(picks, points)
+    )(picks, points, omega)
 
 
 def cosines(chosen, omega, phase, base, width, store, between=None):
@@ -109,20 +124,32 @@
 
 def rates_kernel(start, size, low, high, width, own, begun, keep, ends, f, p, chosen, omega, phase, weights, *refs):
     refs = list(refs)
+    sems = refs.pop() if keep else None
     total, feats = refs.pop(), refs.pop()
     before = refs.pop(0) if begun else None
     refs.pop()
     owned = None if begun else refs.pop(0)
     count = omega.shape[1] // width
+    if keep:
+        weights_far, weights = weights, refs[2]
+
+        def coming(step):
+            at = pl.ds(pl.multiple_of(lax.rem(step + p[0] * own, count) * width, width), width)
+            return pltpu.make_async_copy(weights_far.at[at, :], weights.at[at, :], sems.at[step])
+
+        for step in range(count):
+            coming(step).start()
     total[...] = before[...] if begun else jnp.zeros_like(total)
 
-    def block(place, into, offset):
+    def block(place, into, offset, step):
         parts = []
 
         def store(cols, value):
             into[:, offset + cols.start : offset + cols.stop] = value
 
         def between(at, rows, group):
+            if keep and at == 0:
+                coming(step).wait()
             done = into[:, offset + at : offset + at + group]
             parts.append(jnp.dot(done, weights[rows, :], preferred_element_type=f32))
 
@@ -136,10 +163,10 @@
 
     if not begun:
         for step in range(own):
-            block(p[0] * own + step, owned, step * width)
+            block(p[0] * own + step, owned, step * width, step)
 
     def turn(step, _):
-        block(lax.rem(step + p[0] * own, count), feats, 0)
+        block(lax.rem(step + p[0] * own, count), feats, 0, step)
         return _
 
     lax.fori_loop(low if begun else own, high, turn, 0)
@@ -174,6 +201,7 @@
         outs.append(jax.ShapeDtypeStruct((size, owned), bf16))
     if keep:
         outs += [jax.ShapeDtypeStruct((ins, owned), bf16), jax.ShapeDtypeStruct((1, owned), f32)]
+        outs.append(jax.ShapeDtypeStruct(weights.shape, bf16))
     if ends:
         outs += [jax.ShapeDtypeStruct((size // 2, k), t) for t in (f32, bf16)]
     else:
@@ -191,9 +219,10 @@
         grid_spec=pltpu.PrefetchScalarGridSpec(
             num_scalar_prefetch=2,
             grid=(1,),
-            in_specs=[IN_VMEM] * (4 + begun) + [ANYWHERE] * len(deps),
+            in_specs=[IN_VMEM] * 3 + [ANYWHERE if keep else IN_VMEM] + [IN_VMEM] * begun + [ANYWHERE] * len(deps),
             out_specs=[IN_VMEM] * len(outs) + [ANYWHERE],
-            scratch_shapes=[pltpu.VMEM((size, width), bf16), pltpu.VMEM((size, k), f32)],
+            scratch_shapes=[pltpu.VMEM((size, width), bf16), pltpu.VMEM((size, k), f32)]
+            + [pltpu.SemaphoreType.DMA((count,))] * keep,
         ),
         out_shape=[*outs, TOKEN],
         compiler_params=params(),
@@ -458,14 +487,15 @@
     p = lax.axis_index("pts").astype(jnp.int32).reshape(1)
     owned, k = master.shape[1:]
     points_here = 2 * picks.shape[1]
-    size_one = points_here * 3 // 8
+    size_one = points_here // 2
     parts = [(0, points_here - size_one), (points_here - size_one, size_one)]
     bits = n_feat.bit_length() - 1
-    points, picks, phase = in_hbm(points), in_hbm(picks), phase[None, :]
+    points, picks, omega, weights = map(in_hbm, (points, picks, omega, weights))
+    phase = phase[None, :]
     outer = counts.shape
     counts = counts.reshape(points_here, k)
 
-    chosen, token = gather(picks, points)
+    chosen, omega, token = gather(picks, points, omega)
     everyone = spread(chosen, n_pts)
 
     def some_rates(m, blocks, before, keep, ends, token):
@@ -486,17 +516,12 @@
             masks = masks + [q ^ 2**bit for q in masks]
         return rows, masks
 
-    feats_zero, own_omega, own_phase, kept_zero, sent, token = some_rates(
+    feats_zero, own_omega, own_phase, weights, kept_zero, sent, token = some_rates(
         0, (0, 2), None, True, True, token
     )
     got_zero = swap(sent, n_feat, 0)
     feats_one, begun, token = some_rates(1, (0, 1), None, False, False, token)
-    for bit in range(1, bits):
-        kept_zero, got_zero, token = add_up(kept_zero, got_zero, bit, token)
-    kept_one, sent, token = some_rates(1, (1, 2), begun, False, True, token)
-    got_one = swap(sent, n_feat, 0)
     features = [[feats_zero], [feats_one]]
-
     todo = [(m, j) for m in range(2) for j in range(1, n_pts)]
     share = len(todo) // 6
 
@@ -509,11 +534,16 @@
             features[m].append(feats)
         return token
 
+    for bit in range(1, bits):
+        kept_zero, got_zero, token = add_up(kept_zero, got_zero, bit, token)
+    token = some(token, 1)
+    kept_one, sent, token = some_rates(1, (1, 2), begun, False, True, token)
+    got_one = swap(sent, n_feat, 0)
+    chunk, token = total(f, kept_zero, got_zero, 0, False, [token])
+    rows_zero, masks = give_back(chunk)
     token = some(token, 1)
     for bit in range(1, bits):
         kept_one, got_one, token = add_up(kept_one, got_one, bit, token)
-    chunk, token = total(f, kept_zero, got_zero, 0, False, [token])
-    rows_zero, masks = give_back(chunk)
     token = some(token, 1)
     chunk, token = total(f, kept_one, got_one, 0, False, [token])
     rows_one, masks = give_back(chunk)
@@ -527,7 +557,6 @@
     token = some(token, 2, 0.1)
     *far_zero, token = lax.optimization_barrier((*far_zero, token))
     res_zero = [y for g in [res_zero] + far_zero for y in (g, mate(g, n_pts))]
-    token = some(token, 1, 0.1)
     *far_one, token = lax.optimization_barrier((*far_one, token))
     res_one = [y for g in [res_one] + far_one for y in (g, mate(g, n_pts))]
     begun, token = first_part(features[0], res_zero, master, [token])

time: 98.7 us -> 102 us (1.033)
  waiting for transfers between devices: 18.5 us -> 23.4 us
  starting transfers between devices: 22 us -> 17.7 us
  Pallas kernels: 52.5 us -> 55.1 us
    ppermute x6, waiting for transfers between devices: 5.47 us -> 8.77 us  [swap(): return lax.ppermute(x, 'feat', [(i, i ^ 2 ** bit) for i in range(n)])]
    ppermute x6, starting transfers between devices: 10.8 us -> 7.49 us  [swap(): return lax.ppermute(x, 'feat', [(i, i ^ 2 ** bit) for i in range(n)])]
    pallas_call x3, Pallas kernels: 18.6 us -> 21.1 us  [rates(): pl.pallas_call(kernel, grid_spec=pltpu.PrefetchScalarGridSpec(num_scalar_...]
    ppermute x7, waiting for transfers between devices: 9.76 us -> 11.4 us  [ring(): return lax.ppermute(x, axis, [(i, (i + distance) % n) for i in range(n)])]
    ppermute x7, starting transfers between devices: 8.81 us -> 7.75 us  [ring(): return lax.ppermute(x, axis, [(i, (i + distance) % n) for i in range(n)])]
    unnamed x20 -> x18, local copies, waits for them, and re-layouts: 4.41 us -> 4.24 us
  transfers between devices with their start and end apart: 27 -> 27, of which waited for: 14 -> 10; matrix products, arithmetic and copies ran while one was open for 0% -> 0% of each run, Pallas kernels for 48% -> 48%
where the time goes in v9:
time: 102 us; the launch traced here: 101 us
  Pallas kernels  55.1 us (54%)
  waiting for transfers between devices  23.4 us (23%)
  starting transfers between devices  17.7 us (17%)
  local copies, waits for them, and re-layouts  4.24 us (4%)
  between operations  1.15 us (1%)
    pallas_call x3, Pallas kernels, rates(): pl.pallas_call(kernel, grid_spec=pltpu.PrefetchScalarGridSpec(num_scalar_...  21.1 us
    pallas_call x6, Pallas kernels, owned_features(): pl.pallas_call(functools.partial(features_kernel, start, size), in_specs=...  12.5 us
    ppermute x7, waiting for transfers between devices, ring(): return lax.ppermute(x, axis, [(i, (i + distance) % n) for i in range(n)])  11.4 us
    pallas_call x4, Pallas kernels, update(): pl.pallas_call(functools.partial(update_kernel, n, at), grid=(steps,), in...  10.3 us
    ppermute x6, waiting for transfers between devices, swap(): return lax.ppermute(x, 'feat', [(i, i ^ 2 ** bit) for i in range(n)])  8.77 us
    ppermute x7, starting transfers between devices, ring(): return lax.ppermute(x, axis, [(i, (i + distance) % n) for i in range(n)])  7.75 us
    ppermute x6, starting transfers between devices, swap(): return lax.ppermute(x, 'feat', [(i, i ^ 2 ** bit) for i in range(n)])  7.49 us
    unnamed x18, local copies, waits for them, and re-layouts  4.24 us
  transfers between devices with their start and end apart: 27, of which 10 were waited for; matrix products, arithmetic and copies ran while one was open for 0% of the time, Pallas kernels for 48%

profile of v9, /device:TPU:0, one launch (start us, length us, event | category | flops | bytes accessed | tf_op | source)
XLA Modules:
  0.0 101.5 jit_solution(3371394541892541493)
XLA Ops:
  0.6 3.5 %chosen_points.1 = (bf16[1024,256]{1,0:T(8,128)(2,1)S(1)}, bf16[256,8192]{1,0:T(8,128)(2,1)S(1)}, f32[8,128]{1,0:T(8,128)S(1)}) custom-call(s32[2,512]{1,0:T(2,128)} %picks.1, bf16[2048,256]{1,0:T(8,128)(2,1)} %points.1, bf16[256,8192]{1,0:T(8,128)(2,1)} %omega.1), custom_call_target="tpu_custom_call" | custom-call | flops 3000000000 | bytes 1024 | tf_op jit(solution)/shard_map/chosen_points/pallas_call | solution.py:79
  4.1 0.0 copy-start.6
  4.1 2.0 %copy-done.6 = bf16[256,8192]{1,0:T(8,128)(2,1)} copy-done((bf16[256,8192]{1,0:T(8,128)(2,1)}, bf16[256,8192]{1,0:T(8,128)(2,1)S(1)}, u32[]{:S(2)}) %copy-start.6) | copy-done | bytes 4194328
  6.1 0.5 collective-permute-start
  6.6 2.5 %collective-permute-start.3 = (bf16[1024,256]{1,0:T(8,128)(2,1)S(1)}, bf16[1024,256]{1,0:T(8,128)(2,1)S(1)}, u32[]{:S(2)}, u32[]{:S(2)}) collective-permute-start(bf16[1024,256]{1,0:T(8,128)(2,1)S(1)} %get-tuple-element.73.refs_2_), channel_id=1, source_target_pairs={{0,8},{4,12},{8,0},{12,4},{1,9},{5,13},{9,1},{13,5},{2,10},{6,14},... | collective-permute-start | bytes 1572872 | tf_op jit(solution)/shard_map/ppermute | solution.py:465
  9.1 2.2 %copy-done.7 = bf16[256,8192]{1,0:T(8,128)(2,1)S(1)} copy-done((bf16[256,8192]{1,0:T(8,128)(2,1)S(1)}, bf16[256,8192]{1,0:T(8,128)(2,1)}, u32[]{:S(2)}) %copy-start.7) | copy-done | bytes 4194328
  11.3 12.1 %partial_log_rates.3 = (bf16[512,2048]{1,0:T(8,128)(2,1)S(1)}, bf16[256,2048]{1,0:T(8,128)(2,1)S(1)}, f32[1,2048]{1,0:T(1,128)S(1)}, bf16[8192,256]{1,0:T(8,128)...) custom-call(s32[1]{0:T(128)} %bitcast.refs_0_.f, s32[1]{0:T(128)} %bitcast.1.refs_1_.p, ...), custom_call_target="tpu_custom_call" | custom-call | flops 12000000000 | bytes 1024 | tf_op jit(solution)/shard_map/partial_log_rates/pallas_call | solution.py:217
  23.4 1.6 %collective-permute-start.1 = (bf16[256,256]{1,0:T(8,128)(2,1)S(1)}, bf16[256,256]{1,0:T(8,128)(2,1)S(1)}, u32[]{:S(2)}, u32[]{:S(2)}) collective-permute-start(bf16[256,256]{1,0:T(8,128)(2,1)S(1)} %get-tuple-element.82), channel_id=1, source_target_pairs={{0,1},{1,0},{2,3},{3,2},{4,5},{5,4},{6,7},{7,6},{8,9},{9,8},{10,11... | collective-permute-start | bytes 393224 | tf_op jit(solution)/shard_map/ppermute | solution.py:477
  25.0 4.3 %partial_log_rates.4 = (bf16[512,2048]{1,0:T(8,128)(2,1)S(1)}, f32[512,256]{1,0:T(8,128)S(1)}, f32[8,128]{1,0:T(8,128)S(1)}) custom-call(s32[1]{0:T(128)} %bitcast.refs_0_.f, s32[1]{0:T(128)} %bitcast.1.refs_1_.p, bf16[1024,256]{1,0:T(8,128)(2,1)S(1)} %get-tuple-element.73.refs_2_, bf16[256,8192]{1,0:T(8,128)(2,1)S(1)} %copy-done.7, f32[1,8192]{1,0:T(1,128)S(1)} %bitcast.8, ...), custom_call_target="tpu_custom_call" | custom-call | flops 6000000000 | bytes 1024 | tf_op jit(solution)/shard_map/partial_log_rates/pallas_call | solution.py:217
  29.3 0.0 collective-permute-done.1.b
  29.3 0.0 copy-start.8
  29.3 2.7 %collective-permute-start.4 = (bf16[256,256]{1,0:T(8,128)(2,1)S(1)}, bf16[256,256]{1,0:T(8,128)(2,1)S(1)}, u32[]{:S(2)}, u32[]{:S(2)}) collective-permute-start(bf16[256,256]{1,0:T(8,128)(2,1)S(1)} %get-tuple-element.88.a), channel_id=1, source_target_pairs={{0,2},{1,3},{2,0},{3,1},{4,6},{5,7},{6,4},{7,5},{8,10},{9,11},{10,... | collective-permute-start | bytes 393224 | tf_op jit(solution)/shard_map/ppermute | solution.py:477
  32.0 0.0 collective-permute-done.3.chosen
  32.0 0.0 collective-permute-start.6
  32.0 0.0 collective-permute-done.chosen
  32.0 2.1 %owned_features.6 = (bf16[512,2048]{1,0:T(8,128)(2,1)S(1)}, f32[8,128]{1,0:T(8,128)S(1)}) custom-call(bf16[1024,256]{1,0:T(8,128)(2,1)S(1)} %collective-permute-done.chosen, bf16[256,2048]{1,0:T(8,128)(2,1)S(1)} %get-tuple-element.79.omega, f32[1,2048]{1,0:T(1,128)S(1)} %get-tuple-element.80.phase, f32[8,128]{1,0:T(8,128)S(1)} %get-tuple-element.84.refs_0_), custom_call_target="tpu_custom_call" | custom-call | flops 1000000000 | bytes 1024 | tf_op jit(solution)/shard_map/owned_features/pallas_call | solution.py:245
  34.1 4.8 %partial_log_rates.5 = (f32[256,256]{1,0:T(8,128)S(1)}, bf16[256,256]{1,0:T(8,128)(2,1)S(1)}, f32[8,128]{1,0:T(8,128)S(1)}) custom-call(s32[1]{0:T(128)} %bitcast.refs_0_.f, s32[1]{0:T(128)} %bitcast.1.refs_1_.p, bf16[1024,256]{1,0:T(8,128)(2,1)S(1)} %get-tuple-element.73.refs_2_, bf16[256,8192]{1,0:T(8,128)(2,1)S(1)} %copy-done.8, f32[1,8192]{1,0:T(1,128)S(1)} %bitcast.9, ...), custom_call_target="tpu_custom_call" | custom-call | flops 6000000000 | bytes 1024 | tf_op jit(solution)/shard_map/partial_log_rates/pallas_call | solution.py:217
  38.9 1.4 %collective-permute-start.2 = (bf16[256,256]{1,0:T(8,128)(2,1)S(1)}, bf16[256,256]{1,0:T(8,128)(2,1)S(1)}, u32[]{:S(2)}, u32[]{:S(2)}) collective-permute-start(bf16[256,256]{1,0:T(8,128)(2,1)S(1)} %get-tuple-element.87), channel_id=1, source_target_pairs={{0,1},{1,0},{2,3},{3,2},{4,5},{5,4},{6,7},{7,6},{8,9},{9,8},{10,11... | collective-permute-start | bytes 393224 | tf_op jit(solution)/shard_map/ppermute | solution.py:477
  40.3 0.0 collective-permute-done.4.b
  40.4 2.1 %owned_features.7 = (bf16[512,2048]{1,0:T(8,128)(2,1)S(1)}, f32[8,128]{1,0:T(8,128)S(1)}) custom-call(bf16[1024,256]{1,0:T(8,128)(2,1)S(1)} %collective-permute-done.3.chosen, bf16[256,2048]{1,0:T(8,128)(2,1)S(1)} %get-tuple-element.79.omega, f32[1,2048]{1,0:T(1,128)S(1)} %get-tuple-element.80.phase, f32[8,128]{1,0:T(8,128)S(1)} %get-tuple-element.90.refs_0_), custom_call_target="tpu_custom_call" | custom-call | flops 1000000000 | bytes 1024 | tf_op jit(solution)/shard_map/owned_features/pallas_call | solution.py:245
  42.5 2.4 %collective-permute-done.2.b = bf16[256,256]{1,0:T(8,128)(2,1)S(1)} collective-permute-done((bf16[256,256]{1,0:T(8,128)(2,1)S(1)}, bf16[256,256]{1,0:T(8,128)(2,1)S(1)}, u32[]{:S(2)}, u32[]{:S(2)}) %collective-permute-start.2) | collective-permute-done | bytes 131104 | tf_op jit(solution)/shard_map/ppermute | solution.py:477
  44.9 0.4 collective-permute-start.5
  45.3 1.3 %collective-permute-start.8 = (bf16[256,256]{1,0:T(8,128)(2,1)S(1)}, bf16[256,256]{1,0:T(8,128)(2,1)S(1)}, u32[]{:S(2)}, u32[]{:S(2)}) collective-permute-start(bf16[256,256]{1,0:T(8,128)(2,1)S(1)} %get-tuple-element.96.refs_0_), channel_id=1, source_target_pairs={{0,1},{1,0},{2,3},{3,2},{4,5},{5,4},{6,7},{7,6},{8,9},{9,8},{10,11... | collective-permute-start | bytes 393224 | tf_op jit(solution)/shard_map/ppermute | solution.py:477
  46.7 2.1 %owned_features.8 = (bf16[512,2048]{1,0:T(8,128)(2,1)S(1)}, f32[8,128]{1,0:T(8,128)S(1)}) custom-call(bf16[1024,256]{1,0:T(8,128)(2,1)S(1)} %collective-permute-done.6.chosen, bf16[256,2048]{1,0:T(8,128)(2,1)S(1)} %get-tuple-element.79.omega, f32[1,2048]{1,0:T(1,128)S(1)} %get-tuple-element.80.phase, f32[8,128]{1,0:T(8,128)S(1)} %get-tuple-element.93.refs_0_), custom_call_target="tpu_custom_call" | custom-call | flops 1000000000 | bytes 1024 | tf_op jit(solution)/shard_map/owned_features/pallas_call | solution.py:245
  48.7 5.1 %collective-permute-done.5.b = bf16[256,256]{1,0:T(8,128)(2,1)S(1)} collective-permute-done((bf16[256,256]{1,0:T(8,128)(2,1)S(1)}, bf16[256,256]{1,0:T(8,128)(2,1)S(1)}, u32[]{:S(2)}, u32[]{:S(2)}) %collective-permute-start.5) | collective-permute-done | bytes 131104 | tf_op jit(solution)/shard_map/ppermute | solution.py:477
  53.9 0.1 collective-permute-start.7
  54.0 1.0 residuals.2
  55.0 0.6 collective-permute-start.11
  55.5 2.1 %owned_features.9 = (bf16[512,2048]{1,0:T(8,128)(2,1)S(1)}, f32[8,128]{1,0:T(8,128)S(1)}) custom-call(bf16[1024,256]{1,0:T(8,128)(2,1)S(1)} %collective-permute-done.chosen, bf16[256,2048]{1,0:T(8,128)(2,1)S(1)} %get-tuple-element.79.omega, f32[1,2048]{1,0:T(1,128)S(1)} %get-tuple-element.80.phase, f32[8,128]{1,0:T(8,128)S(1)} %get-tuple-element.98.refs_0_), custom_call_target="tpu_custom_call" | custom-call | flops 1000000000 | bytes 1024 | tf_op jit(solution)/shard_map/owned_features/pallas_call | solution.py:245
  57.6 1.3 %collective-permute-done.7.refs_1_ = bf16[256,256]{1,0:T(8,128)(2,1)S(1)} collective-permute-done((bf16[256,256]{1,0:T(8,128)(2,1)S(1)}, bf16[256,256]{1,0:T(8,128)(2,1)S(1)}, u32[]{:S(2)}, u32[]{:S(2)}) %collective-permute-start.7) | collective-permute-done | bytes 131104 | tf_op jit(solution)/shard_map/ppermute | solution.py:477
  58.9 1.0 residuals.3
  59.9 0.0 copy-start
  59.9 0.6 collective-permute-start.10
  60.5 2.1 %owned_features.10 = (bf16[512,2048]{1,0:T(8,128)(2,1)S(1)}, f32[8,128]{1,0:T(8,128)S(1)}) custom-call(bf16[1024,256]{1,0:T(8,128)(2,1)S(1)} %collective-permute-done.3.chosen, bf16[256,2048]{1,0:T(8,128)(2,1)S(1)} %get-tuple-element.79.omega, f32[1,2048]{1,0:T(1,128)S(1)} %get-tuple-element.80.phase, f32[8,128]{1,0:T(8,128)S(1)} %get-tuple-element.104.refs_0_), custom_call_target="tpu_custom_call" | custom-call | flops 100000000 | bytes 1024 | tf_op jit(solution)/shard_map/owned_features/pallas_call | solution.py:245
  62.6 2.1 %owned_features.11 = (bf16[512,2048]{1,0:T(8,128)(2,1)S(1)}, f32[8,128]{1,0:T(8,128)S(1)}) custom-call(bf16[1024,256]{1,0:T(8,128)(2,1)S(1)} %collective-permute-done.6.chosen, bf16[256,2048]{1,0:T(8,128)(2,1)S(1)} %get-tuple-element.79.omega, f32[1,2048]{1,0:T(1,128)S(1)} %get-tuple-element.80.phase, f32[8,128]{1,0:T(8,128)S(1)} %get-tuple-element.106.refs_0_), custom_call_target="tpu_custom_call" | custom-call | flops 100000000 | bytes 1024 | tf_op jit(solution)/shard_map/owned_features/pallas_call | solution.py:245
  64.7 0.6 collective-permute-start.14
  65.2 0.1 collective-permute-start.9
  65.3 2.6 %collective-permute-done.10.refs_6_ = bf16[256,512]{1,0:T(8,128)(2,1)S(1)} collective-permute-done((bf16[256,512]{1,0:T(8,128)(2,1)S(1)}, bf16[256,512]{1,0:T(8,128)(2,1)S(1)}, u32[]{:S(2)}, u32[]{:S(2)}) %collective-permute-start.10) | collective-permute-done | bytes 262176 | tf_op jit(solution)/shard_map/ppermute | solution.py:465
  67.9 0.0 copy-start.1
  68.0 0.0 copy-start.2
  68.0 0.0 copy-start.3
  68.0 2.8 %first_part.1 = (f32[2048,256]{1,0:T(8,128)S(1)}, f32[8,128]{1,0:T(8,128)S(1)}) custom-call(bf16[512,2048]{1,0:T(8,128)(2,1)S(1)} %get-tuple-element.113.refs_0_, bf16[512,2048]{1,0:T(8,128)(2,1)S(1)} %get-tuple-element.114.refs_1_, bf16[512,2048]{1,0:T(8,128)(2,1)S(1)} %get-tuple-element.115.refs_2_, bf16[512,2048]{1,0:T(8,128)(2,1)S(1)} %get-tuple-element.116.refs_3_, ...), custom_call_target="tpu_custom_call" | custom-call | flops 300000000 | bytes 1024 | tf_op jit(solution)/shard_map/first_part/pallas_call | solution.py:365
  70.8 1.7 %update.4 = (f32[1,2048,256]{2,1,0:T(8,128)}, f32[1,2048,256]{2,1,0:T(8,128)}, f32[1,2048,256]{2,1,0:T(8,128)}, bf16[256,256]{1,0:T(8,128)(2,1)S(1)}) custom-call(bf16[512,2048]{1,0:T(8,128)(2,1)S(1)} %get-tuple-element.102.refs_0_, bf16[512,2048]{1,0:T(8,128)(2,1)S(1)} %get-tuple-element.103.refs_1_, bf16[512,2048]{1,0:T(8,128)(2,1)S(1)} %get-tuple-element.105.refs_2_, ...), custom_call_target="tpu_custom_call" | custom-call | flops 4000000000 | bytes 1024 | tf_op jit(solution)/shard_map/update/pallas_call | solution.py:413
  72.5 0.5 collective-permute-start.15
  73.1 0.2 collective-permute-start.19
  73.3 2.6 %update.5 = (f32[1,2048,256]{2,1,0:T(8,128)}, f32[1,2048,256]{2,1,0:T(8,128)}, f32[1,2048,256]{2,1,0:T(8,128)}, bf16[512,256]{1,0:T(8,128)(2,1)S(1)}) custom-call(bf16[512,2048]{1,0:T(8,128)(2,1)S(1)} %get-tuple-element.102.refs_0_, bf16[512,2048]{1,0:T(8,128)(2,1)S(1)} %get-tuple-element.103.refs_1_, ...), custom_call_target="tpu_custom_call", output_to_operand_aliasing={{0}: (13, {}), {1}: (14, {}), {2}: (15, {})} | custom-call | flops 4000000000 | bytes 1024 | tf_op jit(solution)/shard_map/update/pallas_call | solution.py:413
  75.8 1.5 %collective-permute-start.16 = (bf16[512,256]{1,0:T(8,128)(2,1)S(1)}, bf16[512,256]{1,0:T(8,128)(2,1)S(1)}, u32[]{:S(2)}, u32[]{:S(2)}) collective-permute-start(bf16[512,256]{1,0:T(8,128)(2,1)S(1)} %get-tuple-element.131.refs_4_), channel_id=1, source_target_pairs={{0,8},{4,12},{8,0},{12,4},{1,9},{5,13},{9,1},{13,5},{2,10},{6,14},... | collective-permute-start | bytes 786440 | tf_op jit(solution)/shard_map/ppermute | solution.py:465
  77.4 0.0 collective-permute-start.21
  77.4 1.1 %collective-permute-done.15.refs_17_.refs_2_ = bf16[256,256]{1,0:T(8,128)(2,1)S(1)} collective-permute-done((bf16[256,256]{1,0:T(8,128)(2,1)S(1)}, bf16[256,256]{1,0:T(8,128)(2,1)S(1)}, u32[]{:S(2)}, u32[]{:S(2)}) %collective-permute-start.15) | collective-permute-done | bytes 131104 | tf_op jit(solution)/shard_map/ppermute | solution.py:465
  78.5 2.6 %update.6 = (f32[1,2048,256]{2,1,0:T(8,128)}, f32[1,2048,256]{2,1,0:T(8,128)}, f32[1,2048,256]{2,1,0:T(8,128)}, bf16[512,256]{1,0:T(8,128)(2,1)S(1)}) custom-call(bf16[512,2048]{1,0:T(8,128)(2,1)S(1)} %get-tuple-element.102.refs_0_, bf16[512,2048]{1,0:T(8,128)(2,1)S(1)} %get-tuple-element.103.refs_1_, ...), custom_call_target="tpu_custom_call", output_to_operand_aliasing={{0}: (13, {}), {1}: (14, {}), {2}: (15, {})} | custom-call | flops 4000000000 | bytes 1024 | tf_op jit(solution)/shard_map/update/pallas_call | solution.py:413
  81.0 0.5 collective-permute-start.24
  81.5 3.4 %collective-permute-done.16.refs_17_.refs_6_ = bf16[512,256]{1,0:T(8,128)(2,1)S(1)} collective-permute-done((bf16[512,256]{1,0:T(8,128)(2,1)S(1)}, bf16[512,256]{1,0:T(8,128)(2,1)S(1)}, u32[]{:S(2)}, u32[]{:S(2)}) %collective-permute-start.16) | collective-permute-done | bytes 262176 | tf_op jit(solution)/shard_map/ppermute | solution.py:465
  85.0 3.4 %update.7 = (f32[1,2048,256]{2,1,0:T(8,128)}, f32[1,2048,256]{2,1,0:T(8,128)}, f32[1,2048,256]{2,1,0:T(8,128)}, bf16[768,256]{1,0:T(8,128)(2,1)S(1)}) custom-call(bf16[512,2048]{1,0:T(8,128)(2,1)S(1)} %get-tuple-element.102.refs_0_, bf16[512,2048]{1,0:T(8,128)(2,1)S(1)} %get-tuple-element.103.refs_1_, ...), custom_call_target="tpu_custom_call", output_to_operand_aliasing={{0}: (13, {}), {1}: (14, {}), {2}: (15, {})} | custom-call | flops 4000000000 | bytes 1024 | tf_op jit(solution)/shard_map/update/pallas_call | solution.py:413
  88.4 1.5 %collective-permute-start.18 = (bf16[768,256]{1,0:T(8,128)(2,1)S(1)}, bf16[768,256]{1,0:T(8,128)(2,1)S(1)}, u32[]{:S(2)}, u32[]{:S(2)}) collective-permute-start(bf16[768,256]{1,0:T(8,128)(2,1)S(1)} %get-tuple-element.135.refs_0_), channel_id=1, source_target_pairs={{0,8},{4,12},{8,0},{12,4},{1,9},{5,13},{9,1},{13,5},{2,10},{6,14},... | collective-permute-start | bytes 1179656 | tf_op jit(solution)/shard_map/ppermute | solution.py:465
  89.9 0.1 collective-permute-done.24.refs_10_
  90.0 0.4 collective-permute-start.22
  90.4 0.1 collective-permute-start.25
  90.5 0.4 collective-permute-start.20
  91.0 1.4 %collective-permute-done.20.refs_3_ = bf16[256,256]{1,0:T(8,128)(2,1)S(1)} collective-permute-done((bf16[256,256]{1,0:T(8,128)(2,1)S(1)}, bf16[256,256]{1,0:T(8,128)(2,1)S(1)}, u32[]{:S(2)}, u32[]{:S(2)}) %collective-permute-start.20) | collective-permute-done | bytes 131104 | tf_op jit(solution)/shard_map/ppermute | solution.py:469
  92.4 0.1 collective-permute-start.17
  92.6 1.6 %put_rows.2.refs_4_ = bf16[8192,256]{1,0:T(8,128)(2,1)} custom-call(s32[1]{0:T(128)} %bitcast.1.refs_1_.p, bf16[256,256]{1,0:T(8,128)(2,1)S(1)} %get-tuple-element.127.refs_0_, bf16[256,256]{1,0:T(8,128)(2,1)S(1)} %collective-permute-done.19.refs_1_, bf16[256,256]{1,0:T(8,128)(2,1)S(1)} %collective-permute-done.15.refs_17_.refs_2_, ...), custom_call_target="tpu_custom_call" | custom-call | flops 10000000 | bytes 1024 | tf_op jit(solution)/shard_map/put_rows/pallas_call | solution.py:447
  94.2 4.2 %collective-permute-done.18.refs_2_ = bf16[768,256]{1,0:T(8,128)(2,1)S(1)} collective-permute-done((bf16[768,256]{1,0:T(8,128)(2,1)S(1)}, bf16[768,256]{1,0:T(8,128)(2,1)S(1)}, u32[]{:S(2)}, u32[]{:S(2)}) %collective-permute-start.18) | collective-permute-done | bytes 393248 | tf_op jit(solution)/shard_map/ppermute | solution.py:465
  98.4 1.7 %collective-permute-done.26.refs_3_ = bf16[768,256]{1,0:T(8,128)(2,1)S(1)} collective-permute-done((bf16[768,256]{1,0:T(8,128)(2,1)S(1)}, bf16[768,256]{1,0:T(8,128)(2,1)S(1)}, u32[]{:S(2)}, u32[]{:S(2)}) %collective-permute-start.26) | collective-permute-done | bytes 393248 | tf_op jit(solution)/shard_map/ppermute | solution.py:469
  100.1 1.2 %put_rows.3 = bf16[8192,256]{1,0:T(8,128)(2,1)} custom-call(s32[1]{0:T(128)} %bitcast.1.refs_1_.p, bf16[768,256]{1,0:T(8,128)(2,1)S(1)} %get-tuple-element.135.refs_0_, bf16[768,256]{1,0:T(8,128)(2,1)S(1)} %collective-permute-done.17.refs_1_, bf16[768,256]{1,0:T(8,128)(2,1)S(1)} %collective-permute-done.18.refs_2_, ...), custom_call_target="tpu_custom_call", output_to_operand_aliasing={{}: (5, {})} | custom-call | flops 10000000 | bytes 1024 | tf_op jit(solution)/shard_map/put_rows/pallas_call | solution.py:447
  (31 shorter events, 0.2 us)
Async XLA Ops:
  0.6 8.5 %copy-start.5 = (f32[8192]{0:T(1024)S(1)}, f32[8192]{0:T(1024)}, u32[]{:S(2)}) copy-start(f32[8192]{0:T(1024)} %param.13) | copy-start | bytes 98308
  4.1 2.0 %copy-start.6 = (bf16[256,8192]{1,0:T(8,128)(2,1)}, bf16[256,8192]{1,0:T(8,128)(2,1)S(1)}, u32[]{:S(2)}) copy-start(bf16[256,8192]{1,0:T(8,128)(2,1)S(1)} %get-tuple-element.74.refs_3_) | copy-start | bytes 12582916
  6.1 25.9 %collective-permute-start = (bf16[1024,256]{1,0:T(8,128)(2,1)S(1)}, bf16[1024,256]{1,0:T(8,128)(2,1)S(1)}, u32[]{:S(2)}, u32[]{:S(2)}) collective-permute-start(bf16[1024,256]{1,0:T(8,128)(2,1)S(1)} %get-tuple-element.73.refs_2_), channel_id=1, source_target_pairs={{0,4},{4,0},{8,12},{12,8},{1,5},{5,1},{9,13},{13,9},{2,6},{6,2},{1... | collective-permute-start | bytes 1572872 | tf_op jit(solution)/shard_map/ppermute | solution.py:469
  6.6 25.4 %collective-permute-start.3 = (bf16[1024,256]{1,0:T(8,128)(2,1)S(1)}, bf16[1024,256]{1,0:T(8,128)(2,1)S(1)}, u32[]{:S(2)}, u32[]{:S(2)}) collective-permute-start(bf16[1024,256]{1,0:T(8,128)(2,1)S(1)} %get-tuple-element.73.refs_2_), channel_id=1, source_target_pairs={{0,8},{4,12},{8,0},{12,4},{1,9},{5,13},{9,1},{13,5},{2,10},{6,14},... | collective-permute-start | bytes 1572872 | tf_op jit(solution)/shard_map/ppermute | solution.py:465
  9.1 2.2 %copy-start.7 = (bf16[256,8192]{1,0:T(8,128)(2,1)S(1)}, bf16[256,8192]{1,0:T(8,128)(2,1)}, u32[]{:S(2)}) copy-start(bf16[256,8192]{1,0:T(8,128)(2,1)} %copy-done.6) | copy-start | bytes 12582916
  23.4 5.9 %collective-permute-start.1 = (bf16[256,256]{1,0:T(8,128)(2,1)S(1)}, bf16[256,256]{1,0:T(8,128)(2,1)S(1)}, u32[]{:S(2)}, u32[]{:S(2)}) collective-permute-start(bf16[256,256]{1,0:T(8,128)(2,1)S(1)} %get-tuple-element.82), channel_id=1, source_target_pairs={{0,1},{1,0},{2,3},{3,2},{4,5},{5,4},{6,7},{7,6},{8,9},{9,8},{10,11... | collective-permute-start | bytes 393224 | tf_op jit(solution)/shard_map/ppermute | solution.py:477
  29.3 4.8 %copy-start.8 = (bf16[256,8192]{1,0:T(8,128)(2,1)S(1)}, bf16[256,8192]{1,0:T(8,128)(2,1)}, u32[]{:S(2)}) copy-start(bf16[256,8192]{1,0:T(8,128)(2,1)} %copy-done.6) | copy-start | bytes 12582916
  29.3 11.0 %collective-permute-start.4 = (bf16[256,256]{1,0:T(8,128)(2,1)S(1)}, bf16[256,256]{1,0:T(8,128)(2,1)S(1)}, u32[]{:S(2)}, u32[]{:S(2)}) collective-permute-start(bf16[256,256]{1,0:T(8,128)(2,1)S(1)} %get-tuple-element.88.a), channel_id=1, source_target_pairs={{0,2},{1,3},{2,0},{3,1},{4,6},{5,7},{6,4},{7,5},{8,10},{9,11},{10,... | collective-permute-start | bytes 393224 | tf_op jit(solution)/shard_map/ppermute | solution.py:477
  32.0 14.7 %collective-permute-start.6 = (bf16[1024,256]{1,0:T(8,128)(2,1)S(1)}, bf16[1024,256]{1,0:T(8,128)(2,1)S(1)}, u32[]{:S(2)}, u32[]{:S(2)}) collective-permute-start(bf16[1024,256]{1,0:T(8,128)(2,1)S(1)} %collective-permute-done.3.chosen), channel_id=1, source_target_pairs={{0,4},{4,0},{8,12},{12,8},{1,5},{5,1},{9,13},{13,9},{2,6},{6,2},{1... | collective-permute-start | bytes 1572872 | tf_op jit(solution)/shard_map/ppermute | solution.py:469
  38.9 6.0 %collective-permute-start.2 = (bf16[256,256]{1,0:T(8,128)(2,1)S(1)}, bf16[256,256]{1,0:T(8,128)(2,1)S(1)}, u32[]{:S(2)}, u32[]{:S(2)}) collective-permute-start(bf16[256,256]{1,0:T(8,128)(2,1)S(1)} %get-tuple-element.87), channel_id=1, source_target_pairs={{0,1},{1,0},{2,3},{3,2},{4,5},{5,4},{6,7},{7,6},{8,9},{9,8},{10,11... | collective-permute-start | bytes 393224 | tf_op jit(solution)/shard_map/ppermute | solution.py:477
  44.9 8.9 %collective-permute-start.5 = (bf16[256,256]{1,0:T(8,128)(2,1)S(1)}, bf16[256,256]{1,0:T(8,128)(2,1)S(1)}, u32[]{:S(2)}, u32[]{:S(2)}) collective-permute-start(bf16[256,256]{1,0:T(8,128)(2,1)S(1)} %get-tuple-element.92.a), channel_id=1, source_target_pairs={{0,2},{1,3},{2,0},{3,1},{4,6},{5,7},{6,4},{7,5},{8,10},{9,11},{10,... | collective-permute-start | bytes 393224 | tf_op jit(solution)/shard_map/ppermute | solution.py:477
  45.3 8.6 %collective-permute-start.8 = (bf16[256,256]{1,0:T(8,128)(2,1)S(1)}, bf16[256,256]{1,0:T(8,128)(2,1)S(1)}, u32[]{:S(2)}, u32[]{:S(2)}) collective-permute-start(bf16[256,256]{1,0:T(8,128)(2,1)S(1)} %get-tuple-element.96.refs_0_), channel_id=1, source_target_pairs={{0,1},{1,0},{2,3},{3,2},{4,5},{5,4},{6,7},{7,6},{8,9},{9,8},{10,11... | collective-permute-start | bytes 393224 | tf_op jit(solution)/shard_map/ppermute | solution.py:477
  46.7 7.3 %copy-start.4 = (s32[2,512,256]{2,1,0:T(8,128)S(1)}, s32[2,512,256]{2,1,0:T(8,128)}, u32[]{:S(2)}) copy-start(s32[2,512,256]{2,1,0:T(8,128)} %param.15) | copy-start | bytes 3145732
  53.9 5.0 %collective-permute-start.7 = (bf16[256,256]{1,0:T(8,128)(2,1)S(1)}, bf16[256,256]{1,0:T(8,128)(2,1)S(1)}, u32[]{:S(2)}, u32[]{:S(2)}) collective-permute-start(bf16[256,256]{1,0:T(8,128)(2,1)S(1)} %get-tuple-element.95.refs_0_), channel_id=1, source_target_pairs={{0,1},{1,0},{2,3},{3,2},{4,5},{5,4},{6,7},{7,6},{8,9},{9,8},{10,11... | collective-permute-start | bytes 393224 | tf_op jit(solution)/shard_map/ppermute | solution.py:477
  55.0 9.7 %collective-permute-start.11 = (bf16[256,512]{1,0:T(8,128)(2,1)S(1)}, bf16[256,512]{1,0:T(8,128)(2,1)S(1)}, u32[]{:S(2)}, u32[]{:S(2)}) collective-permute-start(bf16[256,512]{1,0:T(8,128)(2,1)S(1)} %get-tuple-element.109.refs_4_), channel_id=1, source_target_pairs={{0,8},{4,12},{8,0},{12,4},{1,9},{5,13},{9,1},{13,5},{2,10},{6,14},... | collective-permute-start | bytes 786440 | tf_op jit(solution)/shard_map/ppermute | solution.py:465
  59.9 8.1 %copy-start = (f32[1,2048,256]{2,1,0:T(8,128)S(1)}, f32[1,2048,256]{2,1,0:T(8,128)}, u32[]{:S(2)}) copy-start(f32[1,2048,256]{2,1,0:T(8,128)} %refs_10_.7) | copy-start | bytes 6291460
  59.9 8.0 %collective-permute-start.10 = (bf16[256,512]{1,0:T(8,128)(2,1)S(1)}, bf16[256,512]{1,0:T(8,128)(2,1)S(1)}, u32[]{:S(2)}, u32[]{:S(2)}) collective-permute-start(bf16[256,512]{1,0:T(8,128)(2,1)S(1)} %get-tuple-element.108.refs_4_), channel_id=1, source_target_pairs={{0,8},{4,12},{8,0},{12,4},{1,9},{5,13},{9,1},{13,5},{2,10},{6,14},... | collective-permute-start | bytes 786440 | tf_op jit(solution)/shard_map/ppermute | solution.py:465
  60.5 7.5 %collective-permute-start.13 = (bf16[256,512]{1,0:T(8,128)(2,1)S(1)}, bf16[256,512]{1,0:T(8,128)(2,1)S(1)}, u32[]{:S(2)}, u32[]{:S(2)}) collective-permute-start(bf16[256,512]{1,0:T(8,128)(2,1)S(1)} %get-tuple-element.109.refs_4_), channel_id=1, source_target_pairs={{0,4},{4,0},{8,12},{12,8},{1,5},{5,1},{9,13},{13,9},{2,6},{6,2},{1... | collective-permute-start | bytes 786440 | tf_op jit(solution)/shard_map/ppermute | solution.py:469
  64.7 3.3 %collective-permute-start.14 = (bf16[256,512]{1,0:T(8,128)(2,1)S(1)}, bf16[256,512]{1,0:T(8,128)(2,1)S(1)}, u32[]{:S(2)}, u32[]{:S(2)}) collective-permute-start(bf16[256,512]{1,0:T(8,128)(2,1)S(1)} %collective-permute-done.11.refs_6_), channel_id=1, source_target_pairs={{0,4},{4,0},{8,12},{12,8},{1,5},{5,1},{9,13},{13,9},{2,6},{6,2},{1... | collective-permute-start | bytes 786440 | tf_op jit(solution)/shard_map/ppermute | solution.py:469
  65.2 5.6 %collective-permute-start.9 = (bf16[256,512]{1,0:T(8,128)(2,1)S(1)}, bf16[256,512]{1,0:T(8,128)(2,1)S(1)}, u32[]{:S(2)}, u32[]{:S(2)}) collective-permute-start(bf16[256,512]{1,0:T(8,128)(2,1)S(1)} %get-tuple-element.108.refs_4_), channel_id=1, source_target_pairs={{0,4},{4,0},{8,12},{12,8},{1,5},{5,1},{9,13},{13,9},{2,6},{6,2},{1... | collective-permute-start | bytes 786440 | tf_op jit(solution)/shard_map/ppermute | solution.py:469
  67.9 2.9 %collective-permute-start.12 = (bf16[256,512]{1,0:T(8,128)(2,1)S(1)}, bf16[256,512]{1,0:T(8,128)(2,1)S(1)}, u32[]{:S(2)}, u32[]{:S(2)}) collective-permute-start(bf16[256,512]{1,0:T(8,128)(2,1)S(1)} %collective-permute-done.10.refs_6_), channel_id=1, source_target_pairs={{0,4},{4,0},{8,12},{12,8},{1,5},{5,1},{9,13},{13,9},{2,6},{6,2},{1... | collective-permute-start | bytes 786440 | tf_op jit(solution)/shard_map/ppermute | solution.py:469
  67.9 2.9 %copy-start.1 = (f32[1,2048,256]{2,1,0:T(8,128)S(1)}, f32[1,2048,256]{2,1,0:T(8,128)}, u32[]{:S(2)}) copy-start(f32[1,2048,256]{2,1,0:T(8,128)} %refs_11_.7) | copy-start | bytes 6291460
  68.0 2.9 %copy-start.2 = (f32[1,2048,256]{2,1,0:T(8,128)S(1)}, f32[1,2048,256]{2,1,0:T(8,128)}, u32[]{:S(2)}) copy-start(f32[1,2048,256]{2,1,0:T(8,128)} %refs_12_.7) | copy-start | bytes 6291460
  68.0 2.9 %copy-start.3 = (bf16[256,256]{1,0:T(8,128)(2,1)S(1)}, bf16[256,256]{1,0:T(8,128)(2,1)}, u32[]{:S(2)}) copy-start(bf16[256,256]{1,0:T(8,128)(2,1)} %refs_9_.7) | copy-start | bytes 393220
  72.5 5.9 %collective-permute-start.15 = (bf16[256,256]{1,0:T(8,128)(2,1)S(1)}, bf16[256,256]{1,0:T(8,128)(2,1)S(1)}, u32[]{:S(2)}, u32[]{:S(2)}) collective-permute-start(bf16[256,256]{1,0:T(8,128)(2,1)S(1)} %get-tuple-element.127.refs_0_), channel_id=1, source_target_pairs={{0,8},{4,12},{8,0},{12,4},{1,9},{5,13},{9,1},{13,5},{2,10},{6,14},... | collective-permute-start | bytes 393224 | tf_op jit(solution)/shard_map/ppermute | solution.py:465
  73.1 17.4 %collective-permute-start.19 = (bf16[256,256]{1,0:T(8,128)(2,1)S(1)}, bf16[256,256]{1,0:T(8,128)(2,1)S(1)}, u32[]{:S(2)}, u32[]{:S(2)}) collective-permute-start(bf16[256,256]{1,0:T(8,128)(2,1)S(1)} %get-tuple-element.127.refs_0_), channel_id=1, source_target_pairs={{0,4},{4,0},{8,12},{12,8},{1,5},{5,1},{9,13},{13,9},{2,6},{6,2},{1... | collective-permute-start | bytes 393224 | tf_op jit(solution)/shard_map/ppermute | solution.py:469
  75.8 9.1 %collective-permute-start.16 = (bf16[512,256]{1,0:T(8,128)(2,1)S(1)}, bf16[512,256]{1,0:T(8,128)(2,1)S(1)}, u32[]{:S(2)}, u32[]{:S(2)}) collective-permute-start(bf16[512,256]{1,0:T(8,128)(2,1)S(1)} %get-tuple-element.131.refs_4_), channel_id=1, source_target_pairs={{0,8},{4,12},{8,0},{12,4},{1,9},{5,13},{9,1},{13,5},{2,10},{6,14},... | collective-permute-start | bytes 786440 | tf_op jit(solution)/shard_map/ppermute | solution.py:465
  77.4 13.2 %collective-permute-start.21 = (bf16[512,256]{1,0:T(8,128)(2,1)S(1)}, bf16[512,256]{1,0:T(8,128)(2,1)S(1)}, u32[]{:S(2)}, u32[]{:S(2)}) collective-permute-start(bf16[512,256]{1,0:T(8,128)(2,1)S(1)} %get-tuple-element.131.refs_4_), channel_id=1, source_target_pairs={{0,4},{4,0},{8,12},{12,8},{1,5},{5,1},{9,13},{13,9},{2,6},{6,2},{1... | collective-permute-start | bytes 786440 | tf_op jit(solution)/shard_map/ppermute | solution.py:469
  81.0 9.0 %collective-permute-start.24 = (bf16[512,256]{1,0:T(8,128)(2,1)S(1)}, bf16[512,256]{1,0:T(8,128)(2,1)S(1)}, u32[]{:S(2)}, u32[]{:S(2)}) collective-permute-start(bf16[512,256]{1,0:T(8,128)(2,1)S(1)} %get-tuple-element.137.refs_8_), channel_id=1, source_target_pairs={{0,8},{4,12},{8,0},{12,4},{1,9},{5,13},{9,1},{13,5},{2,10},{6,14},... | collective-permute-start | bytes 786440 | tf_op jit(solution)/shard_map/ppermute | solution.py:465
  88.4 10.0 %collective-permute-start.18 = (bf16[768,256]{1,0:T(8,128)(2,1)S(1)}, bf16[768,256]{1,0:T(8,128)(2,1)S(1)}, u32[]{:S(2)}, u32[]{:S(2)}) collective-permute-start(bf16[768,256]{1,0:T(8,128)(2,1)S(1)} %get-tuple-element.135.refs_0_), channel_id=1, source_target_pairs={{0,8},{4,12},{8,0},{12,4},{1,9},{5,13},{9,1},{13,5},{2,10},{6,14},... | collective-permute-start | bytes 1179656 | tf_op jit(solution)/shard_map/ppermute | solution.py:465
  89.9 2.6 %collective-permute-start.23 = (bf16[512,256]{1,0:T(8,128)(2,1)S(1)}, bf16[512,256]{1,0:T(8,128)(2,1)S(1)}, u32[]{:S(2)}, u32[]{:S(2)}) collective-permute-start(bf16[512,256]{1,0:T(8,128)(2,1)S(1)} %get-tuple-element.137.refs_8_), channel_id=1, source_target_pairs={{0,4},{4,0},{8,12},{12,8},{1,5},{5,1},{9,13},{13,9},{2,6},{6,2},{1... | collective-permute-start | bytes 786440 | tf_op jit(solution)/shard_map/ppermute | solution.py:469
  90.0 2.5 %collective-permute-start.22 = (bf16[512,256]{1,0:T(8,128)(2,1)S(1)}, bf16[512,256]{1,0:T(8,128)(2,1)S(1)}, u32[]{:S(2)}, u32[]{:S(2)}) collective-permute-start(bf16[512,256]{1,0:T(8,128)(2,1)S(1)} %collective-permute-done.16.refs_17_.refs_6_), channel_id=1, source_target_pairs={{0,4},{4,0},{8,12},{12,8},{1,5},{5,1},{9,13},{13,9},{2,6},{6,2},{1... | collective-permute-start | bytes 786440 | tf_op jit(solution)/shard_map/ppermute | solution.py:469
  90.4 2.1 %collective-permute-start.25 = (bf16[512,256]{1,0:T(8,128)(2,1)S(1)}, bf16[512,256]{1,0:T(8,128)(2,1)S(1)}, u32[]{:S(2)}, u32[]{:S(2)}) collective-permute-start(bf16[512,256]{1,0:T(8,128)(2,1)S(1)} %collective-permute-done.24.refs_10_), channel_id=1, source_target_pairs={{0,4},{4,0},{8,12},{12,8},{1,5},{5,1},{9,13},{13,9},{2,6},{6,2},{1... | collective-permute-start | bytes 786440 | tf_op jit(solution)/shard_map/ppermute | solution.py:469
  90.5 1.9 %collective-permute-start.20 = (bf16[256,256]{1,0:T(8,128)(2,1)S(1)}, bf16[256,256]{1,0:T(8,128)(2,1)S(1)}, u32[]{:S(2)}, u32[]{:S(2)}) collective-permute-start(bf16[256,256]{1,0:T(8,128)(2,1)S(1)} %collective-permute-done.15.refs_17_.refs_2_), channel_id=1, source_target_pairs={{0,4},{4,0},{8,12},{12,8},{1,5},{5,1},{9,13},{13,9},{2,6},{6,2},{1... | collective-permute-start | bytes 393224 | tf_op jit(solution)/shard_map/ppermute | solution.py:469
  92.4 6.0 %collective-permute-start.17 = (bf16[768,256]{1,0:T(8,128)(2,1)S(1)}, bf16[768,256]{1,0:T(8,128)(2,1)S(1)}, u32[]{:S(2)}, u32[]{:S(2)}) collective-permute-start(bf16[768,256]{1,0:T(8,128)(2,1)S(1)} %get-tuple-element.135.refs_0_), channel_id=1, source_target_pairs={{0,4},{4,0},{8,12},{12,8},{1,5},{5,1},{9,13},{13,9},{2,6},{6,2},{1... | collective-permute-start | bytes 1179656 | tf_op jit(solution)/shard_map/ppermute | solution.py:469
  98.4 1.7 %collective-permute-start.26 = (bf16[768,256]{1,0:T(8,128)(2,1)S(1)}, bf16[768,256]{1,0:T(8,128)(2,1)S(1)}, u32[]{:S(2)}, u32[]{:S(2)}) collective-permute-start(bf16[768,256]{1,0:T(8,128)(2,1)S(1)} %collective-permute-done.18.refs_2_), channel_id=1, source_target_pairs={{0,4},{4,0},{8,12},{12,8},{1,5},{5,1},{9,13},{13,9},{2,6},{6,2},{1... | collective-permute-start | bytes 1179656 | tf_op jit(solution)/shard_map/ppermute | solution.py:469

commit v10 on v8

--- a/solution.py
+++ b/solution.py
@@ -82,7 +82,7 @@
     )(picks, points)
 
 
-def cosines(chosen, omega, phase, base, width, store, between=None):
+def cosines(chosen, omega, phase, base, width, store, between=None, ahead=None):
     tile = min(256, width)
     count = width // tile
     group = min(512, width)
@@ -93,6 +93,8 @@
         return pl.ds(pl.multiple_of(base + start, tile), size)
 
     def product(c):
+        if ahead is not None and c * tile % group == 0:
+            ahead(c * tile // group)
         return jnp.dot(chosen, omega[:, part(c * tile, tile)], preferred_element_type=f32)
 
     ready = product(0)
@@ -109,15 +111,37 @@
 
 def rates_kernel(start, size, low, high, width, own, begun, keep, ends, f, p, chosen, omega, phase, weights, *refs):
     refs = list(refs)
+    sems = refs.pop() if keep else None
     total, feats = refs.pop(), refs.pop()
     before = refs.pop(0) if begun else None
     refs.pop()
     owned = None if begun else refs.pop(0)
     count = omega.shape[1] // width
+    group = min(512, width)
+    if keep:
+        sources, (omega, weights) = (omega, weights), refs[2:4]
+
+        def coming(step, piece):
+            first = lax.rem(step + p[0] * own, count) * width + piece * group
+            at = pl.ds(pl.multiple_of(first, group), group)
+            n = step * (width // group) + piece
+            return (
+                pltpu.make_async_copy(sources[0].at[:, at], omega.at[:, at], sems.at[0, n]),
+                pltpu.make_async_copy(sources[1].at[at, :], weights.at[at, :], sems.at[1, n]),
+            )
+
+        for step in range(count):
+            for piece in range(width // group):
+                for copy in coming(step, piece):
+                    copy.start()
     total[...] = before[...] if begun else jnp.zeros_like(total)
 
-    def block(place, into, offset):
+    def block(place, into, offset, step):
         parts = []
+
+        def ahead(piece):
+            for copy in coming(step, piece):
+                copy.wait()
 
         def store(cols, value):
             into[:, offset + cols.start : offset + cols.stop] = value
@@ -127,7 +151,14 @@
             parts.append(jnp.dot(done, weights[rows, :], preferred_element_type=f32))
 
         cosines(
-            chosen[start : start + size, :], omega, phase, place * width, width, store, between
+            chosen[start : start + size, :],
+            omega,
+            phase,
+            place * width,
+            width,
+            store,
+            between,
+            ahead if keep else None,
         )
         part = parts[0]
         for q in parts[1:]:
@@ -136,10 +167,10 @@
 
     if not begun:
         for step in range(own):
-            block(p[0] * own + step, owned, step * width)
+            block(p[0] * own + step, owned, step * width, step)
 
     def turn(step, _):
-        block(lax.rem(step + p[0] * own, count), feats, 0)
+        block(lax.rem(step + p[0] * own, count), feats, 0, step)
         return _
 
     lax.fori_loop(low if begun else own, high, turn, 0)
@@ -174,6 +205,7 @@
         outs.append(jax.ShapeDtypeStruct((size, owned), bf16))
     if keep:
         outs += [jax.ShapeDtypeStruct((ins, owned), bf16), jax.ShapeDtypeStruct((1, owned), f32)]
+        outs += [jax.ShapeDtypeStruct(x.shape, bf16) for x in (omega, weights)]
     if ends:
         outs += [jax.ShapeDtypeStruct((size // 2, k), t) for t in (f32, bf16)]
     else:
@@ -191,9 +223,13 @@
         grid_spec=pltpu.PrefetchScalarGridSpec(
             num_scalar_prefetch=2,
             grid=(1,),
-            in_specs=[IN_VMEM] * (4 + begun) + [ANYWHERE] * len(deps),
+            in_specs=(
+                [IN_VMEM, ANYWHERE, IN_VMEM, ANYWHERE] if keep else [IN_VMEM] * (4 + begun)
+            )
+            + [ANYWHERE] * len(deps),
             out_specs=[IN_VMEM] * len(outs) + [ANYWHERE],
-            scratch_shapes=[pltpu.VMEM((size, width), bf16), pltpu.VMEM((size, k), f32)],
+            scratch_shapes=[pltpu.VMEM((size, width), bf16), pltpu.VMEM((size, k), f32)]
+            + [pltpu.SemaphoreType.DMA((2, feat_dev // min(512, width)))] * keep,
         ),
         out_shape=[*outs, TOKEN],
         compiler_params=params(),
@@ -461,7 +497,8 @@
     size_one = points_here * 3 // 8
     parts = [(0, points_here - size_one), (points_here - size_one, size_one)]
     bits = n_feat.bit_length() - 1
-    points, picks, phase = in_hbm(points), in_hbm(picks), phase[None, :]
+    points, picks, omega, weights = map(in_hbm, (points, picks, omega, weights))
+    phase = phase[None, :]
     outer = counts.shape
     counts = counts.reshape(points_here, k)
 
@@ -486,7 +523,7 @@
             masks = masks + [q ^ 2**bit for q in masks]
         return rows, masks
 
-    feats_zero, own_omega, own_phase, kept_zero, sent, token = some_rates(
+    feats_zero, own_omega, own_phase, omega, weights, kept_zero, sent, token = some_rates(
         0, (0, 2), None, True, True, token
     )
     got_zero = swap(sent, n_feat, 0)

time: 98.7 us -> 99.3 us (level)
  Pallas kernels: 52.5 us -> 57.5 us
  local copies, waits for them, and re-layouts: 4.41 us -> 0.03 us
    pallas_call x3, Pallas kernels: 18.6 us -> 23.6 us  [rates(): pl.pallas_call(kernel, grid_spec=pltpu.PrefetchScalarGridSpec(num_scalar_...]
    unnamed x20 -> x12, local copies, waits for them, and re-layouts: 4.41 us -> 0.03 us
  transfers between devices with their start and end apart: 27 -> 27, of which waited for: 14 -> 14; matrix products, arithmetic and copies ran while one was open for 0% -> 0% of each run, Pallas kernels for 48% -> 53%
where the time goes in v10:
time: 99.3 us; the launch traced here: 99.1 us
  Pallas kernels  57.5 us (58%)
  starting transfers between devices  22 us (22%)
  waiting for transfers between devices  18.5 us (19%)
  between operations  1.09 us (1%)
    pallas_call x3, Pallas kernels, rates(): pl.pallas_call(kernel, grid_spec=pltpu.PrefetchScalarGridSpec(num_scalar_...  23.6 us
    pallas_call x6, Pallas kernels, owned_features(): pl.pallas_call(functools.partial(features_kernel, start, size), in_specs=...  13 us
    ppermute x6, starting transfers between devices, swap(): return lax.ppermute(x, 'feat', [(i, i ^ 2 ** bit) for i in range(n)])  10.8 us
    pallas_call x4, Pallas kernels, update(): pl.pallas_call(functools.partial(update_kernel, n, at), grid=(steps,), in...  9.97 us
    ppermute x7, waiting for transfers between devices, ring(): return lax.ppermute(x, axis, [(i, (i + distance) % n) for i in range(n)])  9.83 us
    ppermute x7, starting transfers between devices, ring(): return lax.ppermute(x, axis, [(i, (i + distance) % n) for i in range(n)])  8.8 us
    ppermute x6, waiting for transfers between devices, swap(): return lax.ppermute(x, 'feat', [(i, i ^ 2 ** bit) for i in range(n)])  5.39 us
    pallas_call x1, Pallas kernels, first_part(): pl.pallas_call(functools.partial(first_part_kernel, n), in_specs=[IN_VMEM...  3.61 us
  transfers between devices with their start and end apart: 27, of which 14 were waited for; matrix products, arithmetic and copies ran while one was open for 0% of the time, Pallas kernels for 53%

profile of v10, /device:TPU:0, one launch (start us, length us, event | category | flops | bytes accessed | tf_op | source)
XLA Modules:
  0.0 99.1 jit_solution(11353560113854826280)
XLA Ops:
  0.6 2.5 %chosen_points.1 = (bf16[1024,256]{1,0:T(8,128)(2,1)S(1)}, f32[8,128]{1,0:T(8,128)S(1)}) custom-call(s32[2,512]{1,0:T(2,128)} %picks.1, bf16[2048,256]{1,0:T(8,128)(2,1)} %points.1), custom_call_target="tpu_custom_call" | custom-call | flops 3000000000 | bytes 1024 | tf_op jit(solution)/shard_map/chosen_points/pallas_call | solution.py:70
  3.2 0.5 collective-permute-start.2
  3.7 2.6 %collective-permute-start.4 = (bf16[1024,256]{1,0:T(8,128)(2,1)S(1)}, bf16[1024,256]{1,0:T(8,128)(2,1)S(1)}, u32[]{:S(2)}, u32[]{:S(2)}) collective-permute-start(bf16[1024,256]{1,0:T(8,128)(2,1)S(1)} %get-tuple-element.73.refs_2_), channel_id=1, source_target_pairs={{0,8},{4,12},{8,0},{12,4},{1,9},{5,13},{9,1},{13,5},{2,10},{6,14},... | collective-permute-start | bytes 1572872 | tf_op jit(solution)/shard_map/ppermute | solution.py:472
  6.3 16.5 %partial_log_rates.3 = (bf16[640,2048]{1,0:T(8,128)(2,1)S(1)}, bf16[256,2048]{1,0:T(8,128)(2,1)S(1)}, f32[1,2048]{1,0:T(1,128)S(1)}, bf16[256,8192]{1,0:T(8,128)...) custom-call(s32[1]{0:T(128)} %bitcast.refs_0_.f, ...), custom_call_target="tpu_custom_call" | custom-call | flops 12000000000 | bytes 1024 | tf_op jit(solution)/shard_map/partial_log_rates/pallas_call | solution.py:221
  22.8 1.6 %collective-permute-start = (bf16[320,256]{1,0:T(8,128)(2,1)S(1)}, bf16[320,256]{1,0:T(8,128)(2,1)S(1)}, u32[]{:S(2)}, u32[]{:S(2)}) collective-permute-start(bf16[320,256]{1,0:T(8,128)(2,1)S(1)} %get-tuple-element.80), channel_id=1, source_target_pairs={{0,1},{1,0},{2,3},{3,2},{4,5},{5,4},{6,7},{7,6},{8,9},{9,8},{10,11... | collective-permute-start | bytes 491528 | tf_op jit(solution)/shard_map/ppermute | solution.py:484
  24.4 3.3 %partial_log_rates.4 = (bf16[384,2048]{1,0:T(8,128)(2,1)S(1)}, f32[384,256]{1,0:T(8,128)S(1)}, f32[8,128]{1,0:T(8,128)S(1)}) custom-call(s32[1]{0:T(128)} %bitcast.refs_0_.f, s32[1]{0:T(128)} %bitcast.1.refs_1_.p, bf16[1024,256]{1,0:T(8,128)(2,1)S(1)} %get-tuple-element.73.refs_2_, bf16[256,8192]{1,0:T(8,128)(2,1)S(1)} %get-tuple-element.75.refs_3_, ...), custom_call_target="tpu_custom_call" | custom-call | flops 6000000000 | bytes 1024 | tf_op jit(solution)/shard_map/partial_log_rates/pallas_call | solution.py:221
  27.7 1.4 %collective-permute-done.b = bf16[320,256]{1,0:T(8,128)(2,1)S(1)} collective-permute-done((bf16[320,256]{1,0:T(8,128)(2,1)S(1)}, bf16[320,256]{1,0:T(8,128)(2,1)S(1)}, u32[]{:S(2)}, u32[]{:S(2)}) %collective-permute-start) | collective-permute-done | bytes 163872 | tf_op jit(solution)/shard_map/ppermute | solution.py:484
  29.2 2.7 %collective-permute-start.5 = (bf16[320,256]{1,0:T(8,128)(2,1)S(1)}, bf16[320,256]{1,0:T(8,128)(2,1)S(1)}, u32[]{:S(2)}, u32[]{:S(2)}) collective-permute-start(bf16[320,256]{1,0:T(8,128)(2,1)S(1)} %get-tuple-element.90.a), channel_id=1, source_target_pairs={{0,2},{1,3},{2,0},{3,1},{4,6},{5,7},{6,4},{7,5},{8,10},{9,11},{10,... | collective-permute-start | bytes 491528 | tf_op jit(solution)/shard_map/ppermute | solution.py:484
  31.8 3.8 %partial_log_rates.5 = (f32[192,256]{1,0:T(8,128)S(1)}, bf16[192,256]{1,0:T(8,128)(2,1)S(1)}, f32[8,128]{1,0:T(8,128)S(1)}) custom-call(s32[1]{0:T(128)} %bitcast.refs_0_.f, s32[1]{0:T(128)} %bitcast.1.refs_1_.p, bf16[1024,256]{1,0:T(8,128)(2,1)S(1)} %get-tuple-element.73.refs_2_, bf16[256,8192]{1,0:T(8,128)(2,1)S(1)} %get-tuple-element.75.refs_3_, ...), custom_call_target="tpu_custom_call" | custom-call | flops 6000000000 | bytes 1024 | tf_op jit(solution)/shard_map/partial_log_rates/pallas_call | solution.py:221
  35.6 1.6 %collective-permute-start.1 = (bf16[192,256]{1,0:T(8,128)(2,1)S(1)}, bf16[192,256]{1,0:T(8,128)(2,1)S(1)}, u32[]{:S(2)}, u32[]{:S(2)}) collective-permute-start(bf16[192,256]{1,0:T(8,128)(2,1)S(1)} %get-tuple-element.84), channel_id=1, source_target_pairs={{0,1},{1,0},{2,3},{3,2},{4,5},{5,4},{6,7},{7,6},{8,9},{9,8},{10,11... | collective-permute-start | bytes 294920 | tf_op jit(solution)/shard_map/ppermute | solution.py:484
  37.3 2.6 %owned_features.6 = (bf16[640,2048]{1,0:T(8,128)(2,1)S(1)}, f32[8,128]{1,0:T(8,128)S(1)}) custom-call(bf16[1024,256]{1,0:T(8,128)(2,1)S(1)} %collective-permute-done.2.chosen, bf16[256,2048]{1,0:T(8,128)(2,1)S(1)} %get-tuple-element.85.omega, f32[1,2048]{1,0:T(1,128)S(1)} %get-tuple-element.86.phase, f32[8,128]{1,0:T(8,128)S(1)} %get-tuple-element.87.refs_0_), custom_call_target="tpu_custom_call" | custom-call | flops 1000000000 | bytes 1024 | tf_op jit(solution)/shard_map/owned_features/pallas_call | solution.py:252
  39.9 1.3 %collective-permute-done.1.b = bf16[192,256]{1,0:T(8,128)(2,1)S(1)} collective-permute-done((bf16[192,256]{1,0:T(8,128)(2,1)S(1)}, bf16[192,256]{1,0:T(8,128)(2,1)S(1)}, u32[]{:S(2)}, u32[]{:S(2)}) %collective-permute-start.1) | collective-permute-done | bytes 98336 | tf_op jit(solution)/shard_map/ppermute | solution.py:484
  41.2 0.0 collective-permute-done.5.b
  41.3 0.8 collective-permute-start.8
  42.1 2.9 %collective-permute-start.3 = (bf16[192,256]{1,0:T(8,128)(2,1)S(1)}, bf16[192,256]{1,0:T(8,128)(2,1)S(1)}, u32[]{:S(2)}, u32[]{:S(2)}) collective-permute-start(bf16[192,256]{1,0:T(8,128)(2,1)S(1)} %get-tuple-element.89.a), channel_id=1, source_target_pairs={{0,2},{1,3},{2,0},{3,1},{4,6},{5,7},{6,4},{7,5},{8,10},{9,11},{10,... | collective-permute-start | bytes 294920 | tf_op jit(solution)/shard_map/ppermute | solution.py:484
  44.9 2.6 %owned_features.7 = (bf16[640,2048]{1,0:T(8,128)(2,1)S(1)}, f32[8,128]{1,0:T(8,128)S(1)}) custom-call(bf16[1024,256]{1,0:T(8,128)(2,1)S(1)} %collective-permute-done.4.chosen, bf16[256,2048]{1,0:T(8,128)(2,1)S(1)} %get-tuple-element.85.omega, f32[1,2048]{1,0:T(1,128)S(1)} %get-tuple-element.86.phase, f32[8,128]{1,0:T(8,128)S(1)} %get-tuple-element.92.refs_0_), custom_call_target="tpu_custom_call" | custom-call | flops 1000000000 | bytes 1024 | tf_op jit(solution)/shard_map/owned_features/pallas_call | solution.py:252
  47.5 0.6 collective-permute-done.3.b
  48.2 1.3 %collective-permute-done.8.refs_1_ = bf16[320,256]{1,0:T(8,128)(2,1)S(1)} collective-permute-done((bf16[320,256]{1,0:T(8,128)(2,1)S(1)}, bf16[320,256]{1,0:T(8,128)(2,1)S(1)}, u32[]{:S(2)}, u32[]{:S(2)}) %collective-permute-start.8) | collective-permute-done | bytes 163872 | tf_op jit(solution)/shard_map/ppermute | solution.py:484
  49.5 1.0 %residuals.2 = (f32[1024,256]{1,0:T(8,128)}, bf16[256,640]{1,0:T(8,128)(2,1)S(1)}, f32[8,128]{1,0:T(8,128)S(1)}) custom-call(s32[1]{0:T(128)} %bitcast.refs_0_.f, bf16[320,256]{1,0:T(8,128)(2,1)S(1)} %get-tuple-element.95.refs_0_, bf16[320,256]{1,0:T(8,128)(2,1)S(1)} %collective-permute-done.8.refs_1_, s32[1024,256]{1,0:T(8,128)S(1)} %bitcast.5, ...), custom_call_target="tpu_custom_call" | custom-call | flops 1000000000 | bytes 1024 | tf_op jit(solution)/shard_map/residuals/pallas_call | solution.py:330
  50.5 0.9 collective-permute-start.9
  51.4 1.2 %collective-permute-start.6 = (bf16[192,256]{1,0:T(8,128)(2,1)S(1)}, bf16[192,256]{1,0:T(8,128)(2,1)S(1)}, u32[]{:S(2)}, u32[]{:S(2)}) collective-permute-start(bf16[192,256]{1,0:T(8,128)(2,1)S(1)} %get-tuple-element.94.refs_0_), channel_id=1, source_target_pairs={{0,1},{1,0},{2,3},{3,2},{4,5},{5,4},{6,7},{7,6},{8,9},{9,8},{10,11... | collective-permute-start | bytes 294920 | tf_op jit(solution)/shard_map/ppermute | solution.py:484
  52.6 2.6 %owned_features.8 = (bf16[640,2048]{1,0:T(8,128)(2,1)S(1)}, f32[8,128]{1,0:T(8,128)S(1)}) custom-call(bf16[1024,256]{1,0:T(8,128)(2,1)S(1)} %collective-permute-done.7.chosen, bf16[256,2048]{1,0:T(8,128)(2,1)S(1)} %get-tuple-element.85.omega, f32[1,2048]{1,0:T(1,128)S(1)} %get-tuple-element.86.phase, f32[8,128]{1,0:T(8,128)S(1)} %get-tuple-element.97.refs_0_), custom_call_target="tpu_custom_call" | custom-call | flops 1000000000 | bytes 1024 | tf_op jit(solution)/shard_map/owned_features/pallas_call | solution.py:252
  55.2 0.8 collective-permute-done.6.refs_1_
  56.0 0.9 residuals.3
  56.9 1.3 %collective-permute-start.11 = (bf16[256,384]{1,0:T(8,128)(2,1)S(1)}, bf16[256,384]{1,0:T(8,128)(2,1)S(1)}, u32[]{:S(2)}, u32[]{:S(2)}) collective-permute-start(bf16[256,384]{1,0:T(8,128)(2,1)S(1)} %get-tuple-element.110.refs_4_), channel_id=1, source_target_pairs={{0,8},{4,12},{8,0},{12,4},{1,9},{5,13},{9,1},{13,5},{2,10},{6,14},... | collective-permute-start | bytes 589832 | tf_op jit(solution)/shard_map/ppermute | solution.py:472
  58.2 1.6 %owned_features.9 = (bf16[384,2048]{1,0:T(8,128)(2,1)S(1)}, f32[8,128]{1,0:T(8,128)S(1)}) custom-call(bf16[1024,256]{1,0:T(8,128)(2,1)S(1)} %collective-permute-done.2.chosen, bf16[256,2048]{1,0:T(8,128)(2,1)S(1)} %get-tuple-element.85.omega, f32[1,2048]{1,0:T(1,128)S(1)} %get-tuple-element.86.phase, f32[8,128]{1,0:T(8,128)S(1)} %get-tuple-element.102.refs_0_), custom_call_target="tpu_custom_call" | custom-call | flops 100000000 | bytes 1024 | tf_op jit(solution)/shard_map/owned_features/pallas_call | solution.py:252
  59.9 1.9 %owned_features.10 = (bf16[384,2048]{1,0:T(8,128)(2,1)S(1)}, f32[8,128]{1,0:T(8,128)S(1)}) custom-call(bf16[1024,256]{1,0:T(8,128)(2,1)S(1)} %collective-permute-done.4.chosen, bf16[256,2048]{1,0:T(8,128)(2,1)S(1)} %get-tuple-element.85.omega, f32[1,2048]{1,0:T(1,128)S(1)} %get-tuple-element.86.phase, f32[8,128]{1,0:T(8,128)S(1)} %get-tuple-element.104.refs_0_), custom_call_target="tpu_custom_call" | custom-call | flops 100000000 | bytes 1024 | tf_op jit(solution)/shard_map/owned_features/pallas_call | solution.py:252
  61.8 0.6 collective-permute-start.14
  62.4 0.1 collective-permute-start.10
  62.4 1.6 %owned_features.11 = (bf16[384,2048]{1,0:T(8,128)(2,1)S(1)}, f32[8,128]{1,0:T(8,128)S(1)}) custom-call(bf16[1024,256]{1,0:T(8,128)(2,1)S(1)} %collective-permute-done.7.chosen, bf16[256,2048]{1,0:T(8,128)(2,1)S(1)} %get-tuple-element.85.omega, f32[1,2048]{1,0:T(1,128)S(1)} %get-tuple-element.86.phase, f32[8,128]{1,0:T(8,128)S(1)} %get-tuple-element.108.refs_0_), custom_call_target="tpu_custom_call" | custom-call | flops 100000000 | bytes 1024 | tf_op jit(solution)/shard_map/owned_features/pallas_call | solution.py:252
  64.1 0.5 collective-permute-start.12
  64.6 0.0 collective-permute-done.13.refs_5_
  64.6 0.0 collective-permute-done.14.refs_7_
  64.6 0.0 copy-start.1
  64.6 0.0 copy-start.2
  64.6 0.0 copy-start.3
  64.6 3.6 %first_part.1 = (f32[2048,256]{1,0:T(8,128)S(1)}, f32[8,128]{1,0:T(8,128)S(1)}) custom-call(bf16[640,2048]{1,0:T(8,128)(2,1)S(1)} %get-tuple-element.113.refs_0_, bf16[640,2048]{1,0:T(8,128)(2,1)S(1)} %get-tuple-element.114.refs_1_, bf16[640,2048]{1,0:T(8,128)(2,1)S(1)} %get-tuple-element.115.refs_2_, bf16[640,2048]{1,0:T(8,128)(2,1)S(1)} %get-tuple-element.116.refs_3_, ...), custom_call_target="tpu_custom_call" | custom-call | flops 300000000 | bytes 1024 | tf_op jit(solution)/shard_map/first_part/pallas_call | solution.py:372
  68.3 0.0 collective-permute-done.10.refs_5_
  68.3 0.0 collective-permute-done.12.refs_7_
  68.3 1.7 %update.4 = (f32[1,2048,256]{2,1,0:T(8,128)}, f32[1,2048,256]{2,1,0:T(8,128)}, f32[1,2048,256]{2,1,0:T(8,128)}, bf16[256,256]{1,0:T(8,128)(2,1)S(1)}) custom-call(bf16[384,2048]{1,0:T(8,128)(2,1)S(1)} %get-tuple-element.101.refs_0_, bf16[384,2048]{1,0:T(8,128)(2,1)S(1)} %get-tuple-element.103.refs_1_, bf16[384,2048]{1,0:T(8,128)(2,1)S(1)} %get-tuple-element.105.refs_2_, ...), custom_call_target="tpu_custom_call" | custom-call | flops 4000000000 | bytes 1024 | tf_op jit(solution)/shard_map/update/pallas_call | solution.py:420
  70.0 0.8 collective-permute-start.15
  70.8 0.0 collective-permute-start.19
  70.8 2.5 %update.5 = (f32[1,2048,256]{2,1,0:T(8,128)}, f32[1,2048,256]{2,1,0:T(8,128)}, f32[1,2048,256]{2,1,0:T(8,128)}, bf16[512,256]{1,0:T(8,128)(2,1)S(1)}) custom-call(bf16[384,2048]{1,0:T(8,128)(2,1)S(1)} %get-tuple-element.101.refs_0_, bf16[384,2048]{1,0:T(8,128)(2,1)S(1)} %get-tuple-element.103.refs_1_, ...), custom_call_target="tpu_custom_call", output_to_operand_aliasing={{0}: (13, {}), {1}: (14, {}), {2}: (15, {})} | custom-call | flops 4000000000 | bytes 1024 | tf_op jit(solution)/shard_map/update/pallas_call | solution.py:420
  73.2 1.2 %collective-permute-start.16 = (bf16[512,256]{1,0:T(8,128)(2,1)S(1)}, bf16[512,256]{1,0:T(8,128)(2,1)S(1)}, u32[]{:S(2)}, u32[]{:S(2)}) collective-permute-start(bf16[512,256]{1,0:T(8,128)(2,1)S(1)} %get-tuple-element.131.refs_4_), channel_id=1, source_target_pairs={{0,8},{4,12},{8,0},{12,4},{1,9},{5,13},{9,1},{13,5},{2,10},{6,14},... | collective-permute-start | bytes 786440 | tf_op jit(solution)/shard_map/ppermute | solution.py:472
  74.5 1.0 collective-permute-done.15.refs_17_.refs_2_
  75.4 2.5 %update.6 = (f32[1,2048,256]{2,1,0:T(8,128)}, f32[1,2048,256]{2,1,0:T(8,128)}, f32[1,2048,256]{2,1,0:T(8,128)}, bf16[512,256]{1,0:T(8,128)(2,1)S(1)}) custom-call(bf16[384,2048]{1,0:T(8,128)(2,1)S(1)} %get-tuple-element.101.refs_0_, bf16[384,2048]{1,0:T(8,128)(2,1)S(1)} %get-tuple-element.103.refs_1_, ...), custom_call_target="tpu_custom_call", output_to_operand_aliasing={{0}: (13, {}), {1}: (14, {}), {2}: (15, {})} | custom-call | flops 4000000000 | bytes 1024 | tf_op jit(solution)/shard_map/update/pallas_call | solution.py:420
  77.9 0.8 collective-permute-start.24
  78.7 0.0 collective-permute-start.20
  78.7 3.6 %collective-permute-done.16.refs_17_.refs_6_ = bf16[512,256]{1,0:T(8,128)(2,1)S(1)} collective-permute-done((bf16[512,256]{1,0:T(8,128)(2,1)S(1)}, bf16[512,256]{1,0:T(8,128)(2,1)S(1)}, u32[]{:S(2)}, u32[]{:S(2)}) %collective-permute-start.16) | collective-permute-done | bytes 262176 | tf_op jit(solution)/shard_map/ppermute | solution.py:472
  82.3 3.3 %update.7 = (f32[1,2048,256]{2,1,0:T(8,128)}, f32[1,2048,256]{2,1,0:T(8,128)}, f32[1,2048,256]{2,1,0:T(8,128)}, bf16[768,256]{1,0:T(8,128)(2,1)S(1)}) custom-call(bf16[384,2048]{1,0:T(8,128)(2,1)S(1)} %get-tuple-element.101.refs_0_, bf16[384,2048]{1,0:T(8,128)(2,1)S(1)} %get-tuple-element.103.refs_1_, ...), custom_call_target="tpu_custom_call", output_to_operand_aliasing={{0}: (13, {}), {1}: (14, {}), {2}: (15, {})} | custom-call | flops 4000000000 | bytes 1024 | tf_op jit(solution)/shard_map/update/pallas_call | solution.py:420
  85.7 1.2 %collective-permute-start.18 = (bf16[768,256]{1,0:T(8,128)(2,1)S(1)}, bf16[768,256]{1,0:T(8,128)(2,1)S(1)}, u32[]{:S(2)}, u32[]{:S(2)}) collective-permute-start(bf16[768,256]{1,0:T(8,128)(2,1)S(1)} %get-tuple-element.135.refs_0_), channel_id=1, source_target_pairs={{0,8},{4,12},{8,0},{12,4},{1,9},{5,13},{9,1},{13,5},{2,10},{6,14},... | collective-permute-start | bytes 1179656 | tf_op jit(solution)/shard_map/ppermute | solution.py:472
  86.9 0.0 collective-permute-start.21
  86.9 0.7 collective-permute-done.24.refs_10_
  87.6 0.5 collective-permute-start.22
  88.1 0.1 collective-permute-start.25
  88.2 0.3 collective-permute-done.21.refs_5_
  88.5 0.2 collective-permute-start.17
  88.6 0.5 collective-permute-done.23.refs_9_
  89.1 0.4 collective-permute-done.22.refs_7_
  89.5 0.4 collective-permute-done.25.refs_11_
  89.9 1.6 %put_rows.2.refs_4_ = bf16[8192,256]{1,0:T(8,128)(2,1)} custom-call(s32[1]{0:T(128)} %bitcast.1.refs_1_.p, bf16[256,256]{1,0:T(8,128)(2,1)S(1)} %get-tuple-element.127.refs_0_, bf16[256,256]{1,0:T(8,128)(2,1)S(1)} %collective-permute-done.19.refs_1_, bf16[256,256]{1,0:T(8,128)(2,1)S(1)} %collective-permute-done.15.refs_17_.refs_2_, ...), custom_call_target="tpu_custom_call" | custom-call | flops 10000000 | bytes 1024 | tf_op jit(solution)/shard_map/put_rows/pallas_call | solution.py:454
  91.5 4.6 %collective-permute-done.18.refs_2_ = bf16[768,256]{1,0:T(8,128)(2,1)S(1)} collective-permute-done((bf16[768,256]{1,0:T(8,128)(2,1)S(1)}, bf16[768,256]{1,0:T(8,128)(2,1)S(1)}, u32[]{:S(2)}, u32[]{:S(2)}) %collective-permute-start.18) | collective-permute-done | bytes 393248 | tf_op jit(solution)/shard_map/ppermute | solution.py:472
  96.0 1.7 %collective-permute-done.26.refs_3_ = bf16[768,256]{1,0:T(8,128)(2,1)S(1)} collective-permute-done((bf16[768,256]{1,0:T(8,128)(2,1)S(1)}, bf16[768,256]{1,0:T(8,128)(2,1)S(1)}, u32[]{:S(2)}, u32[]{:S(2)}) %collective-permute-start.26) | collective-permute-done | bytes 393248 | tf_op jit(solution)/shard_map/ppermute | solution.py:476
  97.8 1.2 %put_rows.3 = bf16[8192,256]{1,0:T(8,128)(2,1)} custom-call(s32[1]{0:T(128)} %bitcast.1.refs_1_.p, bf16[768,256]{1,0:T(8,128)(2,1)S(1)} %get-tuple-element.135.refs_0_, bf16[768,256]{1,0:T(8,128)(2,1)S(1)} %collective-permute-done.17.refs_1_, bf16[768,256]{1,0:T(8,128)(2,1)S(1)} %collective-permute-done.18.refs_2_, ...), custom_call_target="tpu_custom_call", output_to_operand_aliasing={{}: (5, {})} | custom-call | flops 10000000 | bytes 1024 | tf_op jit(solution)/shard_map/put_rows/pallas_call | solution.py:454
  (25 shorter events, 0.2 us)
Async XLA Ops:
  0.6 5.7 %copy-start.5 = (f32[8192]{0:T(1024)S(1)}, f32[8192]{0:T(1024)}, u32[]{:S(2)}) copy-start(f32[8192]{0:T(1024)} %param.13) | copy-start | bytes 98308
  3.2 34.1 %collective-permute-start.2 = (bf16[1024,256]{1,0:T(8,128)(2,1)S(1)}, bf16[1024,256]{1,0:T(8,128)(2,1)S(1)}, u32[]{:S(2)}, u32[]{:S(2)}) collective-permute-start(bf16[1024,256]{1,0:T(8,128)(2,1)S(1)} %get-tuple-element.73.refs_2_), channel_id=1, source_target_pairs={{0,4},{4,0},{8,12},{12,8},{1,5},{5,1},{9,13},{13,9},{2,6},{6,2},{1... | collective-permute-start | bytes 1572872 | tf_op jit(solution)/shard_map/ppermute | solution.py:476
  3.7 33.6 %collective-permute-start.4 = (bf16[1024,256]{1,0:T(8,128)(2,1)S(1)}, bf16[1024,256]{1,0:T(8,128)(2,1)S(1)}, u32[]{:S(2)}, u32[]{:S(2)}) collective-permute-start(bf16[1024,256]{1,0:T(8,128)(2,1)S(1)} %get-tuple-element.73.refs_2_), channel_id=1, source_target_pairs={{0,8},{4,12},{8,0},{12,4},{1,9},{5,13},{9,1},{13,5},{2,10},{6,14},... | collective-permute-start | bytes 1572872 | tf_op jit(solution)/shard_map/ppermute | solution.py:472
  22.8 6.3 %collective-permute-start = (bf16[320,256]{1,0:T(8,128)(2,1)S(1)}, bf16[320,256]{1,0:T(8,128)(2,1)S(1)}, u32[]{:S(2)}, u32[]{:S(2)}) collective-permute-start(bf16[320,256]{1,0:T(8,128)(2,1)S(1)} %get-tuple-element.80), channel_id=1, source_target_pairs={{0,1},{1,0},{2,3},{3,2},{4,5},{5,4},{6,7},{7,6},{8,9},{9,8},{10,11... | collective-permute-start | bytes 491528 | tf_op jit(solution)/shard_map/ppermute | solution.py:484
  29.2 12.0 %collective-permute-start.5 = (bf16[320,256]{1,0:T(8,128)(2,1)S(1)}, bf16[320,256]{1,0:T(8,128)(2,1)S(1)}, u32[]{:S(2)}, u32[]{:S(2)}) collective-permute-start(bf16[320,256]{1,0:T(8,128)(2,1)S(1)} %get-tuple-element.90.a), channel_id=1, source_target_pairs={{0,2},{1,3},{2,0},{3,1},{4,6},{5,7},{6,4},{7,5},{8,10},{9,11},{10,... | collective-permute-start | bytes 491528 | tf_op jit(solution)/shard_map/ppermute | solution.py:484
  35.6 5.5 %collective-permute-start.1 = (bf16[192,256]{1,0:T(8,128)(2,1)S(1)}, bf16[192,256]{1,0:T(8,128)(2,1)S(1)}, u32[]{:S(2)}, u32[]{:S(2)}) collective-permute-start(bf16[192,256]{1,0:T(8,128)(2,1)S(1)} %get-tuple-element.84), channel_id=1, source_target_pairs={{0,1},{1,0},{2,3},{3,2},{4,5},{5,4},{6,7},{7,6},{8,9},{9,8},{10,11... | collective-permute-start | bytes 294920 | tf_op jit(solution)/shard_map/ppermute | solution.py:484
  37.3 15.3 %collective-permute-start.7 = (bf16[1024,256]{1,0:T(8,128)(2,1)S(1)}, bf16[1024,256]{1,0:T(8,128)(2,1)S(1)}, u32[]{:S(2)}, u32[]{:S(2)}) collective-permute-start(bf16[1024,256]{1,0:T(8,128)(2,1)S(1)} %collective-permute-done.4.chosen), channel_id=1, source_target_pairs={{0,4},{4,0},{8,12},{12,8},{1,5},{5,1},{9,13},{13,9},{2,6},{6,2},{1... | collective-permute-start | bytes 1572872 | tf_op jit(solution)/shard_map/ppermute | solution.py:476
  41.3 8.2 %collective-permute-start.8 = (bf16[320,256]{1,0:T(8,128)(2,1)S(1)}, bf16[320,256]{1,0:T(8,128)(2,1)S(1)}, u32[]{:S(2)}, u32[]{:S(2)}) collective-permute-start(bf16[320,256]{1,0:T(8,128)(2,1)S(1)} %get-tuple-element.95.refs_0_), channel_id=1, source_target_pairs={{0,1},{1,0},{2,3},{3,2},{4,5},{5,4},{6,7},{7,6},{8,9},{9,8},{10,11... | collective-permute-start | bytes 491528 | tf_op jit(solution)/shard_map/ppermute | solution.py:484
  42.1 6.1 %collective-permute-start.3 = (bf16[192,256]{1,0:T(8,128)(2,1)S(1)}, bf16[192,256]{1,0:T(8,128)(2,1)S(1)}, u32[]{:S(2)}, u32[]{:S(2)}) collective-permute-start(bf16[192,256]{1,0:T(8,128)(2,1)S(1)} %get-tuple-element.89.a), channel_id=1, source_target_pairs={{0,2},{1,3},{2,0},{3,1},{4,6},{5,7},{6,4},{7,5},{8,10},{9,11},{10,... | collective-permute-start | bytes 294920 | tf_op jit(solution)/shard_map/ppermute | solution.py:484
  44.9 4.5 %copy-start.4 = (s32[2,512,256]{2,1,0:T(8,128)S(1)}, s32[2,512,256]{2,1,0:T(8,128)}, u32[]{:S(2)}) copy-start(s32[2,512,256]{2,1,0:T(8,128)} %param.15) | copy-start | bytes 3145732
  50.5 11.3 %collective-permute-start.9 = (bf16[256,640]{1,0:T(8,128)(2,1)S(1)}, bf16[256,640]{1,0:T(8,128)(2,1)S(1)}, u32[]{:S(2)}, u32[]{:S(2)}) collective-permute-start(bf16[256,640]{1,0:T(8,128)(2,1)S(1)} %get-tuple-element.106.refs_4_), channel_id=1, source_target_pairs={{0,8},{4,12},{8,0},{12,4},{1,9},{5,13},{9,1},{13,5},{2,10},{6,14},... | collective-permute-start | bytes 983048 | tf_op jit(solution)/shard_map/ppermute | solution.py:472
  51.4 4.6 %collective-permute-start.6 = (bf16[192,256]{1,0:T(8,128)(2,1)S(1)}, bf16[192,256]{1,0:T(8,128)(2,1)S(1)}, u32[]{:S(2)}, u32[]{:S(2)}) collective-permute-start(bf16[192,256]{1,0:T(8,128)(2,1)S(1)} %get-tuple-element.94.refs_0_), channel_id=1, source_target_pairs={{0,1},{1,0},{2,3},{3,2},{4,5},{5,4},{6,7},{7,6},{8,9},{9,8},{10,11... | collective-permute-start | bytes 294920 | tf_op jit(solution)/shard_map/ppermute | solution.py:484
  56.9 7.2 %collective-permute-start.11 = (bf16[256,384]{1,0:T(8,128)(2,1)S(1)}, bf16[256,384]{1,0:T(8,128)(2,1)S(1)}, u32[]{:S(2)}, u32[]{:S(2)}) collective-permute-start(bf16[256,384]{1,0:T(8,128)(2,1)S(1)} %get-tuple-element.110.refs_4_), channel_id=1, source_target_pairs={{0,8},{4,12},{8,0},{12,4},{1,9},{5,13},{9,1},{13,5},{2,10},{6,14},... | collective-permute-start | bytes 589832 | tf_op jit(solution)/shard_map/ppermute | solution.py:472
  58.2 6.4 %collective-permute-start.13 = (bf16[256,640]{1,0:T(8,128)(2,1)S(1)}, bf16[256,640]{1,0:T(8,128)(2,1)S(1)}, u32[]{:S(2)}, u32[]{:S(2)}) collective-permute-start(bf16[256,640]{1,0:T(8,128)(2,1)S(1)} %get-tuple-element.106.refs_4_), channel_id=1, source_target_pairs={{0,4},{4,0},{8,12},{12,8},{1,5},{5,1},{9,13},{13,9},{2,6},{6,2},{1... | collective-permute-start | bytes 983048 | tf_op jit(solution)/shard_map/ppermute | solution.py:476
  58.2 6.4 %copy-start = (f32[1,2048,256]{2,1,0:T(8,128)S(1)}, f32[1,2048,256]{2,1,0:T(8,128)}, u32[]{:S(2)}) copy-start(f32[1,2048,256]{2,1,0:T(8,128)} %refs_10_.7) | copy-start | bytes 6291460
  61.8 2.8 %collective-permute-start.14 = (bf16[256,640]{1,0:T(8,128)(2,1)S(1)}, bf16[256,640]{1,0:T(8,128)(2,1)S(1)}, u32[]{:S(2)}, u32[]{:S(2)}) collective-permute-start(bf16[256,640]{1,0:T(8,128)(2,1)S(1)} %collective-permute-done.9.refs_6_), channel_id=1, source_target_pairs={{0,4},{4,0},{8,12},{12,8},{1,5},{5,1},{9,13},{13,9},{2,6},{6,2},{1... | collective-permute-start | bytes 983048 | tf_op jit(solution)/shard_map/ppermute | solution.py:476
  62.4 5.9 %collective-permute-start.10 = (bf16[256,384]{1,0:T(8,128)(2,1)S(1)}, bf16[256,384]{1,0:T(8,128)(2,1)S(1)}, u32[]{:S(2)}, u32[]{:S(2)}) collective-permute-start(bf16[256,384]{1,0:T(8,128)(2,1)S(1)} %get-tuple-element.110.refs_4_), channel_id=1, source_target_pairs={{0,4},{4,0},{8,12},{12,8},{1,5},{5,1},{9,13},{13,9},{2,6},{6,2},{1... | collective-permute-start | bytes 589832 | tf_op jit(solution)/shard_map/ppermute | solution.py:476
  64.1 4.2 %collective-permute-start.12 = (bf16[256,384]{1,0:T(8,128)(2,1)S(1)}, bf16[256,384]{1,0:T(8,128)(2,1)S(1)}, u32[]{:S(2)}, u32[]{:S(2)}) collective-permute-start(bf16[256,384]{1,0:T(8,128)(2,1)S(1)} %collective-permute-done.11.refs_6_), channel_id=1, source_target_pairs={{0,4},{4,0},{8,12},{12,8},{1,5},{5,1},{9,13},{13,9},{2,6},{6,2},{1... | collective-permute-start | bytes 589832 | tf_op jit(solution)/shard_map/ppermute | solution.py:476
  64.6 3.7 %copy-start.1 = (f32[1,2048,256]{2,1,0:T(8,128)S(1)}, f32[1,2048,256]{2,1,0:T(8,128)}, u32[]{:S(2)}) copy-start(f32[1,2048,256]{2,1,0:T(8,128)} %refs_11_.7) | copy-start | bytes 6291460
  64.6 3.7 %copy-start.2 = (f32[1,2048,256]{2,1,0:T(8,128)S(1)}, f32[1,2048,256]{2,1,0:T(8,128)}, u32[]{:S(2)}) copy-start(f32[1,2048,256]{2,1,0:T(8,128)} %refs_12_.7) | copy-start | bytes 6291460
  64.6 3.7 %copy-start.3 = (bf16[256,256]{1,0:T(8,128)(2,1)S(1)}, bf16[256,256]{1,0:T(8,128)(2,1)}, u32[]{:S(2)}) copy-start(bf16[256,256]{1,0:T(8,128)(2,1)} %refs_9_.7) | copy-start | bytes 393220
  70.0 5.5 %collective-permute-start.15 = (bf16[256,256]{1,0:T(8,128)(2,1)S(1)}, bf16[256,256]{1,0:T(8,128)(2,1)S(1)}, u32[]{:S(2)}, u32[]{:S(2)}) collective-permute-start(bf16[256,256]{1,0:T(8,128)(2,1)S(1)} %get-tuple-element.127.refs_0_), channel_id=1, source_target_pairs={{0,8},{4,12},{8,0},{12,4},{1,9},{5,13},{9,1},{13,5},{2,10},{6,14},... | collective-permute-start | bytes 393224 | tf_op jit(solution)/shard_map/ppermute | solution.py:472
  70.8 16.8 %collective-permute-start.19 = (bf16[256,256]{1,0:T(8,128)(2,1)S(1)}, bf16[256,256]{1,0:T(8,128)(2,1)S(1)}, u32[]{:S(2)}, u32[]{:S(2)}) collective-permute-start(bf16[256,256]{1,0:T(8,128)(2,1)S(1)} %get-tuple-element.127.refs_0_), channel_id=1, source_target_pairs={{0,4},{4,0},{8,12},{12,8},{1,5},{5,1},{9,13},{13,9},{2,6},{6,2},{1... | collective-permute-start | bytes 393224 | tf_op jit(solution)/shard_map/ppermute | solution.py:476
  73.2 9.1 %collective-permute-start.16 = (bf16[512,256]{1,0:T(8,128)(2,1)S(1)}, bf16[512,256]{1,0:T(8,128)(2,1)S(1)}, u32[]{:S(2)}, u32[]{:S(2)}) collective-permute-start(bf16[512,256]{1,0:T(8,128)(2,1)S(1)} %get-tuple-element.131.refs_4_), channel_id=1, source_target_pairs={{0,8},{4,12},{8,0},{12,4},{1,9},{5,13},{9,1},{13,5},{2,10},{6,14},... | collective-permute-start | bytes 786440 | tf_op jit(solution)/shard_map/ppermute | solution.py:472
  77.9 9.7 %collective-permute-start.24 = (bf16[512,256]{1,0:T(8,128)(2,1)S(1)}, bf16[512,256]{1,0:T(8,128)(2,1)S(1)}, u32[]{:S(2)}, u32[]{:S(2)}) collective-permute-start(bf16[512,256]{1,0:T(8,128)(2,1)S(1)} %get-tuple-element.137.refs_8_), channel_id=1, source_target_pairs={{0,8},{4,12},{8,0},{12,4},{1,9},{5,13},{9,1},{13,5},{2,10},{6,14},... | collective-permute-start | bytes 786440 | tf_op jit(solution)/shard_map/ppermute | solution.py:472
  78.7 9.4 %collective-permute-start.20 = (bf16[256,256]{1,0:T(8,128)(2,1)S(1)}, bf16[256,256]{1,0:T(8,128)(2,1)S(1)}, u32[]{:S(2)}, u32[]{:S(2)}) collective-permute-start(bf16[256,256]{1,0:T(8,128)(2,1)S(1)} %collective-permute-done.15.refs_17_.refs_2_), channel_id=1, source_target_pairs={{0,4},{4,0},{8,12},{12,8},{1,5},{5,1},{9,13},{13,9},{2,6},{6,2},{1... | collective-permute-start | bytes 393224 | tf_op jit(solution)/shard_map/ppermute | solution.py:476
  85.7 10.4 %collective-permute-start.18 = (bf16[768,256]{1,0:T(8,128)(2,1)S(1)}, bf16[768,256]{1,0:T(8,128)(2,1)S(1)}, u32[]{:S(2)}, u32[]{:S(2)}) collective-permute-start(bf16[768,256]{1,0:T(8,128)(2,1)S(1)} %get-tuple-element.135.refs_0_), channel_id=1, source_target_pairs={{0,8},{4,12},{8,0},{12,4},{1,9},{5,13},{9,1},{13,5},{2,10},{6,14},... | collective-permute-start | bytes 1179656 | tf_op jit(solution)/shard_map/ppermute | solution.py:472
  86.9 1.5 %collective-permute-start.21 = (bf16[512,256]{1,0:T(8,128)(2,1)S(1)}, bf16[512,256]{1,0:T(8,128)(2,1)S(1)}, u32[]{:S(2)}, u32[]{:S(2)}) collective-permute-start(bf16[512,256]{1,0:T(8,128)(2,1)S(1)} %get-tuple-element.131.refs_4_), channel_id=1, source_target_pairs={{0,4},{4,0},{8,12},{12,8},{1,5},{5,1},{9,13},{13,9},{2,6},{6,2},{1... | collective-permute-start | bytes 786440 | tf_op jit(solution)/shard_map/ppermute | solution.py:476
  87.6 1.5 %collective-permute-start.23 = (bf16[512,256]{1,0:T(8,128)(2,1)S(1)}, bf16[512,256]{1,0:T(8,128)(2,1)S(1)}, u32[]{:S(2)}, u32[]{:S(2)}) collective-permute-start(bf16[512,256]{1,0:T(8,128)(2,1)S(1)} %get-tuple-element.137.refs_8_), channel_id=1, source_target_pairs={{0,4},{4,0},{8,12},{12,8},{1,5},{5,1},{9,13},{13,9},{2,6},{6,2},{1... | collective-permute-start | bytes 786440 | tf_op jit(solution)/shard_map/ppermute | solution.py:476
  87.6 1.9 %collective-permute-start.22 = (bf16[512,256]{1,0:T(8,128)(2,1)S(1)}, bf16[512,256]{1,0:T(8,128)(2,1)S(1)}, u32[]{:S(2)}, u32[]{:S(2)}) collective-permute-start(bf16[512,256]{1,0:T(8,128)(2,1)S(1)} %collective-permute-done.16.refs_17_.refs_6_), channel_id=1, source_target_pairs={{0,4},{4,0},{8,12},{12,8},{1,5},{5,1},{9,13},{13,9},{2,6},{6,2},{1... | collective-permute-start | bytes 786440 | tf_op jit(solution)/shard_map/ppermute | solution.py:476
  88.1 1.8 %collective-permute-start.25 = (bf16[512,256]{1,0:T(8,128)(2,1)S(1)}, bf16[512,256]{1,0:T(8,128)(2,1)S(1)}, u32[]{:S(2)}, u32[]{:S(2)}) collective-permute-start(bf16[512,256]{1,0:T(8,128)(2,1)S(1)} %collective-permute-done.24.refs_10_), channel_id=1, source_target_pairs={{0,4},{4,0},{8,12},{12,8},{1,5},{5,1},{9,13},{13,9},{2,6},{6,2},{1... | collective-permute-start | bytes 786440 | tf_op jit(solution)/shard_map/ppermute | solution.py:476
  88.5 7.6 %collective-permute-start.17 = (bf16[768,256]{1,0:T(8,128)(2,1)S(1)}, bf16[768,256]{1,0:T(8,128)(2,1)S(1)}, u32[]{:S(2)}, u32[]{:S(2)}) collective-permute-start(bf16[768,256]{1,0:T(8,128)(2,1)S(1)} %get-tuple-element.135.refs_0_), channel_id=1, source_target_pairs={{0,4},{4,0},{8,12},{12,8},{1,5},{5,1},{9,13},{13,9},{2,6},{6,2},{1... | collective-permute-start | bytes 1179656 | tf_op jit(solution)/shard_map/ppermute | solution.py:476
  96.0 1.7 %collective-permute-start.26 = (bf16[768,256]{1,0:T(8,128)(2,1)S(1)}, bf16[768,256]{1,0:T(8,128)(2,1)S(1)}, u32[]{:S(2)}, u32[]{:S(2)}) collective-permute-start(bf16[768,256]{1,0:T(8,128)(2,1)S(1)} %collective-permute-done.18.refs_2_), channel_id=1, source_target_pairs={{0,4},{4,0},{8,12},{12,8},{1,5},{5,1},{9,13},{13,9},{2,6},{6,2},{1... | collective-permute-start | bytes 1179656 | tf_op jit(solution)/shard_map/ppermute | solution.py:476

commit v11 on v8

--- a/solution.py
+++ b/solution.py
@@ -200,6 +200,83 @@
         cost_estimate=cost(12 * (high - low) / count),
         name="partial_log_rates",
     )(*args)
+
+
+def first_rates_kernel(start, size, own, f, p, chosen, omega, phase, weights, *refs):
+    owned, own_omega, own_phase, kept, sent, _, feats, total = refs
+    step = pl.program_id(0)
+    width = omega.shape[1]
+    parts = []
+
+    @pl.when(step == 0)
+    def _():
+        total[...] = jnp.zeros_like(total)
+
+    def store(cols, value):
+        feats[:, cols] = value
+
+    def between(at, rows, group):
+        done = feats[:, at : at + group]
+        parts.append(jnp.dot(done, weights[rows, :], preferred_element_type=f32))
+
+    cosines(chosen[start : start + size, :], omega, phase, 0, width, store, between)
+    part = parts[0]
+    for q in parts[1:]:
+        part = part + q
+    total[...] += part
+
+    @pl.when(step < own)
+    def _():
+        at = pl.ds(pl.multiple_of(step * width, width), width)
+        owned[:, at] = feats[...]
+        own_omega[:, at] = omega[...]
+        own_phase[:, at] = phase[...]
+
+    @pl.when(step == pl.num_programs(0) - 1)
+    def _():
+        split(total, f[0], 0, kept, sent)
+
+
+def first_rates(f, p, chosen, omega, phase, weights, start, size, owned, deps):
+    ins, feat_dev = omega.shape
+    k = weights.shape[1]
+    width = min(2048, owned)
+    count = feat_dev // width
+    own = owned // width
+
+    def turned(i, p):
+        return lax.rem(i + p[0] * own, count)
+
+    def kernel(*refs):
+        first_rates_kernel(start, size, own, *refs[:6], *refs[6 + len(deps) :])
+
+    return pl.pallas_call(
+        kernel,
+        grid_spec=pltpu.PrefetchScalarGridSpec(
+            num_scalar_prefetch=2,
+            grid=(count,),
+            in_specs=[
+                IN_VMEM,
+                pl.BlockSpec((ins, width), lambda i, f, p: (0, turned(i, p))),
+                pl.BlockSpec((1, width), lambda i, f, p: (0, turned(i, p))),
+                pl.BlockSpec((width, k), lambda i, f, p: (turned(i, p), 0)),
+            ]
+            + [ANYWHERE] * len(deps),
+            out_specs=[IN_VMEM] * 5 + [ANYWHERE],
+            scratch_shapes=[pltpu.VMEM((size, width), bf16), pltpu.VMEM((size, k), f32)],
+        ),
+        out_shape=[
+            jax.ShapeDtypeStruct((size, owned), bf16),
+            jax.ShapeDtypeStruct((ins, owned), bf16),
+            jax.ShapeDtypeStruct((1, owned), f32),
+            jax.ShapeDtypeStruct((size // 2, k), f32),
+            jax.ShapeDtypeStruct((size // 2, k), bf16),
+            TOKEN,
+        ],
+        compiler_params=params(),
+        cost_estimate=cost(12),
+        name="first_log_rates",
+    )(f, p, chosen, omega, phase, weights, *deps)
 
 
 def features_kernel(start, size, chosen, omega, phase, *refs):
@@ -486,8 +563,8 @@
             masks = masks + [q ^ 2**bit for q in masks]
         return rows, masks
 
-    feats_zero, own_omega, own_phase, kept_zero, sent, token = some_rates(
-        0, (0, 2), None, True, True, token
+    feats_zero, own_omega, own_phase, kept_zero, sent, token = first_rates(
+        f, p, chosen, in_hbm(omega), phase, in_hbm(weights), *parts[0], owned, [token]
     )
     got_zero = swap(sent, n_feat, 0)
     feats_one, begun, token = some_rates(1, (0, 1), None, False, False, token)

time: 98.7 us -> 97.1 us (0.984)
  local copies, waits for them, and re-layouts: 4.41 us -> 0.04 us
  Pallas kernels: 52.5 us -> 55.3 us
    pallas_call x0 -> x1, Pallas kernels: none -> 14.4 us  [first_rates(): pl.pallas_call(kernel, grid_spec=pltpu.PrefetchScalarGridSpec(num_scalar_...]
    pallas_call x3 -> x2, Pallas kernels: 18.6 us -> 7.04 us  [rates(): pl.pallas_call(kernel, grid_spec=pltpu.PrefetchScalarGridSpec(num_scalar_...]
    unnamed x20 -> x16, local copies, waits for them, and re-layouts: 4.41 us -> 0.04 us
  transfers between devices with their start and end apart: 27 -> 27, of which waited for: 14 -> 14; matrix products, arithmetic and copies ran while one was open for 0% -> 0% of each run, Pallas kernels for 48% -> 52%
where the time goes in v11:
time: 97.1 us; the launch traced here: 96.9 us
  Pallas kernels  55.3 us (57%)
  starting transfers between devices  21.9 us (23%)
  waiting for transfers between devices  18.6 us (19%)
  between operations  1.07 us (1%)
    pallas_call x1, Pallas kernels, first_rates(): pl.pallas_call(kernel, grid_spec=pltpu.PrefetchScalarGridSpec(num_scalar_...  14.4 us
    pallas_call x6, Pallas kernels, owned_features(): pl.pallas_call(functools.partial(features_kernel, start, size), in_specs=...  12.9 us
    ppermute x6, starting transfers between devices, swap(): return lax.ppermute(x, 'feat', [(i, i ^ 2 ** bit) for i in range(n)])  10.7 us
    pallas_call x4, Pallas kernels, update(): pl.pallas_call(functools.partial(update_kernel, n, at), grid=(steps,), in...  9.97 us
    ppermute x7, waiting for transfers between devices, ring(): return lax.ppermute(x, axis, [(i, (i + distance) % n) for i in range(n)])  9.72 us
    ppermute x7, starting transfers between devices, ring(): return lax.ppermute(x, axis, [(i, (i + distance) % n) for i in range(n)])  8.8 us
    pallas_call x2, Pallas kernels, rates(): pl.pallas_call(kernel, grid_spec=pltpu.PrefetchScalarGridSpec(num_scalar_...  7.04 us
    ppermute x6, waiting for transfers between devices, swap(): return lax.ppermute(x, 'feat', [(i, i ^ 2 ** bit) for i in range(n)])  5.63 us
  transfers between devices with their start and end apart: 27, of which 14 were waited for; matrix products, arithmetic and copies ran while one was open for 0% of the time, Pallas kernels for 52%

profile of v11, /device:TPU:0, one launch (start us, length us, event | category | flops | bytes accessed | tf_op | source)
XLA Modules:
  0.0 96.9 jit_solution(3119535193392288962)
XLA Ops:
  0.6 2.5 %chosen_points.1 = (bf16[1024,256]{1,0:T(8,128)(2,1)S(1)}, f32[8,128]{1,0:T(8,128)S(1)}) custom-call(s32[2,512]{1,0:T(2,128)} %picks.1, bf16[2048,256]{1,0:T(8,128)(2,1)} %points.1), custom_call_target="tpu_custom_call" | custom-call | flops 3000000000 | bytes 1024 | tf_op jit(solution)/shard_map/chosen_points/pallas_call | solution.py:70
  3.2 0.5 collective-permute-start.2
  3.7 2.6 %collective-permute-start.4 = (bf16[1024,256]{1,0:T(8,128)(2,1)S(1)}, bf16[1024,256]{1,0:T(8,128)(2,1)S(1)}, u32[]{:S(2)}, u32[]{:S(2)}) collective-permute-start(bf16[1024,256]{1,0:T(8,128)(2,1)S(1)} %get-tuple-element.71.refs_2_), channel_id=1, source_target_pairs={{0,8},{4,12},{8,0},{12,4},{1,9},{5,13},{9,1},{13,5},{2,10},{6,14},... | collective-permute-start | bytes 1572872 | tf_op jit(solution)/shard_map/ppermute | solution.py:513
  6.3 14.4 %first_log_rates.1 = (bf16[640,2048]{1,0:T(8,128)(2,1)S(1)}, bf16[256,2048]{1,0:T(8,128)(2,1)S(1)}, f32[1,2048]{1,0:T(1,128)S(1)}, f32[320,256]{1,0:T(8,128)S(1)...) custom-call(s32[1]{0:T(128)} %bitcast.refs_0_.f, s32[1]{0:T(128)} %bitcast.1.refs_1_.p, ...), custom_call_target="tpu_custom_call" | custom-call | flops 12000000000 | bytes 1024 | tf_op jit(solution)/shard_map/first_log_rates/pallas_call | solution.py:253
  20.7 1.6 %collective-permute-start = (bf16[320,256]{1,0:T(8,128)(2,1)S(1)}, bf16[320,256]{1,0:T(8,128)(2,1)S(1)}, u32[]{:S(2)}, u32[]{:S(2)}) collective-permute-start(bf16[320,256]{1,0:T(8,128)(2,1)S(1)} %get-tuple-element.76), channel_id=1, source_target_pairs={{0,1},{1,0},{2,3},{3,2},{4,5},{5,4},{6,7},{7,6},{8,9},{9,8},{10,11... | collective-permute-start | bytes 491528 | tf_op jit(solution)/shard_map/ppermute | solution.py:525
  22.4 3.3 %partial_log_rates.2 = (bf16[384,2048]{1,0:T(8,128)(2,1)S(1)}, f32[384,256]{1,0:T(8,128)S(1)}, f32[8,128]{1,0:T(8,128)S(1)}) custom-call(s32[1]{0:T(128)} %bitcast.refs_0_.f, s32[1]{0:T(128)} %bitcast.1.refs_1_.p, bf16[1024,256]{1,0:T(8,128)(2,1)S(1)} %get-tuple-element.71.refs_2_, bf16[256,8192]{1,0:T(8,128)(2,1)S(1)} %copy-done.4, f32[1,8192]{1,0:T(1,128)S(1)} %bitcast.8, ...), custom_call_target="tpu_custom_call" | custom-call | flops 6000000000 | bytes 1024 | tf_op jit(solution)/shard_map/partial_log_rates/pallas_call | solution.py:189
  25.6 1.4 %collective-permute-done.b = bf16[320,256]{1,0:T(8,128)(2,1)S(1)} collective-permute-done((bf16[320,256]{1,0:T(8,128)(2,1)S(1)}, bf16[320,256]{1,0:T(8,128)(2,1)S(1)}, u32[]{:S(2)}, u32[]{:S(2)}) %collective-permute-start) | collective-permute-done | bytes 163872 | tf_op jit(solution)/shard_map/ppermute | solution.py:525
  27.1 2.7 %collective-permute-start.5 = (bf16[320,256]{1,0:T(8,128)(2,1)S(1)}, bf16[320,256]{1,0:T(8,128)(2,1)S(1)}, u32[]{:S(2)}, u32[]{:S(2)}) collective-permute-start(bf16[320,256]{1,0:T(8,128)(2,1)S(1)} %get-tuple-element.86.a), channel_id=1, source_target_pairs={{0,2},{1,3},{2,0},{3,1},{4,6},{5,7},{6,4},{7,5},{8,10},{9,11},{10,... | collective-permute-start | bytes 491528 | tf_op jit(solution)/shard_map/ppermute | solution.py:525
  29.7 3.8 %partial_log_rates.3 = (f32[192,256]{1,0:T(8,128)S(1)}, bf16[192,256]{1,0:T(8,128)(2,1)S(1)}, f32[8,128]{1,0:T(8,128)S(1)}) custom-call(s32[1]{0:T(128)} %bitcast.refs_0_.f, s32[1]{0:T(128)} %bitcast.1.refs_1_.p, bf16[1024,256]{1,0:T(8,128)(2,1)S(1)} %get-tuple-element.71.refs_2_, bf16[256,8192]{1,0:T(8,128)(2,1)S(1)} %copy-done.4, f32[1,8192]{1,0:T(1,128)S(1)} %bitcast.9, ...), custom_call_target="tpu_custom_call" | custom-call | flops 6000000000 | bytes 1024 | tf_op jit(solution)/shard_map/partial_log_rates/pallas_call | solution.py:189
  33.5 1.6 %collective-permute-start.1 = (bf16[192,256]{1,0:T(8,128)(2,1)S(1)}, bf16[192,256]{1,0:T(8,128)(2,1)S(1)}, u32[]{:S(2)}, u32[]{:S(2)}) collective-permute-start(bf16[192,256]{1,0:T(8,128)(2,1)S(1)} %get-tuple-element.80), channel_id=1, source_target_pairs={{0,1},{1,0},{2,3},{3,2},{4,5},{5,4},{6,7},{7,6},{8,9},{9,8},{10,11... | collective-permute-start | bytes 294920 | tf_op jit(solution)/shard_map/ppermute | solution.py:525
  35.2 2.6 %owned_features.6 = (bf16[640,2048]{1,0:T(8,128)(2,1)S(1)}, f32[8,128]{1,0:T(8,128)S(1)}) custom-call(bf16[1024,256]{1,0:T(8,128)(2,1)S(1)} %collective-permute-done.2.chosen, bf16[256,2048]{1,0:T(8,128)(2,1)S(1)} %get-tuple-element.81.omega, f32[1,2048]{1,0:T(1,128)S(1)} %get-tuple-element.82.phase, f32[8,128]{1,0:T(8,128)S(1)} %get-tuple-element.83.refs_0_), custom_call_target="tpu_custom_call" | custom-call | flops 1000000000 | bytes 1024 | tf_op jit(solution)/shard_map/owned_features/pallas_call | solution.py:293
  37.8 1.4 %collective-permute-done.1.b = bf16[192,256]{1,0:T(8,128)(2,1)S(1)} collective-permute-done((bf16[192,256]{1,0:T(8,128)(2,1)S(1)}, bf16[192,256]{1,0:T(8,128)(2,1)S(1)}, u32[]{:S(2)}, u32[]{:S(2)}) %collective-permute-start.1) | collective-permute-done | bytes 98336 | tf_op jit(solution)/shard_map/ppermute | solution.py:525
  39.2 0.7 collective-permute-start.8
  39.9 2.9 %collective-permute-start.3 = (bf16[192,256]{1,0:T(8,128)(2,1)S(1)}, bf16[192,256]{1,0:T(8,128)(2,1)S(1)}, u32[]{:S(2)}, u32[]{:S(2)}) collective-permute-start(bf16[192,256]{1,0:T(8,128)(2,1)S(1)} %get-tuple-element.85.a), channel_id=1, source_target_pairs={{0,2},{1,3},{2,0},{3,1},{4,6},{5,7},{6,4},{7,5},{8,10},{9,11},{10,... | collective-permute-start | bytes 294920 | tf_op jit(solution)/shard_map/ppermute | solution.py:525
  42.8 2.6 %owned_features.7 = (bf16[640,2048]{1,0:T(8,128)(2,1)S(1)}, f32[8,128]{1,0:T(8,128)S(1)}) custom-call(bf16[1024,256]{1,0:T(8,128)(2,1)S(1)} %collective-permute-done.4.chosen, bf16[256,2048]{1,0:T(8,128)(2,1)S(1)} %get-tuple-element.81.omega, f32[1,2048]{1,0:T(1,128)S(1)} %get-tuple-element.82.phase, f32[8,128]{1,0:T(8,128)S(1)} %get-tuple-element.88.refs_0_), custom_call_target="tpu_custom_call" | custom-call | flops 1000000000 | bytes 1024 | tf_op jit(solution)/shard_map/owned_features/pallas_call | solution.py:293
  45.4 0.7 collective-permute-done.3.b
  46.1 1.3 %collective-permute-done.8.refs_1_ = bf16[320,256]{1,0:T(8,128)(2,1)S(1)} collective-permute-done((bf16[320,256]{1,0:T(8,128)(2,1)S(1)}, bf16[320,256]{1,0:T(8,128)(2,1)S(1)}, u32[]{:S(2)}, u32[]{:S(2)}) %collective-permute-start.8) | collective-permute-done | bytes 163872 | tf_op jit(solution)/shard_map/ppermute | solution.py:525
  47.5 1.1 %residuals.2 = (f32[1024,256]{1,0:T(8,128)}, bf16[256,640]{1,0:T(8,128)(2,1)S(1)}, f32[8,128]{1,0:T(8,128)S(1)}) custom-call(s32[1]{0:T(128)} %bitcast.refs_0_.f, bf16[320,256]{1,0:T(8,128)(2,1)S(1)} %get-tuple-element.91.refs_0_, bf16[320,256]{1,0:T(8,128)(2,1)S(1)} %collective-permute-done.8.refs_1_, s32[1024,256]{1,0:T(8,128)S(1)} %bitcast.5, ...), custom_call_target="tpu_custom_call" | custom-call | flops 1000000000 | bytes 1024 | tf_op jit(solution)/shard_map/residuals/pallas_call | solution.py:371
  48.5 0.7 collective-permute-start.9
  49.3 1.1 %collective-permute-start.6 = (bf16[192,256]{1,0:T(8,128)(2,1)S(1)}, bf16[192,256]{1,0:T(8,128)(2,1)S(1)}, u32[]{:S(2)}, u32[]{:S(2)}) collective-permute-start(bf16[192,256]{1,0:T(8,128)(2,1)S(1)} %get-tuple-element.90.refs_0_), channel_id=1, source_target_pairs={{0,1},{1,0},{2,3},{3,2},{4,5},{5,4},{6,7},{7,6},{8,9},{9,8},{10,11... | collective-permute-start | bytes 294920 | tf_op jit(solution)/shard_map/ppermute | solution.py:525
  50.4 0.0 collective-permute-done.7.chosen
  50.4 2.6 %owned_features.8 = (bf16[640,2048]{1,0:T(8,128)(2,1)S(1)}, f32[8,128]{1,0:T(8,128)S(1)}) custom-call(bf16[1024,256]{1,0:T(8,128)(2,1)S(1)} %collective-permute-done.7.chosen, bf16[256,2048]{1,0:T(8,128)(2,1)S(1)} %get-tuple-element.81.omega, f32[1,2048]{1,0:T(1,128)S(1)} %get-tuple-element.82.phase, f32[8,128]{1,0:T(8,128)S(1)} %get-tuple-element.93.refs_0_), custom_call_target="tpu_custom_call" | custom-call | flops 1000000000 | bytes 1024 | tf_op jit(solution)/shard_map/owned_features/pallas_call | solution.py:293
  53.0 0.9 collective-permute-done.6.refs_1_
  53.9 0.9 residuals.3
  54.8 1.4 %collective-permute-start.11 = (bf16[256,384]{1,0:T(8,128)(2,1)S(1)}, bf16[256,384]{1,0:T(8,128)(2,1)S(1)}, u32[]{:S(2)}, u32[]{:S(2)}) collective-permute-start(bf16[256,384]{1,0:T(8,128)(2,1)S(1)} %get-tuple-element.106.refs_4_), channel_id=1, source_target_pairs={{0,8},{4,12},{8,0},{12,4},{1,9},{5,13},{9,1},{13,5},{2,10},{6,14},... | collective-permute-start | bytes 589832 | tf_op jit(solution)/shard_map/ppermute | solution.py:513
  56.2 0.0 collective-permute-start.13
  56.2 1.6 %owned_features.9 = (bf16[384,2048]{1,0:T(8,128)(2,1)S(1)}, f32[8,128]{1,0:T(8,128)S(1)}) custom-call(bf16[1024,256]{1,0:T(8,128)(2,1)S(1)} %collective-permute-done.2.chosen, bf16[256,2048]{1,0:T(8,128)(2,1)S(1)} %get-tuple-element.81.omega, f32[1,2048]{1,0:T(1,128)S(1)} %get-tuple-element.82.phase, f32[8,128]{1,0:T(8,128)S(1)} %get-tuple-element.98.refs_0_), custom_call_target="tpu_custom_call" | custom-call | flops 100000000 | bytes 1024 | tf_op jit(solution)/shard_map/owned_features/pallas_call | solution.py:293
  57.9 1.9 %owned_features.10 = (bf16[384,2048]{1,0:T(8,128)(2,1)S(1)}, f32[8,128]{1,0:T(8,128)S(1)}) custom-call(bf16[1024,256]{1,0:T(8,128)(2,1)S(1)} %collective-permute-done.4.chosen, bf16[256,2048]{1,0:T(8,128)(2,1)S(1)} %get-tuple-element.81.omega, f32[1,2048]{1,0:T(1,128)S(1)} %get-tuple-element.82.phase, f32[8,128]{1,0:T(8,128)S(1)} %get-tuple-element.100.refs_0_), custom_call_target="tpu_custom_call" | custom-call | flops 100000000 | bytes 1024 | tf_op jit(solution)/shard_map/owned_features/pallas_call | solution.py:293
  59.7 0.6 collective-permute-start.14
  60.3 0.1 collective-permute-start.10
  60.4 1.6 %owned_features.11 = (bf16[384,2048]{1,0:T(8,128)(2,1)S(1)}, f32[8,128]{1,0:T(8,128)S(1)}) custom-call(bf16[1024,256]{1,0:T(8,128)(2,1)S(1)} %collective-permute-done.7.chosen, bf16[256,2048]{1,0:T(8,128)(2,1)S(1)} %get-tuple-element.81.omega, f32[1,2048]{1,0:T(1,128)S(1)} %get-tuple-element.82.phase, f32[8,128]{1,0:T(8,128)S(1)} %get-tuple-element.104.refs_0_), custom_call_target="tpu_custom_call" | custom-call | flops 100000000 | bytes 1024 | tf_op jit(solution)/shard_map/owned_features/pallas_call | solution.py:293
  62.0 0.0 collective-permute-done.11.refs_6_
  62.0 0.5 collective-permute-start.12
  62.5 0.0 collective-permute-done.13.refs_5_
  62.5 0.0 collective-permute-done.14.refs_7_
  62.5 0.0 copy-start.1
  62.6 0.0 copy-start.2
  62.6 0.0 copy-start.3
  62.6 3.6 %first_part.1 = (f32[2048,256]{1,0:T(8,128)S(1)}, f32[8,128]{1,0:T(8,128)S(1)}) custom-call(bf16[640,2048]{1,0:T(8,128)(2,1)S(1)} %get-tuple-element.109.refs_0_, bf16[640,2048]{1,0:T(8,128)(2,1)S(1)} %get-tuple-element.110.refs_1_, bf16[640,2048]{1,0:T(8,128)(2,1)S(1)} %get-tuple-element.111.refs_2_, bf16[640,2048]{1,0:T(8,128)(2,1)S(1)} %get-tuple-element.112.refs_3_, ...), custom_call_target="tpu_custom_call" | custom-call | flops 300000000 | bytes 1024 | tf_op jit(solution)/shard_map/first_part/pallas_call | solution.py:413
  66.2 0.0 collective-permute-done.12.refs_7_
  66.2 1.7 %update.4 = (f32[1,2048,256]{2,1,0:T(8,128)}, f32[1,2048,256]{2,1,0:T(8,128)}, f32[1,2048,256]{2,1,0:T(8,128)}, bf16[256,256]{1,0:T(8,128)(2,1)S(1)}) custom-call(bf16[384,2048]{1,0:T(8,128)(2,1)S(1)} %get-tuple-element.97.refs_0_, bf16[384,2048]{1,0:T(8,128)(2,1)S(1)} %get-tuple-element.99.refs_1_, bf16[384,2048]{1,0:T(8,128)(2,1)S(1)} %get-tuple-element.101.refs_2_, ...), custom_call_target="tpu_custom_call" | custom-call | flops 4000000000 | bytes 1024 | tf_op jit(solution)/shard_map/update/pallas_call | solution.py:461
  67.9 0.7 collective-permute-start.15
  68.6 2.5 %update.5 = (f32[1,2048,256]{2,1,0:T(8,128)}, f32[1,2048,256]{2,1,0:T(8,128)}, f32[1,2048,256]{2,1,0:T(8,128)}, bf16[512,256]{1,0:T(8,128)(2,1)S(1)}) custom-call(bf16[384,2048]{1,0:T(8,128)(2,1)S(1)} %get-tuple-element.97.refs_0_, bf16[384,2048]{1,0:T(8,128)(2,1)S(1)} %get-tuple-element.99.refs_1_, ...), custom_call_target="tpu_custom_call", output_to_operand_aliasing={{0}: (13, {}), {1}: (14, {}), {2}: (15, {})} | custom-call | flops 4000000000 | bytes 1024 | tf_op jit(solution)/shard_map/update/pallas_call | solution.py:461
  71.1 1.4 %collective-permute-start.16 = (bf16[512,256]{1,0:T(8,128)(2,1)S(1)}, bf16[512,256]{1,0:T(8,128)(2,1)S(1)}, u32[]{:S(2)}, u32[]{:S(2)}) collective-permute-start(bf16[512,256]{1,0:T(8,128)(2,1)S(1)} %get-tuple-element.127.refs_4_), channel_id=1, source_target_pairs={{0,8},{4,12},{8,0},{12,4},{1,9},{5,13},{9,1},{13,5},{2,10},{6,14},... | collective-permute-start | bytes 786440 | tf_op jit(solution)/shard_map/ppermute | solution.py:513
  72.4 0.9 collective-permute-done.15.refs_17_.refs_2_
  73.4 2.5 %update.6 = (f32[1,2048,256]{2,1,0:T(8,128)}, f32[1,2048,256]{2,1,0:T(8,128)}, f32[1,2048,256]{2,1,0:T(8,128)}, bf16[512,256]{1,0:T(8,128)(2,1)S(1)}) custom-call(bf16[384,2048]{1,0:T(8,128)(2,1)S(1)} %get-tuple-element.97.refs_0_, bf16[384,2048]{1,0:T(8,128)(2,1)S(1)} %get-tuple-element.99.refs_1_, ...), custom_call_target="tpu_custom_call", output_to_operand_aliasing={{0}: (13, {}), {1}: (14, {}), {2}: (15, {})} | custom-call | flops 4000000000 | bytes 1024 | tf_op jit(solution)/shard_map/update/pallas_call | solution.py:461
  75.9 0.7 collective-permute-start.24
  76.5 3.6 %collective-permute-done.16.refs_17_.refs_6_ = bf16[512,256]{1,0:T(8,128)(2,1)S(1)} collective-permute-done((bf16[512,256]{1,0:T(8,128)(2,1)S(1)}, bf16[512,256]{1,0:T(8,128)(2,1)S(1)}, u32[]{:S(2)}, u32[]{:S(2)}) %collective-permute-start.16) | collective-permute-done | bytes 262176 | tf_op jit(solution)/shard_map/ppermute | solution.py:513
  80.2 3.3 %update.7 = (f32[1,2048,256]{2,1,0:T(8,128)}, f32[1,2048,256]{2,1,0:T(8,128)}, f32[1,2048,256]{2,1,0:T(8,128)}, bf16[768,256]{1,0:T(8,128)(2,1)S(1)}) custom-call(bf16[384,2048]{1,0:T(8,128)(2,1)S(1)} %get-tuple-element.97.refs_0_, bf16[384,2048]{1,0:T(8,128)(2,1)S(1)} %get-tuple-element.99.refs_1_, ...), custom_call_target="tpu_custom_call", output_to_operand_aliasing={{0}: (13, {}), {1}: (14, {}), {2}: (15, {})} | custom-call | flops 4000000000 | bytes 1024 | tf_op jit(solution)/shard_map/update/pallas_call | solution.py:461
  83.5 1.4 %collective-permute-start.18 = (bf16[768,256]{1,0:T(8,128)(2,1)S(1)}, bf16[768,256]{1,0:T(8,128)(2,1)S(1)}, u32[]{:S(2)}, u32[]{:S(2)}) collective-permute-start(bf16[768,256]{1,0:T(8,128)(2,1)S(1)} %get-tuple-element.131.refs_0_), channel_id=1, source_target_pairs={{0,8},{4,12},{8,0},{12,4},{1,9},{5,13},{9,1},{13,5},{2,10},{6,14},... | collective-permute-start | bytes 1179656 | tf_op jit(solution)/shard_map/ppermute | solution.py:513
  84.9 0.5 collective-permute-done.24.refs_10_
  85.4 0.5 collective-permute-start.22
  85.9 0.1 collective-permute-start.25
  86.0 0.4 collective-permute-done.21.refs_5_
  86.4 0.1 collective-permute-start.17
  86.5 0.4 collective-permute-done.23.refs_9_
  86.9 0.4 collective-permute-done.22.refs_7_
  87.3 0.4 collective-permute-done.25.refs_11_
  87.7 1.6 %put_rows.2.refs_4_ = bf16[8192,256]{1,0:T(8,128)(2,1)} custom-call(s32[1]{0:T(128)} %bitcast.1.refs_1_.p, bf16[256,256]{1,0:T(8,128)(2,1)S(1)} %get-tuple-element.123.refs_0_, bf16[256,256]{1,0:T(8,128)(2,1)S(1)} %collective-permute-done.19.refs_1_, bf16[256,256]{1,0:T(8,128)(2,1)S(1)} %collective-permute-done.15.refs_17_.refs_2_, ...), custom_call_target="tpu_custom_call" | custom-call | flops 10000000 | bytes 1024 | tf_op jit(solution)/shard_map/put_rows/pallas_call | solution.py:495
  89.3 4.6 %collective-permute-done.18.refs_2_ = bf16[768,256]{1,0:T(8,128)(2,1)S(1)} collective-permute-done((bf16[768,256]{1,0:T(8,128)(2,1)S(1)}, bf16[768,256]{1,0:T(8,128)(2,1)S(1)}, u32[]{:S(2)}, u32[]{:S(2)}) %collective-permute-start.18) | collective-permute-done | bytes 393248 | tf_op jit(solution)/shard_map/ppermute | solution.py:513
  93.9 0.0 collective-permute-start.26
  93.9 0.0 collective-permute-done.17.refs_1_
  93.9 1.7 %collective-permute-done.26.refs_3_ = bf16[768,256]{1,0:T(8,128)(2,1)S(1)} collective-permute-done((bf16[768,256]{1,0:T(8,128)(2,1)S(1)}, bf16[768,256]{1,0:T(8,128)(2,1)S(1)}, u32[]{:S(2)}, u32[]{:S(2)}) %collective-permute-start.26) | collective-permute-done | bytes 393248 | tf_op jit(solution)/shard_map/ppermute | solution.py:517
  95.6 1.2 %put_rows.3 = bf16[8192,256]{1,0:T(8,128)(2,1)} custom-call(s32[1]{0:T(128)} %bitcast.1.refs_1_.p, bf16[768,256]{1,0:T(8,128)(2,1)S(1)} %get-tuple-element.131.refs_0_, bf16[768,256]{1,0:T(8,128)(2,1)S(1)} %collective-permute-done.17.refs_1_, bf16[768,256]{1,0:T(8,128)(2,1)S(1)} %collective-permute-done.18.refs_2_, ...), custom_call_target="tpu_custom_call", output_to_operand_aliasing={{}: (5, {})} | custom-call | flops 10000000 | bytes 1024 | tf_op jit(solution)/shard_map/put_rows/pallas_call | solution.py:495
  (29 shorter events, 0.2 us)
Async XLA Ops:
  0.6 5.7 %copy-start.7 = (f32[8192]{0:T(1024)S(1)}, f32[8192]{0:T(1024)}, u32[]{:S(2)}) copy-start(f32[8192]{0:T(1024)} %param.13) | copy-start | bytes 98308
  3.2 32.0 %collective-permute-start.2 = (bf16[1024,256]{1,0:T(8,128)(2,1)S(1)}, bf16[1024,256]{1,0:T(8,128)(2,1)S(1)}, u32[]{:S(2)}, u32[]{:S(2)}) collective-permute-start(bf16[1024,256]{1,0:T(8,128)(2,1)S(1)} %get-tuple-element.71.refs_2_), channel_id=1, source_target_pairs={{0,4},{4,0},{8,12},{12,8},{1,5},{5,1},{9,13},{13,9},{2,6},{6,2},{1... | collective-permute-start | bytes 1572872 | tf_op jit(solution)/shard_map/ppermute | solution.py:517
  3.7 31.5 %collective-permute-start.4 = (bf16[1024,256]{1,0:T(8,128)(2,1)S(1)}, bf16[1024,256]{1,0:T(8,128)(2,1)S(1)}, u32[]{:S(2)}, u32[]{:S(2)}) collective-permute-start(bf16[1024,256]{1,0:T(8,128)(2,1)S(1)} %get-tuple-element.71.refs_2_), channel_id=1, source_target_pairs={{0,8},{4,12},{8,0},{12,4},{1,9},{5,13},{9,1},{13,5},{2,10},{6,14},... | collective-permute-start | bytes 1572872 | tf_op jit(solution)/shard_map/ppermute | solution.py:513
  6.3 16.1 %copy-start.4 = (bf16[256,8192]{1,0:T(8,128)(2,1)S(1)}, bf16[256,8192]{1,0:T(8,128)(2,1)}, u32[]{:S(2)}) copy-start(bf16[256,8192]{1,0:T(8,128)(2,1)} %refs_3_.5) | copy-start | bytes 12582916
  6.3 16.1 %copy-start.5 = (bf16[8192,256]{1,0:T(8,128)(2,1)S(1)}, bf16[8192,256]{1,0:T(8,128)(2,1)}, u32[]{:S(2)}) copy-start(bf16[8192,256]{1,0:T(8,128)(2,1)} %refs_5_.5) | copy-start | bytes 12582916
  20.7 6.3 %collective-permute-start = (bf16[320,256]{1,0:T(8,128)(2,1)S(1)}, bf16[320,256]{1,0:T(8,128)(2,1)S(1)}, u32[]{:S(2)}, u32[]{:S(2)}) collective-permute-start(bf16[320,256]{1,0:T(8,128)(2,1)S(1)} %get-tuple-element.76), channel_id=1, source_target_pairs={{0,1},{1,0},{2,3},{3,2},{4,5},{5,4},{6,7},{7,6},{8,9},{9,8},{10,11... | collective-permute-start | bytes 491528 | tf_op jit(solution)/shard_map/ppermute | solution.py:525
  27.1 12.1 %collective-permute-start.5 = (bf16[320,256]{1,0:T(8,128)(2,1)S(1)}, bf16[320,256]{1,0:T(8,128)(2,1)S(1)}, u32[]{:S(2)}, u32[]{:S(2)}) collective-permute-start(bf16[320,256]{1,0:T(8,128)(2,1)S(1)} %get-tuple-element.86.a), channel_id=1, source_target_pairs={{0,2},{1,3},{2,0},{3,1},{4,6},{5,7},{6,4},{7,5},{8,10},{9,11},{10,... | collective-permute-start | bytes 491528 | tf_op jit(solution)/shard_map/ppermute | solution.py:525
  33.5 5.6 %collective-permute-start.1 = (bf16[192,256]{1,0:T(8,128)(2,1)S(1)}, bf16[192,256]{1,0:T(8,128)(2,1)S(1)}, u32[]{:S(2)}, u32[]{:S(2)}) collective-permute-start(bf16[192,256]{1,0:T(8,128)(2,1)S(1)} %get-tuple-element.80), channel_id=1, source_target_pairs={{0,1},{1,0},{2,3},{3,2},{4,5},{5,4},{6,7},{7,6},{8,9},{9,8},{10,11... | collective-permute-start | bytes 294920 | tf_op jit(solution)/shard_map/ppermute | solution.py:525
  35.2 15.3 %collective-permute-start.7 = (bf16[1024,256]{1,0:T(8,128)(2,1)S(1)}, bf16[1024,256]{1,0:T(8,128)(2,1)S(1)}, u32[]{:S(2)}, u32[]{:S(2)}) collective-permute-start(bf16[1024,256]{1,0:T(8,128)(2,1)S(1)} %collective-permute-done.4.chosen), channel_id=1, source_target_pairs={{0,4},{4,0},{8,12},{12,8},{1,5},{5,1},{9,13},{13,9},{2,6},{6,2},{1... | collective-permute-start | bytes 1572872 | tf_op jit(solution)/shard_map/ppermute | solution.py:517
  39.2 8.3 %collective-permute-start.8 = (bf16[320,256]{1,0:T(8,128)(2,1)S(1)}, bf16[320,256]{1,0:T(8,128)(2,1)S(1)}, u32[]{:S(2)}, u32[]{:S(2)}) collective-permute-start(bf16[320,256]{1,0:T(8,128)(2,1)S(1)} %get-tuple-element.91.refs_0_), channel_id=1, source_target_pairs={{0,1},{1,0},{2,3},{3,2},{4,5},{5,4},{6,7},{7,6},{8,9},{9,8},{10,11... | collective-permute-start | bytes 491528 | tf_op jit(solution)/shard_map/ppermute | solution.py:525
  39.9 6.2 %collective-permute-start.3 = (bf16[192,256]{1,0:T(8,128)(2,1)S(1)}, bf16[192,256]{1,0:T(8,128)(2,1)S(1)}, u32[]{:S(2)}, u32[]{:S(2)}) collective-permute-start(bf16[192,256]{1,0:T(8,128)(2,1)S(1)} %get-tuple-element.85.a), channel_id=1, source_target_pairs={{0,2},{1,3},{2,0},{3,1},{4,6},{5,7},{6,4},{7,5},{8,10},{9,11},{10,... | collective-permute-start | bytes 294920 | tf_op jit(solution)/shard_map/ppermute | solution.py:525
  42.8 4.6 %copy-start.6 = (s32[2,512,256]{2,1,0:T(8,128)S(1)}, s32[2,512,256]{2,1,0:T(8,128)}, u32[]{:S(2)}) copy-start(s32[2,512,256]{2,1,0:T(8,128)} %param.15) | copy-start | bytes 3145732
  48.5 11.2 %collective-permute-start.9 = (bf16[256,640]{1,0:T(8,128)(2,1)S(1)}, bf16[256,640]{1,0:T(8,128)(2,1)S(1)}, u32[]{:S(2)}, u32[]{:S(2)}) collective-permute-start(bf16[256,640]{1,0:T(8,128)(2,1)S(1)} %get-tuple-element.102.refs_4_), channel_id=1, source_target_pairs={{0,8},{4,12},{8,0},{12,4},{1,9},{5,13},{9,1},{13,5},{2,10},{6,14},... | collective-permute-start | bytes 983048 | tf_op jit(solution)/shard_map/ppermute | solution.py:513
  49.3 4.6 %collective-permute-start.6 = (bf16[192,256]{1,0:T(8,128)(2,1)S(1)}, bf16[192,256]{1,0:T(8,128)(2,1)S(1)}, u32[]{:S(2)}, u32[]{:S(2)}) collective-permute-start(bf16[192,256]{1,0:T(8,128)(2,1)S(1)} %get-tuple-element.90.refs_0_), channel_id=1, source_target_pairs={{0,1},{1,0},{2,3},{3,2},{4,5},{5,4},{6,7},{7,6},{8,9},{9,8},{10,11... | collective-permute-start | bytes 294920 | tf_op jit(solution)/shard_map/ppermute | solution.py:525
  54.8 7.2 %collective-permute-start.11 = (bf16[256,384]{1,0:T(8,128)(2,1)S(1)}, bf16[256,384]{1,0:T(8,128)(2,1)S(1)}, u32[]{:S(2)}, u32[]{:S(2)}) collective-permute-start(bf16[256,384]{1,0:T(8,128)(2,1)S(1)} %get-tuple-element.106.refs_4_), channel_id=1, source_target_pairs={{0,8},{4,12},{8,0},{12,4},{1,9},{5,13},{9,1},{13,5},{2,10},{6,14},... | collective-permute-start | bytes 589832 | tf_op jit(solution)/shard_map/ppermute | solution.py:513
  56.2 6.3 %collective-permute-start.13 = (bf16[256,640]{1,0:T(8,128)(2,1)S(1)}, bf16[256,640]{1,0:T(8,128)(2,1)S(1)}, u32[]{:S(2)}, u32[]{:S(2)}) collective-permute-start(bf16[256,640]{1,0:T(8,128)(2,1)S(1)} %get-tuple-element.102.refs_4_), channel_id=1, source_target_pairs={{0,4},{4,0},{8,12},{12,8},{1,5},{5,1},{9,13},{13,9},{2,6},{6,2},{1... | collective-permute-start | bytes 983048 | tf_op jit(solution)/shard_map/ppermute | solution.py:517
  56.2 6.3 %copy-start = (f32[1,2048,256]{2,1,0:T(8,128)S(1)}, f32[1,2048,256]{2,1,0:T(8,128)}, u32[]{:S(2)}) copy-start(f32[1,2048,256]{2,1,0:T(8,128)} %refs_10_.7) | copy-start | bytes 6291460
  59.7 2.8 %collective-permute-start.14 = (bf16[256,640]{1,0:T(8,128)(2,1)S(1)}, bf16[256,640]{1,0:T(8,128)(2,1)S(1)}, u32[]{:S(2)}, u32[]{:S(2)}) collective-permute-start(bf16[256,640]{1,0:T(8,128)(2,1)S(1)} %collective-permute-done.9.refs_6_), channel_id=1, source_target_pairs={{0,4},{4,0},{8,12},{12,8},{1,5},{5,1},{9,13},{13,9},{2,6},{6,2},{1... | collective-permute-start | bytes 983048 | tf_op jit(solution)/shard_map/ppermute | solution.py:517
  60.3 5.9 %collective-permute-start.10 = (bf16[256,384]{1,0:T(8,128)(2,1)S(1)}, bf16[256,384]{1,0:T(8,128)(2,1)S(1)}, u32[]{:S(2)}, u32[]{:S(2)}) collective-permute-start(bf16[256,384]{1,0:T(8,128)(2,1)S(1)} %get-tuple-element.106.refs_4_), channel_id=1, source_target_pairs={{0,4},{4,0},{8,12},{12,8},{1,5},{5,1},{9,13},{13,9},{2,6},{6,2},{1... | collective-permute-start | bytes 589832 | tf_op jit(solution)/shard_map/ppermute | solution.py:517
  62.0 4.2 %collective-permute-start.12 = (bf16[256,384]{1,0:T(8,128)(2,1)S(1)}, bf16[256,384]{1,0:T(8,128)(2,1)S(1)}, u32[]{:S(2)}, u32[]{:S(2)}) collective-permute-start(bf16[256,384]{1,0:T(8,128)(2,1)S(1)} %collective-permute-done.11.refs_6_), channel_id=1, source_target_pairs={{0,4},{4,0},{8,12},{12,8},{1,5},{5,1},{9,13},{13,9},{2,6},{6,2},{1... | collective-permute-start | bytes 589832 | tf_op jit(solution)/shard_map/ppermute | solution.py:517
  62.5 3.7 %copy-start.1 = (f32[1,2048,256]{2,1,0:T(8,128)S(1)}, f32[1,2048,256]{2,1,0:T(8,128)}, u32[]{:S(2)}) copy-start(f32[1,2048,256]{2,1,0:T(8,128)} %refs_11_.7) | copy-start | bytes 6291460
  62.6 3.7 %copy-start.2 = (f32[1,2048,256]{2,1,0:T(8,128)S(1)}, f32[1,2048,256]{2,1,0:T(8,128)}, u32[]{:S(2)}) copy-start(f32[1,2048,256]{2,1,0:T(8,128)} %refs_12_.7) | copy-start | bytes 6291460
  62.6 3.7 %copy-start.3 = (bf16[256,256]{1,0:T(8,128)(2,1)S(1)}, bf16[256,256]{1,0:T(8,128)(2,1)}, u32[]{:S(2)}) copy-start(bf16[256,256]{1,0:T(8,128)(2,1)} %refs_9_.7) | copy-start | bytes 393220
  67.9 5.5 %collective-permute-start.15 = (bf16[256,256]{1,0:T(8,128)(2,1)S(1)}, bf16[256,256]{1,0:T(8,128)(2,1)S(1)}, u32[]{:S(2)}, u32[]{:S(2)}) collective-permute-start(bf16[256,256]{1,0:T(8,128)(2,1)S(1)} %get-tuple-element.123.refs_0_), channel_id=1, source_target_pairs={{0,8},{4,12},{8,0},{12,4},{1,9},{5,13},{9,1},{13,5},{2,10},{6,14},... | collective-permute-start | bytes 393224 | tf_op jit(solution)/shard_map/ppermute | solution.py:513
  68.6 16.8 %collective-permute-start.19 = (bf16[256,256]{1,0:T(8,128)(2,1)S(1)}, bf16[256,256]{1,0:T(8,128)(2,1)S(1)}, u32[]{:S(2)}, u32[]{:S(2)}) collective-permute-start(bf16[256,256]{1,0:T(8,128)(2,1)S(1)} %get-tuple-element.123.refs_0_), channel_id=1, source_target_pairs={{0,4},{4,0},{8,12},{12,8},{1,5},{5,1},{9,13},{13,9},{2,6},{6,2},{1... | collective-permute-start | bytes 393224 | tf_op jit(solution)/shard_map/ppermute | solution.py:517
  71.1 9.1 %collective-permute-start.16 = (bf16[512,256]{1,0:T(8,128)(2,1)S(1)}, bf16[512,256]{1,0:T(8,128)(2,1)S(1)}, u32[]{:S(2)}, u32[]{:S(2)}) collective-permute-start(bf16[512,256]{1,0:T(8,128)(2,1)S(1)} %get-tuple-element.127.refs_4_), channel_id=1, source_target_pairs={{0,8},{4,12},{8,0},{12,4},{1,9},{5,13},{9,1},{13,5},{2,10},{6,14},... | collective-permute-start | bytes 786440 | tf_op jit(solution)/shard_map/ppermute | solution.py:513
  75.9 9.5 %collective-permute-start.24 = (bf16[512,256]{1,0:T(8,128)(2,1)S(1)}, bf16[512,256]{1,0:T(8,128)(2,1)S(1)}, u32[]{:S(2)}, u32[]{:S(2)}) collective-permute-start(bf16[512,256]{1,0:T(8,128)(2,1)S(1)} %get-tuple-element.133.refs_8_), channel_id=1, source_target_pairs={{0,8},{4,12},{8,0},{12,4},{1,9},{5,13},{9,1},{13,5},{2,10},{6,14},... | collective-permute-start | bytes 786440 | tf_op jit(solution)/shard_map/ppermute | solution.py:513
  76.5 9.4 %collective-permute-start.20 = (bf16[256,256]{1,0:T(8,128)(2,1)S(1)}, bf16[256,256]{1,0:T(8,128)(2,1)S(1)}, u32[]{:S(2)}, u32[]{:S(2)}) collective-permute-start(bf16[256,256]{1,0:T(8,128)(2,1)S(1)} %collective-permute-done.15.refs_17_.refs_2_), channel_id=1, source_target_pairs={{0,4},{4,0},{8,12},{12,8},{1,5},{5,1},{9,13},{13,9},{2,6},{6,2},{1... | collective-permute-start | bytes 393224 | tf_op jit(solution)/shard_map/ppermute | solution.py:517
  83.5 10.4 %collective-permute-start.18 = (bf16[768,256]{1,0:T(8,128)(2,1)S(1)}, bf16[768,256]{1,0:T(8,128)(2,1)S(1)}, u32[]{:S(2)}, u32[]{:S(2)}) collective-permute-start(bf16[768,256]{1,0:T(8,128)(2,1)S(1)} %get-tuple-element.131.refs_0_), channel_id=1, source_target_pairs={{0,8},{4,12},{8,0},{12,4},{1,9},{5,13},{9,1},{13,5},{2,10},{6,14},... | collective-permute-start | bytes 1179656 | tf_op jit(solution)/shard_map/ppermute | solution.py:513
  84.9 1.5 %collective-permute-start.21 = (bf16[512,256]{1,0:T(8,128)(2,1)S(1)}, bf16[512,256]{1,0:T(8,128)(2,1)S(1)}, u32[]{:S(2)}, u32[]{:S(2)}) collective-permute-start(bf16[512,256]{1,0:T(8,128)(2,1)S(1)} %get-tuple-element.127.refs_4_), channel_id=1, source_target_pairs={{0,4},{4,0},{8,12},{12,8},{1,5},{5,1},{9,13},{13,9},{2,6},{6,2},{1... | collective-permute-start | bytes 786440 | tf_op jit(solution)/shard_map/ppermute | solution.py:517
  85.4 1.5 %collective-permute-start.23 = (bf16[512,256]{1,0:T(8,128)(2,1)S(1)}, bf16[512,256]{1,0:T(8,128)(2,1)S(1)}, u32[]{:S(2)}, u32[]{:S(2)}) collective-permute-start(bf16[512,256]{1,0:T(8,128)(2,1)S(1)} %get-tuple-element.133.refs_8_), channel_id=1, source_target_pairs={{0,4},{4,0},{8,12},{12,8},{1,5},{5,1},{9,13},{13,9},{2,6},{6,2},{1... | collective-permute-start | bytes 786440 | tf_op jit(solution)/shard_map/ppermute | solution.py:517
  85.4 1.9 %collective-permute-start.22 = (bf16[512,256]{1,0:T(8,128)(2,1)S(1)}, bf16[512,256]{1,0:T(8,128)(2,1)S(1)}, u32[]{:S(2)}, u32[]{:S(2)}) collective-permute-start(bf16[512,256]{1,0:T(8,128)(2,1)S(1)} %collective-permute-done.16.refs_17_.refs_6_), channel_id=1, source_target_pairs={{0,4},{4,0},{8,12},{12,8},{1,5},{5,1},{9,13},{13,9},{2,6},{6,2},{1... | collective-permute-start | bytes 786440 | tf_op jit(solution)/shard_map/ppermute | solution.py:517
  85.9 1.8 %collective-permute-start.25 = (bf16[512,256]{1,0:T(8,128)(2,1)S(1)}, bf16[512,256]{1,0:T(8,128)(2,1)S(1)}, u32[]{:S(2)}, u32[]{:S(2)}) collective-permute-start(bf16[512,256]{1,0:T(8,128)(2,1)S(1)} %collective-permute-done.24.refs_10_), channel_id=1, source_target_pairs={{0,4},{4,0},{8,12},{12,8},{1,5},{5,1},{9,13},{13,9},{2,6},{6,2},{1... | collective-permute-start | bytes 786440 | tf_op jit(solution)/shard_map/ppermute | solution.py:517
  86.4 7.5 %collective-permute-start.17 = (bf16[768,256]{1,0:T(8,128)(2,1)S(1)}, bf16[768,256]{1,0:T(8,128)(2,1)S(1)}, u32[]{:S(2)}, u32[]{:S(2)}) collective-permute-start(bf16[768,256]{1,0:T(8,128)(2,1)S(1)} %get-tuple-element.131.refs_0_), channel_id=1, source_target_pairs={{0,4},{4,0},{8,12},{12,8},{1,5},{5,1},{9,13},{13,9},{2,6},{6,2},{1... | collective-permute-start | bytes 1179656 | tf_op jit(solution)/shard_map/ppermute | solution.py:517
  93.9 1.7 %collective-permute-start.26 = (bf16[768,256]{1,0:T(8,128)(2,1)S(1)}, bf16[768,256]{1,0:T(8,128)(2,1)S(1)}, u32[]{:S(2)}, u32[]{:S(2)}) collective-permute-start(bf16[768,256]{1,0:T(8,128)(2,1)S(1)} %collective-permute-done.18.refs_2_), channel_id=1, source_target_pairs={{0,4},{4,0},{8,12},{12,8},{1,5},{5,1},{9,13},{13,9},{2,6},{6,2},{1... | collective-permute-start | bytes 1179656 | tf_op jit(solution)/shard_map/ppermute | solution.py:517

commit v12 on v11

--- a/solution.py
+++ b/solution.py
@@ -535,7 +535,7 @@
     p = lax.axis_index("pts").astype(jnp.int32).reshape(1)
     owned, k = master.shape[1:]
     points_here = 2 * picks.shape[1]
-    size_one = points_here * 3 // 8
+    size_one = points_here // 2
     parts = [(0, points_here - size_one), (points_here - size_one, size_one)]
     bits = n_feat.bit_length() - 1
     points, picks, phase = in_hbm(points), in_hbm(picks), phase[None, :]
@@ -586,11 +586,11 @@
             features[m].append(feats)
         return token
 
+    chunk, token = total(f, kept_zero, got_zero, 0, False, [token])
+    rows_zero, masks = give_back(chunk)
     token = some(token, 1)
     for bit in range(1, bits):
         kept_one, got_one, token = add_up(kept_one, got_one, bit, token)
-    chunk, token = total(f, kept_zero, got_zero, 0, False, [token])
-    rows_zero, masks = give_back(chunk)
     token = some(token, 1)
     chunk, token = total(f, kept_one, got_one, 0, False, [token])
     rows_one, masks = give_back(chunk)

time: 97.1 us -> 95.6 us (0.985)
  starting transfers between devices: 21.9 us -> 17.6 us
  waiting for transfers between devices: 18.6 us -> 22.7 us
  Pallas kernels: 55.3 us -> 54.1 us
    ppermute x6, starting transfers between devices: 10.7 us -> 7.53 us  [swap(): return lax.ppermute(x, 'feat', [(i, i ^ 2 ** bit) for i in range(n)])]
    ppermute x6, waiting for transfers between devices: 5.63 us -> 8.73 us  [swap(): return lax.ppermute(x, 'feat', [(i, i ^ 2 ** bit) for i in range(n)])]
    pallas_call x1, Pallas kernels: 14.4 us -> 12.1 us  [first_rates(): pl.pallas_call(kernel, grid_spec=pltpu.PrefetchScalarGridSpec(num_scalar_...]
    pallas_call x2, Pallas kernels: 7.04 us -> 9.05 us  [rates(): pl.pallas_call(kernel, grid_spec=pltpu.PrefetchScalarGridSpec(num_scalar_...]
    ppermute x7, waiting for transfers between devices: 9.72 us -> 10.9 us  [ring(): return lax.ppermute(x, axis, [(i, (i + distance) % n) for i in range(n)])]
    pallas_call x1, Pallas kernels: 3.61 us -> 2.57 us  [first_part(): pl.pallas_call(functools.partial(first_part_kernel, n), in_specs=[IN_VMEM...]
    ppermute x7, starting transfers between devices: 8.8 us -> 7.78 us  [ring(): return lax.ppermute(x, axis, [(i, (i + distance) % n) for i in range(n)])]
  transfers between devices with their start and end apart: 27 -> 27, of which waited for: 14 -> 13; matrix products, arithmetic and copies ran while one was open for 0% -> 0% of each run, Pallas kernels for 52% -> 51%
where the time goes in v12:
time: 95.6 us; the launch traced here: 95.5 us
  Pallas kernels  54.1 us (57%)
  waiting for transfers between devices  22.7 us (24%)
  starting transfers between devices  17.6 us (18%)
  between operations  1.09 us (1%)
    pallas_call x6, Pallas kernels, owned_features(): pl.pallas_call(functools.partial(features_kernel, start, size), in_specs=...  12.7 us
    pallas_call x1, Pallas kernels, first_rates(): pl.pallas_call(kernel, grid_spec=pltpu.PrefetchScalarGridSpec(num_scalar_...  12.1 us
    ppermute x7, waiting for transfers between devices, ring(): return lax.ppermute(x, axis, [(i, (i + distance) % n) for i in range(n)])  10.9 us
    pallas_call x4, Pallas kernels, update(): pl.pallas_call(functools.partial(update_kernel, n, at), grid=(steps,), in...  10.3 us
    pallas_call x2, Pallas kernels, rates(): pl.pallas_call(kernel, grid_spec=pltpu.PrefetchScalarGridSpec(num_scalar_...  9.05 us
    ppermute x6, waiting for transfers between devices, swap(): return lax.ppermute(x, 'feat', [(i, i ^ 2 ** bit) for i in range(n)])  8.73 us
    ppermute x7, starting transfers between devices, ring(): return lax.ppermute(x, axis, [(i, (i + distance) % n) for i in range(n)])  7.78 us
    ppermute x6, starting transfers between devices, swap(): return lax.ppermute(x, 'feat', [(i, i ^ 2 ** bit) for i in range(n)])  7.53 us
  transfers between devices with their start and end apart: 27, of which 13 were waited for; matrix products, arithmetic and copies ran while one was open for 0% of the time, Pallas kernels for 51%

profile of v12, /device:TPU:0, one launch (start us, length us, event | category | flops | bytes accessed | tf_op | source)
XLA Modules:
  0.0 95.5 jit_solution(4767808553625410040)
XLA Ops:
  0.6 2.5 %chosen_points.1 = (bf16[1024,256]{1,0:T(8,128)(2,1)S(1)}, f32[8,128]{1,0:T(8,128)S(1)}) custom-call(s32[2,512]{1,0:T(2,128)} %picks.1, bf16[2048,256]{1,0:T(8,128)(2,1)} %points.1), custom_call_target="tpu_custom_call" | custom-call | flops 3000000000 | bytes 1024 | tf_op jit(solution)/shard_map/chosen_points/pallas_call | solution.py:70
  3.2 0.5 collective-permute-start.2
  3.7 2.6 %collective-permute-start.5 = (bf16[1024,256]{1,0:T(8,128)(2,1)S(1)}, bf16[1024,256]{1,0:T(8,128)(2,1)S(1)}, u32[]{:S(2)}, u32[]{:S(2)}) collective-permute-start(bf16[1024,256]{1,0:T(8,128)(2,1)S(1)} %get-tuple-element.71.refs_2_), channel_id=1, source_target_pairs={{0,8},{4,12},{8,0},{12,4},{1,9},{5,13},{9,1},{13,5},{2,10},{6,14},... | collective-permute-start | bytes 1572872 | tf_op jit(solution)/shard_map/ppermute | solution.py:513
  6.3 12.1 %first_log_rates.1 = (bf16[512,2048]{1,0:T(8,128)(2,1)S(1)}, bf16[256,2048]{1,0:T(8,128)(2,1)S(1)}, f32[1,2048]{1,0:T(1,128)S(1)}, f32[256,256]{1,0:T(8,128)S(1)...) custom-call(s32[1]{0:T(128)} %bitcast.refs_0_.f, s32[1]{0:T(128)} %bitcast.1.refs_1_.p, ...), custom_call_target="tpu_custom_call" | custom-call | flops 12000000000 | bytes 1024 | tf_op jit(solution)/shard_map/first_log_rates/pallas_call | solution.py:253
  18.4 1.6 %collective-permute-start = (bf16[256,256]{1,0:T(8,128)(2,1)S(1)}, bf16[256,256]{1,0:T(8,128)(2,1)S(1)}, u32[]{:S(2)}, u32[]{:S(2)}) collective-permute-start(bf16[256,256]{1,0:T(8,128)(2,1)S(1)} %get-tuple-element.76), channel_id=1, source_target_pairs={{0,1},{1,0},{2,3},{3,2},{4,5},{5,4},{6,7},{7,6},{8,9},{9,8},{10,11... | collective-permute-start | bytes 393224 | tf_op jit(solution)/shard_map/ppermute | solution.py:525
  20.1 4.3 %partial_log_rates.2 = (bf16[512,2048]{1,0:T(8,128)(2,1)S(1)}, f32[512,256]{1,0:T(8,128)S(1)}, f32[8,128]{1,0:T(8,128)S(1)}) custom-call(s32[1]{0:T(128)} %bitcast.refs_0_.f, s32[1]{0:T(128)} %bitcast.1.refs_1_.p, bf16[1024,256]{1,0:T(8,128)(2,1)S(1)} %get-tuple-element.71.refs_2_, bf16[256,8192]{1,0:T(8,128)(2,1)S(1)} %copy-done.4, f32[1,8192]{1,0:T(1,128)S(1)} %bitcast.8, ...), custom_call_target="tpu_custom_call" | custom-call | flops 6000000000 | bytes 1024 | tf_op jit(solution)/shard_map/partial_log_rates/pallas_call | solution.py:189
  24.4 0.0 collective-permute-done.b
  24.4 2.7 %collective-permute-start.3 = (bf16[256,256]{1,0:T(8,128)(2,1)S(1)}, bf16[256,256]{1,0:T(8,128)(2,1)S(1)}, u32[]{:S(2)}, u32[]{:S(2)}) collective-permute-start(bf16[256,256]{1,0:T(8,128)(2,1)S(1)} %get-tuple-element.83.a), channel_id=1, source_target_pairs={{0,2},{1,3},{2,0},{3,1},{4,6},{5,7},{6,4},{7,5},{8,10},{9,11},{10,... | collective-permute-start | bytes 393224 | tf_op jit(solution)/shard_map/ppermute | solution.py:525
  27.1 4.8 %partial_log_rates.3 = (f32[256,256]{1,0:T(8,128)S(1)}, bf16[256,256]{1,0:T(8,128)(2,1)S(1)}, f32[8,128]{1,0:T(8,128)S(1)}) custom-call(s32[1]{0:T(128)} %bitcast.refs_0_.f, s32[1]{0:T(128)} %bitcast.1.refs_1_.p, bf16[1024,256]{1,0:T(8,128)(2,1)S(1)} %get-tuple-element.71.refs_2_, bf16[256,8192]{1,0:T(8,128)(2,1)S(1)} %copy-done.4, f32[1,8192]{1,0:T(1,128)S(1)} %bitcast.9, ...), custom_call_target="tpu_custom_call" | custom-call | flops 6000000000 | bytes 1024 | tf_op jit(solution)/shard_map/partial_log_rates/pallas_call | solution.py:189
  31.8 1.3 %collective-permute-start.1 = (bf16[256,256]{1,0:T(8,128)(2,1)S(1)}, bf16[256,256]{1,0:T(8,128)(2,1)S(1)}, u32[]{:S(2)}, u32[]{:S(2)}) collective-permute-start(bf16[256,256]{1,0:T(8,128)(2,1)S(1)} %get-tuple-element.80), channel_id=1, source_target_pairs={{0,1},{1,0},{2,3},{3,2},{4,5},{5,4},{6,7},{7,6},{8,9},{9,8},{10,11... | collective-permute-start | bytes 393224 | tf_op jit(solution)/shard_map/ppermute | solution.py:525
  33.2 0.3 collective-permute-done.3.b
  33.5 0.0 collective-permute-done.2.chosen
  33.5 2.1 %owned_features.6 = (bf16[512,2048]{1,0:T(8,128)(2,1)S(1)}, f32[8,128]{1,0:T(8,128)S(1)}) custom-call(bf16[1024,256]{1,0:T(8,128)(2,1)S(1)} %collective-permute-done.2.chosen, bf16[256,2048]{1,0:T(8,128)(2,1)S(1)} %get-tuple-element.81.omega, f32[1,2048]{1,0:T(1,128)S(1)} %get-tuple-element.82.phase, f32[8,128]{1,0:T(8,128)S(1)} %get-tuple-element.85.refs_0_), custom_call_target="tpu_custom_call" | custom-call | flops 1000000000 | bytes 1024 | tf_op jit(solution)/shard_map/owned_features/pallas_call | solution.py:293
  35.6 2.2 %collective-permute-done.1.b = bf16[256,256]{1,0:T(8,128)(2,1)S(1)} collective-permute-done((bf16[256,256]{1,0:T(8,128)(2,1)S(1)}, bf16[256,256]{1,0:T(8,128)(2,1)S(1)}, u32[]{:S(2)}, u32[]{:S(2)}) %collective-permute-start.1) | collective-permute-done | bytes 131104 | tf_op jit(solution)/shard_map/ppermute | solution.py:525
  37.8 0.4 collective-permute-start.4
  38.2 1.4 %collective-permute-start.8 = (bf16[256,256]{1,0:T(8,128)(2,1)S(1)}, bf16[256,256]{1,0:T(8,128)(2,1)S(1)}, u32[]{:S(2)}, u32[]{:S(2)}) collective-permute-start(bf16[256,256]{1,0:T(8,128)(2,1)S(1)} %get-tuple-element.91.refs_0_), channel_id=1, source_target_pairs={{0,1},{1,0},{2,3},{3,2},{4,5},{5,4},{6,7},{7,6},{8,9},{9,8},{10,11... | collective-permute-start | bytes 393224 | tf_op jit(solution)/shard_map/ppermute | solution.py:525
  39.7 2.1 %owned_features.7 = (bf16[512,2048]{1,0:T(8,128)(2,1)S(1)}, f32[8,128]{1,0:T(8,128)S(1)}) custom-call(bf16[1024,256]{1,0:T(8,128)(2,1)S(1)} %collective-permute-done.5.chosen, bf16[256,2048]{1,0:T(8,128)(2,1)S(1)} %get-tuple-element.81.omega, f32[1,2048]{1,0:T(1,128)S(1)} %get-tuple-element.82.phase, f32[8,128]{1,0:T(8,128)S(1)} %get-tuple-element.88.refs_0_), custom_call_target="tpu_custom_call" | custom-call | flops 1000000000 | bytes 1024 | tf_op jit(solution)/shard_map/owned_features/pallas_call | solution.py:293
  41.8 5.0 %collective-permute-done.4.b = bf16[256,256]{1,0:T(8,128)(2,1)S(1)} collective-permute-done((bf16[256,256]{1,0:T(8,128)(2,1)S(1)}, bf16[256,256]{1,0:T(8,128)(2,1)S(1)}, u32[]{:S(2)}, u32[]{:S(2)}) %collective-permute-start.4) | collective-permute-done | bytes 131104 | tf_op jit(solution)/shard_map/ppermute | solution.py:525
  46.8 0.1 collective-permute-start.6
  46.9 0.0 collective-permute-done.8.refs_1_
  46.9 1.0 %residuals.2 = (f32[1024,256]{1,0:T(8,128)}, bf16[256,512]{1,0:T(8,128)(2,1)S(1)}, f32[8,128]{1,0:T(8,128)S(1)}) custom-call(s32[1]{0:T(128)} %bitcast.refs_0_.f, bf16[256,256]{1,0:T(8,128)(2,1)S(1)} %get-tuple-element.91.refs_0_, bf16[256,256]{1,0:T(8,128)(2,1)S(1)} %collective-permute-done.8.refs_1_, s32[1024,256]{1,0:T(8,128)S(1)} %bitcast.5, ...), custom_call_target="tpu_custom_call" | custom-call | flops 1000000000 | bytes 1024 | tf_op jit(solution)/shard_map/residuals/pallas_call | solution.py:371
  47.9 0.6 collective-permute-start.9
  48.5 2.1 %owned_features.8 = (bf16[512,2048]{1,0:T(8,128)(2,1)S(1)}, f32[8,128]{1,0:T(8,128)S(1)}) custom-call(bf16[1024,256]{1,0:T(8,128)(2,1)S(1)} %collective-permute-done.7.chosen, bf16[256,2048]{1,0:T(8,128)(2,1)S(1)} %get-tuple-element.81.omega, f32[1,2048]{1,0:T(1,128)S(1)} %get-tuple-element.82.phase, f32[8,128]{1,0:T(8,128)S(1)} %get-tuple-element.93.refs_0_), custom_call_target="tpu_custom_call" | custom-call | flops 1000000000 | bytes 1024 | tf_op jit(solution)/shard_map/owned_features/pallas_call | solution.py:293
  50.6 1.3 %collective-permute-done.6.refs_1_ = bf16[256,256]{1,0:T(8,128)(2,1)S(1)} collective-permute-done((bf16[256,256]{1,0:T(8,128)(2,1)S(1)}, bf16[256,256]{1,0:T(8,128)(2,1)S(1)}, u32[]{:S(2)}, u32[]{:S(2)}) %collective-permute-start.6) | collective-permute-done | bytes 131104 | tf_op jit(solution)/shard_map/ppermute | solution.py:525
  51.8 1.0 %residuals.3 = (f32[1024,256]{1,0:T(8,128)}, bf16[256,512]{1,0:T(8,128)(2,1)S(1)}, f32[8,128]{1,0:T(8,128)S(1)}) custom-call(s32[1]{0:T(128)} %bitcast.refs_0_.f, bf16[256,256]{1,0:T(8,128)(2,1)S(1)} %get-tuple-element.90.refs_0_, bf16[256,256]{1,0:T(8,128)(2,1)S(1)} %collective-permute-done.6.refs_1_, ...), custom_call_target="tpu_custom_call", output_to_operand_aliasing={{0}: (5, {})} | custom-call | flops 1000000000 | bytes 1024 | tf_op jit(solution)/shard_map/residuals/pallas_call | solution.py:371
  52.8 0.6 collective-permute-start.11
  53.4 0.0 collective-permute-start.13
  53.4 2.1 %owned_features.9 = (bf16[512,2048]{1,0:T(8,128)(2,1)S(1)}, f32[8,128]{1,0:T(8,128)S(1)}) custom-call(bf16[1024,256]{1,0:T(8,128)(2,1)S(1)} %collective-permute-done.2.chosen, bf16[256,2048]{1,0:T(8,128)(2,1)S(1)} %get-tuple-element.81.omega, f32[1,2048]{1,0:T(1,128)S(1)} %get-tuple-element.82.phase, f32[8,128]{1,0:T(8,128)S(1)} %get-tuple-element.98.refs_0_), custom_call_target="tpu_custom_call" | custom-call | flops 100000000 | bytes 1024 | tf_op jit(solution)/shard_map/owned_features/pallas_call | solution.py:293
  55.5 2.1 %owned_features.10 = (bf16[512,2048]{1,0:T(8,128)(2,1)S(1)}, f32[8,128]{1,0:T(8,128)S(1)}) custom-call(bf16[1024,256]{1,0:T(8,128)(2,1)S(1)} %collective-permute-done.5.chosen, bf16[256,2048]{1,0:T(8,128)(2,1)S(1)} %get-tuple-element.81.omega, f32[1,2048]{1,0:T(1,128)S(1)} %get-tuple-element.82.phase, f32[8,128]{1,0:T(8,128)S(1)} %get-tuple-element.100.refs_0_), custom_call_target="tpu_custom_call" | custom-call | flops 100000000 | bytes 1024 | tf_op jit(solution)/shard_map/owned_features/pallas_call | solution.py:293
  57.6 0.6 collective-permute-start.14
  58.2 0.1 collective-permute-start.10
  58.2 2.3 %owned_features.11 = (bf16[512,2048]{1,0:T(8,128)(2,1)S(1)}, f32[8,128]{1,0:T(8,128)S(1)}) custom-call(bf16[1024,256]{1,0:T(8,128)(2,1)S(1)} %collective-permute-done.7.chosen, bf16[256,2048]{1,0:T(8,128)(2,1)S(1)} %get-tuple-element.81.omega, f32[1,2048]{1,0:T(1,128)S(1)} %get-tuple-element.82.phase, f32[8,128]{1,0:T(8,128)S(1)} %get-tuple-element.104.refs_0_), custom_call_target="tpu_custom_call" | custom-call | flops 100000000 | bytes 1024 | tf_op jit(solution)/shard_map/owned_features/pallas_call | solution.py:293
  60.6 0.4 collective-permute-done.11.refs_6_
  61.0 0.1 collective-permute-start.12
  61.1 0.0 collective-permute-done.13.refs_5_
  61.1 0.0 copy-start.1
  61.1 0.0 copy-start.2
  61.1 0.0 copy-start.3
  61.1 2.6 %first_part.1 = (f32[2048,256]{1,0:T(8,128)S(1)}, f32[8,128]{1,0:T(8,128)S(1)}) custom-call(bf16[512,2048]{1,0:T(8,128)(2,1)S(1)} %get-tuple-element.109.refs_0_, bf16[512,2048]{1,0:T(8,128)(2,1)S(1)} %get-tuple-element.110.refs_1_, bf16[512,2048]{1,0:T(8,128)(2,1)S(1)} %get-tuple-element.111.refs_2_, bf16[512,2048]{1,0:T(8,128)(2,1)S(1)} %get-tuple-element.112.refs_3_, ...), custom_call_target="tpu_custom_call" | custom-call | flops 300000000 | bytes 1024 | tf_op jit(solution)/shard_map/first_part/pallas_call | solution.py:413
  63.7 0.0 collective-permute-done.10.refs_5_
  63.7 0.0 collective-permute-done.12.refs_7_
  63.7 1.7 %update.4 = (f32[1,2048,256]{2,1,0:T(8,128)}, f32[1,2048,256]{2,1,0:T(8,128)}, f32[1,2048,256]{2,1,0:T(8,128)}, bf16[256,256]{1,0:T(8,128)(2,1)S(1)}) custom-call(bf16[512,2048]{1,0:T(8,128)(2,1)S(1)} %get-tuple-element.97.refs_0_, bf16[512,2048]{1,0:T(8,128)(2,1)S(1)} %get-tuple-element.99.refs_1_, bf16[512,2048]{1,0:T(8,128)(2,1)S(1)} %get-tuple-element.101.refs_2_, ...), custom_call_target="tpu_custom_call" | custom-call | flops 4000000000 | bytes 1024 | tf_op jit(solution)/shard_map/update/pallas_call | solution.py:461
  65.5 1.5 %collective-permute-start.15 = (bf16[256,256]{1,0:T(8,128)(2,1)S(1)}, bf16[256,256]{1,0:T(8,128)(2,1)S(1)}, u32[]{:S(2)}, u32[]{:S(2)}) collective-permute-start(bf16[256,256]{1,0:T(8,128)(2,1)S(1)} %get-tuple-element.123.refs_0_), channel_id=1, source_target_pairs={{0,8},{4,12},{8,0},{12,4},{1,9},{5,13},{9,1},{13,5},{2,10},{6,14},... | collective-permute-start | bytes 393224 | tf_op jit(solution)/shard_map/ppermute | solution.py:513
  67.0 0.0 collective-permute-start.19
  67.0 2.6 %update.5 = (f32[1,2048,256]{2,1,0:T(8,128)}, f32[1,2048,256]{2,1,0:T(8,128)}, f32[1,2048,256]{2,1,0:T(8,128)}, bf16[512,256]{1,0:T(8,128)(2,1)S(1)}) custom-call(bf16[512,2048]{1,0:T(8,128)(2,1)S(1)} %get-tuple-element.97.refs_0_, bf16[512,2048]{1,0:T(8,128)(2,1)S(1)} %get-tuple-element.99.refs_1_, ...), custom_call_target="tpu_custom_call", output_to_operand_aliasing={{0}: (13, {}), {1}: (14, {}), {2}: (15, {})} | custom-call | flops 4000000000 | bytes 1024 | tf_op jit(solution)/shard_map/update/pallas_call | solution.py:461
  69.5 0.7 collective-permute-start.16
  70.2 1.1 %collective-permute-done.15.refs_17_.refs_2_ = bf16[256,256]{1,0:T(8,128)(2,1)S(1)} collective-permute-done((bf16[256,256]{1,0:T(8,128)(2,1)S(1)}, bf16[256,256]{1,0:T(8,128)(2,1)S(1)}, u32[]{:S(2)}, u32[]{:S(2)}) %collective-permute-start.15) | collective-permute-done | bytes 131104 | tf_op jit(solution)/shard_map/ppermute | solution.py:513
  71.3 2.6 %update.6 = (f32[1,2048,256]{2,1,0:T(8,128)}, f32[1,2048,256]{2,1,0:T(8,128)}, f32[1,2048,256]{2,1,0:T(8,128)}, bf16[512,256]{1,0:T(8,128)(2,1)S(1)}) custom-call(bf16[512,2048]{1,0:T(8,128)(2,1)S(1)} %get-tuple-element.97.refs_0_, bf16[512,2048]{1,0:T(8,128)(2,1)S(1)} %get-tuple-element.99.refs_1_, ...), custom_call_target="tpu_custom_call", output_to_operand_aliasing={{0}: (13, {}), {1}: (14, {}), {2}: (15, {})} | custom-call | flops 4000000000 | bytes 1024 | tf_op jit(solution)/shard_map/update/pallas_call | solution.py:461
  73.9 1.2 %collective-permute-start.24 = (bf16[512,256]{1,0:T(8,128)(2,1)S(1)}, bf16[512,256]{1,0:T(8,128)(2,1)S(1)}, u32[]{:S(2)}, u32[]{:S(2)}) collective-permute-start(bf16[512,256]{1,0:T(8,128)(2,1)S(1)} %get-tuple-element.133.refs_8_), channel_id=1, source_target_pairs={{0,8},{4,12},{8,0},{12,4},{1,9},{5,13},{9,1},{13,5},{2,10},{6,14},... | collective-permute-start | bytes 786440 | tf_op jit(solution)/shard_map/ppermute | solution.py:513
  75.0 0.0 collective-permute-start.20
  75.0 3.6 %collective-permute-done.16.refs_17_.refs_6_ = bf16[512,256]{1,0:T(8,128)(2,1)S(1)} collective-permute-done((bf16[512,256]{1,0:T(8,128)(2,1)S(1)}, bf16[512,256]{1,0:T(8,128)(2,1)S(1)}, u32[]{:S(2)}, u32[]{:S(2)}) %collective-permute-start.16) | collective-permute-done | bytes 262176 | tf_op jit(solution)/shard_map/ppermute | solution.py:513
  78.6 3.4 %update.7 = (f32[1,2048,256]{2,1,0:T(8,128)}, f32[1,2048,256]{2,1,0:T(8,128)}, f32[1,2048,256]{2,1,0:T(8,128)}, bf16[768,256]{1,0:T(8,128)(2,1)S(1)}) custom-call(bf16[512,2048]{1,0:T(8,128)(2,1)S(1)} %get-tuple-element.97.refs_0_, bf16[512,2048]{1,0:T(8,128)(2,1)S(1)} %get-tuple-element.99.refs_1_, ...), custom_call_target="tpu_custom_call", output_to_operand_aliasing={{0}: (13, {}), {1}: (14, {}), {2}: (15, {})} | custom-call | flops 4000000000 | bytes 1024 | tf_op jit(solution)/shard_map/update/pallas_call | solution.py:461
  82.1 0.7 collective-permute-start.18
  82.8 1.1 %collective-permute-done.24.refs_10_ = bf16[512,256]{1,0:T(8,128)(2,1)S(1)} collective-permute-done((bf16[512,256]{1,0:T(8,128)(2,1)S(1)}, bf16[512,256]{1,0:T(8,128)(2,1)S(1)}, u32[]{:S(2)}, u32[]{:S(2)}) %collective-permute-start.24) | collective-permute-done | bytes 262176 | tf_op jit(solution)/shard_map/ppermute | solution.py:513
  83.9 0.5 collective-permute-start.22
  84.4 0.1 collective-permute-start.25
  84.5 0.4 collective-permute-start.17
  84.9 0.5 collective-permute-done.23.refs_9_
  85.4 0.4 collective-permute-done.22.refs_7_
  85.8 0.4 collective-permute-done.25.refs_11_
  86.2 1.6 %put_rows.2.refs_4_ = bf16[8192,256]{1,0:T(8,128)(2,1)} custom-call(s32[1]{0:T(128)} %bitcast.1.refs_1_.p, bf16[256,256]{1,0:T(8,128)(2,1)S(1)} %get-tuple-element.123.refs_0_, bf16[256,256]{1,0:T(8,128)(2,1)S(1)} %collective-permute-done.19.refs_1_, bf16[256,256]{1,0:T(8,128)(2,1)S(1)} %collective-permute-done.15.refs_17_.refs_2_, ...), custom_call_target="tpu_custom_call" | custom-call | flops 10000000 | bytes 1024 | tf_op jit(solution)/shard_map/put_rows/pallas_call | solution.py:495
  87.7 4.7 %collective-permute-done.18.refs_2_ = bf16[768,256]{1,0:T(8,128)(2,1)S(1)} collective-permute-done((bf16[768,256]{1,0:T(8,128)(2,1)S(1)}, bf16[768,256]{1,0:T(8,128)(2,1)S(1)}, u32[]{:S(2)}, u32[]{:S(2)}) %collective-permute-start.18) | collective-permute-done | bytes 393248 | tf_op jit(solution)/shard_map/ppermute | solution.py:513
  92.4 1.7 %collective-permute-done.26.refs_3_ = bf16[768,256]{1,0:T(8,128)(2,1)S(1)} collective-permute-done((bf16[768,256]{1,0:T(8,128)(2,1)S(1)}, bf16[768,256]{1,0:T(8,128)(2,1)S(1)}, u32[]{:S(2)}, u32[]{:S(2)}) %collective-permute-start.26) | collective-permute-done | bytes 393248 | tf_op jit(solution)/shard_map/ppermute | solution.py:517
  94.2 1.2 %put_rows.3 = bf16[8192,256]{1,0:T(8,128)(2,1)} custom-call(s32[1]{0:T(128)} %bitcast.1.refs_1_.p, bf16[768,256]{1,0:T(8,128)(2,1)S(1)} %get-tuple-element.131.refs_0_, bf16[768,256]{1,0:T(8,128)(2,1)S(1)} %collective-permute-done.17.refs_1_, bf16[768,256]{1,0:T(8,128)(2,1)S(1)} %collective-permute-done.18.refs_2_, ...), custom_call_target="tpu_custom_call", output_to_operand_aliasing={{}: (5, {})} | custom-call | flops 10000000 | bytes 1024 | tf_op jit(solution)/shard_map/put_rows/pallas_call | solution.py:495
  (29 shorter events, 0.2 us)
Async XLA Ops:
  0.6 5.7 %copy-start.7 = (f32[8192]{0:T(1024)S(1)}, f32[8192]{0:T(1024)}, u32[]{:S(2)}) copy-start(f32[8192]{0:T(1024)} %param.13) | copy-start | bytes 98308
  3.2 30.3 %collective-permute-start.2 = (bf16[1024,256]{1,0:T(8,128)(2,1)S(1)}, bf16[1024,256]{1,0:T(8,128)(2,1)S(1)}, u32[]{:S(2)}, u32[]{:S(2)}) collective-permute-start(bf16[1024,256]{1,0:T(8,128)(2,1)S(1)} %get-tuple-element.71.refs_2_), channel_id=1, source_target_pairs={{0,4},{4,0},{8,12},{12,8},{1,5},{5,1},{9,13},{13,9},{2,6},{6,2},{1... | collective-permute-start | bytes 1572872 | tf_op jit(solution)/shard_map/ppermute | solution.py:517
  3.7 23.4 %collective-permute-start.5 = (bf16[1024,256]{1,0:T(8,128)(2,1)S(1)}, bf16[1024,256]{1,0:T(8,128)(2,1)S(1)}, u32[]{:S(2)}, u32[]{:S(2)}) collective-permute-start(bf16[1024,256]{1,0:T(8,128)(2,1)S(1)} %get-tuple-element.71.refs_2_), channel_id=1, source_target_pairs={{0,8},{4,12},{8,0},{12,4},{1,9},{5,13},{9,1},{13,5},{2,10},{6,14},... | collective-permute-start | bytes 1572872 | tf_op jit(solution)/shard_map/ppermute | solution.py:513
  6.3 13.8 %copy-start.4 = (bf16[256,8192]{1,0:T(8,128)(2,1)S(1)}, bf16[256,8192]{1,0:T(8,128)(2,1)}, u32[]{:S(2)}) copy-start(bf16[256,8192]{1,0:T(8,128)(2,1)} %refs_3_.5) | copy-start | bytes 12582916
  6.3 13.8 %copy-start.5 = (bf16[8192,256]{1,0:T(8,128)(2,1)S(1)}, bf16[8192,256]{1,0:T(8,128)(2,1)}, u32[]{:S(2)}) copy-start(bf16[8192,256]{1,0:T(8,128)(2,1)} %refs_5_.5) | copy-start | bytes 12582916
  18.4 5.9 %collective-permute-start = (bf16[256,256]{1,0:T(8,128)(2,1)S(1)}, bf16[256,256]{1,0:T(8,128)(2,1)S(1)}, u32[]{:S(2)}, u32[]{:S(2)}) collective-permute-start(bf16[256,256]{1,0:T(8,128)(2,1)S(1)} %get-tuple-element.76), channel_id=1, source_target_pairs={{0,1},{1,0},{2,3},{3,2},{4,5},{5,4},{6,7},{7,6},{8,9},{9,8},{10,11... | collective-permute-start | bytes 393224 | tf_op jit(solution)/shard_map/ppermute | solution.py:525
  24.4 9.1 %collective-permute-start.3 = (bf16[256,256]{1,0:T(8,128)(2,1)S(1)}, bf16[256,256]{1,0:T(8,128)(2,1)S(1)}, u32[]{:S(2)}, u32[]{:S(2)}) collective-permute-start(bf16[256,256]{1,0:T(8,128)(2,1)S(1)} %get-tuple-element.83.a), channel_id=1, source_target_pairs={{0,2},{1,3},{2,0},{3,1},{4,6},{5,7},{6,4},{7,5},{8,10},{9,11},{10,... | collective-permute-start | bytes 393224 | tf_op jit(solution)/shard_map/ppermute | solution.py:525
  27.1 21.4 %collective-permute-start.7 = (bf16[1024,256]{1,0:T(8,128)(2,1)S(1)}, bf16[1024,256]{1,0:T(8,128)(2,1)S(1)}, u32[]{:S(2)}, u32[]{:S(2)}) collective-permute-start(bf16[1024,256]{1,0:T(8,128)(2,1)S(1)} %collective-permute-done.5.chosen), channel_id=1, source_target_pairs={{0,4},{4,0},{8,12},{12,8},{1,5},{5,1},{9,13},{13,9},{2,6},{6,2},{1... | collective-permute-start | bytes 1572872 | tf_op jit(solution)/shard_map/ppermute | solution.py:517
  31.8 6.0 %collective-permute-start.1 = (bf16[256,256]{1,0:T(8,128)(2,1)S(1)}, bf16[256,256]{1,0:T(8,128)(2,1)S(1)}, u32[]{:S(2)}, u32[]{:S(2)}) collective-permute-start(bf16[256,256]{1,0:T(8,128)(2,1)S(1)} %get-tuple-element.80), channel_id=1, source_target_pairs={{0,1},{1,0},{2,3},{3,2},{4,5},{5,4},{6,7},{7,6},{8,9},{9,8},{10,11... | collective-permute-start | bytes 393224 | tf_op jit(solution)/shard_map/ppermute | solution.py:525
  37.8 8.9 %collective-permute-start.4 = (bf16[256,256]{1,0:T(8,128)(2,1)S(1)}, bf16[256,256]{1,0:T(8,128)(2,1)S(1)}, u32[]{:S(2)}, u32[]{:S(2)}) collective-permute-start(bf16[256,256]{1,0:T(8,128)(2,1)S(1)} %get-tuple-element.87.a), channel_id=1, source_target_pairs={{0,2},{1,3},{2,0},{3,1},{4,6},{5,7},{6,4},{7,5},{8,10},{9,11},{10,... | collective-permute-start | bytes 393224 | tf_op jit(solution)/shard_map/ppermute | solution.py:525
  38.2 8.6 %collective-permute-start.8 = (bf16[256,256]{1,0:T(8,128)(2,1)S(1)}, bf16[256,256]{1,0:T(8,128)(2,1)S(1)}, u32[]{:S(2)}, u32[]{:S(2)}) collective-permute-start(bf16[256,256]{1,0:T(8,128)(2,1)S(1)} %get-tuple-element.91.refs_0_), channel_id=1, source_target_pairs={{0,1},{1,0},{2,3},{3,2},{4,5},{5,4},{6,7},{7,6},{8,9},{9,8},{10,11... | collective-permute-start | bytes 393224 | tf_op jit(solution)/shard_map/ppermute | solution.py:525
  39.7 7.2 %copy-start.6 = (s32[2,512,256]{2,1,0:T(8,128)S(1)}, s32[2,512,256]{2,1,0:T(8,128)}, u32[]{:S(2)}) copy-start(s32[2,512,256]{2,1,0:T(8,128)} %param.15) | copy-start | bytes 3145732
  46.8 5.0 %collective-permute-start.6 = (bf16[256,256]{1,0:T(8,128)(2,1)S(1)}, bf16[256,256]{1,0:T(8,128)(2,1)S(1)}, u32[]{:S(2)}, u32[]{:S(2)}) collective-permute-start(bf16[256,256]{1,0:T(8,128)(2,1)S(1)} %get-tuple-element.90.refs_0_), channel_id=1, source_target_pairs={{0,1},{1,0},{2,3},{3,2},{4,5},{5,4},{6,7},{7,6},{8,9},{9,8},{10,11... | collective-permute-start | bytes 393224 | tf_op jit(solution)/shard_map/ppermute | solution.py:525
  47.9 9.7 %collective-permute-start.9 = (bf16[256,512]{1,0:T(8,128)(2,1)S(1)}, bf16[256,512]{1,0:T(8,128)(2,1)S(1)}, u32[]{:S(2)}, u32[]{:S(2)}) collective-permute-start(bf16[256,512]{1,0:T(8,128)(2,1)S(1)} %get-tuple-element.102.refs_4_), channel_id=1, source_target_pairs={{0,8},{4,12},{8,0},{12,4},{1,9},{5,13},{9,1},{13,5},{2,10},{6,14},... | collective-permute-start | bytes 786440 | tf_op jit(solution)/shard_map/ppermute | solution.py:513
  52.8 8.2 %collective-permute-start.11 = (bf16[256,512]{1,0:T(8,128)(2,1)S(1)}, bf16[256,512]{1,0:T(8,128)(2,1)S(1)}, u32[]{:S(2)}, u32[]{:S(2)}) collective-permute-start(bf16[256,512]{1,0:T(8,128)(2,1)S(1)} %get-tuple-element.106.refs_4_), channel_id=1, source_target_pairs={{0,8},{4,12},{8,0},{12,4},{1,9},{5,13},{9,1},{13,5},{2,10},{6,14},... | collective-permute-start | bytes 786440 | tf_op jit(solution)/shard_map/ppermute | solution.py:513
  53.4 7.7 %collective-permute-start.13 = (bf16[256,512]{1,0:T(8,128)(2,1)S(1)}, bf16[256,512]{1,0:T(8,128)(2,1)S(1)}, u32[]{:S(2)}, u32[]{:S(2)}) collective-permute-start(bf16[256,512]{1,0:T(8,128)(2,1)S(1)} %get-tuple-element.102.refs_4_), channel_id=1, source_target_pairs={{0,4},{4,0},{8,12},{12,8},{1,5},{5,1},{9,13},{13,9},{2,6},{6,2},{1... | collective-permute-start | bytes 786440 | tf_op jit(solution)/shard_map/ppermute | solution.py:517
  53.4 7.7 %copy-start = (f32[1,2048,256]{2,1,0:T(8,128)S(1)}, f32[1,2048,256]{2,1,0:T(8,128)}, u32[]{:S(2)}) copy-start(f32[1,2048,256]{2,1,0:T(8,128)} %refs_10_.7) | copy-start | bytes 6291460
  57.6 3.5 %collective-permute-start.14 = (bf16[256,512]{1,0:T(8,128)(2,1)S(1)}, bf16[256,512]{1,0:T(8,128)(2,1)S(1)}, u32[]{:S(2)}, u32[]{:S(2)}) collective-permute-start(bf16[256,512]{1,0:T(8,128)(2,1)S(1)} %collective-permute-done.9.refs_6_), channel_id=1, source_target_pairs={{0,4},{4,0},{8,12},{12,8},{1,5},{5,1},{9,13},{13,9},{2,6},{6,2},{1... | collective-permute-start | bytes 786440 | tf_op jit(solution)/shard_map/ppermute | solution.py:517
  58.2 5.5 %collective-permute-start.10 = (bf16[256,512]{1,0:T(8,128)(2,1)S(1)}, bf16[256,512]{1,0:T(8,128)(2,1)S(1)}, u32[]{:S(2)}, u32[]{:S(2)}) collective-permute-start(bf16[256,512]{1,0:T(8,128)(2,1)S(1)} %get-tuple-element.106.refs_4_), channel_id=1, source_target_pairs={{0,4},{4,0},{8,12},{12,8},{1,5},{5,1},{9,13},{13,9},{2,6},{6,2},{1... | collective-permute-start | bytes 786440 | tf_op jit(solution)/shard_map/ppermute | solution.py:517
  61.0 2.7 %collective-permute-start.12 = (bf16[256,512]{1,0:T(8,128)(2,1)S(1)}, bf16[256,512]{1,0:T(8,128)(2,1)S(1)}, u32[]{:S(2)}, u32[]{:S(2)}) collective-permute-start(bf16[256,512]{1,0:T(8,128)(2,1)S(1)} %collective-permute-done.11.refs_6_), channel_id=1, source_target_pairs={{0,4},{4,0},{8,12},{12,8},{1,5},{5,1},{9,13},{13,9},{2,6},{6,2},{1... | collective-permute-start | bytes 786440 | tf_op jit(solution)/shard_map/ppermute | solution.py:517
  61.1 2.6 %copy-start.1 = (f32[1,2048,256]{2,1,0:T(8,128)S(1)}, f32[1,2048,256]{2,1,0:T(8,128)}, u32[]{:S(2)}) copy-start(f32[1,2048,256]{2,1,0:T(8,128)} %refs_11_.7) | copy-start | bytes 6291460
  61.1 2.6 %copy-start.2 = (f32[1,2048,256]{2,1,0:T(8,128)S(1)}, f32[1,2048,256]{2,1,0:T(8,128)}, u32[]{:S(2)}) copy-start(f32[1,2048,256]{2,1,0:T(8,128)} %refs_12_.7) | copy-start | bytes 6291460
  61.1 2.6 %copy-start.3 = (bf16[256,256]{1,0:T(8,128)(2,1)S(1)}, bf16[256,256]{1,0:T(8,128)(2,1)}, u32[]{:S(2)}) copy-start(bf16[256,256]{1,0:T(8,128)(2,1)} %refs_9_.7) | copy-start | bytes 393220
  65.5 5.8 %collective-permute-start.15 = (bf16[256,256]{1,0:T(8,128)(2,1)S(1)}, bf16[256,256]{1,0:T(8,128)(2,1)S(1)}, u32[]{:S(2)}, u32[]{:S(2)}) collective-permute-start(bf16[256,256]{1,0:T(8,128)(2,1)S(1)} %get-tuple-element.123.refs_0_), channel_id=1, source_target_pairs={{0,8},{4,12},{8,0},{12,4},{1,9},{5,13},{9,1},{13,5},{2,10},{6,14},... | collective-permute-start | bytes 393224 | tf_op jit(solution)/shard_map/ppermute | solution.py:513
  67.0 16.9 %collective-permute-start.19 = (bf16[256,256]{1,0:T(8,128)(2,1)S(1)}, bf16[256,256]{1,0:T(8,128)(2,1)S(1)}, u32[]{:S(2)}, u32[]{:S(2)}) collective-permute-start(bf16[256,256]{1,0:T(8,128)(2,1)S(1)} %get-tuple-element.123.refs_0_), channel_id=1, source_target_pairs={{0,4},{4,0},{8,12},{12,8},{1,5},{5,1},{9,13},{13,9},{2,6},{6,2},{1... | collective-permute-start | bytes 393224 | tf_op jit(solution)/shard_map/ppermute | solution.py:517
  69.5 9.1 %collective-permute-start.16 = (bf16[512,256]{1,0:T(8,128)(2,1)S(1)}, bf16[512,256]{1,0:T(8,128)(2,1)S(1)}, u32[]{:S(2)}, u32[]{:S(2)}) collective-permute-start(bf16[512,256]{1,0:T(8,128)(2,1)S(1)} %get-tuple-element.127.refs_4_), channel_id=1, source_target_pairs={{0,8},{4,12},{8,0},{12,4},{1,9},{5,13},{9,1},{13,5},{2,10},{6,14},... | collective-permute-start | bytes 786440 | tf_op jit(solution)/shard_map/ppermute | solution.py:513
  73.9 10.0 %collective-permute-start.24 = (bf16[512,256]{1,0:T(8,128)(2,1)S(1)}, bf16[512,256]{1,0:T(8,128)(2,1)S(1)}, u32[]{:S(2)}, u32[]{:S(2)}) collective-permute-start(bf16[512,256]{1,0:T(8,128)(2,1)S(1)} %get-tuple-element.133.refs_8_), channel_id=1, source_target_pairs={{0,8},{4,12},{8,0},{12,4},{1,9},{5,13},{9,1},{13,5},{2,10},{6,14},... | collective-permute-start | bytes 786440 | tf_op jit(solution)/shard_map/ppermute | solution.py:513
  75.0 9.4 %collective-permute-start.20 = (bf16[256,256]{1,0:T(8,128)(2,1)S(1)}, bf16[256,256]{1,0:T(8,128)(2,1)S(1)}, u32[]{:S(2)}, u32[]{:S(2)}) collective-permute-start(bf16[256,256]{1,0:T(8,128)(2,1)S(1)} %collective-permute-done.15.refs_17_.refs_2_), channel_id=1, source_target_pairs={{0,4},{4,0},{8,12},{12,8},{1,5},{5,1},{9,13},{13,9},{2,6},{6,2},{1... | collective-permute-start | bytes 393224 | tf_op jit(solution)/shard_map/ppermute | solution.py:517
  82.1 10.4 %collective-permute-start.18 = (bf16[768,256]{1,0:T(8,128)(2,1)S(1)}, bf16[768,256]{1,0:T(8,128)(2,1)S(1)}, u32[]{:S(2)}, u32[]{:S(2)}) collective-permute-start(bf16[768,256]{1,0:T(8,128)(2,1)S(1)} %get-tuple-element.131.refs_0_), channel_id=1, source_target_pairs={{0,8},{4,12},{8,0},{12,4},{1,9},{5,13},{9,1},{13,5},{2,10},{6,14},... | collective-permute-start | bytes 1179656 | tf_op jit(solution)/shard_map/ppermute | solution.py:513
  82.8 1.7 %collective-permute-start.21 = (bf16[512,256]{1,0:T(8,128)(2,1)S(1)}, bf16[512,256]{1,0:T(8,128)(2,1)S(1)}, u32[]{:S(2)}, u32[]{:S(2)}) collective-permute-start(bf16[512,256]{1,0:T(8,128)(2,1)S(1)} %get-tuple-element.127.refs_4_), channel_id=1, source_target_pairs={{0,4},{4,0},{8,12},{12,8},{1,5},{5,1},{9,13},{13,9},{2,6},{6,2},{1... | collective-permute-start | bytes 786440 | tf_op jit(solution)/shard_map/ppermute | solution.py:517
  83.9 1.5 %collective-permute-start.23 = (bf16[512,256]{1,0:T(8,128)(2,1)S(1)}, bf16[512,256]{1,0:T(8,128)(2,1)S(1)}, u32[]{:S(2)}, u32[]{:S(2)}) collective-permute-start(bf16[512,256]{1,0:T(8,128)(2,1)S(1)} %get-tuple-element.133.refs_8_), channel_id=1, source_target_pairs={{0,4},{4,0},{8,12},{12,8},{1,5},{5,1},{9,13},{13,9},{2,6},{6,2},{1... | collective-permute-start | bytes 786440 | tf_op jit(solution)/shard_map/ppermute | solution.py:517
  83.9 1.9 %collective-permute-start.22 = (bf16[512,256]{1,0:T(8,128)(2,1)S(1)}, bf16[512,256]{1,0:T(8,128)(2,1)S(1)}, u32[]{:S(2)}, u32[]{:S(2)}) collective-permute-start(bf16[512,256]{1,0:T(8,128)(2,1)S(1)} %collective-permute-done.16.refs_17_.refs_6_), channel_id=1, source_target_pairs={{0,4},{4,0},{8,12},{12,8},{1,5},{5,1},{9,13},{13,9},{2,6},{6,2},{1... | collective-permute-start | bytes 786440 | tf_op jit(solution)/shard_map/ppermute | solution.py:517
  84.4 1.8 %collective-permute-start.25 = (bf16[512,256]{1,0:T(8,128)(2,1)S(1)}, bf16[512,256]{1,0:T(8,128)(2,1)S(1)}, u32[]{:S(2)}, u32[]{:S(2)}) collective-permute-start(bf16[512,256]{1,0:T(8,128)(2,1)S(1)} %collective-permute-done.24.refs_10_), channel_id=1, source_target_pairs={{0,4},{4,0},{8,12},{12,8},{1,5},{5,1},{9,13},{13,9},{2,6},{6,2},{1... | collective-permute-start | bytes 786440 | tf_op jit(solution)/shard_map/ppermute | solution.py:517
  84.5 8.0 %collective-permute-start.17 = (bf16[768,256]{1,0:T(8,128)(2,1)S(1)}, bf16[768,256]{1,0:T(8,128)(2,1)S(1)}, u32[]{:S(2)}, u32[]{:S(2)}) collective-permute-start(bf16[768,256]{1,0:T(8,128)(2,1)S(1)} %get-tuple-element.131.refs_0_), channel_id=1, source_target_pairs={{0,4},{4,0},{8,12},{12,8},{1,5},{5,1},{9,13},{13,9},{2,6},{6,2},{1... | collective-permute-start | bytes 1179656 | tf_op jit(solution)/shard_map/ppermute | solution.py:517
  92.4 1.7 %collective-permute-start.26 = (bf16[768,256]{1,0:T(8,128)(2,1)S(1)}, bf16[768,256]{1,0:T(8,128)(2,1)S(1)}, u32[]{:S(2)}, u32[]{:S(2)}) collective-permute-start(bf16[768,256]{1,0:T(8,128)(2,1)S(1)} %collective-permute-done.18.refs_2_), channel_id=1, source_target_pairs={{0,4},{4,0},{8,12},{12,8},{1,5},{5,1},{9,13},{13,9},{2,6},{6,2},{1... | collective-permute-start | bytes 1179656 | tf_op jit(solution)/shard_map/ppermute | solution.py:517
